TPU v7x, 32 devices: a whole 2x2x4 slice. The times are simulated.
32 devices in a mesh: ctx: 32 (over z, y, x, core), tp: 1.
Axes of the slice: x: 2, y: 2, z: 4, core: 2. Of those that a mesh axis runs over, the one named last changes fastest.
Arguments:
- x_raw: bfloat16 [4096, 2560], P('ctx', 'tp'), may hold values from -6 to 6
- bc_raw: bfloat16 [4096, 256], P('ctx'), may hold values from -6 to 6
- gate_branch: bfloat16 [4096, 2560], P('ctx', 'tp'), may hold values from -6 to 6
- dt_raw: float32 [4096, 40], P('ctx', 'tp'), may hold values from -2 to 4
- conv_x: float32 [4, 2560], P(None, 'tp'), may hold values from -3 to 3
- conv_x_bias: float32 [2560], P('tp'), may hold values from -0.75 to -0.15
- conv_bc: float32 [4, 256], replicated, may hold values from -3 to 3
- conv_bc_bias: float32 [256], replicated, may hold values from -0.75 to -0.15
- dt_bias: float32 [40], P('tp'), may hold values from -4.2 to -3.6
- a_log: float32 [40], P('tp'), may hold values from -10 to 2
- d_skip: float32 [40], P('tp'), may hold values from 0.5 to 2
- out_weight: bfloat16 [2560, 2560], P('tp'), may hold values from -0.125 to 0.125
- grad_out: bfloat16 [4096, 2560], P('ctx'), may hold values from -6 to 6
Outputs:
- grad_x_conv: bfloat16 [4096, 2560], P('ctx', 'tp')
- grad_bc_conv: bfloat16 [4096, 256], P('ctx')
- grad_z: bfloat16 [4096, 2560], P('ctx', 'tp')
- grad_dt_raw: float32 [4096, 40], P('ctx', 'tp')
- out_weight_grad: float32 [2560, 2560], P('ctx', 'tp')
All inputs are finite; a program needn't handle non-finite values.
Results may differ from a plain program's by a relative error of at most 0.003.
Values may be sent and summed in bfloat16 or wider, within the bound.
No kernel may reach another device: no remote copies, remote signals or barrier semaphores. Data moves between devices by JAX's collectives and lax.ppermute only.
A program may use at most 192 MiB of HBM per device.

v0:
```python
import functools

import jax
import jax.numpy as jnp
from jax import lax
from jax.experimental import pallas as pl
from jax.experimental.pallas import tpu as pltpu
from jax.sharding import PartitionSpec as P

KERNEL = 4
LANES = 128
F32 = jnp.float32
BF16 = jnp.bfloat16
NN = ((1,), (0,))
NT = ((1,), (1,))
HIGH = lax.Precision.HIGHEST
MIB = 1024 * 1024


def call(kernel, out_shapes, operands, flops, vmem, scratch=(), specs=None):
    extra = {} if specs is None else {"in_specs": specs}
    moved = sum(a.size * a.dtype.itemsize for a in (*operands, *out_shapes))
    return pl.pallas_call(
        kernel,
        out_shape=tuple(out_shapes),
        scratch_shapes=list(scratch),
        compiler_params=pltpu.CompilerParams(vmem_limit_bytes=vmem * MIB),
        cost_estimate=pl.CostEstimate(flops=flops, bytes_accessed=moved, transcendentals=0),
        **extra,
    )(*operands)


def shape(dims, dtype=F32):
    return jax.ShapeDtypeStruct(dims, dtype)


def split(value):
    high = value.astype(BF16)
    return high, (value - high.astype(F32)).astype(BF16)


def dot(a, b, dims):
    return lax.dot_general(a, b, (dims, ((), ())), preferred_element_type=F32)


def dot3(a, b, dims=NN):
    return dot(a[0], b[0], dims) + (dot(a[0], b[1], dims) + dot(a[1], b[0], dims))


def sigmoid(value):
    return 1.0 / (1.0 + jnp.exp(-value))


def lane_ids(rows, cols=LANES):
    return lax.broadcasted_iota(jnp.int32, (rows, cols), 1)


def row_ids(rows, cols=LANES):
    return lax.broadcasted_iota(jnp.int32, (rows, cols), 0)


def spread(columns, block, heads, size):
    first = block * heads
    lanes = lane_ids(columns.shape[0])
    wide = jnp.broadcast_to(columns[:, first : first + 1], (columns.shape[0], LANES))
    for k in range(1, heads):
        wide = jnp.where(lanes >= k * size, columns[:, first + k : first + k + 1], wide)
    return wide


def head_of(block, heads, size):
    inner = row_ids(LANES)
    target = lane_ids(LANES)
    result = jnp.zeros((LANES, LANES), F32)
    for k in range(heads):
        here = (inner >= k * size) & (inner < (k + 1) * size) & (target == block * heads + k)
        result = jnp.where(here, 1.0, result)
    return result.astype(BF16)


def stacked(value, heads, size):
    lanes = lane_ids(value.shape[0])
    return jnp.concatenate(
        [jnp.where((lanes >= k * size) & (lanes < (k + 1) * size), value, 0.0) for k in range(heads)],
        axis=0,
    )


def up8(value):
    return -(-value // 8) * 8


def notes_of(rows):
    return -(-rows // LANES)


def exponent_of(block):
    top = jnp.max(jnp.max(jnp.abs(block), axis=0, keepdims=True), axis=1, keepdims=True)
    return jnp.floor(jnp.log2(jnp.maximum(jnp.broadcast_to(top, (1, LANES)), 1e-30)))


def write_block(message, at, first, block, decays, exponent):
    rows = block.shape[0]
    padded = up8(rows)
    message[at, first : first + rows, :] = block * jnp.exp2(13.0 - exponent)
    if padded > rows:
        message[at, first + rows : first + padded, :] = jnp.zeros((padded - rows, LANES), F32)
    highs = [d.astype(BF16).astype(F32) for d in decays]
    lows = [d - h for d, h in zip(decays, highs)]
    place = row_ids(8)
    notes = jnp.broadcast_to(exponent, (8, LANES))
    for k, line in enumerate(highs + lows):
        notes = jnp.where(place == k, line, notes)
    message[at, first + padded : first + padded + 8, :] = notes


def decay_tables(last_exp, heads, size, rows, count):
    shift = size.bit_length() - 1
    tables = []
    for d in range(count):
        lines = []
        for k in range(notes_of(rows)):
            first = rows * d + LANES * k
            owner = lax.shift_right_logical(lane_ids(1) + first, shift)
            table = jnp.zeros((1, LANES), F32)
            for h in range(first // size, min(heads, (first + LANES - 1) // size + 1)):
                table = jnp.where(owner == h, last_exp[:, h : h + 1], table)
            lines.append(table)
        tables.append(lines)
    return tables


def pack_blocks(source, message, last_exp, size, rows):
    count = message.shape[0]
    tables = decay_tables(last_exp, source.shape[0] // size, size, rows, count)
    for d in range(count):
        block = source[rows * d : rows * (d + 1), :]
        write_block(message, d, 0, block, tables[d], exponent_of(block))


def decay_lines(message, at, rows):
    padded, lines = up8(rows), notes_of(rows)
    return [
        message[at, padded + k : padded + k + 1, :] + message[at, padded + lines + k : padded + lines + k + 1, :]
        for k in range(lines)
    ]


def decay_columns(message, rows):
    padded, lines = up8(rows), notes_of(rows)
    turned = [
        jnp.transpose(message[:, padded + k, :] + message[:, padded + lines + k, :]) for k in range(lines)
    ]
    return jnp.concatenate(turned, axis=0)[0:rows]


def read_block(message, at, rows):
    padded = up8(rows)
    return message[at, 0:rows, :] * jnp.exp2(message[at, padded + 7 : padded + 8, :] - 13.0)


def unpack_blocks(message, target, rows):
    for d in range(message.shape[0]):
        target[rows * d : rows * (d + 1), :] = read_block(message, d, rows)


def total_kernel(rows, reverse, held_ref, out_ref):
    count = held_ref.shape[0]
    columns = decay_columns(held_ref, rows)
    state = None
    for s in range(count - 1, -1, -1) if reverse else range(count):
        block = read_block(held_ref, s, rows)
        state = block if state is None else columns[:, s : s + 1] * state + block
    decays = decay_lines(held_ref, 0, rows)
    for s in range(1, count):
        decays = [a * b for a, b in zip(decays, decay_lines(held_ref, s, rows))]
    write_block(out_ref, 0, 0, state, decays, exponent_of(state))


def fold_kernel(rows, reverse, held_ref, *refs):
    others, out_ref = refs[:-1], refs[-1]
    count = held_ref.shape[0]
    columns = decay_columns(held_ref, rows)
    state = jnp.zeros((rows, LANES), F32)
    for other in reversed(others):
        state = decay_columns(other, rows) * state + read_block(other, 0, rows)
    for s in range(count - 1, -1, -1) if reverse else range(count):
        write_block(out_ref, s, 0, state, [], exponent_of(state))
        if s != (0 if reverse else count - 1):
            state = columns[:, s : s + 1] * state + read_block(held_ref, s, rows)


def prepare_kernel(
    heads_in, size, rows, x_ref, rim_ref, bc_ref, rim_bc_ref, wx_ref, bx_ref, wbc_ref, bbc_ref, dt_ref,
    per_ref, act_ref, slope_ref, abc_ref, sbc_ref, step_ref, ld_ref, stept_ref, ldt_ref, dtw_ref, perw_ref, msg_ref,
    xs_ref, bs_ref, st_ref,
):
    length = x_ref.shape[0]
    blocks = x_ref.shape[1] // LANES

    def convolved(raw, rim, padded, weight, bias, cols):
        padded[0:8, cols] = rim[:, cols].astype(F32)[8:16]
        padded[8 : 8 + length, cols] = raw[:, cols].astype(F32)
        pre = bias[:, cols] + weight[0:1, cols] * padded[5 : 5 + length, cols]
        for k in range(1, KERNEL):
            pre = pre + weight[k : k + 1, cols] * padded[5 + k : 5 + k + length, cols]
        gate = sigmoid(pre)
        return pre * gate, gate * (1.0 + pre * (1.0 - gate))

    for j in range(bc_ref.shape[1] // LANES):
        cols = slice(j * LANES, (j + 1) * LANES)
        value, slope = convolved(bc_ref, rim_bc_ref, bs_ref, wbc_ref, bbc_ref, cols)
        abc_ref[:, cols] = value
        sbc_ref[:, cols] = slope
    b_rows = split(abc_ref[:, 0:LANES])
    heads = dt_ref.shape[1]
    dtw_ref[...] = jnp.zeros_like(dtw_ref)
    dtw_ref[:, 0:heads] = dt_ref[...]
    perw_ref[...] = jnp.zeros_like(perw_ref)
    perw_ref[0:2, 0:heads] = per_ref[...]
    raised = dtw_ref[...] + perw_ref[0:1, :]
    dtw_ref[...] = raised
    step = jnp.maximum(raised, 0.0) + jnp.log1p(jnp.exp(-jnp.abs(raised)))
    lower = jnp.where(row_ids(length) >= lane_ids(length), 1.0, 0.0)
    ld = lax.dot_general(
        lower, step * -jnp.exp(perw_ref[1:2, :]), (NN, ((), ())), precision=HIGH, preferred_element_type=F32
    )
    step_ref[...] = step
    ld_ref[...] = ld
    stept_ref[...] = step.T
    ldt_ref[...] = ld.T
    last = ld[length - 1 : length]
    weight = jnp.exp(last - ld) * step
    for j in range(blocks):
        cols = slice(j * LANES, (j + 1) * LANES)
        value, slope = convolved(x_ref, rim_ref, xs_ref, wx_ref, bx_ref, cols)
        act_ref[:, cols] = value
        slope_ref[:, cols] = slope
        scaled = value * spread(weight, j, heads_in, size)
        st_ref[cols, :] = dot3(split(scaled.T), b_rows)
    pack_blocks(st_ref, msg_ref, jnp.exp(last), size, rows)


def grad_kernel(heads_in, size, rows, gy_ref, abc_ref, ld_ref, msg_ref, st_ref):
    length = gy_ref.shape[0]
    c_rows = split(abc_ref[:, LANES : 2 * LANES])
    grown = jnp.exp(ld_ref[...])
    for j in range(gy_ref.shape[1] // LANES):
        cols = slice(j * LANES, (j + 1) * LANES)
        scaled = gy_ref[:, cols] * spread(grown, j, heads_in, size)
        st_ref[cols, :] = dot3(split(scaled.T), c_rows)
    pack_blocks(st_ref, msg_ref, grown[length - 1 : length], size, rows)


def gate_kernel(go_ref, w_ref, gate_ref, gg_ref, gy_ref):
    grad = dot(w_ref[...], go_ref[...], NT).T
    gate = gate_ref[...].astype(F32)
    gg_ref[...] = grad
    gy_ref[...] = grad * (gate * sigmoid(gate))


def local_kernel(
    heads_in, size, act_ref, gy_ref, abc_ref, step_ref, ld_ref, stept_ref, ldt_ref, yw_ref, gw_ref, gbc_ref, sh_ref
):
    length = act_ref.shape[0]
    b_rows = split(abc_ref[:, 0:LANES])
    c_rows = split(abc_ref[:, LANES : 2 * LANES])
    scores = dot3(c_rows, b_rows, NT)
    turned = dot3(b_rows, c_rows, NT)
    causal = row_ids(length) >= lane_ids(length)
    causal_t = row_ids(length) <= lane_ids(length)
    sh_ref[...] = jnp.zeros_like(sh_ref)
    for j in range(act_ref.shape[1] // LANES):
        cols = slice(j * LANES, (j + 1) * LANES)
        mixes, mixes_t, steps = [], [], []
        for h in range(j * heads_in, (j + 1) * heads_in):
            column, row = ld_ref[:, h : h + 1], ldt_ref[h : h + 1, :]
            decays = jnp.exp(jnp.where(causal, column - row, -1e30))
            stepped = decays * stept_ref[h : h + 1, :]
            decays_t = jnp.exp(jnp.where(causal_t, row - column, -1e30))
            steps.append(stepped)
            mixes.append(stepped * scores)
            mixes_t.append(decays_t * turned * step_ref[:, h : h + 1])
        inputs = act_ref[:, cols]
        grad_y = gy_ref[:, cols]
        inputs_s = stacked(inputs, heads_in, size)
        grads_s = split(stacked(grad_y, heads_in, size))
        yw_ref[:, cols] = dot3(split(jnp.concatenate(mixes, axis=1)), split(inputs_s))
        gw_ref[:, cols] = dot3(split(jnp.concatenate(mixes_t, axis=1)), grads_s)
        products = dot3(grads_s, split(inputs), NT)
        total = sh_ref[...]
        for k in range(heads_in):
            total = total + steps[k] * products[k * length : (k + 1) * length]
        sh_ref[...] = total
    shared = sh_ref[...]
    gbc_ref[:, 0:LANES] = dot3(split(shared.T), c_rows)
    gbc_ref[:, LANES : 2 * LANES] = dot3(split(shared), b_rows)


def place_of(channel, share, size):
    if share > LANES:
        if channel < LANES * size:
            return channel // LANES, channel % LANES
        rest = share - LANES
        return (channel - LANES * size) // rest, LANES + (channel - LANES * size) % rest
    return channel // share, channel % share


def forward_kernel(
    heads_in, size, rows, msg_ref, act_ref, gate_ref, abc_ref, ld_ref, yw_ref, skip_ref, gt_ref, ys_ref, st_ref
):
    share = gt_ref.shape[1]
    unpack_blocks(msg_ref, st_ref, rows)
    c_rows = split(abc_ref[:, LANES : 2 * LANES])
    grown = jnp.exp(ld_ref[...])
    for j in range(act_ref.shape[1] // LANES):
        cols = slice(j * LANES, (j + 1) * LANES)
        carried = dot3(c_rows, split(st_ref[cols, :]), NT)
        within = yw_ref[:, cols] + spread(grown, j, heads_in, size) * carried
        ys_ref[:, cols] = within
        output = within + skip_ref[:, cols] * act_ref[:, cols]
        gate = gate_ref[:, cols].astype(F32)
        turned = (output * (gate * sigmoid(gate))).T.astype(BF16)
        for k in range(0, LANES, 16):
            to, at = place_of(j * LANES + k, share, gt_ref.shape[0])
            gt_ref[to, at : at + 16, :] = turned[k : k + 16]


def backward_kernel(
    heads_in, size, rows, msg_ref, msgf_ref, act_ref, slope_ref, gy_ref, abc_ref, step_ref, ld_ref, gw_ref,
    gbcl_ref, ys_ref, gg_ref, gate_ref, skip_ref, dtw_ref, perw_ref, gx_ref, gbc_ref, gdt_ref, gz_ref,
    ca_ref, st_ref, cs_ref,
):
    length = act_ref.shape[0]
    unpack_blocks(msg_ref, ca_ref, rows)
    unpack_blocks(msgf_ref, st_ref, rows)
    b_rows = split(abc_ref[:, 0:LANES])
    ld = ld_ref[...]
    step = step_ref[...]
    last = ld[length - 1 : length]
    grown = jnp.exp(ld)
    weight = jnp.exp(last - ld) * step
    sums = jnp.zeros((length, LANES), F32)
    sums_y = jnp.zeros((length, LANES), F32)
    leaving = jnp.zeros((8, LANES), F32)
    grad_b = gbcl_ref[:, 0:LANES]
    grad_c = gbcl_ref[:, LANES : 2 * LANES]
    cs_ref[...] = jnp.zeros_like(cs_ref)
    for j in range(act_ref.shape[1] // LANES):
        cols = slice(j * LANES, (j + 1) * LANES)
        inputs = act_ref[:, cols]
        grad_y = gy_ref[:, cols]
        carry = ca_ref[cols, :]
        state = st_ref[cols, :]
        carry_s = split(carry)
        wide = spread(weight, j, heads_in, size)
        gone = wide * dot3(b_rows, carry_s, NT)
        grad_in = gw_ref[:, cols] + gone
        gx_ref[:, cols] = ((skip_ref[:, cols] * grad_y + grad_in) * slope_ref[:, cols]).astype(BF16)
        onehot = head_of(j, heads_in, size)
        within = ys_ref[:, cols]
        gate = gate_ref[:, cols].astype(F32)
        opened = sigmoid(gate)
        output = within + skip_ref[:, cols] * inputs
        gz_ref[:, cols] = (gg_ref[:, cols] * output * (opened * (1.0 + gate * (1.0 - opened)))).astype(BF16)
        high, low = split(grad_y * within)
        sums_y = sums_y + (dot(high, onehot, NN) + dot(low, onehot, NN))
        high, low = split(inputs * grad_in)
        sums = sums + (dot(high, onehot, NN) + dot(low, onehot, NN))
        folded = jnp.sum((inputs * gone).reshape(length // 8, 8, LANES), axis=0)
        high, low = split(folded)
        leaving = leaving + (dot(high, onehot, NN) + dot(low, onehot, NN))
        product = carry * state
        for k in range(heads_in):
            h = j * heads_in + k
            cs_ref[h : h + 1, :] = jnp.sum(product[k * size : (k + 1) * size], axis=0, keepdims=True)
        grad_b = grad_b + dot3(split(wide * inputs), carry_s)
        grad_c = grad_c + dot3(split(spread(grown, j, heads_in, size) * grad_y), split(state))
    gbc_ref[:, 0:LANES] = grad_b
    gbc_ref[:, LANES : 2 * LANES] = grad_c
    both = lax.dot_general(
        jnp.ones((8, LANES), F32), cs_ref[...], (NT, ((), ())), precision=HIGH, preferred_element_type=F32
    )
    constant = jnp.sum(leaving, axis=0, keepdims=True) + jnp.exp(last) * both[0:1]
    upper = jnp.where(row_ids(length) <= lane_ids(length), 1.0, 0.0)
    grad_rate = constant + lax.dot_general(
        upper, sums_y - sums, (NN, ((), ())), precision=HIGH, preferred_element_type=F32
    )
    grad_step = sums / step - jnp.exp(perw_ref[1:2, :]) * grad_rate
    gdt_ref[...] = (grad_step * sigmoid(dtw_ref[...]))[:, 0 : gdt_ref.shape[1]]


def product_kernel(rows, held_ref, go_ref, out_ref, lhs_ref):
    size, share, length = held_ref.shape

    @pl.when(pl.program_id(0) == 0)
    def _():
        for s in range(size):
            lhs_ref[:, s * length : (s + 1) * length] = held_ref[s]

    result = dot(lhs_ref[...], go_ref[...], NN).T
    for d in range(out_ref.shape[0]):
        block = result[rows * d : rows * (d + 1)]
        if share > LANES:
            rest = share - LANES
            across = LANES // rest
            out_ref[d, 0:rows, :] = block[:, 0:LANES].astype(BF16)
            for k in range(0, rows // 16, across):
                pieces = [block[16 * m : 16 * m + 16, LANES:] for m in range(k, min(k + across, rows // 16))]
                if len(pieces) < across:
                    pieces.append(jnp.zeros((16, LANES - rest * len(pieces)), F32))
                at = rows + 16 * (k // across)
                out_ref[d, at : at + 16, :] = jnp.concatenate(pieces, axis=1).astype(BF16)
        else:
            out_ref[d] = block.astype(BF16)


def assemble_kernel(rows, size, share, parts_ref, out_ref):
    count = parts_ref.shape[0]

    def total(c, first, last):
        found = parts_ref[c, first:last, :].astype(F32)
        for s in range(c + size, count, size):
            found = found + parts_ref[s, first:last, :].astype(F32)
        return found

    if share > LANES:
        rest = share - LANES
        across = LANES // rest
        for c in range(size):
            out_ref[:, c * LANES : (c + 1) * LANES] = total(c, 0, rows)
            at = size * LANES + rest * c
            for k in range(0, rows // 16, across):
                extra = total(c, rows + 16 * (k // across), rows + 16 * (k // across) + 16)
                for m in range(k, min(k + across, rows // 16)):
                    lanes = slice(rest * (m - k), rest * (m - k + 1))
                    out_ref[16 * m : 16 * m + 16, at : at + rest] = extra[:, lanes]
    else:
        for c in range(size):
            out_ref[:, c * share : (c + 1) * share] = total(c, 0, rows)


def exchange(message, groups=None):
    half = message.astype(jnp.float16)
    return lax.all_to_all(half, "ctx", 0, 0, axis_index_groups=groups, tiled=True)


def groups_of(count, size):
    return [list(range(at, at + size)) for at in range(0, count, size)]


def enter(held, rows, reverse):
    size = held.shape[0]
    count = lax.axis_size("ctx")
    (total,) = call(
        functools.partial(total_kernel, rows, reverse), [shape((1, *held.shape[1:]))], [held], 4 * held.size, 12
    )
    total = total.astype(jnp.float16)
    others = []
    for hops in range(size, count, size):
        pairs = [(at, at + hops) for at in range(count - hops)]
        if reverse:
            pairs = [(b, a) for a, b in pairs]
        others.append(lax.ppermute(total, "ctx", pairs).astype(F32))
    (folded,) = call(
        functools.partial(fold_kernel, rows, reverse), [shape(held.shape)], [held, *others], 8 * held.size, 12
    )
    return folded


def group_of(count):
    for size in (16, 8, 4, 2):
        if count % size == 0:
            return size
    return 1


def from_behind(value, axis):
    count = lax.axis_size(axis)
    return lax.ppermute(value, axis, [(source, source + 1) for source in range(count - 1)])


def per_device(
    x_raw,
    bc_raw,
    gate_branch,
    dt_raw,
    conv_x,
    conv_x_bias,
    conv_bc,
    conv_bc_bias,
    dt_bias,
    a_log,
    d_skip,
    out_weight,
    grad_out,
):
    length, head_count = dt_raw.shape
    channels = x_raw.shape[1]
    width = grad_out.shape[1]
    head_size = channels // head_count
    heads_in = LANES // head_size
    count = lax.axis_size("ctx")
    plane = min(8, group_of(count))
    planes = groups_of(count, plane)
    rows = channels // plane
    size = group_of(count)
    share = channels // size
    groups = groups_of(count, size)
    gathered = lax.all_gather(grad_out, "ctx", axis_index_groups=groups, tiled=True)

    rim = from_behind(jnp.concatenate([x_raw[length - 16 :], bc_raw[length - 16 :]], axis=1), "ctx")
    skip = jnp.repeat(d_skip, head_size)[None, :]
    whole = (length, channels)
    square = (length, LANES)
    block = up8(rows) + 8
    stored = pltpu.VMEM((channels, LANES), F32)
    unit = 2 * length * channels * LANES

    act_x, slope_x, act_bc, slope_bc, step, ld, step_t, ld_t, raised, per_head, message = call(
        functools.partial(prepare_kernel, heads_in, head_size, rows),
        [shape(whole), shape(whole), shape(bc_raw.shape), shape(bc_raw.shape)]
        + [shape(square)] * 2
        + [shape((LANES, length))] * 2
        + [shape(square), shape((8, LANES))]
        + [shape((plane, block, LANES))],
        [
            x_raw,
            rim[:, :channels],
            bc_raw,
            rim[:, channels:],
            conv_x,
            conv_x_bias[None, :],
            conv_bc,
            conv_bc_bias[None, :],
            dt_raw,
            jnp.stack([dt_bias, a_log]),
        ],
        20 * unit,
        20,
        [
            pltpu.VMEM((length + 8, channels), F32),
            pltpu.VMEM((length + 8, bc_raw.shape[1]), F32),
            stored,
        ],
    )
    message, grad_out_then = lax.optimization_barrier((message, grad_out))
    held_state = exchange(message, planes).astype(F32)
    part = 640 if channels % 640 == 0 else channels
    grad_gated, grad_y = pl.pallas_call(
        gate_kernel,
        grid=(channels // part,),
        in_specs=[
            pl.BlockSpec((length, width), lambda i: (0, 0)),
            pl.BlockSpec((part, width), lambda i: (i, 0)),
            pl.BlockSpec((length, part), lambda i: (0, i)),
        ],
        out_specs=(pl.BlockSpec((length, part), lambda i: (0, i)), pl.BlockSpec((length, part), lambda i: (0, i))),
        out_shape=(shape(whole), shape(whole)),
        compiler_params=pltpu.CompilerParams(vmem_limit_bytes=56 * MIB),
        cost_estimate=pl.CostEstimate(
            flops=2 * length * channels * width, bytes_accessed=2 * channels * width, transcendentals=0
        ),
    )(grad_out_then, out_weight, gate_branch)
    (message,) = call(
        functools.partial(grad_kernel, heads_in, head_size, rows),
        [shape((plane, block, LANES))],
        [grad_y, act_bc, ld],
        10 * unit,
        12,
        [stored],
    )
    message, held_state = lax.optimization_barrier((message, held_state))
    held_carry = exchange(message, planes)
    y_within, grad_within, grad_bc_within = call(
        functools.partial(local_kernel, heads_in, head_size),
        [shape(whole), shape(whole), shape(act_bc.shape)],
        [act_x, grad_y, act_bc, step, ld, step_t, ld_t],
        40 * unit,
        16,
        [pltpu.VMEM(square, F32)],
    )
    folded, held_carry = lax.optimization_barrier((enter(held_state, rows, False), held_carry))
    state_message = exchange(folded, planes).astype(F32)
    gated, y_ahead = call(
        functools.partial(forward_kernel, heads_in, head_size, rows),
        [shape((size, share, length), BF16), shape(whole)],
        [state_message, act_x, gate_branch, act_bc, ld, y_within, skip],
        20 * unit,
        16,
        [stored],
    )
    held = lax.all_to_all(gated, "ctx", 0, 0, axis_index_groups=groups, tiled=True)
    entered, held = lax.optimization_barrier((enter(held_carry.astype(F32), rows, True), held))
    carry_message = exchange(entered, planes).astype(F32)
    out_rows = width // count
    part = width
    for candidate in (640, 1280):
        if width % candidate == 0 and candidate % out_rows == 0:
            part = candidate
            break
    dims = (out_rows, share)
    if share > LANES:
        dims = (out_rows + 16 * (-(-(out_rows // 16) // (LANES // (share - LANES)))), LANES)
    partial = pl.pallas_call(
        functools.partial(product_kernel, out_rows),
        grid=(width // part,),
        in_specs=[
            pl.BlockSpec((size, share, length), lambda i: (0, 0, 0)),
            pl.BlockSpec((size * length, part), lambda i: (0, i)),
        ],
        out_specs=pl.BlockSpec((part // out_rows, *dims), lambda i: (i, 0, 0)),
        out_shape=shape((count, *dims), BF16),
        scratch_shapes=[pltpu.VMEM((share, size * length), BF16)],
        compiler_params=pltpu.CompilerParams(vmem_limit_bytes=48 * MIB),
        cost_estimate=pl.CostEstimate(
            flops=2 * size * length * share * width, bytes_accessed=2 * size * length * width, transcendentals=0
        ),
    )(held, gathered)
    parts = lax.all_to_all(partial, "ctx", 0, 0, tiled=True)
    (weight_grad,) = call(
        functools.partial(assemble_kernel, out_rows, size, share),
        [shape((out_rows, channels))],
        [parts],
        2 * parts.size,
        12,
    )
    grad_x_conv, grad_bc, grad_dt_raw, grad_z = call(
        functools.partial(backward_kernel, heads_in, head_size, rows),
        [shape(whole, BF16), shape(act_bc.shape), shape(dt_raw.shape), shape(whole, BF16)],
        [
            carry_message,
            state_message,
            act_x,
            slope_x,
            grad_y,
            act_bc,
            step,
            ld,
            grad_within,
            grad_bc_within,
            y_ahead,
            grad_gated,
            gate_branch,
            skip,
            raised,
            per_head,
        ],
        40 * unit,
        48,
        [stored, stored, pltpu.VMEM((LANES, LANES), F32)],
    )
    grad_bc_conv = (lax.psum(grad_bc, "tp") * slope_bc).astype(BF16)
    return (grad_x_conv, grad_bc_conv, grad_z, grad_dt_raw, weight_grad)


def solution(mesh):
    placed = (
        P("ctx", "tp"),
        P("ctx", None),
        P("ctx", "tp"),
        P("ctx", "tp"),
        P(None, "tp"),
        P("tp"),
        P(),
        P(),
        P("tp"),
        P("tp"),
        P("tp"),
        P("tp", None),
        P("ctx", None),
    )
    return jax.shard_map(
        per_device,
        mesh=mesh,
        in_specs=placed,
        out_specs=(P("ctx", "tp"), P("ctx", None), P("ctx", "tp"), P("ctx", "tp"), P("ctx", "tp")),
        check_vma=False,
    )
```

profile of v0, /device:TPU:0, one launch (start us, length us, event | category | flops | bytes accessed | tf_op | source)
XLA Modules:
  0.0 174.2 jit_solution(16063310166272039530)
XLA Ops:
  9.5 2.4 %collective-permute-start = (bf16[16,2816]{1,0:T(8,128)(2,1)S(1)}, bf16[16,2816]{1,0:T(8,128)(2,1)S(1)}, u32[]{:S(2)}, u32[]{:S(2)}) collective-permute-start(bf16[16,2816]{1,0:T(8,128)(2,1)S(1)} %pad_maximum_fusion), channel_id=1, source_target_pairs={{0,1},{1,2},{2,3},{3,4},{4,5},{5,6},{6,7},{7,8},{8,9},{9,10},{10,1... | collective-permute-start | bytes 270344 | tf_op jit(solution)/shard_map/ppermute | solution.py:480
  18.2 2.8 %shard_map.164 = (f32[128,2560]{1,0:T(8,128)S(1)}, f32[128,2560]{1,0:T(8,128)S(1)}, f32[128,256]{1,0:T(8,128)S(1)}, f32[128,256]{1,0:T(8,128)S(1)}, f32[128,128]...) custom-call(bf16[128,2560]{1,0:T(8,128)(2,1)S(1)} %copy-done.3, ...), custom_call_target="tpu_custom_call" | custom-call | flops 1677721600 | bytes 5446976 | tf_op jit(solution)/shard_map/pallas_call | solution.py:23
  24.8 6.4 %all-to-all-start = ((f16[8,328,128]{2,1,0:T(8,128)(2,1)}), f16[8,328,128]{2,1,0:T(8,128)(2,1)}, u32[]{:S(2)}, u32[]{:S(2)}) async-start(f16[8,328,128]{2,1,0:T(8,128)(2,1)} %convert_element_type.51), calls=%async_computation | async-start | bytes 1343488 | tf_op jit(solution)/shard_map/all_to_all | solution.py:445
  31.2 9.9 %shard_map.165 = (f32[128,2560]{1,0:T(8,128)}, f32[128,2560]{1,0:T(8,128)}) custom-call(bf16[128,2560]{1,0:T(8,128)(2,1)} %go_ref, bf16[2560,2560]{1,0:T(8,128)(2,1)} %w_ref.1, bf16[128,2560]{1,0:T(8,128)(2,1)} %gate_ref.5), custom_call_target="tpu_custom_call" | custom-call | flops 1677721600 | bytes 13107200 | tf_op jit(solution)/shard_map/pallas_call | solution.py:550
  42.5 1.6 shard_map.166
  44.0 6.1 %all-to-all-done = f16[8,328,128]{2,1,0:T(8,128)(2,1)} async-done(((f16[8,328,128]{2,1,0:T(8,128)(2,1)}), f16[8,328,128]{2,1,0:T(8,128)(2,1)}, u32[]{:S(2)}, u32[]{:S(2)}) %all-to-all-start) | async-done | bytes 671776 | tf_op jit(solution)/shard_map/all_to_all | solution.py:445
  52.3 4.2 %all-to-all-start.1 = ((f16[8,328,128]{2,1,0:T(8,128)(2,1)}), f16[8,328,128]{2,1,0:T(8,128)(2,1)}, u32[]{:S(2)}, u32[]{:S(2)}) async-start(f16[8,328,128]{2,1,0:T(8,128)(2,1)} %convert_element_type.57), calls=%async_computation.1 | async-start | bytes 1343488 | tf_op jit(solution)/shard_map/all_to_all | solution.py:445
  57.2 5.7 %collective-permute-start.1 = (f16[1,328,128]{2,1,0:T(8,128)(2,1)S(1)}, f16[1,328,128]{2,1,0:T(8,128)(2,1)S(1)}, u32[]{:S(2)}, u32[]{:S(2)}) collective-permute-start(f16[1,328,128]{2,1,0:T(8,128)(2,1)S(1)} %convert_element_type.53), channel_id=1, source_target_pairs={{0,8},{1,9},{2,10},{3,11},{4,12},{5,13},{6,14},{7,15},{8,16},{9,17... | collective-permute-start | bytes 251912 | tf_op jit(solution)/shard_map/ppermute | solution.py:464
  62.9 4.5 %collective-permute-start.2 = (f16[1,328,128]{2,1,0:T(8,128)(2,1)S(1)}, f16[1,328,128]{2,1,0:T(8,128)(2,1)S(1)}, u32[]{:S(2)}, u32[]{:S(2)}) collective-permute-start(f16[1,328,128]{2,1,0:T(8,128)(2,1)S(1)} %convert_element_type.53), channel_id=1, source_target_pairs={{0,16},{1,17},{2,18},{3,19},{4,20},{5,21},{6,22},{7,23},{8,24},{9,... | collective-permute-start | bytes 251912 | tf_op jit(solution)/shard_map/ppermute | solution.py:464
  68.8 2.5 %collective-permute-done.2 = f16[1,328,128]{2,1,0:T(8,128)(2,1)S(1)} collective-permute-done((f16[1,328,128]{2,1,0:T(8,128)(2,1)S(1)}, f16[1,328,128]{2,1,0:T(8,128)(2,1)S(1)}, u32[]{:S(2)}, u32[]{:S(2)}) %collective-permute-start.2) | collective-permute-done | bytes 84000 | tf_op jit(solution)/shard_map/ppermute | solution.py:464
  71.3 2.7 %collective-permute-done.3 = f16[1,328,128]{2,1,0:T(8,128)(2,1)S(1)} collective-permute-done((f16[1,328,128]{2,1,0:T(8,128)(2,1)S(1)}, f16[1,328,128]{2,1,0:T(8,128)(2,1)S(1)}, u32[]{:S(2)}, u32[]{:S(2)}) %collective-permute-start.3) | collective-permute-done | bytes 84000 | tf_op jit(solution)/shard_map/ppermute | solution.py:464
  76.3 4.5 %all-to-all-start.2 = ((f16[8,328,128]{2,1,0:T(8,128)(2,1)}), f16[8,328,128]{2,1,0:T(8,128)(2,1)}, u32[]{:S(2)}, u32[]{:S(2)}) async-start(f16[8,328,128]{2,1,0:T(8,128)(2,1)} %convert_element_type.63), calls=%async_computation.2 | async-start | bytes 1343488 | tf_op jit(solution)/shard_map/all_to_all | solution.py:445
  81.0 4.6 %shard_map.171 = (f32[128,2560]{1,0:T(8,128)S(1)}, f32[128,2560]{1,0:T(8,128)S(1)}, f32[128,256]{1,0:T(8,128)S(1)}) custom-call(f32[128,2560]{1,0:T(8,128)S(1)} %copy-done.12, f32[128,2560]{1,0:T(8,128)S(1)} %copy-done.6, f32[128,256]{1,0:T(8,128)S(1)} %get-tuple-element.38.abc_ref, f32[128,128]{1,0:T(8,128)S(1)} %get-tuple-element.46.step_ref, ...), custom_call_target="tpu_custom_call" | custom-call | flops 3355443200 | bytes 5767168 | tf_op jit(solution)/shard_map/pallas_call | solution.py:23
  88.4 4.2 %all-to-all-done.2 = f16[8,328,128]{2,1,0:T(8,128)(2,1)} async-done(((f16[8,328,128]{2,1,0:T(8,128)(2,1)}), f16[8,328,128]{2,1,0:T(8,128)(2,1)}, u32[]{:S(2)}, u32[]{:S(2)}) %all-to-all-start.2) | async-done | bytes 671776 | tf_op jit(solution)/shard_map/all_to_all | solution.py:445
  96.2 2.7 %shard_map.172 = (bf16[16,160,128]{2,1,0:T(8,128)(2,1)}, f32[128,2560]{1,0:T(8,128)S(1)}) custom-call(f32[8,328,128]{2,1,0:T(8,128)S(1)} %convert_element_type.64.msg_ref.msgf_ref, f32[128,2560]{1,0:T(8,128)S(1)} %copy-done.13, bf16[128,2560]{1,0:T(8,128)(2,1)S(1)} %copy-done.1, f32[128,256]{1,0:T(8,128)S(1)} %copy-done.20, ...), custom_call_target="tpu_custom_call" | custom-call | flops 1677721600 | bytes 6793216 | tf_op jit(solution)/shard_map/pallas_call | solution.py:23
  100.1 4.5 %all-to-all-start.3 = ((bf16[16,160,128]{2,1,0:T(8,128)(2,1)}), bf16[16,160,128]{2,1,0:T(8,128)(2,1)S(1)}, u32[]{:S(2)}, u32[]{:S(2)}) async-start(bf16[16,160,128]{2,1,0:T(8,128)(2,1)} %get-tuple-element.50), calls=%async_computation.3 | async-start | bytes 1310720 | tf_op jit(solution)/shard_map/all_to_all | solution.py:593
  110.4 7.9 %collective-permute-done.4 = f16[1,328,128]{2,1,0:T(8,128)(2,1)S(1)} collective-permute-done((f16[1,328,128]{2,1,0:T(8,128)(2,1)S(1)}, f16[1,328,128]{2,1,0:T(8,128)(2,1)S(1)}, u32[]{:S(2)}, u32[]{:S(2)}) %collective-permute-start.4) | collective-permute-done | bytes 84000 | tf_op jit(solution)/shard_map/ppermute | solution.py:464
  118.4 4.3 %collective-permute-done.6 = f16[1,328,128]{2,1,0:T(8,128)(2,1)S(1)} collective-permute-done((f16[1,328,128]{2,1,0:T(8,128)(2,1)S(1)}, f16[1,328,128]{2,1,0:T(8,128)(2,1)S(1)}, u32[]{:S(2)}, u32[]{:S(2)}) %collective-permute-start.6) | collective-permute-done | bytes 84000 | tf_op jit(solution)/shard_map/ppermute | solution.py:464
  125.1 3.7 %all-to-all-start.4 = ((f16[8,328,128]{2,1,0:T(8,128)(2,1)}), f16[8,328,128]{2,1,0:T(8,128)(2,1)S(1)}, u32[]{:S(2)}, u32[]{:S(2)}) async-start(f16[8,328,128]{2,1,0:T(8,128)(2,1)} %convert_element_type.65), calls=%async_computation.4 | async-start | bytes 1343488 | tf_op jit(solution)/shard_map/all_to_all | solution.py:445
  128.8 7.3 %shard_map.174 = bf16[32,112,128]{2,1,0:T(8,128)(2,1)} custom-call(bf16[16,160,128]{2,1,0:T(8,128)(2,1)S(1)} %all-to-all-done.3.held_ref, bf16[2048,2560]{1,0:T(8,128)(2,1)} %all-gather.2.cloned.1.call-done.go_ref), custom_call_target="tpu_custom_call" | custom-call | flops 1677721600 | bytes 10485760 | tf_op jit(solution)/shard_map/pallas_call | solution.py:605
  136.0 4.0 %all-to-all-done.4 = f16[8,328,128]{2,1,0:T(8,128)(2,1)S(1)} async-done(((f16[8,328,128]{2,1,0:T(8,128)(2,1)}), f16[8,328,128]{2,1,0:T(8,128)(2,1)S(1)}, u32[]{:S(2)}, u32[]{:S(2)}) %all-to-all-start.4) | async-done | bytes 671776 | tf_op jit(solution)/shard_map/all_to_all | solution.py:445
  140.1 3.0 %all-to-all-start.5 = ((bf16[32,112,128]{2,1,0:T(8,128)(2,1)}), bf16[32,112,128]{2,1,0:T(8,128)(2,1)S(1)}, u32[]{:S(2)}, u32[]{:S(2)}) async-start(bf16[32,112,128]{2,1,0:T(8,128)(2,1)} %shard_map.174), calls=%async_computation.5 | async-start | bytes 1835008 | tf_op jit(solution)/shard_map/all_to_all | solution.py:620
  146.4 7.7 %shard_map.173 = (bf16[128,2560]{1,0:T(8,128)(2,1)}, f32[128,256]{1,0:T(8,128)S(1)}, f32[128,40]{1,0:T(8,128)S(1)}, bf16[128,2560]{1,0:T(8,128)(2,1)}) custom-call(f32[8,328,128]{2,1,0:T(8,128)} %convert_element_type.66.msg_ref, f32[8,328,128]{2,1,0:T(8,128)} %copy-done, f32[128,2560]{1,0:T(8,128)S(1)} %copy-done.14, f32[128,2560]{1,0:T(8,128)S(1)} %copy-done.16, ...), custom_call_target="tpu_custom_call" | custom-call | flops 3355443200 | bytes 13142016 | tf_op jit(solution)/shard_map/pallas_call | solution.py:23
  155.4 10.8 %all-to-all-done.5.parts_ref = bf16[32,112,128]{2,1,0:T(8,128)(2,1)S(1)} async-done(((bf16[32,112,128]{2,1,0:T(8,128)(2,1)}), bf16[32,112,128]{2,1,0:T(8,128)(2,1)S(1)}, u32[]{:S(2)}, u32[]{:S(2)}) %all-to-all-start.5) | async-done | bytes 917536 | tf_op jit(solution)/shard_map/all_to_all | solution.py:620
  (107 shorter events, 41.6 us)
Async XLA Ops:
  7.2 121.6 %all-gather.2.cloned.1.call-start = ((), (), s32[]{:S(2)}) async-start(), calls=%async_computation.6 | async-start | bytes 11141120 | tf_op jit(solution)/shard_map/all_gather | solution.py:510
  9.5 4.6 %collective-permute-start = (bf16[16,2816]{1,0:T(8,128)(2,1)S(1)}, bf16[16,2816]{1,0:T(8,128)(2,1)S(1)}, u32[]{:S(2)}, u32[]{:S(2)}) collective-permute-start(bf16[16,2816]{1,0:T(8,128)(2,1)S(1)} %pad_maximum_fusion), channel_id=1, source_target_pairs={{0,1},{1,2},{2,3},{3,4},{4,5},{5,6},{6,7},{7,8},{8,9},{9,10},{10,1... | collective-permute-start | bytes 270344 | tf_op jit(solution)/shard_map/ppermute | solution.py:480
  23.9 57.1 %copy-start.19 = (f32[128,256]{1,0:T(8,128)}, f32[128,256]{1,0:T(8,128)S(1)}, u32[]{:S(2)}) copy-start(f32[128,256]{1,0:T(8,128)S(1)} %get-tuple-element.38.abc_ref) | copy-start | bytes 393220
  23.9 57.1 %copy-start.26 = (f32[128,128]{1,0:T(8,128)}, f32[128,128]{1,0:T(8,128)S(1)}, u32[]{:S(2)}) copy-start(f32[128,128]{1,0:T(8,128)S(1)} %get-tuple-element.46.step_ref) | copy-start | bytes 196612
  24.8 25.4 %all-to-all-start = ((f16[8,328,128]{2,1,0:T(8,128)(2,1)}), f16[8,328,128]{2,1,0:T(8,128)(2,1)}, u32[]{:S(2)}, u32[]{:S(2)}) async-start(f16[8,328,128]{2,1,0:T(8,128)(2,1)} %convert_element_type.51), calls=%async_computation | async-start | bytes 1343488 | tf_op jit(solution)/shard_map/all_to_all | solution.py:445
  52.3 23.1 %all-to-all-start.1 = ((f16[8,328,128]{2,1,0:T(8,128)(2,1)}), f16[8,328,128]{2,1,0:T(8,128)(2,1)}, u32[]{:S(2)}, u32[]{:S(2)}) async-start(f16[8,328,128]{2,1,0:T(8,128)(2,1)} %convert_element_type.57), calls=%async_computation.1 | async-start | bytes 1343488 | tf_op jit(solution)/shard_map/all_to_all | solution.py:445
  57.2 11.5 %collective-permute-start.1 = (f16[1,328,128]{2,1,0:T(8,128)(2,1)S(1)}, f16[1,328,128]{2,1,0:T(8,128)(2,1)S(1)}, u32[]{:S(2)}, u32[]{:S(2)}) collective-permute-start(f16[1,328,128]{2,1,0:T(8,128)(2,1)S(1)} %convert_element_type.53), channel_id=1, source_target_pairs={{0,8},{1,9},{2,10},{3,11},{4,12},{5,13},{6,14},{7,15},{8,16},{9,17... | collective-permute-start | bytes 251912 | tf_op jit(solution)/shard_map/ppermute | solution.py:464
  62.9 8.4 %collective-permute-start.2 = (f16[1,328,128]{2,1,0:T(8,128)(2,1)S(1)}, f16[1,328,128]{2,1,0:T(8,128)(2,1)S(1)}, u32[]{:S(2)}, u32[]{:S(2)}) collective-permute-start(f16[1,328,128]{2,1,0:T(8,128)(2,1)S(1)} %convert_element_type.53), channel_id=1, source_target_pairs={{0,16},{1,17},{2,18},{3,19},{4,20},{5,21},{6,22},{7,23},{8,24},{9,... | collective-permute-start | bytes 251912 | tf_op jit(solution)/shard_map/ppermute | solution.py:464
  67.4 6.5 %collective-permute-start.3 = (f16[1,328,128]{2,1,0:T(8,128)(2,1)S(1)}, f16[1,328,128]{2,1,0:T(8,128)(2,1)S(1)}, u32[]{:S(2)}, u32[]{:S(2)}) collective-permute-start(f16[1,328,128]{2,1,0:T(8,128)(2,1)S(1)} %convert_element_type.53), channel_id=1, source_target_pairs={{0,24},{1,25},{2,26},{3,27},{4,28},{5,29},{6,30},{7,31}} | collective-permute-start | bytes 251912 | tf_op jit(solution)/shard_map/ppermute | solution.py:464
  75.3 5.5 %copy-start.30 = (f32[40]{0:T(128)S(1)}, f32[40]{0:T(128)}, u32[]{:S(2)}) copy-start(f32[40]{0:T(128)} %param.23) | copy-start | bytes 484
  75.4 5.7 %copy-start.6 = (f32[128,2560]{1,0:T(8,128)S(1)}, f32[128,2560]{1,0:T(8,128)}, u32[]{:S(2)}) copy-start(f32[128,2560]{1,0:T(8,128)} %get-tuple-element.37.gy_ref) | copy-start | bytes 3932164
  76.3 4.7 %copy-start.12 = (f32[128,2560]{1,0:T(8,128)S(1)}, f32[128,2560]{1,0:T(8,128)}, u32[]{:S(2)}) copy-start(f32[128,2560]{1,0:T(8,128)} %copy-done.11) | copy-start | bytes 3932164
  76.3 16.3 %all-to-all-start.2 = ((f16[8,328,128]{2,1,0:T(8,128)(2,1)}), f16[8,328,128]{2,1,0:T(8,128)(2,1)}, u32[]{:S(2)}, u32[]{:S(2)}) async-start(f16[8,328,128]{2,1,0:T(8,128)(2,1)} %convert_element_type.63), calls=%async_computation.2 | async-start | bytes 1343488 | tf_op jit(solution)/shard_map/all_to_all | solution.py:445
  88.4 5.4 %copy-start.1 = (bf16[128,2560]{1,0:T(8,128)(2,1)S(1)}, bf16[128,2560]{1,0:T(8,128)(2,1)}, u32[]{:S(2)}) copy-start(bf16[128,2560]{1,0:T(8,128)(2,1)} %gate_ref.5) | copy-start | bytes 1966084
  88.4 5.4 %copy-start.13 = (f32[128,2560]{1,0:T(8,128)S(1)}, f32[128,2560]{1,0:T(8,128)}, u32[]{:S(2)}) copy-start(f32[128,2560]{1,0:T(8,128)} %copy-done.11) | copy-start | bytes 3932164
  93.8 5.1 %copy-start = (f32[8,328,128]{2,1,0:T(8,128)}, f32[8,328,128]{2,1,0:T(8,128)S(1)}, u32[]{:S(2)}) copy-start(f32[8,328,128]{2,1,0:T(8,128)S(1)} %convert_element_type.64.msg_ref.msgf_ref) | copy-start | bytes 4030468
  100.1 24.0 %all-to-all-start.3 = ((bf16[16,160,128]{2,1,0:T(8,128)(2,1)}), bf16[16,160,128]{2,1,0:T(8,128)(2,1)S(1)}, u32[]{:S(2)}, u32[]{:S(2)}) async-start(bf16[16,160,128]{2,1,0:T(8,128)(2,1)} %get-tuple-element.50), calls=%async_computation.3 | async-start | bytes 1310720 | tf_op jit(solution)/shard_map/all_to_all | solution.py:593
  106.5 11.8 %collective-permute-start.4 = (f16[1,328,128]{2,1,0:T(8,128)(2,1)S(1)}, f16[1,328,128]{2,1,0:T(8,128)(2,1)S(1)}, u32[]{:S(2)}, u32[]{:S(2)}) collective-permute-start(f16[1,328,128]{2,1,0:T(8,128)(2,1)S(1)} %convert_element_type.59), channel_id=1, source_target_pairs={{8,0},{9,1},{10,2},{11,3},{12,4},{13,5},{14,6},{15,7},{16,8},{17,9... | collective-permute-start | bytes 251912 | tf_op jit(solution)/shard_map/ppermute | solution.py:464
  107.8 10.6 %collective-permute-start.5 = (f16[1,328,128]{2,1,0:T(8,128)(2,1)S(1)}, f16[1,328,128]{2,1,0:T(8,128)(2,1)S(1)}, u32[]{:S(2)}, u32[]{:S(2)}) collective-permute-start(f16[1,328,128]{2,1,0:T(8,128)(2,1)S(1)} %convert_element_type.59), channel_id=1, source_target_pairs={{16,0},{17,1},{18,2},{19,3},{20,4},{21,5},{22,6},{23,7},{24,8},{25... | collective-permute-start | bytes 251912 | tf_op jit(solution)/shard_map/ppermute | solution.py:464
  109.1 13.6 %collective-permute-start.6 = (f16[1,328,128]{2,1,0:T(8,128)(2,1)S(1)}, f16[1,328,128]{2,1,0:T(8,128)(2,1)S(1)}, u32[]{:S(2)}, u32[]{:S(2)}) collective-permute-start(f16[1,328,128]{2,1,0:T(8,128)(2,1)S(1)} %convert_element_type.59), channel_id=1, source_target_pairs={{24,0},{25,1},{26,2},{27,3},{28,4},{29,5},{30,6},{31,7}} | collective-permute-start | bytes 251912 | tf_op jit(solution)/shard_map/ppermute | solution.py:464
  125.1 15.0 %all-to-all-start.4 = ((f16[8,328,128]{2,1,0:T(8,128)(2,1)}), f16[8,328,128]{2,1,0:T(8,128)(2,1)S(1)}, u32[]{:S(2)}, u32[]{:S(2)}) async-start(f16[8,328,128]{2,1,0:T(8,128)(2,1)} %convert_element_type.65), calls=%async_computation.4 | async-start | bytes 1343488 | tf_op jit(solution)/shard_map/all_to_all | solution.py:445
  140.1 4.3 %copy-start.27 = (f32[128,128]{1,0:T(8,128)S(1)}, f32[128,128]{1,0:T(8,128)}, u32[]{:S(2)}) copy-start(f32[128,128]{1,0:T(8,128)} %copy-done.26) | copy-start | bytes 196612
  140.1 4.3 %copy-start.29 = (f32[128,128]{1,0:T(8,128)S(1)}, f32[128,128]{1,0:T(8,128)}, u32[]{:S(2)}) copy-start(f32[128,128]{1,0:T(8,128)} %copy-done.28) | copy-start | bytes 196612
  140.1 26.2 %all-to-all-start.5 = ((bf16[32,112,128]{2,1,0:T(8,128)(2,1)}), bf16[32,112,128]{2,1,0:T(8,128)(2,1)S(1)}, u32[]{:S(2)}, u32[]{:S(2)}) async-start(bf16[32,112,128]{2,1,0:T(8,128)(2,1)} %shard_map.174), calls=%async_computation.5 | async-start | bytes 1835008 | tf_op jit(solution)/shard_map/all_to_all | solution.py:620
  (21 other events, 31.9 us)
Sparse Core Ops, SparseCore 0:
  9.6 77.1 all-gather.1
where the time goes:
time: 176 us; the launch traced here: 174 us
  starting transfers between devices  44.1 us (25%)
  waiting for transfers between devices  43.4 us (25%)
  Pallas kernels  41.7 us (24%)
  local copies, waits for them, and re-layouts  20.6 us (12%)
  between operations  14.5 us (8%)
  other arithmetic  9.92 us (6%)
    pallas_call x10, Pallas kernels, call(): pl.pallas_call(kernel, out_shape=tuple(out_shapes), scratch_shapes=list(s...  24.6 us
    all_to_all x4, starting transfers between devices, exchange(): lax.all_to_all(half, 'ctx', 0, 0, axis_index_groups=groups, tiled=True)  18.8 us
    unnamed x64, local copies, waits for them, and re-layouts  18.1 us
    ppermute x6, waiting for transfers between devices, enter(): others.append(lax.ppermute(total, 'ctx', pairs).astype(F32))  17.5 us
    ppermute x6, starting transfers between devices, enter(): others.append(lax.ppermute(total, 'ctx', pairs).astype(F32))  15.4 us
    all_to_all x4, waiting for transfers between devices, exchange(): lax.all_to_all(half, 'ctx', 0, 0, axis_index_groups=groups, tiled=True)  14.4 us
    all_to_all x1, waiting for transfers between devices, per_device(): parts = lax.all_to_all(partial, 'ctx', 0, 0, tiled=True)  10.8 us
    pallas_call x1, Pallas kernels, per_device(): pl.pallas_call(gate_kernel, grid=(channels // part,), in_specs=[pl.BlockS...  9.92 us
  transfers between devices with their start and end apart: 14, of which 8 were waited for; matrix products, arithmetic and copies ran while one was open for 8% of the time, Pallas kernels for 23%

commit v1 on v0

--- a/solution.py
+++ b/solution.py
@@ -15,6 +15,7 @@
 NT = ((1,), (1,))
 HIGH = lax.Precision.HIGHEST
 MIB = 1024 * 1024
+STREAMS = 4
 
 
 def call(kernel, out_shapes, operands, flops, vmem, scratch=(), specs=None):
@@ -390,7 +391,8 @@
     gdt_ref[...] = (grad_step * sigmoid(dtw_ref[...]))[:, 0 : gdt_ref.shape[1]]
 
 
-def product_kernel(rows, held_ref, go_ref, out_ref, lhs_ref):
+def product_kernel(rows, held_ref, *refs):
+    go_refs, out_ref, lhs_ref = refs[:-2], refs[-2], refs[-1]
     size, share, length = held_ref.shape
 
     @pl.when(pl.program_id(0) == 0)
@@ -398,7 +400,11 @@
         for s in range(size):
             lhs_ref[:, s * length : (s + 1) * length] = held_ref[s]
 
-    result = dot(lhs_ref[...], go_ref[...], NN).T
+    depth = go_refs[0].shape[0]
+    result = dot(lhs_ref[:, 0:depth], go_refs[0][...], NN)
+    for k in range(1, len(go_refs)):
+        result = result + dot(lhs_ref[:, k * depth : (k + 1) * depth], go_refs[k][...], NN)
+    result = result.T
     for d in range(out_ref.shape[0]):
         block = result[rows * d : rows * (d + 1)]
         if share > LANES:
@@ -449,13 +455,16 @@
     return [list(range(at, at + size)) for at in range(0, count, size)]
 
 
-def enter(held, rows, reverse):
+def group_total(held, rows, reverse):
+    (total,) = call(
+        functools.partial(total_kernel, rows, reverse), [shape((1, *held.shape[1:]))], [held], 4 * held.size, 12
+    )
+    return total.astype(jnp.float16)
+
+
+def enter(held, total, rows, reverse):
     size = held.shape[0]
     count = lax.axis_size("ctx")
-    (total,) = call(
-        functools.partial(total_kernel, rows, reverse), [shape((1, *held.shape[1:]))], [held], 4 * held.size, 12
-    )
-    total = total.astype(jnp.float16)
     others = []
     for hops in range(size, count, size):
         pairs = [(at, at + hops) for at in range(count - hops)]
@@ -537,7 +546,7 @@
             jnp.stack([dt_bias, a_log]),
         ],
         20 * unit,
-        20,
+        48,
         [
             pltpu.VMEM((length + 8, channels), F32),
             pltpu.VMEM((length + 8, bc_raw.shape[1]), F32),
@@ -557,7 +566,7 @@
         ],
         out_specs=(pl.BlockSpec((length, part), lambda i: (0, i)), pl.BlockSpec((length, part), lambda i: (0, i))),
         out_shape=(shape(whole), shape(whole)),
-        compiler_params=pltpu.CompilerParams(vmem_limit_bytes=56 * MIB),
+        compiler_params=pltpu.CompilerParams(vmem_limit_bytes=24 * MIB),
         cost_estimate=pl.CostEstimate(
             flops=2 * length * channels * width, bytes_accessed=2 * channels * width, transcendentals=0
         ),
@@ -570,7 +579,7 @@
         12,
         [stored],
     )
-    message, held_state = lax.optimization_barrier((message, held_state))
+    message, total = lax.optimization_barrier((message, group_total(held_state, rows, False)))
     held_carry = exchange(message, planes)
     y_within, grad_within, grad_bc_within = call(
         functools.partial(local_kernel, heads_in, head_size),
@@ -580,7 +589,8 @@
         16,
         [pltpu.VMEM(square, F32)],
     )
-    folded, held_carry = lax.optimization_barrier((enter(held_state, rows, False), held_carry))
+    folded, held_carry = lax.optimization_barrier((enter(held_state, total, rows, False), held_carry))
+    held_carry = held_carry.astype(F32)
     state_message = exchange(folded, planes).astype(F32)
     gated, y_ahead = call(
         functools.partial(forward_kernel, heads_in, head_size, rows),
@@ -590,8 +600,10 @@
         16,
         [stored],
     )
+    entered = enter(held_carry, group_total(held_carry, rows, True), rows, True)
+    gated, entered = lax.optimization_barrier((gated, entered))
     held = lax.all_to_all(gated, "ctx", 0, 0, axis_index_groups=groups, tiled=True)
-    entered, held = lax.optimization_barrier((enter(held_carry.astype(F32), rows, True), held))
+    entered, held = lax.optimization_barrier((entered, held))
     carry_message = exchange(entered, planes).astype(F32)
     out_rows = width // count
     part = width
@@ -607,7 +619,10 @@
         grid=(width // part,),
         in_specs=[
             pl.BlockSpec((size, share, length), lambda i: (0, 0, 0)),
-            pl.BlockSpec((size * length, part), lambda i: (0, i)),
+        ]
+        + [
+            pl.BlockSpec((size * length // STREAMS, part), functools.partial(lambda k, i: (k, i), k))
+            for k in range(STREAMS)
         ],
         out_specs=pl.BlockSpec((part // out_rows, *dims), lambda i: (i, 0, 0)),
         out_shape=shape((count, *dims), BF16),
@@ -616,7 +631,7 @@
         cost_estimate=pl.CostEstimate(
             flops=2 * size * length * share * width, bytes_accessed=2 * size * length * width, transcendentals=0
         ),
-    )(held, gathered)
+    )(held, *[gathered] * STREAMS)
     parts = lax.all_to_all(partial, "ctx", 0, 0, tiled=True)
     (weight_grad,) = call(
         functools.partial(assemble_kernel, out_rows, size, share),

time: 176 us -> 177 us (level)
  blocking collectives: 0 us -> 15.7 us
  waiting for transfers between devices: 43.4 us -> 31.3 us
  local copies, waits for them, and re-layouts: 20.6 us -> 26.8 us
  Pallas kernels: 41.7 us -> 35.8 us
  starting transfers between devices: 44.1 us -> 41 us
    all_to_all x0 -> x1, blocking collectives: none -> 15.7 us  [per_device(): lax.all_to_all(gated, 'ctx', 0, 0, axis_index_groups=groups, tiled=True)]
    ppermute x6, waiting for transfers between devices: 17.5 us -> 9.43 us  [enter(): others.append(lax.ppermute(total, 'ctx', pairs).astype(F32))]
    unnamed x64 -> x84, local copies, waits for them, and re-layouts: 18.1 us -> 24.3 us
    pallas_call x1, Pallas kernels: 9.92 us -> 4.56 us  [per_device(): pl.pallas_call(gate_kernel, grid=(channels // part,), in_specs=[pl.BlockS...]
    all_to_all x1 -> x0, starting transfers between devices: 4.49 us -> none  [per_device(): lax.all_to_all(gated, 'ctx', 0, 0, axis_index_groups=groups, tiled=True)]
    all_to_all x4, waiting for transfers between devices: 14.4 us -> 10.3 us  [exchange(): lax.all_to_all(half, 'ctx', 0, 0, axis_index_groups=groups, tiled=True)]
  transfers between devices with their start and end apart: 14 -> 13, of which waited for: 8 -> 7; matrix products, arithmetic and copies ran while one was open for 8% -> 8% of each run, Pallas kernels for 23% -> 20%
where the time goes in v1:
time: 177 us; the launch traced here: 175 us
  starting transfers between devices  41 us (23%)
  Pallas kernels  35.8 us (20%)
  waiting for transfers between devices  31.3 us (18%)
  local copies, waits for them, and re-layouts  26.8 us (15%)
  blocking collectives  15.7 us (9%)
  between operations  14.6 us (8%)
  other arithmetic  10.2 us (6%)
    unnamed x84, local copies, waits for them, and re-layouts  24.3 us
    pallas_call x10, Pallas kernels, call(): pl.pallas_call(kernel, out_shape=tuple(out_shapes), scratch_shapes=list(s...  24.1 us
    all_to_all x4, starting transfers between devices, exchange(): lax.all_to_all(half, 'ctx', 0, 0, axis_index_groups=groups, tiled=True)  18.4 us
    all_to_all x1, blocking collectives, per_device(): lax.all_to_all(gated, 'ctx', 0, 0, axis_index_groups=groups, tiled=True)  15.7 us
    ppermute x6, starting transfers between devices, enter(): others.append(lax.ppermute(total, 'ctx', pairs).astype(F32))  15.6 us
    all_to_all x1, waiting for transfers between devices, per_device(): parts = lax.all_to_all(partial, 'ctx', 0, 0, tiled=True)  10.9 us
    all_to_all x4, waiting for transfers between devices, exchange(): lax.all_to_all(half, 'ctx', 0, 0, axis_index_groups=groups, tiled=True)  10.3 us
    ppermute x6, waiting for transfers between devices, enter(): others.append(lax.ppermute(total, 'ctx', pairs).astype(F32))  9.43 us
  transfers between devices with their start and end apart: 13, of which 7 were waited for; matrix products, arithmetic and copies ran while one was open for 8% of the time, Pallas kernels for 20%

profile of v1, /device:TPU:0, one launch (start us, length us, event | category | flops | bytes accessed | tf_op | source)
XLA Modules:
  0.0 175.3 jit_solution(17836530651642989069)
XLA Ops:
  9.5 2.4 %collective-permute-start = (bf16[16,2816]{1,0:T(8,128)(2,1)S(1)}, bf16[16,2816]{1,0:T(8,128)(2,1)S(1)}, u32[]{:S(2)}, u32[]{:S(2)}) collective-permute-start(bf16[16,2816]{1,0:T(8,128)(2,1)S(1)} %pad_maximum_fusion), channel_id=1, source_target_pairs={{0,1},{1,2},{2,3},{3,4},{4,5},{5,6},{6,7},{7,8},{8,9},{9,10},{10,1... | collective-permute-start | bytes 270344 | tf_op jit(solution)/shard_map/ppermute | solution.py:489
  18.2 2.8 %shard_map.164 = (f32[128,2560]{1,0:T(8,128)S(1)}, f32[128,2560]{1,0:T(8,128)S(1)}, f32[128,256]{1,0:T(8,128)S(1)}, f32[128,256]{1,0:T(8,128)S(1)}, f32[128,128]...) custom-call(bf16[128,2560]{1,0:T(8,128)(2,1)S(1)} %copy-done.6, ...), custom_call_target="tpu_custom_call" | custom-call | flops 1677721600 | bytes 5446976 | tf_op jit(solution)/shard_map/pallas_call | solution.py:24
  26.6 6.4 %all-to-all-start = ((f16[8,328,128]{2,1,0:T(8,128)(2,1)}), f16[8,328,128]{2,1,0:T(8,128)(2,1)}, u32[]{:S(2)}, u32[]{:S(2)}) async-start(f16[8,328,128]{2,1,0:T(8,128)(2,1)} %convert_element_type.51), calls=%async_computation | async-start | bytes 1343488 | tf_op jit(solution)/shard_map/all_to_all | solution.py:451
  33.1 4.9 %copy-done = bf16[2560,2560]{1,0:T(8,128)(2,1)S(1)} copy-done((bf16[2560,2560]{1,0:T(8,128)(2,1)S(1)}, bf16[2560,2560]{1,0:T(8,128)(2,1)}, u32[]{:S(2)}) %copy-start) | copy-done | bytes 13107224
  38.0 4.6 %shard_map.165 = (f32[128,2560]{1,0:T(8,128)S(1)}, f32[128,2560]{1,0:T(8,128)S(1)}) custom-call(bf16[128,2560]{1,0:T(8,128)(2,1)S(1)} %copy-done.1, bf16[2560,2560]{1,0:T(8,128)(2,1)S(1)} %copy-done, bf16[128,2560]{1,0:T(8,128)(2,1)S(1)} %copy-done.3), custom_call_target="tpu_custom_call" | custom-call | flops 1677721600 | bytes 13107200 | tf_op jit(solution)/shard_map/pallas_call | solution.py:559
  43.7 1.6 shard_map.166
  46.3 5.7 %all-to-all-done = f16[8,328,128]{2,1,0:T(8,128)(2,1)} async-done(((f16[8,328,128]{2,1,0:T(8,128)(2,1)}), f16[8,328,128]{2,1,0:T(8,128)(2,1)}, u32[]{:S(2)}, u32[]{:S(2)}) %all-to-all-start) | async-done | bytes 671776 | tf_op jit(solution)/shard_map/all_to_all | solution.py:451
  54.9 4.2 %all-to-all-start.1 = ((f16[8,328,128]{2,1,0:T(8,128)(2,1)}), f16[8,328,128]{2,1,0:T(8,128)(2,1)}, u32[]{:S(2)}, u32[]{:S(2)}) async-start(f16[8,328,128]{2,1,0:T(8,128)(2,1)} %convert_element_type.57), calls=%async_computation.1 | async-start | bytes 1343488 | tf_op jit(solution)/shard_map/all_to_all | solution.py:451
  59.1 5.7 %collective-permute-start.1 = (f16[1,328,128]{2,1,0:T(8,128)(2,1)S(1)}, f16[1,328,128]{2,1,0:T(8,128)(2,1)S(1)}, u32[]{:S(2)}, u32[]{:S(2)}) collective-permute-start(f16[1,328,128]{2,1,0:T(8,128)(2,1)S(1)} %convert_element_type.53), channel_id=1, source_target_pairs={{0,8},{1,9},{2,10},{3,11},{4,12},{5,13},{6,14},{7,15},{8,16},{9,17... | collective-permute-start | bytes 251912 | tf_op jit(solution)/shard_map/ppermute | solution.py:473
  64.8 4.5 %collective-permute-start.2 = (f16[1,328,128]{2,1,0:T(8,128)(2,1)S(1)}, f16[1,328,128]{2,1,0:T(8,128)(2,1)S(1)}, u32[]{:S(2)}, u32[]{:S(2)}) collective-permute-start(f16[1,328,128]{2,1,0:T(8,128)(2,1)S(1)} %convert_element_type.53), channel_id=1, source_target_pairs={{0,16},{1,17},{2,18},{3,19},{4,20},{5,21},{6,22},{7,23},{8,24},{9,... | collective-permute-start | bytes 251912 | tf_op jit(solution)/shard_map/ppermute | solution.py:473
  70.7 2.4 %collective-permute-done.2 = f16[1,328,128]{2,1,0:T(8,128)(2,1)S(1)} collective-permute-done((f16[1,328,128]{2,1,0:T(8,128)(2,1)S(1)}, f16[1,328,128]{2,1,0:T(8,128)(2,1)S(1)}, u32[]{:S(2)}, u32[]{:S(2)}) %collective-permute-start.2) | collective-permute-done | bytes 84000 | tf_op jit(solution)/shard_map/ppermute | solution.py:473
  73.0 2.9 %collective-permute-done.3 = f16[1,328,128]{2,1,0:T(8,128)(2,1)S(1)} collective-permute-done((f16[1,328,128]{2,1,0:T(8,128)(2,1)S(1)}, f16[1,328,128]{2,1,0:T(8,128)(2,1)S(1)}, u32[]{:S(2)}, u32[]{:S(2)}) %collective-permute-start.3) | collective-permute-done | bytes 84000 | tf_op jit(solution)/shard_map/ppermute | solution.py:473
  78.9 4.2 %all-to-all-start.2 = ((f16[8,328,128]{2,1,0:T(8,128)(2,1)}), f16[8,328,128]{2,1,0:T(8,128)(2,1)}, u32[]{:S(2)}, u32[]{:S(2)}) async-start(f16[8,328,128]{2,1,0:T(8,128)(2,1)} %convert_element_type.58), calls=%async_computation.2 | async-start | bytes 1343488 | tf_op jit(solution)/shard_map/all_to_all | solution.py:451
  88.0 1.5 collective-permute-start.6
  89.5 4.8 %shard_map.169 = (f32[128,2560]{1,0:T(8,128)S(1)}, f32[128,2560]{1,0:T(8,128)S(1)}, f32[128,256]{1,0:T(8,128)S(1)}) custom-call(f32[128,2560]{1,0:T(8,128)S(1)} %copy-done.16, f32[128,2560]{1,0:T(8,128)S(1)} %copy-done.10, f32[128,256]{1,0:T(8,128)S(1)} %copy-done.24, f32[128,128]{1,0:T(8,128)S(1)} %copy-done.32, f32[128,128]{1,0:T(8,128)S(1)} %get-tuple-element.42.ld_ref, ...), custom_call_target="tpu_custom_call" | custom-call | flops 3355443200 | bytes 5767168 | tf_op jit(solution)/shard_map/pallas_call | solution.py:24
  96.5 4.1 %collective-permute-done.5 = f16[1,328,128]{2,1,0:T(8,128)(2,1)S(1)} collective-permute-done((f16[1,328,128]{2,1,0:T(8,128)(2,1)S(1)}, f16[1,328,128]{2,1,0:T(8,128)(2,1)S(1)}, u32[]{:S(2)}, u32[]{:S(2)}) %collective-permute-start.5) | collective-permute-done | bytes 84000 | tf_op jit(solution)/shard_map/ppermute | solution.py:473
  106.1 1.9 %shard_map.170 = (bf16[16,160,128]{2,1,0:T(8,128)(2,1)S(1)}, f32[128,2560]{1,0:T(8,128)S(1)}) custom-call(f32[8,328,128]{2,1,0:T(8,128)S(1)} %convert_element_type.59.msg_ref.msgf_ref, f32[128,2560]{1,0:T(8,128)S(1)} %copy-done.17, bf16[128,2560]{1,0:T(8,128)(2,1)S(1)} %copy-done.4, f32[128,256]{1,0:T(8,128)S(1)} %copy-done.25, ...), custom_call_target="tpu_custom_call" | custom-call | flops 1677721600 | bytes 6793216 | tf_op jit(solution)/shard_map/pallas_call | solution.py:24
  108.1 15.7 %all_to_all.30.held_ref = bf16[16,160,128]{2,1,0:T(8,128)(2,1)S(1)} all-to-all(bf16[16,160,128]{2,1,0:T(8,128)(2,1)S(1)} %get-tuple-element.54), channel_id=1, replica_groups={{0,1,2,3,4,5,6,7,8,9,10,11,12,13,14,15},{16,17,18,19,20,21,22,23,24,25,..., dimensions={0} | all-to-all | bytes 1310720 | tf_op jit(solution)/shard_map/all_to_all | solution.py:605
  124.7 3.5 %all-to-all-start.4 = ((f16[8,328,128]{2,1,0:T(8,128)(2,1)}), f16[8,328,128]{2,1,0:T(8,128)(2,1)S(1)}, u32[]{:S(2)}, u32[]{:S(2)}) async-start(f16[8,328,128]{2,1,0:T(8,128)(2,1)} %convert_element_type.65), calls=%async_computation.4 | async-start | bytes 1343488 | tf_op jit(solution)/shard_map/all_to_all | solution.py:451
  128.3 7.2 %shard_map.174 = bf16[32,112,128]{2,1,0:T(8,128)(2,1)} custom-call(bf16[16,160,128]{2,1,0:T(8,128)(2,1)S(1)} %all_to_all.30.held_ref, bf16[2048,2560]{1,0:T(8,128)(2,1)} %all-gather.2.cloned.1.call-done.refs_0_.refs_1_.refs_2_.refs_3_, bf16[2048,2560]{1,0:T(8,128)(2,1)} %all-gather.2.cloned.1.call-done.refs_0_.refs_1_.refs_2_.refs_3_, ...), custom_call_target="tpu_custom_call" | custom-call | flops 1677721600 | bytes 10485760 | tf_op jit(solution)/shard_map/pallas_call | solution.py:617
  135.5 4.1 %all-to-all-done.4 = f16[8,328,128]{2,1,0:T(8,128)(2,1)S(1)} async-done(((f16[8,328,128]{2,1,0:T(8,128)(2,1)}), f16[8,328,128]{2,1,0:T(8,128)(2,1)S(1)}, u32[]{:S(2)}, u32[]{:S(2)}) %all-to-all-start.4) | async-done | bytes 671776 | tf_op jit(solution)/shard_map/all_to_all | solution.py:451
  139.5 4.6 %all-to-all-start.5 = ((bf16[32,112,128]{2,1,0:T(8,128)(2,1)}), bf16[32,112,128]{2,1,0:T(8,128)(2,1)S(1)}, u32[]{:S(2)}, u32[]{:S(2)}) async-start(bf16[32,112,128]{2,1,0:T(8,128)(2,1)} %shard_map.174), calls=%async_computation.5 | async-start | bytes 1835008 | tf_op jit(solution)/shard_map/all_to_all | solution.py:635
  147.5 7.7 %shard_map.173 = (bf16[128,2560]{1,0:T(8,128)(2,1)}, f32[128,256]{1,0:T(8,128)S(1)}, f32[128,40]{1,0:T(8,128)S(1)}, bf16[128,2560]{1,0:T(8,128)(2,1)}) custom-call(f32[8,328,128]{2,1,0:T(8,128)} %convert_element_type.66.msg_ref, f32[8,328,128]{2,1,0:T(8,128)} %copy-done.2, f32[128,2560]{1,0:T(8,128)S(1)} %copy-done.18, f32[128,2560]{1,0:T(8,128)S(1)} %copy-done.20, ...), custom_call_target="tpu_custom_call" | custom-call | flops 3355443200 | bytes 13142016 | tf_op jit(solution)/shard_map/pallas_call | solution.py:24
  156.5 10.9 %all-to-all-done.5.parts_ref = bf16[32,112,128]{2,1,0:T(8,128)(2,1)S(1)} async-done(((bf16[32,112,128]{2,1,0:T(8,128)(2,1)}), bf16[32,112,128]{2,1,0:T(8,128)(2,1)S(1)}, u32[]{:S(2)}, u32[]{:S(2)}) %all-to-all-start.5) | async-done | bytes 917536 | tf_op jit(solution)/shard_map/all_to_all | solution.py:635
  (126 shorter events, 42.4 us)
Async XLA Ops:
  7.2 121.1 %all-gather.2.cloned.1.call-start = ((), (), s32[]{:S(2)}) async-start(), calls=%async_computation.6 | async-start | bytes 11141120 | tf_op jit(solution)/shard_map/all_gather | solution.py:519
  9.5 4.6 %collective-permute-start = (bf16[16,2816]{1,0:T(8,128)(2,1)S(1)}, bf16[16,2816]{1,0:T(8,128)(2,1)S(1)}, u32[]{:S(2)}, u32[]{:S(2)}) collective-permute-start(bf16[16,2816]{1,0:T(8,128)(2,1)S(1)} %pad_maximum_fusion), channel_id=1, source_target_pairs={{0,1},{1,2},{2,3},{3,4},{4,5},{5,6},{6,7},{7,8},{8,9},{9,10},{10,1... | collective-permute-start | bytes 270344 | tf_op jit(solution)/shard_map/ppermute | solution.py:489
  25.7 18.0 %copy-start.23 = (f32[128,256]{1,0:T(8,128)}, f32[128,256]{1,0:T(8,128)S(1)}, u32[]{:S(2)}) copy-start(f32[128,256]{1,0:T(8,128)S(1)} %get-tuple-element.41.abc_ref) | copy-start | bytes 393220
  25.7 7.4 %copy-start.1 = (bf16[128,2560]{1,0:T(8,128)(2,1)S(1)}, bf16[128,2560]{1,0:T(8,128)(2,1)}, u32[]{:S(2)}) copy-start(bf16[128,2560]{1,0:T(8,128)(2,1)} %go_ref) | copy-start | bytes 1966084
  25.7 7.4 %copy-start.3 = (bf16[128,2560]{1,0:T(8,128)(2,1)S(1)}, bf16[128,2560]{1,0:T(8,128)(2,1)}, u32[]{:S(2)}) copy-start(bf16[128,2560]{1,0:T(8,128)(2,1)} %gate_ref.5) | copy-start | bytes 1966084
  26.6 25.4 %all-to-all-start = ((f16[8,328,128]{2,1,0:T(8,128)(2,1)}), f16[8,328,128]{2,1,0:T(8,128)(2,1)}, u32[]{:S(2)}, u32[]{:S(2)}) async-start(f16[8,328,128]{2,1,0:T(8,128)(2,1)} %convert_element_type.51), calls=%async_computation | async-start | bytes 1343488 | tf_op jit(solution)/shard_map/all_to_all | solution.py:451
  54.9 23.1 %all-to-all-start.1 = ((f16[8,328,128]{2,1,0:T(8,128)(2,1)}), f16[8,328,128]{2,1,0:T(8,128)(2,1)}, u32[]{:S(2)}, u32[]{:S(2)}) async-start(f16[8,328,128]{2,1,0:T(8,128)(2,1)} %convert_element_type.57), calls=%async_computation.1 | async-start | bytes 1343488 | tf_op jit(solution)/shard_map/all_to_all | solution.py:451
  59.1 11.6 %collective-permute-start.1 = (f16[1,328,128]{2,1,0:T(8,128)(2,1)S(1)}, f16[1,328,128]{2,1,0:T(8,128)(2,1)S(1)}, u32[]{:S(2)}, u32[]{:S(2)}) collective-permute-start(f16[1,328,128]{2,1,0:T(8,128)(2,1)S(1)} %convert_element_type.53), channel_id=1, source_target_pairs={{0,8},{1,9},{2,10},{3,11},{4,12},{5,13},{6,14},{7,15},{8,16},{9,17... | collective-permute-start | bytes 251912 | tf_op jit(solution)/shard_map/ppermute | solution.py:473
  64.8 8.2 %collective-permute-start.2 = (f16[1,328,128]{2,1,0:T(8,128)(2,1)S(1)}, f16[1,328,128]{2,1,0:T(8,128)(2,1)S(1)}, u32[]{:S(2)}, u32[]{:S(2)}) collective-permute-start(f16[1,328,128]{2,1,0:T(8,128)(2,1)S(1)} %convert_element_type.53), channel_id=1, source_target_pairs={{0,16},{1,17},{2,18},{3,19},{4,20},{5,21},{6,22},{7,23},{8,24},{9,... | collective-permute-start | bytes 251912 | tf_op jit(solution)/shard_map/ppermute | solution.py:473
  69.3 6.6 %collective-permute-start.3 = (f16[1,328,128]{2,1,0:T(8,128)(2,1)S(1)}, f16[1,328,128]{2,1,0:T(8,128)(2,1)S(1)}, u32[]{:S(2)}, u32[]{:S(2)}) collective-permute-start(f16[1,328,128]{2,1,0:T(8,128)(2,1)S(1)} %convert_element_type.53), channel_id=1, source_target_pairs={{0,24},{1,25},{2,26},{3,27},{4,28},{5,29},{6,30},{7,31}} | collective-permute-start | bytes 251912 | tf_op jit(solution)/shard_map/ppermute | solution.py:473
  77.4 5.7 %copy-start.40 = (f32[40]{0:T(128)S(1)}, f32[40]{0:T(128)}, u32[]{:S(2)}) copy-start(f32[40]{0:T(128)} %param.23) | copy-start | bytes 484
  78.9 23.2 %all-to-all-start.2 = ((f16[8,328,128]{2,1,0:T(8,128)(2,1)}), f16[8,328,128]{2,1,0:T(8,128)(2,1)}, u32[]{:S(2)}, u32[]{:S(2)}) async-start(f16[8,328,128]{2,1,0:T(8,128)(2,1)} %convert_element_type.58), calls=%async_computation.2 | async-start | bytes 1343488 | tf_op jit(solution)/shard_map/all_to_all | solution.py:451
  83.2 6.2 %copy-start.16 = (f32[128,2560]{1,0:T(8,128)S(1)}, f32[128,2560]{1,0:T(8,128)}, u32[]{:S(2)}) copy-start(f32[128,2560]{1,0:T(8,128)} %copy-done.15) | copy-start | bytes 3932164
  85.4 11.1 %collective-permute-start.4 = (f16[1,328,128]{2,1,0:T(8,128)(2,1)S(1)}, f16[1,328,128]{2,1,0:T(8,128)(2,1)S(1)}, u32[]{:S(2)}, u32[]{:S(2)}) collective-permute-start(f16[1,328,128]{2,1,0:T(8,128)(2,1)S(1)} %convert_element_type.61), channel_id=1, source_target_pairs={{8,0},{9,1},{10,2},{11,3},{12,4},{13,5},{14,6},{15,7},{16,8},{17,9... | collective-permute-start | bytes 251912 | tf_op jit(solution)/shard_map/ppermute | solution.py:473
  86.7 14.0 %collective-permute-start.5 = (f16[1,328,128]{2,1,0:T(8,128)(2,1)S(1)}, f16[1,328,128]{2,1,0:T(8,128)(2,1)S(1)}, u32[]{:S(2)}, u32[]{:S(2)}) collective-permute-start(f16[1,328,128]{2,1,0:T(8,128)(2,1)S(1)} %convert_element_type.61), channel_id=1, source_target_pairs={{16,0},{17,1},{18,2},{19,3},{20,4},{21,5},{22,6},{23,7},{24,8},{25... | collective-permute-start | bytes 251912 | tf_op jit(solution)/shard_map/ppermute | solution.py:473
  88.0 12.7 %collective-permute-start.6 = (f16[1,328,128]{2,1,0:T(8,128)(2,1)S(1)}, f16[1,328,128]{2,1,0:T(8,128)(2,1)S(1)}, u32[]{:S(2)}, u32[]{:S(2)}) collective-permute-start(f16[1,328,128]{2,1,0:T(8,128)(2,1)S(1)} %convert_element_type.61), channel_id=1, source_target_pairs={{24,0},{25,1},{26,2},{27,3},{28,4},{29,5},{30,6},{31,7}} | collective-permute-start | bytes 251912 | tf_op jit(solution)/shard_map/ppermute | solution.py:473
  108.0 15.7 %copy-start.22 = (f32[128,2560]{1,0:T(8,128)}, f32[128,2560]{1,0:T(8,128)S(1)}, u32[]{:S(2)}) copy-start(f32[128,2560]{1,0:T(8,128)S(1)} %get-tuple-element.59.ys_ref) | copy-start | bytes 3932164
  124.7 14.8 %all-to-all-start.4 = ((f16[8,328,128]{2,1,0:T(8,128)(2,1)}), f16[8,328,128]{2,1,0:T(8,128)(2,1)S(1)}, u32[]{:S(2)}, u32[]{:S(2)}) async-start(f16[8,328,128]{2,1,0:T(8,128)(2,1)} %convert_element_type.65), calls=%async_computation.4 | async-start | bytes 1343488 | tf_op jit(solution)/shard_map/all_to_all | solution.py:451
  139.5 5.9 %copy-start.18 = (f32[128,2560]{1,0:T(8,128)S(1)}, f32[128,2560]{1,0:T(8,128)}, u32[]{:S(2)}) copy-start(f32[128,2560]{1,0:T(8,128)} %copy-done.15) | copy-start | bytes 3932164
  139.5 5.9 %copy-start.26 = (f32[128,256]{1,0:T(8,128)S(1)}, f32[128,256]{1,0:T(8,128)}, u32[]{:S(2)}) copy-start(f32[128,256]{1,0:T(8,128)} %copy-done.23) | copy-start | bytes 393220
  139.5 5.9 %copy-start.30 = (f32[128,256]{1,0:T(8,128)S(1)}, f32[128,256]{1,0:T(8,128)}, u32[]{:S(2)}) copy-start(f32[128,256]{1,0:T(8,128)} %copy-done.29) | copy-start | bytes 393220
  139.5 5.9 %copy-start.33 = (f32[128,128]{1,0:T(8,128)S(1)}, f32[128,128]{1,0:T(8,128)}, u32[]{:S(2)}) copy-start(f32[128,128]{1,0:T(8,128)} %copy-done.31) | copy-start | bytes 196612
  139.5 5.9 %copy-start.35 = (f32[128,128]{1,0:T(8,128)S(1)}, f32[128,128]{1,0:T(8,128)}, u32[]{:S(2)}) copy-start(f32[128,128]{1,0:T(8,128)} %copy-done.34) | copy-start | bytes 196612
  139.5 27.8 %all-to-all-start.5 = ((bf16[32,112,128]{2,1,0:T(8,128)(2,1)}), bf16[32,112,128]{2,1,0:T(8,128)(2,1)S(1)}, u32[]{:S(2)}, u32[]{:S(2)}) async-start(bf16[32,112,128]{2,1,0:T(8,128)(2,1)} %shard_map.174), calls=%async_computation.5 | async-start | bytes 1835008 | tf_op jit(solution)/shard_map/all_to_all | solution.py:635
  (30 other events, 61.2 us)
Sparse Core Ops, SparseCore 0:
  9.6 76.4 all-gather.1

commit v2 on v1

--- a/solution.py
+++ b/solution.py
@@ -14,18 +14,20 @@
 NN = ((1,), (0,))
 NT = ((1,), (1,))
 HIGH = lax.Precision.HIGHEST
-MIB = 1024 * 1024
+SMEM = pl.BlockSpec(memory_space=pltpu.SMEM)
+VMEM = pl.BlockSpec(memory_space=pltpu.VMEM)
+GRANT = 60 * 1024 * 1024
 STREAMS = 4
 
 
-def call(kernel, out_shapes, operands, flops, vmem, scratch=(), specs=None):
+def call(kernel, out_shapes, operands, flops, scratch=(), specs=None):
     extra = {} if specs is None else {"in_specs": specs}
     moved = sum(a.size * a.dtype.itemsize for a in (*operands, *out_shapes))
     return pl.pallas_call(
         kernel,
         out_shape=tuple(out_shapes),
         scratch_shapes=list(scratch),
-        compiler_params=pltpu.CompilerParams(vmem_limit_bytes=vmem * MIB),
+        compiler_params=pltpu.CompilerParams(vmem_limit_bytes=GRANT),
         cost_estimate=pl.CostEstimate(flops=flops, bytes_accessed=moved, transcendentals=0),
         **extra,
     )(*operands)
@@ -160,9 +162,9 @@
     return message[at, 0:rows, :] * jnp.exp2(message[at, padded + 7 : padded + 8, :] - 13.0)
 
 
-def unpack_blocks(message, target, rows):
+def unpack_blocks(message, target, rows, me=0):
     for d in range(message.shape[0]):
-        target[rows * d : rows * (d + 1), :] = read_block(message, d, rows)
+        target[rows * d : rows * (d + 1), :] = read_block(message, me ^ d, rows)
 
 
 def total_kernel(rows, reverse, held_ref, out_ref):
@@ -178,7 +180,7 @@
     write_block(out_ref, 0, 0, state, decays, exponent_of(state))
 
 
-def fold_kernel(rows, reverse, held_ref, *refs):
+def fold_kernel(rows, reverse, me_ref, held_ref, *refs):
     others, out_ref = refs[:-1], refs[-1]
     count = held_ref.shape[0]
     columns = decay_columns(held_ref, rows)
@@ -186,7 +188,7 @@
     for other in reversed(others):
         state = decay_columns(other, rows) * state + read_block(other, 0, rows)
     for s in range(count - 1, -1, -1) if reverse else range(count):
-        write_block(out_ref, s, 0, state, [], exponent_of(state))
+        write_block(out_ref, me_ref[0] ^ s if reverse else s, 0, state, [], exponent_of(state))
         if s != (0 if reverse else count - 1):
             state = columns[:, s : s + 1] * state + read_block(held_ref, s, rows)
 
@@ -253,8 +255,13 @@
     pack_blocks(st_ref, msg_ref, grown[length - 1 : length], size, rows)
 
 
-def gate_kernel(go_ref, w_ref, gate_ref, gg_ref, gy_ref):
-    grad = dot(w_ref[...], go_ref[...], NT).T
+def gate_kernel(go_ref, *refs):
+    w_refs, (gate_ref, gg_ref, gy_ref) = refs[:-3], refs[-3:]
+    depth = w_refs[0].shape[1]
+    grad = dot(w_refs[0][...], go_ref[:, 0:depth], NT)
+    for k in range(1, len(w_refs)):
+        grad = grad + dot(w_refs[k][...], go_ref[:, k * depth : (k + 1) * depth], NT)
+    grad = grad.T
     gate = gate_ref[...].astype(F32)
     gg_ref[...] = grad
     gy_ref[...] = grad * (gate * sigmoid(gate))
@@ -328,12 +335,12 @@
 
 
 def backward_kernel(
-    heads_in, size, rows, msg_ref, msgf_ref, act_ref, slope_ref, gy_ref, abc_ref, step_ref, ld_ref, gw_ref,
+    heads_in, size, rows, me_ref, msg_ref, msgf_ref, act_ref, slope_ref, gy_ref, abc_ref, step_ref, ld_ref, gw_ref,
     gbcl_ref, ys_ref, gg_ref, gate_ref, skip_ref, dtw_ref, perw_ref, gx_ref, gbc_ref, gdt_ref, gz_ref,
     ca_ref, st_ref, cs_ref,
 ):
     length = act_ref.shape[0]
-    unpack_blocks(msg_ref, ca_ref, rows)
+    unpack_blocks(msg_ref, ca_ref, rows, me_ref[0])
     unpack_blocks(msgf_ref, st_ref, rows)
     b_rows = split(abc_ref[:, 0:LANES])
     ld = ld_ref[...]
@@ -451,18 +458,27 @@
     return lax.all_to_all(half, "ctx", 0, 0, axis_index_groups=groups, tiled=True)
 
 
+def swapped(message):
+    half = message.astype(jnp.float16)
+    count = lax.axis_size("ctx")
+    slots = [half[0:1]]
+    for m in range(1, message.shape[0]):
+        slots.append(lax.ppermute(half[m : m + 1], "ctx", [(at, at ^ m) for at in range(count)]))
+    return jnp.concatenate(slots).astype(F32)
+
+
 def groups_of(count, size):
     return [list(range(at, at + size)) for at in range(0, count, size)]
 
 
 def group_total(held, rows, reverse):
     (total,) = call(
-        functools.partial(total_kernel, rows, reverse), [shape((1, *held.shape[1:]))], [held], 4 * held.size, 12
+        functools.partial(total_kernel, rows, reverse), [shape((1, *held.shape[1:]))], [held], 4 * held.size
     )
     return total.astype(jnp.float16)
 
 
-def enter(held, total, rows, reverse):
+def enter(me, held, total, rows, reverse):
     size = held.shape[0]
     count = lax.axis_size("ctx")
     others = []
@@ -472,7 +488,11 @@
             pairs = [(b, a) for a, b in pairs]
         others.append(lax.ppermute(total, "ctx", pairs).astype(F32))
     (folded,) = call(
-        functools.partial(fold_kernel, rows, reverse), [shape(held.shape)], [held, *others], 8 * held.size, 12
+        functools.partial(fold_kernel, rows, reverse),
+        [shape(held.shape)],
+        [me, held, *others],
+        8 * held.size,
+        specs=[SMEM] + [VMEM] * (1 + len(others)),
     )
     return folded
 
@@ -525,6 +545,7 @@
     block = up8(rows) + 8
     stored = pltpu.VMEM((channels, LANES), F32)
     unit = 2 * length * channels * LANES
+    me = (lax.axis_index("ctx") % plane).astype(jnp.int32).reshape(1)
 
     act_x, slope_x, act_bc, slope_bc, step, ld, step_t, ld_t, raised, per_head, message = call(
         functools.partial(prepare_kernel, heads_in, head_size, rows),
@@ -546,7 +567,6 @@
             jnp.stack([dt_bias, a_log]),
         ],
         20 * unit,
-        48,
         [
             pltpu.VMEM((length + 8, channels), F32),
             pltpu.VMEM((length + 8, bc_raw.shape[1]), F32),
@@ -561,35 +581,38 @@
         grid=(channels // part,),
         in_specs=[
             pl.BlockSpec((length, width), lambda i: (0, 0)),
-            pl.BlockSpec((part, width), lambda i: (i, 0)),
-            pl.BlockSpec((length, part), lambda i: (0, i)),
-        ],
+        ]
+        + [
+            pl.BlockSpec((part, width // STREAMS), functools.partial(lambda k, i: (i, k), k))
+            for k in range(STREAMS)
+        ]
+        + [pl.BlockSpec((length, part), lambda i: (0, i))],
         out_specs=(pl.BlockSpec((length, part), lambda i: (0, i)), pl.BlockSpec((length, part), lambda i: (0, i))),
         out_shape=(shape(whole), shape(whole)),
-        compiler_params=pltpu.CompilerParams(vmem_limit_bytes=24 * MIB),
+        compiler_params=pltpu.CompilerParams(vmem_limit_bytes=GRANT),
         cost_estimate=pl.CostEstimate(
             flops=2 * length * channels * width, bytes_accessed=2 * channels * width, transcendentals=0
         ),
-    )(grad_out_then, out_weight, gate_branch)
+    )(grad_out_then, *[out_weight] * STREAMS, gate_branch)
     (message,) = call(
         functools.partial(grad_kernel, heads_in, head_size, rows),
         [shape((plane, block, LANES))],
         [grad_y, act_bc, ld],
         10 * unit,
-        12,
         [stored],
     )
-    message, total = lax.optimization_barrier((message, group_total(held_state, rows, False)))
-    held_carry = exchange(message, planes)
     y_within, grad_within, grad_bc_within = call(
         functools.partial(local_kernel, heads_in, head_size),
         [shape(whole), shape(whole), shape(act_bc.shape)],
         [act_x, grad_y, act_bc, step, ld, step_t, ld_t],
         40 * unit,
-        16,
         [pltpu.VMEM(square, F32)],
     )
-    folded, held_carry = lax.optimization_barrier((enter(held_state, total, rows, False), held_carry))
+    message, total, y_within = lax.optimization_barrier(
+        (message, group_total(held_state, rows, False), y_within)
+    )
+    held_carry = exchange(message, planes)
+    folded, held_carry = lax.optimization_barrier((enter(me, held_state, total, rows, False), held_carry))
     held_carry = held_carry.astype(F32)
     state_message = exchange(folded, planes).astype(F32)
     gated, y_ahead = call(
@@ -597,14 +620,12 @@
         [shape((size, share, length), BF16), shape(whole)],
         [state_message, act_x, gate_branch, act_bc, ld, y_within, skip],
         20 * unit,
-        16,
         [stored],
     )
-    entered = enter(held_carry, group_total(held_carry, rows, True), rows, True)
+    entered = enter(me, held_carry, group_total(held_carry, rows, True), rows, True)
     gated, entered = lax.optimization_barrier((gated, entered))
     held = lax.all_to_all(gated, "ctx", 0, 0, axis_index_groups=groups, tiled=True)
-    entered, held = lax.optimization_barrier((entered, held))
-    carry_message = exchange(entered, planes).astype(F32)
+    carry_message = swapped(entered)
     out_rows = width // count
     part = width
     for candidate in (640, 1280):
@@ -627,7 +648,7 @@
         out_specs=pl.BlockSpec((part // out_rows, *dims), lambda i: (i, 0, 0)),
         out_shape=shape((count, *dims), BF16),
         scratch_shapes=[pltpu.VMEM((share, size * length), BF16)],
-        compiler_params=pltpu.CompilerParams(vmem_limit_bytes=48 * MIB),
+        compiler_params=pltpu.CompilerParams(vmem_limit_bytes=GRANT),
         cost_estimate=pl.CostEstimate(
             flops=2 * size * length * share * width, bytes_accessed=2 * size * length * width, transcendentals=0
         ),
@@ -638,12 +659,12 @@
         [shape((out_rows, channels))],
         [parts],
         2 * parts.size,
-        12,
     )
     grad_x_conv, grad_bc, grad_dt_raw, grad_z = call(
         functools.partial(backward_kernel, heads_in, head_size, rows),
         [shape(whole, BF16), shape(act_bc.shape), shape(dt_raw.shape), shape(whole, BF16)],
         [
+            me,
             carry_message,
             state_message,
             act_x,
@@ -662,8 +683,8 @@
             per_head,
         ],
         40 * unit,
-        48,
         [stored, stored, pltpu.VMEM((LANES, LANES), F32)],
+        [SMEM] + [VMEM] * 16,
     )
     grad_bc_conv = (lax.psum(grad_bc, "tp") * slope_bc).astype(BF16)
     return (grad_x_conv, grad_bc_conv, grad_z, grad_dt_raw, weight_grad)

time: 177 us -> 187 us (1.056)
  Pallas kernels: 35.8 us -> 64.2 us
  local copies, waits for them, and re-layouts: 26.8 us -> 9.21 us
  other arithmetic: 10.2 us -> 18.9 us
  waiting for transfers between devices: 31.3 us -> 23.5 us
  starting transfers between devices: 41 us -> 38.8 us
    pallas_call x10, Pallas kernels: 24.1 us -> 47 us  [call(): pl.pallas_call(kernel, out_shape=tuple(out_shapes), scratch_shapes=list(s...]
    unnamed x84 -> x18, local copies, waits for them, and re-layouts: 24.3 us -> 4.13 us
    ppermute x0 -> x7, waiting for transfers between devices: none -> 12.2 us  [swapped(): lax.ppermute(half[m:m + 1], 'ctx', [(at, at ^ m) for at in range(count)])]
    all_to_all x1, waiting for transfers between devices: 10.9 us -> 0.01 us  [per_device(): parts = lax.all_to_all(partial, 'ctx', 0, 0, tiled=True)]
    all_to_all x4 -> x3, waiting for transfers between devices: 10.3 us -> 0.01 us  [exchange(): lax.all_to_all(half, 'ctx', 0, 0, axis_index_groups=groups, tiled=True)]
    ppermute x0 -> x7, starting transfers between devices: none -> 6.29 us  [swapped(): lax.ppermute(half[m:m + 1], 'ctx', [(at, at ^ m) for at in range(count)])]
    pallas_call x1, Pallas kernels: 4.56 us -> 9.6 us  [per_device(): pl.pallas_call(gate_kernel, grid=(channels // part,), in_specs=[pl.BlockS...]
    all_to_all x4 -> x3, starting transfers between devices: 18.4 us -> 13.9 us  [exchange(): lax.all_to_all(half, 'ctx', 0, 0, axis_index_groups=groups, tiled=True)]
  transfers between devices with their start and end apart: 13 -> 19, of which waited for: 7 -> 9; matrix products, arithmetic and copies ran while one was open for 8% -> 15% of each run, Pallas kernels for 20% -> 29%
where the time goes in v2:
time: 187 us; the launch traced here: 185 us
  Pallas kernels  64.2 us (34%)
  starting transfers between devices  38.8 us (21%)
  waiting for transfers between devices  23.5 us (13%)
  other arithmetic  18.9 us (10%)
  blocking collectives  16.2 us (9%)
  between operations  14.2 us (8%)
  local copies, waits for them, and re-layouts  9.21 us (5%)
    pallas_call x10, Pallas kernels, call(): pl.pallas_call(kernel, out_shape=tuple(out_shapes), scratch_shapes=list(s...  47 us
    all_to_all x1, blocking collectives, per_device(): lax.all_to_all(gated, 'ctx', 0, 0, axis_index_groups=groups, tiled=True)  16.2 us
    all_to_all x3, starting transfers between devices, exchange(): lax.all_to_all(half, 'ctx', 0, 0, axis_index_groups=groups, tiled=True)  13.9 us
    ppermute x6, starting transfers between devices, enter(): others.append(lax.ppermute(total, 'ctx', pairs).astype(F32))  13.4 us
    ppermute x7, waiting for transfers between devices, swapped(): lax.ppermute(half[m:m + 1], 'ctx', [(at, at ^ m) for at in range(count)])  12.2 us
    ppermute x6, waiting for transfers between devices, enter(): others.append(lax.ppermute(total, 'ctx', pairs).astype(F32))  10.6 us
    pallas_call x1, Pallas kernels, per_device(): pl.pallas_call(gate_kernel, grid=(channels // part,), in_specs=[pl.BlockS...  9.6 us
    pallas_call x1, Pallas kernels, per_device(): pl.pallas_call(functools.partial(product_kernel, out_rows), grid=(width /...  7.58 us
  transfers between devices with their start and end apart: 19, of which 9 were waited for; matrix products, arithmetic and copies ran while one was open for 15% of the time, Pallas kernels for 29%

profile of v2, /device:TPU:0, one launch (start us, length us, event | category | flops | bytes accessed | tf_op | source)
XLA Modules:
  0.0 185.0 jit_solution(13619955871359445554)
XLA Ops:
  9.5 2.4 %collective-permute-start = (bf16[16,2816]{1,0:T(8,128)(2,1)S(1)}, bf16[16,2816]{1,0:T(8,128)(2,1)S(1)}, u32[]{:S(2)}, u32[]{:S(2)}) collective-permute-start(bf16[16,2816]{1,0:T(8,128)(2,1)S(1)} %pad_maximum_fusion), channel_id=1, source_target_pairs={{0,1},{1,2},{2,3},{3,4},{4,5},{5,6},{6,7},{7,8},{8,9},{9,10},{10,1... | collective-permute-start | bytes 270344 | tf_op jit(solution)/shard_map/ppermute | solution.py:509
  17.1 5.7 %shard_map.164 = (f32[128,2560]{1,0:T(8,128)}, f32[128,2560]{1,0:T(8,128)}, f32[128,256]{1,0:T(8,128)}, f32[128,256]{1,0:T(8,128)}, f32[128,128]{1,0:T(8,128)}, ...) custom-call(bf16[128,2560]{1,0:T(8,128)(2,1)} %x_ref.1, ...), custom_call_target="tpu_custom_call" | custom-call | flops 1677721600 | bytes 5446976 | tf_op jit(solution)/shard_map/pallas_call | solution.py:26
  25.0 6.0 %all-to-all-start = ((f16[8,328,128]{2,1,0:T(8,128)(2,1)}), f16[8,328,128]{2,1,0:T(8,128)(2,1)S(1)}, u32[]{:S(2)}, u32[]{:S(2)}) async-start(f16[8,328,128]{2,1,0:T(8,128)(2,1)} %convert_element_type.51), calls=%async_computation | async-start | bytes 1343488 | tf_op jit(solution)/shard_map/all_to_all | solution.py:458
  31.0 9.6 %shard_map.165 = (f32[128,2560]{1,0:T(8,128)}, f32[128,2560]{1,0:T(8,128)}) custom-call(bf16[128,2560]{1,0:T(8,128)(2,1)} %go_ref, bf16[2560,2560]{1,0:T(8,128)(2,1)} %refs_3_.1, bf16[2560,2560]{1,0:T(8,128)(2,1)} %refs_3_.1, bf16[2560,2560]{1,0:T(8,128)(2,1)} %refs_3_.1, bf16[2560,2560]{1,0:T(8,128)(2,1)} %refs_3_.1, bf16[128,2560]{1,0:T(8,128)(2,1)} %gate_ref.3), custom_call_target="tpu_custom_call" | custom-call | flops 1677721600 | bytes 13107200 | tf_op jit(solution)/shard_map/pallas_call | solution.py:579
  40.6 4.0 %shard_map.166 = f32[8,328,128]{2,1,0:T(8,128)} custom-call(f32[128,2560]{1,0:T(8,128)} %get-tuple-element.39.gy_ref, f32[128,256]{1,0:T(8,128)} %get-tuple-element.40.abc_ref, f32[128,128]{1,0:T(8,128)} %get-tuple-element.41.ld_ref), custom_call_target="tpu_custom_call" | custom-call | flops 838860800 | bytes 2850816 | tf_op jit(solution)/shard_map/pallas_call | solution.py:26
  44.6 7.5 %shard_map.168 = (f32[128,2560]{1,0:T(8,128)}, f32[128,2560]{1,0:T(8,128)}, f32[128,256]{1,0:T(8,128)}) custom-call(f32[128,2560]{1,0:T(8,128)} %get-tuple-element.42.act_ref, f32[128,2560]{1,0:T(8,128)} %get-tuple-element.39.gy_ref, f32[128,256]{1,0:T(8,128)} %get-tuple-element.40.abc_ref, f32[128,128]{1,0:T(8,128)} %get-tuple-element.43.step_ref, ...), custom_call_target="tpu_custom_call" | custom-call | flops 3355443200 | bytes 5767168 | tf_op jit(solution)/shard_map/pallas_call | solution.py:26
  53.4 2.8 %shard_map.167 = f32[1,328,128]{2,1,0:T(8,128)} custom-call(f32[8,328,128]{2,1,0:T(8,128)} %convert_element_type.52.held_ref), custom_call_target="tpu_custom_call" | custom-call | flops 1343488 | bytes 1511424 | tf_op jit(solution)/shard_map/pallas_call | solution.py:26
  58.0 4.4 %all-to-all-start.1 = ((f16[8,328,128]{2,1,0:T(8,128)(2,1)}), f16[8,328,128]{2,1,0:T(8,128)(2,1)S(1)}, u32[]{:S(2)}, u32[]{:S(2)}) async-start(f16[8,328,128]{2,1,0:T(8,128)(2,1)} %convert_element_type.57), calls=%async_computation.1 | async-start | bytes 1343488 | tf_op jit(solution)/shard_map/all_to_all | solution.py:458
  62.4 3.6 %collective-permute-start.1 = (f16[1,328,128]{2,1,0:T(8,128)(2,1)S(1)}, f16[1,328,128]{2,1,0:T(8,128)(2,1)S(1)}, u32[]{:S(2)}, u32[]{:S(2)}) collective-permute-start(f16[1,328,128]{2,1,0:T(8,128)(2,1)S(1)} %convert_element_type.53), channel_id=1, source_target_pairs={{0,8},{1,9},{2,10},{3,11},{4,12},{5,13},{6,14},{7,15},{8,16},{9,17... | collective-permute-start | bytes 251912 | tf_op jit(solution)/shard_map/ppermute | solution.py:489
  66.0 4.5 %collective-permute-start.2 = (f16[1,328,128]{2,1,0:T(8,128)(2,1)S(1)}, f16[1,328,128]{2,1,0:T(8,128)(2,1)S(1)}, u32[]{:S(2)}, u32[]{:S(2)}) collective-permute-start(f16[1,328,128]{2,1,0:T(8,128)(2,1)S(1)} %convert_element_type.53), channel_id=1, source_target_pairs={{0,16},{1,17},{2,18},{3,19},{4,20},{5,21},{6,22},{7,23},{8,24},{9,... | collective-permute-start | bytes 251912 | tf_op jit(solution)/shard_map/ppermute | solution.py:489
  78.1 3.9 %shard_map.169 = f32[8,328,128]{2,1,0:T(8,128)} custom-call(s32[1]{0:T(128)} %bitcast.me_ref, f32[8,328,128]{2,1,0:T(8,128)} %convert_element_type.52.held_ref, f32[1,328,128]{2,1,0:T(8,128)} %convert_element_type.54.refs_0_, f32[1,328,128]{2,1,0:T(8,128)} %convert_element_type.55.refs_1_, f32[1,328,128]{2,1,0:T(8,128)} %convert_element_type.56.refs_2_), custom_call_target="tpu_custom_call" | custom-call | flops 2686976 | bytes 3190788 | tf_op jit(solution)/shard_map/pallas_call | solution.py:26
  84.3 3.5 %all-to-all-start.2 = ((f16[8,328,128]{2,1,0:T(8,128)(2,1)}), f16[8,328,128]{2,1,0:T(8,128)(2,1)S(1)}, u32[]{:S(2)}, u32[]{:S(2)}) async-start(f16[8,328,128]{2,1,0:T(8,128)(2,1)} %convert_element_type.58), calls=%async_computation.2 | async-start | bytes 1343488 | tf_op jit(solution)/shard_map/all_to_all | solution.py:458
  89.0 2.7 %shard_map.171 = f32[1,328,128]{2,1,0:T(8,128)} custom-call(f32[8,328,128]{2,1,0:T(8,128)} %convert_element_type.60.held_ref), custom_call_target="tpu_custom_call" | custom-call | flops 1343488 | bytes 1511424 | tf_op jit(solution)/shard_map/pallas_call | solution.py:26
  102.2 2.9 %collective-permute-done.6 = f16[1,328,128]{2,1,0:T(8,128)(2,1)S(1)} collective-permute-done((f16[1,328,128]{2,1,0:T(8,128)(2,1)S(1)}, f16[1,328,128]{2,1,0:T(8,128)(2,1)S(1)}, u32[]{:S(2)}, u32[]{:S(2)}) %collective-permute-start.6) | collective-permute-done | bytes 84000 | tf_op jit(solution)/shard_map/ppermute | solution.py:489
  105.7 3.9 %shard_map.172 = f32[8,328,128]{2,1,0:T(8,128)} custom-call(s32[1]{0:T(128)} %bitcast.me_ref, f32[8,328,128]{2,1,0:T(8,128)} %convert_element_type.60.held_ref, f32[1,328,128]{2,1,0:T(8,128)} %convert_element_type.62.refs_0_, f32[1,328,128]{2,1,0:T(8,128)} %convert_element_type.63.refs_1_, f32[1,328,128]{2,1,0:T(8,128)} %convert_element_type.64.refs_2_), custom_call_target="tpu_custom_call" | custom-call | flops 2686976 | bytes 3190788 | tf_op jit(solution)/shard_map/pallas_call | solution.py:26
  110.8 5.3 %shard_map.170 = (bf16[16,160,128]{2,1,0:T(8,128)(2,1)}, f32[128,2560]{1,0:T(8,128)}) custom-call(f32[8,328,128]{2,1,0:T(8,128)} %convert_element_type.59.msg_ref.msgf_ref, f32[128,2560]{1,0:T(8,128)} %get-tuple-element.42.act_ref, bf16[128,2560]{1,0:T(8,128)(2,1)} %gate_ref.3, f32[128,256]{1,0:T(8,128)} %get-tuple-element.40.abc_ref, ...), custom_call_target="tpu_custom_call" | custom-call | flops 1677721600 | bytes 6793216 | tf_op jit(solution)/shard_map/pallas_call | solution.py:26
  116.2 16.2 %all_to_all.25.held_ref = bf16[16,160,128]{2,1,0:T(8,128)(2,1)} all-to-all(bf16[16,160,128]{2,1,0:T(8,128)(2,1)} %get-tuple-element.66), channel_id=1, replica_groups={{0,1,2,3,4,5,6,7,8,9,10,11,12,13,14,15},{16,17,18,19,20,21,22,23,24,25,..., dimensions={0} | all-to-all | bytes 1310720 | tf_op jit(solution)/shard_map/all_to_all | solution.py:627
  132.4 7.6 %shard_map.174 = bf16[32,112,128]{2,1,0:T(8,128)(2,1)} custom-call(bf16[16,160,128]{2,1,0:T(8,128)(2,1)} %all_to_all.25.held_ref, bf16[2048,2560]{1,0:T(8,128)(2,1)} %all-gather.2.cloned.1.call-done.refs_0_.refs_1_.refs_2_.refs_3_, bf16[2048,2560]{1,0:T(8,128)(2,1)} %all-gather.2.cloned.1.call-done.refs_0_.refs_1_.refs_2_.refs_3_, ...), custom_call_target="tpu_custom_call" | custom-call | flops 1677721600 | bytes 10485760 | tf_op jit(solution)/shard_map/pallas_call | solution.py:638
  140.0 2.8 %all-to-all-start.4 = ((bf16[32,112,128]{2,1,0:T(8,128)(2,1)}), bf16[32,112,128]{2,1,0:T(8,128)(2,1)S(1)}, u32[]{:S(2)}, u32[]{:S(2)}) async-start(bf16[32,112,128]{2,1,0:T(8,128)(2,1)} %shard_map.174), calls=%async_computation.4 | async-start | bytes 1835008 | tf_op jit(solution)/shard_map/all_to_all | solution.py:656
  146.7 2.6 %collective-permute-start.12 = (f16[1,328,128]{2,1,0:T(8,128)(2,1)S(1)}, f16[1,328,128]{2,1,0:T(8,128)(2,1)S(1)}, u32[]{:S(2)}, u32[]{:S(2)}) collective-permute-start(f16[1,328,128]{2,1,0:T(8,128)(2,1)S(1)} %get-tuple-element.73), channel_id=1, source_target_pairs={{0,6},{1,7},{2,4},{3,5},{4,2},{5,3},{6,0},{7,1},{8,14},{9,15},{10,... | collective-permute-start | bytes 251912 | tf_op jit(solution)/shard_map/ppermute | solution.py:466
  149.3 5.5 %collective-permute-done.8 = f16[1,328,128]{2,1,0:T(8,128)(2,1)S(1)} collective-permute-done((f16[1,328,128]{2,1,0:T(8,128)(2,1)S(1)}, f16[1,328,128]{2,1,0:T(8,128)(2,1)S(1)}, u32[]{:S(2)}, u32[]{:S(2)}) %collective-permute-start.8) | collective-permute-done | bytes 84000 | tf_op jit(solution)/shard_map/ppermute | solution.py:466
  156.1 4.7 %collective-permute-done.12 = f16[1,328,128]{2,1,0:T(8,128)(2,1)S(1)} collective-permute-done((f16[1,328,128]{2,1,0:T(8,128)(2,1)S(1)}, f16[1,328,128]{2,1,0:T(8,128)(2,1)S(1)}, u32[]{:S(2)}, u32[]{:S(2)}) %collective-permute-start.12) | collective-permute-done | bytes 84000 | tf_op jit(solution)/shard_map/ppermute | solution.py:466
  162.9 9.0 %shard_map.173 = (bf16[128,2560]{1,0:T(8,128)(2,1)}, f32[128,256]{1,0:T(8,128)}, f32[128,40]{1,0:T(8,128)}, bf16[128,2560]{1,0:T(8,128)(2,1)}) custom-call(s32[1]{0:T(128)} %bitcast.me_ref, f32[8,328,128]{2,1,0:T(8,128)} %convert_element_type.66.msg_ref, f32[8,328,128]{2,1,0:T(8,128)} %convert_element_type.59.msg_ref.msgf_ref, ...), custom_call_target="tpu_custom_call" | custom-call | flops 3355443200 | bytes 13142020 | tf_op jit(solution)/shard_map/pallas_call | solution.py:26
  175.9 2.3 %shard_map.175 = f32[80,2560]{1,0:T(8,128)} custom-call(bf16[32,112,128]{2,1,0:T(8,128)(2,1)} %copy-done.1), custom_call_target="tpu_custom_call" | custom-call | flops 917504 | bytes 1736704 | tf_op jit(solution)/shard_map/pallas_call | solution.py:26
  (74 shorter events, 47.6 us)
Async XLA Ops:
  7.2 125.2 %all-gather.2.cloned.1.call-start = ((), (), s32[]{:S(2)}) async-start(), calls=%async_computation.5 | async-start | bytes 11141120 | tf_op jit(solution)/shard_map/all_gather | solution.py:539
  9.5 6.3 %collective-permute-start = (bf16[16,2816]{1,0:T(8,128)(2,1)S(1)}, bf16[16,2816]{1,0:T(8,128)(2,1)S(1)}, u32[]{:S(2)}, u32[]{:S(2)}) collective-permute-start(bf16[16,2816]{1,0:T(8,128)(2,1)S(1)} %pad_maximum_fusion), channel_id=1, source_target_pairs={{0,1},{1,2},{2,3},{3,4},{4,5},{5,6},{6,7},{7,8},{8,9},{9,10},{10,1... | collective-permute-start | bytes 270344 | tf_op jit(solution)/shard_map/ppermute | solution.py:509
  25.0 27.1 %all-to-all-start = ((f16[8,328,128]{2,1,0:T(8,128)(2,1)}), f16[8,328,128]{2,1,0:T(8,128)(2,1)S(1)}, u32[]{:S(2)}, u32[]{:S(2)}) async-start(f16[8,328,128]{2,1,0:T(8,128)(2,1)} %convert_element_type.51), calls=%async_computation | async-start | bytes 1343488 | tf_op jit(solution)/shard_map/all_to_all | solution.py:458
  53.4 3.7 %copy-start.2 = (f32[8,328,128]{2,1,0:T(8,128)S(1)}, f32[8,328,128]{2,1,0:T(8,128)}, u32[]{:S(2)}) copy-start(f32[8,328,128]{2,1,0:T(8,128)} %shard_map.166) | copy-start | bytes 4030468
  58.0 24.0 %all-to-all-start.1 = ((f16[8,328,128]{2,1,0:T(8,128)(2,1)}), f16[8,328,128]{2,1,0:T(8,128)(2,1)S(1)}, u32[]{:S(2)}, u32[]{:S(2)}) async-start(f16[8,328,128]{2,1,0:T(8,128)(2,1)} %convert_element_type.57), calls=%async_computation.1 | async-start | bytes 1343488 | tf_op jit(solution)/shard_map/all_to_all | solution.py:458
  62.4 9.6 %collective-permute-start.1 = (f16[1,328,128]{2,1,0:T(8,128)(2,1)S(1)}, f16[1,328,128]{2,1,0:T(8,128)(2,1)S(1)}, u32[]{:S(2)}, u32[]{:S(2)}) collective-permute-start(f16[1,328,128]{2,1,0:T(8,128)(2,1)S(1)} %convert_element_type.53), channel_id=1, source_target_pairs={{0,8},{1,9},{2,10},{3,11},{4,12},{5,13},{6,14},{7,15},{8,16},{9,17... | collective-permute-start | bytes 251912 | tf_op jit(solution)/shard_map/ppermute | solution.py:489
  66.0 8.6 %collective-permute-start.2 = (f16[1,328,128]{2,1,0:T(8,128)(2,1)S(1)}, f16[1,328,128]{2,1,0:T(8,128)(2,1)S(1)}, u32[]{:S(2)}, u32[]{:S(2)}) collective-permute-start(f16[1,328,128]{2,1,0:T(8,128)(2,1)S(1)} %convert_element_type.53), channel_id=1, source_target_pairs={{0,16},{1,17},{2,18},{3,19},{4,20},{5,21},{6,22},{7,23},{8,24},{9,... | collective-permute-start | bytes 251912 | tf_op jit(solution)/shard_map/ppermute | solution.py:489
  70.5 7.0 %collective-permute-start.3 = (f16[1,328,128]{2,1,0:T(8,128)(2,1)S(1)}, f16[1,328,128]{2,1,0:T(8,128)(2,1)S(1)}, u32[]{:S(2)}, u32[]{:S(2)}) collective-permute-start(f16[1,328,128]{2,1,0:T(8,128)(2,1)S(1)} %convert_element_type.53), channel_id=1, source_target_pairs={{0,24},{1,25},{2,26},{3,27},{4,28},{5,29},{6,30},{7,31}} | collective-permute-start | bytes 251912 | tf_op jit(solution)/shard_map/ppermute | solution.py:489
  84.3 25.4 %all-to-all-start.2 = ((f16[8,328,128]{2,1,0:T(8,128)(2,1)}), f16[8,328,128]{2,1,0:T(8,128)(2,1)S(1)}, u32[]{:S(2)}, u32[]{:S(2)}) async-start(f16[8,328,128]{2,1,0:T(8,128)(2,1)} %convert_element_type.58), calls=%async_computation.2 | async-start | bytes 1343488 | tf_op jit(solution)/shard_map/all_to_all | solution.py:458
  89.0 7.5 %copy-start.4 = (f32[40]{0:T(128)S(1)}, f32[40]{0:T(128)}, u32[]{:S(2)}) copy-start(f32[40]{0:T(128)} %param.23) | copy-start | bytes 484
  92.6 6.7 %collective-permute-start.4 = (f16[1,328,128]{2,1,0:T(8,128)(2,1)S(1)}, f16[1,328,128]{2,1,0:T(8,128)(2,1)S(1)}, u32[]{:S(2)}, u32[]{:S(2)}) collective-permute-start(f16[1,328,128]{2,1,0:T(8,128)(2,1)S(1)} %convert_element_type.61), channel_id=1, source_target_pairs={{8,0},{9,1},{10,2},{11,3},{12,4},{13,5},{14,6},{15,7},{16,8},{17,9... | collective-permute-start | bytes 251912 | tf_op jit(solution)/shard_map/ppermute | solution.py:489
  93.9 7.6 %collective-permute-start.5 = (f16[1,328,128]{2,1,0:T(8,128)(2,1)S(1)}, f16[1,328,128]{2,1,0:T(8,128)(2,1)S(1)}, u32[]{:S(2)}, u32[]{:S(2)}) collective-permute-start(f16[1,328,128]{2,1,0:T(8,128)(2,1)S(1)} %convert_element_type.61), channel_id=1, source_target_pairs={{16,0},{17,1},{18,2},{19,3},{20,4},{21,5},{22,6},{23,7},{24,8},{25... | collective-permute-start | bytes 251912 | tf_op jit(solution)/shard_map/ppermute | solution.py:489
  95.2 9.9 %collective-permute-start.6 = (f16[1,328,128]{2,1,0:T(8,128)(2,1)S(1)}, f16[1,328,128]{2,1,0:T(8,128)(2,1)S(1)}, u32[]{:S(2)}, u32[]{:S(2)}) collective-permute-start(f16[1,328,128]{2,1,0:T(8,128)(2,1)S(1)} %convert_element_type.61), channel_id=1, source_target_pairs={{24,0},{25,1},{26,2},{27,3},{28,4},{29,5},{30,6},{31,7}} | collective-permute-start | bytes 251912 | tf_op jit(solution)/shard_map/ppermute | solution.py:489
  140.0 2.8 %copy-start = (f32[8,328,128]{2,1,0:T(8,128)S(1)}, f32[8,328,128]{2,1,0:T(8,128)}, u32[]{:S(2)}) copy-start(f32[8,328,128]{2,1,0:T(8,128)} %shard_map.172) | copy-start | bytes 4030468
  140.0 35.0 %all-to-all-start.4 = ((bf16[32,112,128]{2,1,0:T(8,128)(2,1)}), bf16[32,112,128]{2,1,0:T(8,128)(2,1)S(1)}, u32[]{:S(2)}, u32[]{:S(2)}) async-start(bf16[32,112,128]{2,1,0:T(8,128)(2,1)} %shard_map.174), calls=%async_computation.4 | async-start | bytes 1835008 | tf_op jit(solution)/shard_map/all_to_all | solution.py:656
  143.0 3.7 %collective-permute-start.7 = (f16[1,328,128]{2,1,0:T(8,128)(2,1)S(1)}, f16[1,328,128]{2,1,0:T(8,128)(2,1)S(1)}, u32[]{:S(2)}, u32[]{:S(2)}) collective-permute-start(f16[1,328,128]{2,1,0:T(8,128)(2,1)S(1)} %get-tuple-element.78), channel_id=1, source_target_pairs={{0,1},{1,0},{2,3},{3,2},{4,5},{5,4},{6,7},{7,6},{8,9},{9,8},{10,11... | collective-permute-start | bytes 251912 | tf_op jit(solution)/shard_map/ppermute | solution.py:466
  143.2 11.6 %collective-permute-start.8 = (f16[1,328,128]{2,1,0:T(8,128)(2,1)S(1)}, f16[1,328,128]{2,1,0:T(8,128)(2,1)S(1)}, u32[]{:S(2)}, u32[]{:S(2)}) collective-permute-start(f16[1,328,128]{2,1,0:T(8,128)(2,1)S(1)} %get-tuple-element.77), channel_id=1, source_target_pairs={{0,2},{1,3},{2,0},{3,1},{4,6},{5,7},{6,4},{7,5},{8,10},{9,11},{10,... | collective-permute-start | bytes 251912 | tf_op jit(solution)/shard_map/ppermute | solution.py:466
  144.9 11.1 %collective-permute-start.9 = (f16[1,328,128]{2,1,0:T(8,128)(2,1)S(1)}, f16[1,328,128]{2,1,0:T(8,128)(2,1)S(1)}, u32[]{:S(2)}, u32[]{:S(2)}) collective-permute-start(f16[1,328,128]{2,1,0:T(8,128)(2,1)S(1)} %get-tuple-element.76), channel_id=1, source_target_pairs={{0,3},{1,2},{2,1},{3,0},{4,7},{5,6},{6,5},{7,4},{8,11},{9,10},{10,... | collective-permute-start | bytes 251912 | tf_op jit(solution)/shard_map/ppermute | solution.py:466
  145.0 11.0 %collective-permute-start.10 = (f16[1,328,128]{2,1,0:T(8,128)(2,1)S(1)}, f16[1,328,128]{2,1,0:T(8,128)(2,1)S(1)}, u32[]{:S(2)}, u32[]{:S(2)}) collective-permute-start(f16[1,328,128]{2,1,0:T(8,128)(2,1)S(1)} %get-tuple-element.75), channel_id=1, source_target_pairs={{0,4},{1,5},{2,6},{3,7},{4,0},{5,1},{6,2},{7,3},{8,12},{9,13},{10,... | collective-permute-start | bytes 251912 | tf_op jit(solution)/shard_map/ppermute | solution.py:466
  146.6 9.5 %collective-permute-start.11 = (f16[1,328,128]{2,1,0:T(8,128)(2,1)S(1)}, f16[1,328,128]{2,1,0:T(8,128)(2,1)S(1)}, u32[]{:S(2)}, u32[]{:S(2)}) collective-permute-start(f16[1,328,128]{2,1,0:T(8,128)(2,1)S(1)} %get-tuple-element.74), channel_id=1, source_target_pairs={{0,5},{1,4},{2,7},{3,6},{4,1},{5,0},{6,3},{7,2},{8,13},{9,12},{10,... | collective-permute-start | bytes 251912 | tf_op jit(solution)/shard_map/ppermute | solution.py:466
  146.7 14.1 %collective-permute-start.12 = (f16[1,328,128]{2,1,0:T(8,128)(2,1)S(1)}, f16[1,328,128]{2,1,0:T(8,128)(2,1)S(1)}, u32[]{:S(2)}, u32[]{:S(2)}) collective-permute-start(f16[1,328,128]{2,1,0:T(8,128)(2,1)S(1)} %get-tuple-element.73), channel_id=1, source_target_pairs={{0,6},{1,7},{2,4},{3,5},{4,2},{5,3},{6,0},{7,1},{8,14},{9,15},{10,... | collective-permute-start | bytes 251912 | tf_op jit(solution)/shard_map/ppermute | solution.py:466
  154.8 6.9 %collective-permute-start.13 = (f16[1,328,128]{2,1,0:T(8,128)(2,1)S(1)}, f16[1,328,128]{2,1,0:T(8,128)(2,1)S(1)}, u32[]{:S(2)}, u32[]{:S(2)}) collective-permute-start(f16[1,328,128]{2,1,0:T(8,128)(2,1)S(1)} %get-tuple-element.72), channel_id=1, source_target_pairs={{0,7},{1,6},{2,5},{3,4},{4,3},{5,2},{6,1},{7,0},{8,15},{9,14},{10,... | collective-permute-start | bytes 251912 | tf_op jit(solution)/shard_map/ppermute | solution.py:466
  162.9 10.5 %copy-start.3 = (f32[128,256]{1,0:T(8,128)S(1)}, f32[128,256]{1,0:T(8,128)}, u32[]{:S(2)}) copy-start(f32[128,256]{1,0:T(8,128)} %get-tuple-element.63) | copy-start | bytes 393220
  174.9 0.9 copy-start.1
Sparse Core Ops, SparseCore 0:
  9.6 76.3 all-gather.1

commit v3 on v2

--- a/solution.py
+++ b/solution.py
@@ -16,18 +16,18 @@
 HIGH = lax.Precision.HIGHEST
 SMEM = pl.BlockSpec(memory_space=pltpu.SMEM)
 VMEM = pl.BlockSpec(memory_space=pltpu.VMEM)
-GRANT = 60 * 1024 * 1024
+MIB = 1024 * 1024
 STREAMS = 4
 
 
-def call(kernel, out_shapes, operands, flops, scratch=(), specs=None):
+def call(kernel, out_shapes, operands, flops, vmem, scratch=(), specs=None):
     extra = {} if specs is None else {"in_specs": specs}
     moved = sum(a.size * a.dtype.itemsize for a in (*operands, *out_shapes))
     return pl.pallas_call(
         kernel,
         out_shape=tuple(out_shapes),
         scratch_shapes=list(scratch),
-        compiler_params=pltpu.CompilerParams(vmem_limit_bytes=GRANT),
+        compiler_params=pltpu.CompilerParams(vmem_limit_bytes=vmem * MIB),
         cost_estimate=pl.CostEstimate(flops=flops, bytes_accessed=moved, transcendentals=0),
         **extra,
     )(*operands)
@@ -194,7 +194,7 @@
 
 
 def prepare_kernel(
-    heads_in, size, rows, x_ref, rim_ref, bc_ref, rim_bc_ref, wx_ref, bx_ref, wbc_ref, bbc_ref, dt_ref,
+    heads_in, size, rows, x_ref, bc_ref, wx_ref, wbc_ref, bbc_ref, rim_ref, rim_bc_ref, bx_ref, dt_ref,
     per_ref, act_ref, slope_ref, abc_ref, sbc_ref, step_ref, ld_ref, stept_ref, ldt_ref, dtw_ref, perw_ref, msg_ref,
     xs_ref, bs_ref, st_ref,
 ):
@@ -473,7 +473,7 @@
 
 def group_total(held, rows, reverse):
     (total,) = call(
-        functools.partial(total_kernel, rows, reverse), [shape((1, *held.shape[1:]))], [held], 4 * held.size
+        functools.partial(total_kernel, rows, reverse), [shape((1, *held.shape[1:]))], [held], 4 * held.size, 12
     )
     return total.astype(jnp.float16)
 
@@ -492,6 +492,7 @@
         [shape(held.shape)],
         [me, held, *others],
         8 * held.size,
+        12,
         specs=[SMEM] + [VMEM] * (1 + len(others)),
     )
     return folded
@@ -556,17 +557,18 @@
         + [shape((plane, block, LANES))],
         [
             x_raw,
-            rim[:, :channels],
             bc_raw,
-            rim[:, channels:],
             conv_x,
-            conv_x_bias[None, :],
             conv_bc,
             conv_bc_bias[None, :],
+            rim[:, :channels],
+            rim[:, channels:],
+            conv_x_bias[None, :],
             dt_raw,
             jnp.stack([dt_bias, a_log]),
         ],
         20 * unit,
+        20,
         [
             pltpu.VMEM((length + 8, channels), F32),
             pltpu.VMEM((length + 8, bc_raw.shape[1]), F32),
@@ -589,7 +591,7 @@
         + [pl.BlockSpec((length, part), lambda i: (0, i))],
         out_specs=(pl.BlockSpec((length, part), lambda i: (0, i)), pl.BlockSpec((length, part), lambda i: (0, i))),
         out_shape=(shape(whole), shape(whole)),
-        compiler_params=pltpu.CompilerParams(vmem_limit_bytes=GRANT),
+        compiler_params=pltpu.CompilerParams(vmem_limit_bytes=24 * MIB),
         cost_estimate=pl.CostEstimate(
             flops=2 * length * channels * width, bytes_accessed=2 * channels * width, transcendentals=0
         ),
@@ -599,6 +601,7 @@
         [shape((plane, block, LANES))],
         [grad_y, act_bc, ld],
         10 * unit,
+        12,
         [stored],
     )
     y_within, grad_within, grad_bc_within = call(
@@ -606,6 +609,7 @@
         [shape(whole), shape(whole), shape(act_bc.shape)],
         [act_x, grad_y, act_bc, step, ld, step_t, ld_t],
         40 * unit,
+        16,
         [pltpu.VMEM(square, F32)],
     )
     message, total, y_within = lax.optimization_barrier(
@@ -620,12 +624,13 @@
         [shape((size, share, length), BF16), shape(whole)],
         [state_message, act_x, gate_branch, act_bc, ld, y_within, skip],
         20 * unit,
+        16,
         [stored],
     )
     entered = enter(me, held_carry, group_total(held_carry, rows, True), rows, True)
-    gated, entered = lax.optimization_barrier((gated, entered))
+    gated, entered, gathered = lax.optimization_barrier((gated, entered, gathered))
     held = lax.all_to_all(gated, "ctx", 0, 0, axis_index_groups=groups, tiled=True)
-    carry_message = swapped(entered)
+    held, carry_message = lax.optimization_barrier((held, swapped(entered)))
     out_rows = width // count
     part = width
     for candidate in (640, 1280):
@@ -648,7 +653,7 @@
         out_specs=pl.BlockSpec((part // out_rows, *dims), lambda i: (i, 0, 0)),
         out_shape=shape((count, *dims), BF16),
         scratch_shapes=[pltpu.VMEM((share, size * length), BF16)],
-        compiler_params=pltpu.CompilerParams(vmem_limit_bytes=GRANT),
+        compiler_params=pltpu.CompilerParams(vmem_limit_bytes=24 * MIB),
         cost_estimate=pl.CostEstimate(
             flops=2 * size * length * share * width, bytes_accessed=2 * size * length * width, transcendentals=0
         ),
@@ -659,6 +664,7 @@
         [shape((out_rows, channels))],
         [parts],
         2 * parts.size,
+        12,
     )
     grad_x_conv, grad_bc, grad_dt_raw, grad_z = call(
         functools.partial(backward_kernel, heads_in, head_size, rows),
@@ -683,6 +689,7 @@
             per_head,
         ],
         40 * unit,
+        28,
         [stored, stored, pltpu.VMEM((LANES, LANES), F32)],
         [SMEM] + [VMEM] * 16,
     )

time: 187 us -> 179 us (0.957)
  Pallas kernels: 64.2 us -> 32.6 us
  local copies, waits for them, and re-layouts: 9.21 us -> 39.3 us
  blocking collectives: 16.2 us -> 0 us
  waiting for transfers between devices: 23.5 us -> 34.9 us
  other arithmetic: 18.9 us -> 9.19 us
  starting transfers between devices: 38.8 us -> 46.5 us
    unnamed x18 -> x86, local copies, waits for them, and re-layouts: 4.13 us -> 36.6 us
    pallas_call x10, Pallas kernels: 47 us -> 21.4 us  [call(): pl.pallas_call(kernel, out_shape=tuple(out_shapes), scratch_shapes=list(s...]
    all_to_all x1 -> x0, blocking collectives: 16.2 us -> none  [per_device(): lax.all_to_all(gated, 'ctx', 0, 0, axis_index_groups=groups, tiled=True)]
    all_to_all x1, waiting for transfers between devices: 0.01 us -> 6.43 us  [per_device(): parts = lax.all_to_all(partial, 'ctx', 0, 0, tiled=True)]
    ppermute x6, waiting for transfers between devices: 10.6 us -> 16.1 us  [enter(): others.append(lax.ppermute(total, 'ctx', pairs).astype(F32))]
    all_to_all x0 -> x1, starting transfers between devices: none -> 3.98 us  [per_device(): lax.all_to_all(gated, 'ctx', 0, 0, axis_index_groups=groups, tiled=True)]
    convert_element_type x6, other arithmetic: 4.05 us -> 0.08 us  [enter(): others.append(lax.ppermute(total, 'ctx', pairs).astype(F32))]
    pallas_call x1, Pallas kernels: 9.6 us -> 5.85 us  [per_device(): pl.pallas_call(gate_kernel, grid=(channels // part,), in_specs=[pl.BlockS...]
  transfers between devices with their start and end apart: 19 -> 20, of which waited for: 9 -> 10; matrix products, arithmetic and copies ran while one was open for 15% -> 8% of each run, Pallas kernels for 29% -> 15%
where the time goes in v3:
time: 179 us; the launch traced here: 177 us
  starting transfers between devices  46.5 us (26%)
  local copies, waits for them, and re-layouts  39.3 us (22%)
  waiting for transfers between devices  34.9 us (19%)
  Pallas kernels  32.6 us (18%)
  between operations  14.5 us (8%)
  other arithmetic  9.19 us (5%)
    unnamed x86, local copies, waits for them, and re-layouts  36.6 us
    pallas_call x10, Pallas kernels, call(): pl.pallas_call(kernel, out_shape=tuple(out_shapes), scratch_shapes=list(s...  21.4 us
    ppermute x6, waiting for transfers between devices, enter(): others.append(lax.ppermute(total, 'ctx', pairs).astype(F32))  16.1 us
    ppermute x6, starting transfers between devices, enter(): others.append(lax.ppermute(total, 'ctx', pairs).astype(F32))  15.8 us
    all_to_all x3, starting transfers between devices, exchange(): lax.all_to_all(half, 'ctx', 0, 0, axis_index_groups=groups, tiled=True)  14.8 us
    ppermute x7, waiting for transfers between devices, swapped(): lax.ppermute(half[m:m + 1], 'ctx', [(at, at ^ m) for at in range(count)])  10.9 us
    ppermute x7, starting transfers between devices, swapped(): lax.ppermute(half[m:m + 1], 'ctx', [(at, at ^ m) for at in range(count)])  6.78 us
    all_to_all x1, waiting for transfers between devices, per_device(): parts = lax.all_to_all(partial, 'ctx', 0, 0, tiled=True)  6.43 us
  transfers between devices with their start and end apart: 20, of which 10 were waited for; matrix products, arithmetic and copies ran while one was open for 8% of the time, Pallas kernels for 15%

profile of v3, /device:TPU:0, one launch (start us, length us, event | category | flops | bytes accessed | tf_op | source)
XLA Modules:
  0.0 177.0 jit_solution(2532466527615982474)
XLA Ops:
  9.5 2.4 %collective-permute-start = (bf16[16,2816]{1,0:T(8,128)(2,1)S(1)}, bf16[16,2816]{1,0:T(8,128)(2,1)S(1)}, u32[]{:S(2)}, u32[]{:S(2)}) collective-permute-start(bf16[16,2816]{1,0:T(8,128)(2,1)S(1)} %pad_maximum_fusion), channel_id=1, source_target_pairs={{0,1},{1,2},{2,3},{3,4},{4,5},{5,6},{6,7},{7,8},{8,9},{9,10},{10,1... | collective-permute-start | bytes 270344 | tf_op jit(solution)/shard_map/ppermute | solution.py:510
  18.2 2.8 %shard_map.164 = (f32[128,2560]{1,0:T(8,128)S(1)}, f32[128,2560]{1,0:T(8,128)S(1)}, f32[128,256]{1,0:T(8,128)S(1)}, f32[128,256]{1,0:T(8,128)S(1)}, f32[128,128]...) custom-call(bf16[128,2560]{1,0:T(8,128)(2,1)S(1)} %copy-done.8, ...), custom_call_target="tpu_custom_call" | custom-call | flops 1677721600 | bytes 5446976 | tf_op jit(solution)/shard_map/pallas_call | solution.py:26
  24.7 6.4 %all-to-all-start = ((f16[8,328,128]{2,1,0:T(8,128)(2,1)}), f16[8,328,128]{2,1,0:T(8,128)(2,1)}, u32[]{:S(2)}, u32[]{:S(2)}) async-start(f16[8,328,128]{2,1,0:T(8,128)(2,1)} %convert_element_type.51), calls=%async_computation | async-start | bytes 1343488 | tf_op jit(solution)/shard_map/all_to_all | solution.py:458
  31.1 4.9 %copy-done = bf16[2560,2560]{1,0:T(8,128)(2,1)S(1)} copy-done((bf16[2560,2560]{1,0:T(8,128)(2,1)S(1)}, bf16[2560,2560]{1,0:T(8,128)(2,1)}, u32[]{:S(2)}) %copy-start) | copy-done | bytes 13107224
  36.0 5.9 %shard_map.165 = (f32[128,2560]{1,0:T(8,128)S(1)}, f32[128,2560]{1,0:T(8,128)S(1)}) custom-call(bf16[128,2560]{1,0:T(8,128)(2,1)S(1)} %copy-done.2, bf16[2560,2560]{1,0:T(8,128)(2,1)S(1)} %copy-done, bf16[2560,2560]{1,0:T(8,128)(2,1)S(1)} %copy-done, bf16[2560,2560]{1,0:T(8,128)(2,1)S(1)} %copy-done, bf16[2560,2560]{1,0:T(8,128)(2,1)S(1)} %copy-done, ...), custom_call_target="tpu_custom_call" | custom-call | flops 1677721600 | bytes 13107200 | tf_op jit(solution)/shard_map/pallas_call | solution.py:581
  44.2 4.6 %shard_map.168 = (f32[128,2560]{1,0:T(8,128)S(1)}, f32[128,2560]{1,0:T(8,128)S(1)}, f32[128,256]{1,0:T(8,128)S(1)}) custom-call(f32[128,2560]{1,0:T(8,128)S(1)} %copy-done.18, f32[128,2560]{1,0:T(8,128)S(1)} %get-tuple-element.42.gy_ref, f32[128,256]{1,0:T(8,128)S(1)} %get-tuple-element.43.abc_ref, f32[128,128]{1,0:T(8,128)S(1)} %get-tuple-element.46.step_ref, ...), custom_call_target="tpu_custom_call" | custom-call | flops 3355443200 | bytes 5767168 | tf_op jit(solution)/shard_map/pallas_call | solution.py:26
  54.5 4.2 %all-to-all-start.1 = ((f16[8,328,128]{2,1,0:T(8,128)(2,1)}), f16[8,328,128]{2,1,0:T(8,128)(2,1)}, u32[]{:S(2)}, u32[]{:S(2)}) async-start(f16[8,328,128]{2,1,0:T(8,128)(2,1)} %convert_element_type.57), calls=%async_computation.1 | async-start | bytes 1343488 | tf_op jit(solution)/shard_map/all_to_all | solution.py:458
  58.7 5.8 %collective-permute-start.1 = (f16[1,328,128]{2,1,0:T(8,128)(2,1)S(1)}, f16[1,328,128]{2,1,0:T(8,128)(2,1)S(1)}, u32[]{:S(2)}, u32[]{:S(2)}) collective-permute-start(f16[1,328,128]{2,1,0:T(8,128)(2,1)S(1)} %convert_element_type.53), channel_id=1, source_target_pairs={{0,8},{1,9},{2,10},{3,11},{4,12},{5,13},{6,14},{7,15},{8,16},{9,17... | collective-permute-start | bytes 251912 | tf_op jit(solution)/shard_map/ppermute | solution.py:489
  64.6 4.6 %collective-permute-start.2 = (f16[1,328,128]{2,1,0:T(8,128)(2,1)S(1)}, f16[1,328,128]{2,1,0:T(8,128)(2,1)S(1)}, u32[]{:S(2)}, u32[]{:S(2)}) collective-permute-start(f16[1,328,128]{2,1,0:T(8,128)(2,1)S(1)} %convert_element_type.53), channel_id=1, source_target_pairs={{0,16},{1,17},{2,18},{3,19},{4,20},{5,21},{6,22},{7,23},{8,24},{9,... | collective-permute-start | bytes 251912 | tf_op jit(solution)/shard_map/ppermute | solution.py:489
  70.7 2.0 %collective-permute-done.2 = f16[1,328,128]{2,1,0:T(8,128)(2,1)S(1)} collective-permute-done((f16[1,328,128]{2,1,0:T(8,128)(2,1)S(1)}, f16[1,328,128]{2,1,0:T(8,128)(2,1)S(1)}, u32[]{:S(2)}, u32[]{:S(2)}) %collective-permute-start.2) | collective-permute-done | bytes 84000 | tf_op jit(solution)/shard_map/ppermute | solution.py:489
  72.7 2.8 %collective-permute-done.3 = f16[1,328,128]{2,1,0:T(8,128)(2,1)S(1)} collective-permute-done((f16[1,328,128]{2,1,0:T(8,128)(2,1)S(1)}, f16[1,328,128]{2,1,0:T(8,128)(2,1)S(1)}, u32[]{:S(2)}, u32[]{:S(2)}) %collective-permute-start.3) | collective-permute-done | bytes 84000 | tf_op jit(solution)/shard_map/ppermute | solution.py:489
  78.5 4.2 %all-to-all-start.2 = ((f16[8,328,128]{2,1,0:T(8,128)(2,1)}), f16[8,328,128]{2,1,0:T(8,128)(2,1)}, u32[]{:S(2)}, u32[]{:S(2)}) async-start(f16[8,328,128]{2,1,0:T(8,128)(2,1)} %convert_element_type.58), calls=%async_computation.2 | async-start | bytes 1343488 | tf_op jit(solution)/shard_map/all_to_all | solution.py:458
  88.7 4.8 %collective-permute-done.4 = f16[1,328,128]{2,1,0:T(8,128)(2,1)S(1)} collective-permute-done((f16[1,328,128]{2,1,0:T(8,128)(2,1)S(1)}, f16[1,328,128]{2,1,0:T(8,128)(2,1)S(1)}, u32[]{:S(2)}, u32[]{:S(2)}) %collective-permute-start.4) | collective-permute-done | bytes 84000 | tf_op jit(solution)/shard_map/ppermute | solution.py:489
  93.5 6.6 %collective-permute-done.5 = f16[1,328,128]{2,1,0:T(8,128)(2,1)S(1)} collective-permute-done((f16[1,328,128]{2,1,0:T(8,128)(2,1)S(1)}, f16[1,328,128]{2,1,0:T(8,128)(2,1)S(1)}, u32[]{:S(2)}, u32[]{:S(2)}) %collective-permute-start.5) | collective-permute-done | bytes 84000 | tf_op jit(solution)/shard_map/ppermute | solution.py:489
  105.4 2.6 %shard_map.170 = (bf16[16,160,128]{2,1,0:T(8,128)(2,1)}, f32[128,2560]{1,0:T(8,128)S(1)}) custom-call(f32[8,328,128]{2,1,0:T(8,128)S(1)} %convert_element_type.59.msg_ref.msgf_ref, f32[128,2560]{1,0:T(8,128)S(1)} %copy-done.19, bf16[128,2560]{1,0:T(8,128)(2,1)S(1)} %copy-done.7, f32[128,256]{1,0:T(8,128)S(1)} %copy-done.28, ...), custom_call_target="tpu_custom_call" | custom-call | flops 1677721600 | bytes 6793216 | tf_op jit(solution)/shard_map/pallas_call | solution.py:26
  110.2 4.0 %all-to-all-start.3 = ((bf16[16,160,128]{2,1,0:T(8,128)(2,1)}), bf16[16,160,128]{2,1,0:T(8,128)(2,1)S(1)}, u32[]{:S(2)}, u32[]{:S(2)}) async-start(bf16[16,160,128]{2,1,0:T(8,128)(2,1)} %get-tuple-element.56), calls=%async_computation.3 | async-start | bytes 1310720 | tf_op jit(solution)/shard_map/all_to_all | solution.py:632
  118.4 2.6 %collective-permute-start.12 = (f16[1,328,128]{2,1,0:T(8,128)(2,1)S(1)}, f16[1,328,128]{2,1,0:T(8,128)(2,1)S(1)}, u32[]{:S(2)}, u32[]{:S(2)}) collective-permute-start(f16[1,328,128]{2,1,0:T(8,128)(2,1)S(1)} %get-tuple-element.79), channel_id=1, source_target_pairs={{0,6},{1,7},{2,4},{3,5},{4,2},{5,3},{6,0},{7,1},{8,14},{9,15},{10,... | collective-permute-start | bytes 251912 | tf_op jit(solution)/shard_map/ppermute | solution.py:466
  121.0 5.6 %collective-permute-done.8 = f16[1,328,128]{2,1,0:T(8,128)(2,1)S(1)} collective-permute-done((f16[1,328,128]{2,1,0:T(8,128)(2,1)S(1)}, f16[1,328,128]{2,1,0:T(8,128)(2,1)S(1)}, u32[]{:S(2)}, u32[]{:S(2)}) %collective-permute-start.8) | collective-permute-done | bytes 84000 | tf_op jit(solution)/shard_map/ppermute | solution.py:466
  127.6 3.1 %collective-permute-done.12 = f16[1,328,128]{2,1,0:T(8,128)(2,1)S(1)} collective-permute-done((f16[1,328,128]{2,1,0:T(8,128)(2,1)S(1)}, f16[1,328,128]{2,1,0:T(8,128)(2,1)S(1)}, u32[]{:S(2)}, u32[]{:S(2)}) %collective-permute-start.12) | collective-permute-done | bytes 84000 | tf_op jit(solution)/shard_map/ppermute | solution.py:466
  133.5 4.0 %copy-done.1 = bf16[2048,2560]{1,0:T(8,128)(2,1)S(1)} copy-done((bf16[2048,2560]{1,0:T(8,128)(2,1)S(1)}, bf16[2048,2560]{1,0:T(8,128)(2,1)}, u32[]{:S(2)}) %copy-start.1) | copy-done | bytes 10485784
  137.5 5.3 %shard_map.174 = bf16[32,112,128]{2,1,0:T(8,128)(2,1)} custom-call(bf16[16,160,128]{2,1,0:T(8,128)(2,1)S(1)} %all-to-all-done.3.held_ref, bf16[2048,2560]{1,0:T(8,128)(2,1)S(1)} %copy-done.1, bf16[2048,2560]{1,0:T(8,128)(2,1)S(1)} %copy-done.1, bf16[2048,2560]{1,0:T(8,128)(2,1)S(1)} %copy-done.1, bf16[2048,2560]{1,0:T(8,128)(2,1)S(1)} %copy-done.1), custom_call_target="tpu_custom_call" | custom-call | flops 1677721600 | bytes 10485760 | tf_op jit(solution)/shard_map/pallas_call | solution.py:643
  142.8 2.8 %all-to-all-start.4 = ((bf16[32,112,128]{2,1,0:T(8,128)(2,1)}), bf16[32,112,128]{2,1,0:T(8,128)(2,1)S(1)}, u32[]{:S(2)}, u32[]{:S(2)}) async-start(bf16[32,112,128]{2,1,0:T(8,128)(2,1)} %shard_map.174), calls=%async_computation.4 | async-start | bytes 1835008 | tf_op jit(solution)/shard_map/all_to_all | solution.py:661
  156.6 4.6 %shard_map.173 = (bf16[128,2560]{1,0:T(8,128)(2,1)}, f32[128,256]{1,0:T(8,128)S(1)}, f32[128,40]{1,0:T(8,128)S(1)}, bf16[128,2560]{1,0:T(8,128)(2,1)}) custom-call(s32[1]{0:T(128)} %bitcast.me_ref, f32[8,328,128]{2,1,0:T(8,128)S(1)} %copy-done.5, f32[8,328,128]{2,1,0:T(8,128)S(1)} %copy-done.4, f32[128,2560]{1,0:T(8,128)S(1)} %copy-done.20, ...), custom_call_target="tpu_custom_call" | custom-call | flops 3355443200 | bytes 13142020 | tf_op jit(solution)/shard_map/pallas_call | solution.py:26
  162.6 6.4 %all-to-all-done.4.parts_ref = bf16[32,112,128]{2,1,0:T(8,128)(2,1)S(1)} async-done(((bf16[32,112,128]{2,1,0:T(8,128)(2,1)}), bf16[32,112,128]{2,1,0:T(8,128)(2,1)S(1)}, u32[]{:S(2)}, u32[]{:S(2)}) %all-to-all-start.4) | async-done | bytes 917536 | tf_op jit(solution)/shard_map/all_to_all | solution.py:661
  (143 shorter events, 59.4 us)
Async XLA Ops:
  7.2 103.0 %all-gather.2.cloned.1.call-start = ((), (), s32[]{:S(2)}) async-start(), calls=%async_computation.5 | async-start | bytes 11141120 | tf_op jit(solution)/shard_map/all_gather | solution.py:540
  9.5 4.6 %collective-permute-start = (bf16[16,2816]{1,0:T(8,128)(2,1)S(1)}, bf16[16,2816]{1,0:T(8,128)(2,1)S(1)}, u32[]{:S(2)}, u32[]{:S(2)}) collective-permute-start(bf16[16,2816]{1,0:T(8,128)(2,1)S(1)} %pad_maximum_fusion), channel_id=1, source_target_pairs={{0,1},{1,2},{2,3},{3,4},{4,5},{5,6},{6,7},{7,8},{8,9},{9,10},{10,1... | collective-permute-start | bytes 270344 | tf_op jit(solution)/shard_map/ppermute | solution.py:510
  23.7 19.8 %copy-start.27 = (f32[128,256]{1,0:T(8,128)}, f32[128,256]{1,0:T(8,128)S(1)}, u32[]{:S(2)}) copy-start(f32[128,256]{1,0:T(8,128)S(1)} %get-tuple-element.43.abc_ref) | copy-start | bytes 393220
  23.7 19.8 %copy-start.34 = (f32[128,128]{1,0:T(8,128)}, f32[128,128]{1,0:T(8,128)S(1)}, u32[]{:S(2)}) copy-start(f32[128,128]{1,0:T(8,128)S(1)} %get-tuple-element.46.step_ref) | copy-start | bytes 196612
  23.7 7.4 %copy-start.2 = (bf16[128,2560]{1,0:T(8,128)(2,1)S(1)}, bf16[128,2560]{1,0:T(8,128)(2,1)}, u32[]{:S(2)}) copy-start(bf16[128,2560]{1,0:T(8,128)(2,1)} %go_ref) | copy-start | bytes 1966084
  23.7 7.4 %copy-start.6 = (bf16[128,2560]{1,0:T(8,128)(2,1)S(1)}, bf16[128,2560]{1,0:T(8,128)(2,1)}, u32[]{:S(2)}) copy-start(bf16[128,2560]{1,0:T(8,128)(2,1)} %gate_ref.3) | copy-start | bytes 1966084
  24.7 27.0 %all-to-all-start = ((f16[8,328,128]{2,1,0:T(8,128)(2,1)}), f16[8,328,128]{2,1,0:T(8,128)(2,1)}, u32[]{:S(2)}, u32[]{:S(2)}) async-start(f16[8,328,128]{2,1,0:T(8,128)(2,1)} %convert_element_type.51), calls=%async_computation | async-start | bytes 1343488 | tf_op jit(solution)/shard_map/all_to_all | solution.py:458
  54.5 23.1 %all-to-all-start.1 = ((f16[8,328,128]{2,1,0:T(8,128)(2,1)}), f16[8,328,128]{2,1,0:T(8,128)(2,1)}, u32[]{:S(2)}, u32[]{:S(2)}) async-start(f16[8,328,128]{2,1,0:T(8,128)(2,1)} %convert_element_type.57), calls=%async_computation.1 | async-start | bytes 1343488 | tf_op jit(solution)/shard_map/all_to_all | solution.py:458
  58.7 11.9 %collective-permute-start.1 = (f16[1,328,128]{2,1,0:T(8,128)(2,1)S(1)}, f16[1,328,128]{2,1,0:T(8,128)(2,1)S(1)}, u32[]{:S(2)}, u32[]{:S(2)}) collective-permute-start(f16[1,328,128]{2,1,0:T(8,128)(2,1)S(1)} %convert_element_type.53), channel_id=1, source_target_pairs={{0,8},{1,9},{2,10},{3,11},{4,12},{5,13},{6,14},{7,15},{8,16},{9,17... | collective-permute-start | bytes 251912 | tf_op jit(solution)/shard_map/ppermute | solution.py:489
  64.6 8.1 %collective-permute-start.2 = (f16[1,328,128]{2,1,0:T(8,128)(2,1)S(1)}, f16[1,328,128]{2,1,0:T(8,128)(2,1)S(1)}, u32[]{:S(2)}, u32[]{:S(2)}) collective-permute-start(f16[1,328,128]{2,1,0:T(8,128)(2,1)S(1)} %convert_element_type.53), channel_id=1, source_target_pairs={{0,16},{1,17},{2,18},{3,19},{4,20},{5,21},{6,22},{7,23},{8,24},{9,... | collective-permute-start | bytes 251912 | tf_op jit(solution)/shard_map/ppermute | solution.py:489
  69.1 6.3 %collective-permute-start.3 = (f16[1,328,128]{2,1,0:T(8,128)(2,1)S(1)}, f16[1,328,128]{2,1,0:T(8,128)(2,1)S(1)}, u32[]{:S(2)}, u32[]{:S(2)}) collective-permute-start(f16[1,328,128]{2,1,0:T(8,128)(2,1)S(1)} %convert_element_type.53), channel_id=1, source_target_pairs={{0,24},{1,25},{2,26},{3,27},{4,28},{5,29},{6,30},{7,31}} | collective-permute-start | bytes 251912 | tf_op jit(solution)/shard_map/ppermute | solution.py:489
  78.5 22.9 %all-to-all-start.2 = ((f16[8,328,128]{2,1,0:T(8,128)(2,1)}), f16[8,328,128]{2,1,0:T(8,128)(2,1)}, u32[]{:S(2)}, u32[]{:S(2)}) async-start(f16[8,328,128]{2,1,0:T(8,128)(2,1)} %convert_element_type.58), calls=%async_computation.2 | async-start | bytes 1343488 | tf_op jit(solution)/shard_map/all_to_all | solution.py:458
  84.6 8.8 %collective-permute-start.4 = (f16[1,328,128]{2,1,0:T(8,128)(2,1)S(1)}, f16[1,328,128]{2,1,0:T(8,128)(2,1)S(1)}, u32[]{:S(2)}, u32[]{:S(2)}) collective-permute-start(f16[1,328,128]{2,1,0:T(8,128)(2,1)S(1)} %convert_element_type.61), channel_id=1, source_target_pairs={{8,0},{9,1},{10,2},{11,3},{12,4},{13,5},{14,6},{15,7},{16,8},{17,9... | collective-permute-start | bytes 251912 | tf_op jit(solution)/shard_map/ppermute | solution.py:489
  85.9 14.1 %collective-permute-start.5 = (f16[1,328,128]{2,1,0:T(8,128)(2,1)S(1)}, f16[1,328,128]{2,1,0:T(8,128)(2,1)S(1)}, u32[]{:S(2)}, u32[]{:S(2)}) collective-permute-start(f16[1,328,128]{2,1,0:T(8,128)(2,1)S(1)} %convert_element_type.61), channel_id=1, source_target_pairs={{16,0},{17,1},{18,2},{19,3},{20,4},{21,5},{22,6},{23,7},{24,8},{25... | collective-permute-start | bytes 251912 | tf_op jit(solution)/shard_map/ppermute | solution.py:489
  87.2 12.8 %collective-permute-start.6 = (f16[1,328,128]{2,1,0:T(8,128)(2,1)S(1)}, f16[1,328,128]{2,1,0:T(8,128)(2,1)S(1)}, u32[]{:S(2)}, u32[]{:S(2)}) collective-permute-start(f16[1,328,128]{2,1,0:T(8,128)(2,1)S(1)} %convert_element_type.61), channel_id=1, source_target_pairs={{24,0},{25,1},{26,2},{27,3},{28,4},{29,5},{30,6},{31,7}} | collective-permute-start | bytes 251912 | tf_op jit(solution)/shard_map/ppermute | solution.py:489
  110.2 23.4 %all-to-all-start.3 = ((bf16[16,160,128]{2,1,0:T(8,128)(2,1)}), bf16[16,160,128]{2,1,0:T(8,128)(2,1)S(1)}, u32[]{:S(2)}, u32[]{:S(2)}) async-start(bf16[16,160,128]{2,1,0:T(8,128)(2,1)} %get-tuple-element.56), calls=%async_computation.3 | async-start | bytes 1310720 | tf_op jit(solution)/shard_map/all_to_all | solution.py:632
  114.4 4.0 %collective-permute-start.7 = (f16[1,328,128]{2,1,0:T(8,128)(2,1)S(1)}, f16[1,328,128]{2,1,0:T(8,128)(2,1)S(1)}, u32[]{:S(2)}, u32[]{:S(2)}) collective-permute-start(f16[1,328,128]{2,1,0:T(8,128)(2,1)S(1)} %get-tuple-element.84), channel_id=1, source_target_pairs={{0,1},{1,0},{2,3},{3,2},{4,5},{5,4},{6,7},{7,6},{8,9},{9,8},{10,11... | collective-permute-start | bytes 251912 | tf_op jit(solution)/shard_map/ppermute | solution.py:466
  114.9 11.7 %collective-permute-start.8 = (f16[1,328,128]{2,1,0:T(8,128)(2,1)S(1)}, f16[1,328,128]{2,1,0:T(8,128)(2,1)S(1)}, u32[]{:S(2)}, u32[]{:S(2)}) collective-permute-start(f16[1,328,128]{2,1,0:T(8,128)(2,1)S(1)} %get-tuple-element.83), channel_id=1, source_target_pairs={{0,2},{1,3},{2,0},{3,1},{4,6},{5,7},{6,4},{7,5},{8,10},{9,11},{10,... | collective-permute-start | bytes 251912 | tf_op jit(solution)/shard_map/ppermute | solution.py:466
  116.6 10.9 %collective-permute-start.9 = (f16[1,328,128]{2,1,0:T(8,128)(2,1)S(1)}, f16[1,328,128]{2,1,0:T(8,128)(2,1)S(1)}, u32[]{:S(2)}, u32[]{:S(2)}) collective-permute-start(f16[1,328,128]{2,1,0:T(8,128)(2,1)S(1)} %get-tuple-element.82), channel_id=1, source_target_pairs={{0,3},{1,2},{2,1},{3,0},{4,7},{5,6},{6,5},{7,4},{8,11},{9,10},{10,... | collective-permute-start | bytes 251912 | tf_op jit(solution)/shard_map/ppermute | solution.py:466
  116.6 10.9 %collective-permute-start.10 = (f16[1,328,128]{2,1,0:T(8,128)(2,1)S(1)}, f16[1,328,128]{2,1,0:T(8,128)(2,1)S(1)}, u32[]{:S(2)}, u32[]{:S(2)}) collective-permute-start(f16[1,328,128]{2,1,0:T(8,128)(2,1)S(1)} %get-tuple-element.81), channel_id=1, source_target_pairs={{0,4},{1,5},{2,6},{3,7},{4,0},{5,1},{6,2},{7,3},{8,12},{9,13},{10,... | collective-permute-start | bytes 251912 | tf_op jit(solution)/shard_map/ppermute | solution.py:466
  118.3 9.3 %collective-permute-start.11 = (f16[1,328,128]{2,1,0:T(8,128)(2,1)S(1)}, f16[1,328,128]{2,1,0:T(8,128)(2,1)S(1)}, u32[]{:S(2)}, u32[]{:S(2)}) collective-permute-start(f16[1,328,128]{2,1,0:T(8,128)(2,1)S(1)} %get-tuple-element.80), channel_id=1, source_target_pairs={{0,5},{1,4},{2,7},{3,6},{4,1},{5,0},{6,3},{7,2},{8,13},{9,12},{10,... | collective-permute-start | bytes 251912 | tf_op jit(solution)/shard_map/ppermute | solution.py:466
  118.4 12.3 %collective-permute-start.12 = (f16[1,328,128]{2,1,0:T(8,128)(2,1)S(1)}, f16[1,328,128]{2,1,0:T(8,128)(2,1)S(1)}, u32[]{:S(2)}, u32[]{:S(2)}) collective-permute-start(f16[1,328,128]{2,1,0:T(8,128)(2,1)S(1)} %get-tuple-element.79), channel_id=1, source_target_pairs={{0,6},{1,7},{2,4},{3,5},{4,2},{5,3},{6,0},{7,1},{8,14},{9,15},{10,... | collective-permute-start | bytes 251912 | tf_op jit(solution)/shard_map/ppermute | solution.py:466
  126.6 5.7 %collective-permute-start.13 = (f16[1,328,128]{2,1,0:T(8,128)(2,1)S(1)}, f16[1,328,128]{2,1,0:T(8,128)(2,1)S(1)}, u32[]{:S(2)}, u32[]{:S(2)}) collective-permute-start(f16[1,328,128]{2,1,0:T(8,128)(2,1)S(1)} %get-tuple-element.78), channel_id=1, source_target_pairs={{0,7},{1,6},{2,5},{3,4},{4,3},{5,2},{6,1},{7,0},{8,15},{9,14},{10,... | collective-permute-start | bytes 251912 | tf_op jit(solution)/shard_map/ppermute | solution.py:466
  142.8 26.2 %all-to-all-start.4 = ((bf16[32,112,128]{2,1,0:T(8,128)(2,1)}), bf16[32,112,128]{2,1,0:T(8,128)(2,1)S(1)}, u32[]{:S(2)}, u32[]{:S(2)}) async-start(bf16[32,112,128]{2,1,0:T(8,128)(2,1)} %shard_map.174), calls=%async_computation.4 | async-start | bytes 1835008 | tf_op jit(solution)/shard_map/all_to_all | solution.py:661
  (35 other events, 55.5 us)
Sparse Core Ops, SparseCore 0:
  9.6 76.4 all-gather.1

commit v4 on v3

--- a/solution.py
+++ b/solution.py
@@ -133,12 +133,12 @@
     return tables
 
 
-def pack_blocks(source, message, last_exp, size, rows):
+def pack_blocks(source, message, last_exp, size, rows, me=0):
     count = message.shape[0]
     tables = decay_tables(last_exp, source.shape[0] // size, size, rows, count)
     for d in range(count):
         block = source[rows * d : rows * (d + 1), :]
-        write_block(message, d, 0, block, tables[d], exponent_of(block))
+        write_block(message, me ^ d, 0, block, tables[d], exponent_of(block))
 
 
 def decay_lines(message, at, rows):
@@ -167,8 +167,16 @@
         target[rows * d : rows * (d + 1), :] = read_block(message, me ^ d, rows)
 
 
-def total_kernel(rows, reverse, held_ref, out_ref):
+def in_order(me_ref, held_ref, order_ref):
+    for s in range(held_ref.shape[0]):
+        order_ref[s] = held_ref[me_ref[0] ^ s]
+    return order_ref
+
+
+def total_kernel(rows, reverse, me_ref, held_ref, out_ref, order_ref):
     count = held_ref.shape[0]
+    if reverse:
+        held_ref = in_order(me_ref, held_ref, order_ref)
     columns = decay_columns(held_ref, rows)
     state = None
     for s in range(count - 1, -1, -1) if reverse else range(count):
@@ -181,8 +189,10 @@
 
 
 def fold_kernel(rows, reverse, me_ref, held_ref, *refs):
-    others, out_ref = refs[:-1], refs[-1]
+    others, out_ref, order_ref = refs[:-2], refs[-2], refs[-1]
     count = held_ref.shape[0]
+    if reverse:
+        held_ref = in_order(me_ref, held_ref, order_ref)
     columns = decay_columns(held_ref, rows)
     state = jnp.zeros((rows, LANES), F32)
     for other in reversed(others):
@@ -244,7 +254,7 @@
     pack_blocks(st_ref, msg_ref, jnp.exp(last), size, rows)
 
 
-def grad_kernel(heads_in, size, rows, gy_ref, abc_ref, ld_ref, msg_ref, st_ref):
+def grad_kernel(heads_in, size, rows, me_ref, gy_ref, abc_ref, ld_ref, msg_ref, st_ref):
     length = gy_ref.shape[0]
     c_rows = split(abc_ref[:, LANES : 2 * LANES])
     grown = jnp.exp(ld_ref[...])
@@ -252,7 +262,7 @@
         cols = slice(j * LANES, (j + 1) * LANES)
         scaled = gy_ref[:, cols] * spread(grown, j, heads_in, size)
         st_ref[cols, :] = dot3(split(scaled.T), c_rows)
-    pack_blocks(st_ref, msg_ref, grown[length - 1 : length], size, rows)
+    pack_blocks(st_ref, msg_ref, grown[length - 1 : length], size, rows, me_ref[0])
 
 
 def gate_kernel(go_ref, *refs):
@@ -334,9 +344,34 @@
             gt_ref[to, at : at + 16, :] = turned[k : k + 16]
 
 
+def ahead_kernel(
+    heads_in, size, rows, msg_ref, act_ref, gy_ref, ld_ref, gbcl_ref, ys_ref, gg_ref, gate_ref, skip_ref,
+    gz_ref, yg_ref, gbc_ref, st_ref,
+):
+    unpack_blocks(msg_ref, st_ref, rows)
+    grown = jnp.exp(ld_ref[...])
+    sums = jnp.zeros(yg_ref.shape, F32)
+    grad_c = gbcl_ref[:, LANES : 2 * LANES]
+    for j in range(act_ref.shape[1] // LANES):
+        cols = slice(j * LANES, (j + 1) * LANES)
+        grad_y = gy_ref[:, cols]
+        within = ys_ref[:, cols]
+        gate = gate_ref[:, cols].astype(F32)
+        opened = sigmoid(gate)
+        output = within + skip_ref[:, cols] * act_ref[:, cols]
+        gz_ref[:, cols] = (gg_ref[:, cols] * output * (opened * (1.0 + gate * (1.0 - opened)))).astype(BF16)
+        onehot = head_of(j, heads_in, size)
+        high, low = split(grad_y * within)
+        sums = sums + (dot(high, onehot, NN) + dot(low, onehot, NN))
+        grad_c = grad_c + dot3(split(spread(grown, j, heads_in, size) * grad_y), split(st_ref[cols, :]))
+    yg_ref[...] = sums
+    gbc_ref[:, 0:LANES] = gbcl_ref[:, 0:LANES]
+    gbc_ref[:, LANES : 2 * LANES] = grad_c
+
+
 def backward_kernel(
     heads_in, size, rows, me_ref, msg_ref, msgf_ref, act_ref, slope_ref, gy_ref, abc_ref, step_ref, ld_ref, gw_ref,
-    gbcl_ref, ys_ref, gg_ref, gate_ref, skip_ref, dtw_ref, perw_ref, gx_ref, gbc_ref, gdt_ref, gz_ref,
+    gbcl_ref, yg_ref, skip_ref, dtw_ref, perw_ref, gx_ref, gbc_ref, gdt_ref,
     ca_ref, st_ref, cs_ref,
 ):
     length = act_ref.shape[0]
@@ -346,13 +381,10 @@
     ld = ld_ref[...]
     step = step_ref[...]
     last = ld[length - 1 : length]
-    grown = jnp.exp(ld)
     weight = jnp.exp(last - ld) * step
     sums = jnp.zeros((length, LANES), F32)
-    sums_y = jnp.zeros((length, LANES), F32)
     leaving = jnp.zeros((8, LANES), F32)
     grad_b = gbcl_ref[:, 0:LANES]
-    grad_c = gbcl_ref[:, LANES : 2 * LANES]
     cs_ref[...] = jnp.zeros_like(cs_ref)
     for j in range(act_ref.shape[1] // LANES):
         cols = slice(j * LANES, (j + 1) * LANES)
@@ -366,13 +398,6 @@
         grad_in = gw_ref[:, cols] + gone
         gx_ref[:, cols] = ((skip_ref[:, cols] * grad_y + grad_in) * slope_ref[:, cols]).astype(BF16)
         onehot = head_of(j, heads_in, size)
-        within = ys_ref[:, cols]
-        gate = gate_ref[:, cols].astype(F32)
-        opened = sigmoid(gate)
-        output = within + skip_ref[:, cols] * inputs
-        gz_ref[:, cols] = (gg_ref[:, cols] * output * (opened * (1.0 + gate * (1.0 - opened)))).astype(BF16)
-        high, low = split(grad_y * within)
-        sums_y = sums_y + (dot(high, onehot, NN) + dot(low, onehot, NN))
         high, low = split(inputs * grad_in)
         sums = sums + (dot(high, onehot, NN) + dot(low, onehot, NN))
         folded = jnp.sum((inputs * gone).reshape(length // 8, 8, LANES), axis=0)
@@ -383,16 +408,15 @@
             h = j * heads_in + k
             cs_ref[h : h + 1, :] = jnp.sum(product[k * size : (k + 1) * size], axis=0, keepdims=True)
         grad_b = grad_b + dot3(split(wide * inputs), carry_s)
-        grad_c = grad_c + dot3(split(spread(grown, j, heads_in, size) * grad_y), split(state))
     gbc_ref[:, 0:LANES] = grad_b
-    gbc_ref[:, LANES : 2 * LANES] = grad_c
+    gbc_ref[:, LANES : 2 * LANES] = gbcl_ref[:, LANES : 2 * LANES]
     both = lax.dot_general(
         jnp.ones((8, LANES), F32), cs_ref[...], (NT, ((), ())), precision=HIGH, preferred_element_type=F32
     )
     constant = jnp.sum(leaving, axis=0, keepdims=True) + jnp.exp(last) * both[0:1]
     upper = jnp.where(row_ids(length) <= lane_ids(length), 1.0, 0.0)
     grad_rate = constant + lax.dot_general(
-        upper, sums_y - sums, (NN, ((), ())), precision=HIGH, preferred_element_type=F32
+        upper, yg_ref[...] - sums, (NN, ((), ())), precision=HIGH, preferred_element_type=F32
     )
     grad_step = sums / step - jnp.exp(perw_ref[1:2, :]) * grad_rate
     gdt_ref[...] = (grad_step * sigmoid(dtw_ref[...]))[:, 0 : gdt_ref.shape[1]]
@@ -471,9 +495,15 @@
     return [list(range(at, at + size)) for at in range(0, count, size)]
 
 
-def group_total(held, rows, reverse):
+def group_total(me, held, rows, reverse):
     (total,) = call(
-        functools.partial(total_kernel, rows, reverse), [shape((1, *held.shape[1:]))], [held], 4 * held.size, 12
+        functools.partial(total_kernel, rows, reverse),
+        [shape((1, *held.shape[1:]))],
+        [me, held],
+        4 * held.size,
+        12,
+        [pltpu.VMEM(held.shape, F32)],
+        [SMEM, VMEM],
     )
     return total.astype(jnp.float16)
 
@@ -493,7 +523,8 @@
         [me, held, *others],
         8 * held.size,
         12,
-        specs=[SMEM] + [VMEM] * (1 + len(others)),
+        [pltpu.VMEM(held.shape, F32)],
+        [SMEM] + [VMEM] * (1 + len(others)),
     )
     return folded
 
@@ -591,7 +622,7 @@
         + [pl.BlockSpec((length, part), lambda i: (0, i))],
         out_specs=(pl.BlockSpec((length, part), lambda i: (0, i)), pl.BlockSpec((length, part), lambda i: (0, i))),
         out_shape=(shape(whole), shape(whole)),
-        compiler_params=pltpu.CompilerParams(vmem_limit_bytes=24 * MIB),
+        compiler_params=pltpu.CompilerParams(vmem_limit_bytes=52 * MIB),
         cost_estimate=pl.CostEstimate(
             flops=2 * length * channels * width, bytes_accessed=2 * channels * width, transcendentals=0
         ),
@@ -599,10 +630,11 @@
     (message,) = call(
         functools.partial(grad_kernel, heads_in, head_size, rows),
         [shape((plane, block, LANES))],
-        [grad_y, act_bc, ld],
+        [me, grad_y, act_bc, ld],
         10 * unit,
         12,
         [stored],
+        [SMEM] + [VMEM] * 3,
     )
     y_within, grad_within, grad_bc_within = call(
         functools.partial(local_kernel, heads_in, head_size),
@@ -612,12 +644,11 @@
         16,
         [pltpu.VMEM(square, F32)],
     )
-    message, total, y_within = lax.optimization_barrier(
-        (message, group_total(held_state, rows, False), y_within)
-    )
-    held_carry = exchange(message, planes)
-    folded, held_carry = lax.optimization_barrier((enter(me, held_state, total, rows, False), held_carry))
-    held_carry = held_carry.astype(F32)
+    total, y_within, message = lax.optimization_barrier(
+        (group_total(me, held_state, rows, False), y_within, message)
+    )
+    folded, message = lax.optimization_barrier((enter(me, held_state, total, rows, False), message))
+    held_carry = swapped(message)
     state_message = exchange(folded, planes).astype(F32)
     gated, y_ahead = call(
         functools.partial(forward_kernel, heads_in, head_size, rows),
@@ -627,10 +658,18 @@
         16,
         [stored],
     )
-    entered = enter(me, held_carry, group_total(held_carry, rows, True), rows, True)
-    gated, entered, gathered = lax.optimization_barrier((gated, entered, gathered))
+    gated, held_carry, gathered, y_ahead = lax.optimization_barrier((gated, held_carry, gathered, y_ahead))
     held = lax.all_to_all(gated, "ctx", 0, 0, axis_index_groups=groups, tiled=True)
-    held, carry_message = lax.optimization_barrier((held, swapped(entered)))
+    entered = enter(me, held_carry, group_total(me, held_carry, rows, True), rows, True)
+    grad_z, y_sums, grad_bc_ahead = call(
+        functools.partial(ahead_kernel, heads_in, head_size, rows),
+        [shape(whole, BF16), shape(square), shape(act_bc.shape)],
+        [state_message, act_x, grad_y, ld, grad_bc_within, y_ahead, grad_gated, gate_branch, skip],
+        20 * unit,
+        16,
+        [stored],
+    )
+    held, entered, y_sums = lax.optimization_barrier((held, entered, y_sums))
     out_rows = width // count
     part = width
     for candidate in (640, 1280):
@@ -653,12 +692,14 @@
         out_specs=pl.BlockSpec((part // out_rows, *dims), lambda i: (i, 0, 0)),
         out_shape=shape((count, *dims), BF16),
         scratch_shapes=[pltpu.VMEM((share, size * length), BF16)],
-        compiler_params=pltpu.CompilerParams(vmem_limit_bytes=24 * MIB),
+        compiler_params=pltpu.CompilerParams(vmem_limit_bytes=54 * MIB),
         cost_estimate=pl.CostEstimate(
             flops=2 * size * length * share * width, bytes_accessed=2 * size * length * width, transcendentals=0
         ),
     )(held, *[gathered] * STREAMS)
+    partial, entered = lax.optimization_barrier((partial, entered))
     parts = lax.all_to_all(partial, "ctx", 0, 0, tiled=True)
+    carry_message = swapped(entered)
     (weight_grad,) = call(
         functools.partial(assemble_kernel, out_rows, size, share),
         [shape((out_rows, channels))],
@@ -666,9 +707,9 @@
         2 * parts.size,
         12,
     )
-    grad_x_conv, grad_bc, grad_dt_raw, grad_z = call(
+    grad_x_conv, grad_bc, grad_dt_raw = call(
         functools.partial(backward_kernel, heads_in, head_size, rows),
-        [shape(whole, BF16), shape(act_bc.shape), shape(dt_raw.shape), shape(whole, BF16)],
+        [shape(whole, BF16), shape(act_bc.shape), shape(dt_raw.shape)],
         [
             me,
             carry_message,
@@ -680,10 +721,8 @@
             step,
             ld,
             grad_within,
-            grad_bc_within,
-            y_ahead,
-            grad_gated,
-            gate_branch,
+            grad_bc_ahead,
+            y_sums,
             skip,
             raised,
             per_head,
@@ -691,7 +730,7 @@
         40 * unit,
         28,
         [stored, stored, pltpu.VMEM((LANES, LANES), F32)],
-        [SMEM] + [VMEM] * 16,
+        [SMEM] + [VMEM] * 14,
     )
     grad_bc_conv = (lax.psum(grad_bc, "tp") * slope_bc).astype(BF16)
     return (grad_x_conv, grad_bc_conv, grad_z, grad_dt_raw, weight_grad)

time: 179 us -> 172 us (0.961)
  local copies, waits for them, and re-layouts: 39.3 us -> 25 us
  Pallas kernels: 32.6 us -> 39.9 us
  other arithmetic: 9.19 us -> 5.04 us
  waiting for transfers between devices: 34.9 us -> 37.4 us
  starting transfers between devices: 46.5 us -> 48.6 us
    unnamed x86 -> x98, local copies, waits for them, and re-layouts: 36.6 us -> 21.5 us
    ppermute x7 -> x14, waiting for transfers between devices: 10.9 us -> 23.3 us  [swapped(): lax.ppermute(half[m:m + 1], 'ctx', [(at, at ^ m) for at in range(count)])]
    all_to_all x1, waiting for transfers between devices: 6.43 us -> 0.01 us  [per_device(): parts = lax.all_to_all(partial, 'ctx', 0, 0, tiled=True)]
    ppermute x7 -> x14, starting transfers between devices: 6.78 us -> 12.6 us  [swapped(): lax.ppermute(half[m:m + 1], 'ctx', [(at, at ^ m) for at in range(count)])]
    all_to_all x3 -> x2, starting transfers between devices: 14.8 us -> 10.6 us  [exchange(): lax.all_to_all(half, 'ctx', 0, 0, axis_index_groups=groups, tiled=True)]
    pallas_call x1, Pallas kernels: 5.85 us -> 8.82 us  [per_device(): pl.pallas_call(gate_kernel, grid=(channels // part,), in_specs=[pl.BlockS...]
    ppermute x6, waiting for transfers between devices: 16.1 us -> 13.2 us  [enter(): others.append(lax.ppermute(total, 'ctx', pairs).astype(F32))]
    pallas_call x1, Pallas kernels: 5.29 us -> 7.58 us  [per_device(): pl.pallas_call(functools.partial(product_kernel, out_rows), grid=(width /...]
  transfers between devices with their start and end apart: 20 -> 26, of which waited for: 10 -> 11; matrix products, arithmetic and copies ran while one was open for 8% -> 6% of each run, Pallas kernels for 15% -> 18%
where the time goes in v4:
time: 172 us; the launch traced here: 171 us
  starting transfers between devices  48.6 us (28%)
  Pallas kernels  39.9 us (23%)
  waiting for transfers between devices  37.4 us (22%)
  local copies, waits for them, and re-layouts  25 us (15%)
  between operations  14.7 us (9%)
  other arithmetic  5.04 us (3%)
    pallas_call x11, Pallas kernels, call(): pl.pallas_call(kernel, out_shape=tuple(out_shapes), scratch_shapes=list(s...  23.5 us
    ppermute x14, waiting for transfers between devices, swapped(): lax.ppermute(half[m:m + 1], 'ctx', [(at, at ^ m) for at in range(count)])  23.3 us
    unnamed x98, local copies, waits for them, and re-layouts  21.5 us
    ppermute x6, starting transfers between devices, enter(): others.append(lax.ppermute(total, 'ctx', pairs).astype(F32))  15 us
    ppermute x6, waiting for transfers between devices, enter(): others.append(lax.ppermute(total, 'ctx', pairs).astype(F32))  13.2 us
    ppermute x14, starting transfers between devices, swapped(): lax.ppermute(half[m:m + 1], 'ctx', [(at, at ^ m) for at in range(count)])  12.6 us
    all_to_all x2, starting transfers between devices, exchange(): lax.all_to_all(half, 'ctx', 0, 0, axis_index_groups=groups, tiled=True)  10.6 us
    pallas_call x1, Pallas kernels, per_device(): pl.pallas_call(gate_kernel, grid=(channels // part,), in_specs=[pl.BlockS...  8.82 us
  transfers between devices with their start and end apart: 26, of which 11 were waited for; matrix products, arithmetic and copies ran while one was open for 6% of the time, Pallas kernels for 18%

profile of v4, /device:TPU:0, one launch (start us, length us, event | category | flops | bytes accessed | tf_op | source)
XLA Modules:
  0.0 170.6 jit_solution(11089242836091619101)
XLA Ops:
  9.5 2.4 %collective-permute-start = (bf16[16,2816]{1,0:T(8,128)(2,1)S(1)}, bf16[16,2816]{1,0:T(8,128)(2,1)S(1)}, u32[]{:S(2)}, u32[]{:S(2)}) collective-permute-start(bf16[16,2816]{1,0:T(8,128)(2,1)S(1)} %pad_maximum_fusion), channel_id=1, source_target_pairs={{0,1},{1,2},{2,3},{3,4},{4,5},{5,6},{6,7},{7,8},{8,9},{9,10},{10,1... | collective-permute-start | bytes 270344 | tf_op jit(solution)/shard_map/ppermute | solution.py:541
  18.2 2.8 %shard_map.164 = (f32[128,2560]{1,0:T(8,128)S(1)}, f32[128,2560]{1,0:T(8,128)S(1)}, f32[128,256]{1,0:T(8,128)S(1)}, f32[128,256]{1,0:T(8,128)S(1)}, f32[128,128]...) custom-call(bf16[128,2560]{1,0:T(8,128)(2,1)S(1)} %copy-done.19, ...), custom_call_target="tpu_custom_call" | custom-call | flops 1677721600 | bytes 5446976 | tf_op jit(solution)/shard_map/pallas_call | solution.py:26
  25.3 6.4 %all-to-all-start = ((f16[8,328,128]{2,1,0:T(8,128)(2,1)}), f16[8,328,128]{2,1,0:T(8,128)(2,1)S(1)}, u32[]{:S(2)}, u32[]{:S(2)}) async-start(f16[8,328,128]{2,1,0:T(8,128)(2,1)} %convert_element_type.51), calls=%async_computation | async-start | bytes 1343488 | tf_op jit(solution)/shard_map/all_to_all | solution.py:482
  31.8 8.8 %shard_map.166 = (f32[128,2560]{1,0:T(8,128)}, f32[128,2560]{1,0:T(8,128)}) custom-call(bf16[128,2560]{1,0:T(8,128)(2,1)S(1)} %copy-done.3, bf16[2560,2560]{1,0:T(8,128)(2,1)} %refs_3_.1, bf16[2560,2560]{1,0:T(8,128)(2,1)} %refs_3_.1, bf16[2560,2560]{1,0:T(8,128)(2,1)} %refs_3_.1, bf16[2560,2560]{1,0:T(8,128)(2,1)} %refs_3_.1, bf16[128,2560]{1,0:T(8,128)(2,1)S(1)} %copy-done.2), custom_call_target="tpu_custom_call" | custom-call | flops 1677721600 | bytes 13107200 | tf_op jit(solution)/shard_map/pallas_call | solution.py:612
  43.7 4.6 %shard_map.167 = (f32[128,2560]{1,0:T(8,128)S(1)}, f32[128,2560]{1,0:T(8,128)S(1)}, f32[128,256]{1,0:T(8,128)S(1)}) custom-call(f32[128,2560]{1,0:T(8,128)S(1)} %copy-done.5, f32[128,2560]{1,0:T(8,128)S(1)} %copy-done.10, f32[128,256]{1,0:T(8,128)S(1)} %get-tuple-element.50.abc_ref, f32[128,128]{1,0:T(8,128)S(1)} %get-tuple-element.51.step_ref, ...), custom_call_target="tpu_custom_call" | custom-call | flops 3355443200 | bytes 5767168 | tf_op jit(solution)/shard_map/pallas_call | solution.py:26
  51.4 5.1 %collective-permute-start.1 = (f16[1,328,128]{2,1,0:T(8,128)(2,1)S(1)}, f16[1,328,128]{2,1,0:T(8,128)(2,1)S(1)}, u32[]{:S(2)}, u32[]{:S(2)}) collective-permute-start(f16[1,328,128]{2,1,0:T(8,128)(2,1)S(1)} %convert_element_type.53), channel_id=1, source_target_pairs={{0,8},{1,9},{2,10},{3,11},{4,12},{5,13},{6,14},{7,15},{8,16},{9,17... | collective-permute-start | bytes 251912 | tf_op jit(solution)/shard_map/ppermute | solution.py:519
  56.5 4.5 %collective-permute-start.2 = (f16[1,328,128]{2,1,0:T(8,128)(2,1)S(1)}, f16[1,328,128]{2,1,0:T(8,128)(2,1)S(1)}, u32[]{:S(2)}, u32[]{:S(2)}) collective-permute-start(f16[1,328,128]{2,1,0:T(8,128)(2,1)S(1)} %convert_element_type.53), channel_id=1, source_target_pairs={{0,16},{1,17},{2,18},{3,19},{4,20},{5,21},{6,22},{7,23},{8,24},{9,... | collective-permute-start | bytes 251912 | tf_op jit(solution)/shard_map/ppermute | solution.py:519
  62.5 3.1 %collective-permute-done.2 = f16[1,328,128]{2,1,0:T(8,128)(2,1)S(1)} collective-permute-done((f16[1,328,128]{2,1,0:T(8,128)(2,1)S(1)}, f16[1,328,128]{2,1,0:T(8,128)(2,1)S(1)}, u32[]{:S(2)}, u32[]{:S(2)}) %collective-permute-start.2) | collective-permute-done | bytes 84000 | tf_op jit(solution)/shard_map/ppermute | solution.py:519
  65.6 3.2 %collective-permute-done.3 = f16[1,328,128]{2,1,0:T(8,128)(2,1)S(1)} collective-permute-done((f16[1,328,128]{2,1,0:T(8,128)(2,1)S(1)}, f16[1,328,128]{2,1,0:T(8,128)(2,1)S(1)}, u32[]{:S(2)}, u32[]{:S(2)}) %collective-permute-start.3) | collective-permute-done | bytes 84000 | tf_op jit(solution)/shard_map/ppermute | solution.py:519
  71.4 1.9 %collective-permute-start.6 = (f16[1,328,128]{2,1,0:T(8,128)(2,1)}, f16[1,328,128]{2,1,0:T(8,128)(2,1)S(1)}, u32[]{:S(2)}, u32[]{:S(2)}) collective-permute-start(f16[1,328,128]{2,1,0:T(8,128)(2,1)} %get-tuple-element.102), channel_id=1, source_target_pairs={{0,3},{1,2},{2,1},{3,0},{4,7},{5,6},{6,5},{7,4},{8,11},{9,10},{10,... | collective-permute-start | bytes 251912 | tf_op jit(solution)/shard_map/ppermute | solution.py:490
  76.0 4.2 %all-to-all-start.1 = ((f16[8,328,128]{2,1,0:T(8,128)(2,1)}), f16[8,328,128]{2,1,0:T(8,128)(2,1)}, u32[]{:S(2)}, u32[]{:S(2)}) async-start(f16[8,328,128]{2,1,0:T(8,128)(2,1)} %convert_element_type.57), calls=%async_computation.1 | async-start | bytes 1343488 | tf_op jit(solution)/shard_map/all_to_all | solution.py:482
  80.2 2.8 %collective-permute-start.9 = (f16[1,328,128]{2,1,0:T(8,128)(2,1)}, f16[1,328,128]{2,1,0:T(8,128)(2,1)S(1)}, u32[]{:S(2)}, u32[]{:S(2)}) collective-permute-start(f16[1,328,128]{2,1,0:T(8,128)(2,1)} %get-tuple-element.99), channel_id=1, source_target_pairs={{0,6},{1,7},{2,4},{3,5},{4,2},{5,3},{6,0},{7,1},{8,14},{9,15},{10,... | collective-permute-start | bytes 251912 | tf_op jit(solution)/shard_map/ppermute | solution.py:490
  83.3 10.4 %collective-permute-done.9 = f16[1,328,128]{2,1,0:T(8,128)(2,1)S(1)} collective-permute-done((f16[1,328,128]{2,1,0:T(8,128)(2,1)}, f16[1,328,128]{2,1,0:T(8,128)(2,1)S(1)}, u32[]{:S(2)}, u32[]{:S(2)}) %collective-permute-start.9) | collective-permute-done | bytes 84000 | tf_op jit(solution)/shard_map/ppermute | solution.py:490
  101.3 4.3 %all-to-all-start.2 = ((bf16[16,160,128]{2,1,0:T(8,128)(2,1)}), bf16[16,160,128]{2,1,0:T(8,128)(2,1)}, u32[]{:S(2)}, u32[]{:S(2)}) async-start(bf16[16,160,128]{2,1,0:T(8,128)(2,1)} %copy-done.16), calls=%async_computation.2 | async-start | bytes 1310720 | tf_op jit(solution)/shard_map/all_to_all | solution.py:662
  114.1 2.3 %shard_map.173 = (bf16[128,2560]{1,0:T(8,128)(2,1)}, f32[128,128]{1,0:T(8,128)S(1)}, f32[128,256]{1,0:T(8,128)S(1)}) custom-call(f32[8,328,128]{2,1,0:T(8,128)S(1)} %convert_element_type.58.msg_ref.msgf_ref, f32[128,2560]{1,0:T(8,128)S(1)} %copy-done.7, f32[128,2560]{1,0:T(8,128)S(1)} %copy-done.11, f32[128,128]{1,0:T(8,128)S(1)} %get-tuple-element.52.ld_ref, ...), custom_call_target="tpu_custom_call" | custom-call | flops 1677721600 | bytes 8300544 | tf_op jit(solution)/shard_map/pallas_call | solution.py:26
  116.4 2.8 %collective-permute-done.11 = f16[1,328,128]{2,1,0:T(8,128)(2,1)S(1)} collective-permute-done((f16[1,328,128]{2,1,0:T(8,128)(2,1)S(1)}, f16[1,328,128]{2,1,0:T(8,128)(2,1)S(1)}, u32[]{:S(2)}, u32[]{:S(2)}) %collective-permute-start.11) | collective-permute-done | bytes 84000 | tf_op jit(solution)/shard_map/ppermute | solution.py:519
  119.2 4.1 %collective-permute-done.13 = f16[1,328,128]{2,1,0:T(8,128)(2,1)S(1)} collective-permute-done((f16[1,328,128]{2,1,0:T(8,128)(2,1)S(1)}, f16[1,328,128]{2,1,0:T(8,128)(2,1)S(1)}, u32[]{:S(2)}, u32[]{:S(2)}) %collective-permute-start.13) | collective-permute-done | bytes 84000 | tf_op jit(solution)/shard_map/ppermute | solution.py:519
  125.9 7.6 %shard_map.174 = bf16[32,112,128]{2,1,0:T(8,128)(2,1)} custom-call(bf16[16,160,128]{2,1,0:T(8,128)(2,1)} %all-to-all-done.2.held_ref, bf16[2048,2560]{1,0:T(8,128)(2,1)} %all-gather.2.cloned.1.call-done.refs_0_.refs_1_.refs_2_.refs_3_, bf16[2048,2560]{1,0:T(8,128)(2,1)} %all-gather.2.cloned.1.call-done.refs_0_.refs_1_.refs_2_.refs_3_, ...), custom_call_target="tpu_custom_call" | custom-call | flops 1677721600 | bytes 10485760 | tf_op jit(solution)/shard_map/pallas_call | solution.py:682
  133.4 3.7 %all-to-all-start.3 = ((bf16[32,112,128]{2,1,0:T(8,128)(2,1)}), bf16[32,112,128]{2,1,0:T(8,128)(2,1)}, u32[]{:S(2)}, u32[]{:S(2)}) async-start(bf16[32,112,128]{2,1,0:T(8,128)(2,1)} %shard_map.174), calls=%async_computation.3 | async-start | bytes 1835008 | tf_op jit(solution)/shard_map/all_to_all | solution.py:701
  141.1 2.4 %collective-permute-start.19 = (f16[1,328,128]{2,1,0:T(8,128)(2,1)S(1)}, f16[1,328,128]{2,1,0:T(8,128)(2,1)S(1)}, u32[]{:S(2)}, u32[]{:S(2)}) collective-permute-start(f16[1,328,128]{2,1,0:T(8,128)(2,1)S(1)} %get-tuple-element.91), channel_id=1, source_target_pairs={{0,6},{1,7},{2,4},{3,5},{4,2},{5,3},{6,0},{7,1},{8,14},{9,15},{10,... | collective-permute-start | bytes 251912 | tf_op jit(solution)/shard_map/ppermute | solution.py:490
  143.5 5.4 %collective-permute-done.15 = f16[1,328,128]{2,1,0:T(8,128)(2,1)S(1)} collective-permute-done((f16[1,328,128]{2,1,0:T(8,128)(2,1)S(1)}, f16[1,328,128]{2,1,0:T(8,128)(2,1)S(1)}, u32[]{:S(2)}, u32[]{:S(2)}) %collective-permute-start.15) | collective-permute-done | bytes 84000 | tf_op jit(solution)/shard_map/ppermute | solution.py:490
  150.2 4.7 %collective-permute-done.19 = f16[1,328,128]{2,1,0:T(8,128)(2,1)S(1)} collective-permute-done((f16[1,328,128]{2,1,0:T(8,128)(2,1)S(1)}, f16[1,328,128]{2,1,0:T(8,128)(2,1)S(1)}, u32[]{:S(2)}, u32[]{:S(2)}) %collective-permute-start.19) | collective-permute-done | bytes 84000 | tf_op jit(solution)/shard_map/ppermute | solution.py:490
  156.0 4.1 %shard_map.175 = (bf16[128,2560]{1,0:T(8,128)(2,1)}, f32[128,256]{1,0:T(8,128)S(1)}, f32[128,40]{1,0:T(8,128)S(1)}) custom-call(s32[1]{0:T(128)} %bitcast.me_ref, f32[8,328,128]{2,1,0:T(8,128)S(1)} %convert_element_type.66.msg_ref, f32[8,328,128]{2,1,0:T(8,128)S(1)} %convert_element_type.58.msg_ref.msgf_ref, f32[128,2560]{1,0:T(8,128)S(1)} %copy-done.8, ...), custom_call_target="tpu_custom_call" | custom-call | flops 3355443200 | bytes 9275396 | tf_op jit(solution)/shard_map/pallas_call | solution.py:26
  161.4 2.3 %shard_map.176 = f32[80,2560]{1,0:T(8,128)} custom-call(bf16[32,112,128]{2,1,0:T(8,128)(2,1)} %all-to-all-done.3.parts_ref), custom_call_target="tpu_custom_call" | custom-call | flops 917504 | bytes 1736704 | tf_op jit(solution)/shard_map/pallas_call | solution.py:26
  (170 shorter events, 52.2 us)
Async XLA Ops:
  7.2 94.1 %all-gather.2.cloned.1.call-start = ((), (), s32[]{:S(2)}) async-start(), calls=%async_computation.4 | async-start | bytes 11141120 | tf_op jit(solution)/shard_map/all_gather | solution.py:571
  25.3 25.3 %all-to-all-start = ((f16[8,328,128]{2,1,0:T(8,128)(2,1)}), f16[8,328,128]{2,1,0:T(8,128)(2,1)S(1)}, u32[]{:S(2)}, u32[]{:S(2)}) async-start(f16[8,328,128]{2,1,0:T(8,128)(2,1)} %convert_element_type.51), calls=%async_computation | async-start | bytes 1343488 | tf_op jit(solution)/shard_map/all_to_all | solution.py:482
  51.4 11.1 %collective-permute-start.1 = (f16[1,328,128]{2,1,0:T(8,128)(2,1)S(1)}, f16[1,328,128]{2,1,0:T(8,128)(2,1)S(1)}, u32[]{:S(2)}, u32[]{:S(2)}) collective-permute-start(f16[1,328,128]{2,1,0:T(8,128)(2,1)S(1)} %convert_element_type.53), channel_id=1, source_target_pairs={{0,8},{1,9},{2,10},{3,11},{4,12},{5,13},{6,14},{7,15},{8,16},{9,17... | collective-permute-start | bytes 251912 | tf_op jit(solution)/shard_map/ppermute | solution.py:519
  56.5 9.1 %collective-permute-start.2 = (f16[1,328,128]{2,1,0:T(8,128)(2,1)S(1)}, f16[1,328,128]{2,1,0:T(8,128)(2,1)S(1)}, u32[]{:S(2)}, u32[]{:S(2)}) collective-permute-start(f16[1,328,128]{2,1,0:T(8,128)(2,1)S(1)} %convert_element_type.53), channel_id=1, source_target_pairs={{0,16},{1,17},{2,18},{3,19},{4,20},{5,21},{6,22},{7,23},{8,24},{9,... | collective-permute-start | bytes 251912 | tf_op jit(solution)/shard_map/ppermute | solution.py:519
  61.0 7.8 %collective-permute-start.3 = (f16[1,328,128]{2,1,0:T(8,128)(2,1)S(1)}, f16[1,328,128]{2,1,0:T(8,128)(2,1)S(1)}, u32[]{:S(2)}, u32[]{:S(2)}) collective-permute-start(f16[1,328,128]{2,1,0:T(8,128)(2,1)S(1)} %convert_element_type.53), channel_id=1, source_target_pairs={{0,24},{1,25},{2,26},{3,27},{4,28},{5,29},{6,30},{7,31}} | collective-permute-start | bytes 251912 | tf_op jit(solution)/shard_map/ppermute | solution.py:519
  71.1 9.0 %collective-permute-start.4 = (f16[1,328,128]{2,1,0:T(8,128)(2,1)S(1)}, f16[1,328,128]{2,1,0:T(8,128)(2,1)S(1)}, u32[]{:S(2)}, u32[]{:S(2)}) collective-permute-start(f16[1,328,128]{2,1,0:T(8,128)(2,1)S(1)} %get-tuple-element.104), channel_id=1, source_target_pairs={{0,1},{1,0},{2,3},{3,2},{4,5},{5,4},{6,7},{7,6},{8,9},{9,8},{10,11... | collective-permute-start | bytes 251912 | tf_op jit(solution)/shard_map/ppermute | solution.py:490
  71.3 11.7 %collective-permute-start.5 = (f16[1,328,128]{2,1,0:T(8,128)(2,1)}, f16[1,328,128]{2,1,0:T(8,128)(2,1)S(1)}, u32[]{:S(2)}, u32[]{:S(2)}) collective-permute-start(f16[1,328,128]{2,1,0:T(8,128)(2,1)} %get-tuple-element.103), channel_id=1, source_target_pairs={{0,2},{1,3},{2,0},{3,1},{4,6},{5,7},{6,4},{7,5},{8,10},{9,11},{10,... | collective-permute-start | bytes 251912 | tf_op jit(solution)/shard_map/ppermute | solution.py:490
  71.4 11.8 %collective-permute-start.6 = (f16[1,328,128]{2,1,0:T(8,128)(2,1)}, f16[1,328,128]{2,1,0:T(8,128)(2,1)S(1)}, u32[]{:S(2)}, u32[]{:S(2)}) collective-permute-start(f16[1,328,128]{2,1,0:T(8,128)(2,1)} %get-tuple-element.102), channel_id=1, source_target_pairs={{0,3},{1,2},{2,1},{3,0},{4,7},{5,6},{6,5},{7,4},{8,11},{9,10},{10,... | collective-permute-start | bytes 251912 | tf_op jit(solution)/shard_map/ppermute | solution.py:490
  73.2 10.0 %collective-permute-start.7 = (f16[1,328,128]{2,1,0:T(8,128)(2,1)}, f16[1,328,128]{2,1,0:T(8,128)(2,1)S(1)}, u32[]{:S(2)}, u32[]{:S(2)}) collective-permute-start(f16[1,328,128]{2,1,0:T(8,128)(2,1)} %get-tuple-element.101), channel_id=1, source_target_pairs={{0,4},{1,5},{2,6},{3,7},{4,0},{5,1},{6,2},{7,3},{8,12},{9,13},{10,... | collective-permute-start | bytes 251912 | tf_op jit(solution)/shard_map/ppermute | solution.py:490
  75.0 8.2 %collective-permute-start.8 = (f16[1,328,128]{2,1,0:T(8,128)(2,1)}, f16[1,328,128]{2,1,0:T(8,128)(2,1)S(1)}, u32[]{:S(2)}, u32[]{:S(2)}) collective-permute-start(f16[1,328,128]{2,1,0:T(8,128)(2,1)} %get-tuple-element.100), channel_id=1, source_target_pairs={{0,5},{1,4},{2,7},{3,6},{4,1},{5,0},{6,3},{7,2},{8,13},{9,12},{10,... | collective-permute-start | bytes 251912 | tf_op jit(solution)/shard_map/ppermute | solution.py:490
  76.0 18.7 %all-to-all-start.1 = ((f16[8,328,128]{2,1,0:T(8,128)(2,1)}), f16[8,328,128]{2,1,0:T(8,128)(2,1)}, u32[]{:S(2)}, u32[]{:S(2)}) async-start(f16[8,328,128]{2,1,0:T(8,128)(2,1)} %convert_element_type.57), calls=%async_computation.1 | async-start | bytes 1343488 | tf_op jit(solution)/shard_map/all_to_all | solution.py:482
  80.2 13.5 %collective-permute-start.9 = (f16[1,328,128]{2,1,0:T(8,128)(2,1)}, f16[1,328,128]{2,1,0:T(8,128)(2,1)S(1)}, u32[]{:S(2)}, u32[]{:S(2)}) collective-permute-start(f16[1,328,128]{2,1,0:T(8,128)(2,1)} %get-tuple-element.99), channel_id=1, source_target_pairs={{0,6},{1,7},{2,4},{3,5},{4,2},{5,3},{6,0},{7,1},{8,14},{9,15},{10,... | collective-permute-start | bytes 251912 | tf_op jit(solution)/shard_map/ppermute | solution.py:490
  83.0 11.5 %collective-permute-start.10 = (f16[1,328,128]{2,1,0:T(8,128)(2,1)S(1)}, f16[1,328,128]{2,1,0:T(8,128)(2,1)S(1)}, u32[]{:S(2)}, u32[]{:S(2)}) collective-permute-start(f16[1,328,128]{2,1,0:T(8,128)(2,1)S(1)} %get-tuple-element.98), channel_id=1, source_target_pairs={{0,7},{1,6},{2,5},{3,4},{4,3},{5,2},{6,1},{7,0},{8,15},{9,14},{10,... | collective-permute-start | bytes 251912 | tf_op jit(solution)/shard_map/ppermute | solution.py:490
  101.3 24.6 %all-to-all-start.2 = ((bf16[16,160,128]{2,1,0:T(8,128)(2,1)}), bf16[16,160,128]{2,1,0:T(8,128)(2,1)}, u32[]{:S(2)}, u32[]{:S(2)}) async-start(bf16[16,160,128]{2,1,0:T(8,128)(2,1)} %copy-done.16), calls=%async_computation.2 | async-start | bytes 1310720 | tf_op jit(solution)/shard_map/all_to_all | solution.py:662
  106.2 12.9 %collective-permute-start.11 = (f16[1,328,128]{2,1,0:T(8,128)(2,1)S(1)}, f16[1,328,128]{2,1,0:T(8,128)(2,1)S(1)}, u32[]{:S(2)}, u32[]{:S(2)}) collective-permute-start(f16[1,328,128]{2,1,0:T(8,128)(2,1)S(1)} %convert_element_type.61), channel_id=1, source_target_pairs={{8,0},{9,1},{10,2},{11,3},{12,4},{13,5},{14,6},{15,7},{16,8},{17,9... | collective-permute-start | bytes 251912 | tf_op jit(solution)/shard_map/ppermute | solution.py:519
  107.5 11.6 %collective-permute-start.12 = (f16[1,328,128]{2,1,0:T(8,128)(2,1)S(1)}, f16[1,328,128]{2,1,0:T(8,128)(2,1)S(1)}, u32[]{:S(2)}, u32[]{:S(2)}) collective-permute-start(f16[1,328,128]{2,1,0:T(8,128)(2,1)S(1)} %convert_element_type.61), channel_id=1, source_target_pairs={{16,0},{17,1},{18,2},{19,3},{20,4},{21,5},{22,6},{23,7},{24,8},{25... | collective-permute-start | bytes 251912 | tf_op jit(solution)/shard_map/ppermute | solution.py:519
  108.8 14.5 %collective-permute-start.13 = (f16[1,328,128]{2,1,0:T(8,128)(2,1)S(1)}, f16[1,328,128]{2,1,0:T(8,128)(2,1)S(1)}, u32[]{:S(2)}, u32[]{:S(2)}) collective-permute-start(f16[1,328,128]{2,1,0:T(8,128)(2,1)S(1)} %convert_element_type.61), channel_id=1, source_target_pairs={{24,0},{25,1},{26,2},{27,3},{28,4},{29,5},{30,6},{31,7}} | collective-permute-start | bytes 251912 | tf_op jit(solution)/shard_map/ppermute | solution.py:519
  133.4 28.0 %all-to-all-start.3 = ((bf16[32,112,128]{2,1,0:T(8,128)(2,1)}), bf16[32,112,128]{2,1,0:T(8,128)(2,1)}, u32[]{:S(2)}, u32[]{:S(2)}) async-start(bf16[32,112,128]{2,1,0:T(8,128)(2,1)} %shard_map.174), calls=%async_computation.3 | async-start | bytes 1835008 | tf_op jit(solution)/shard_map/all_to_all | solution.py:701
  137.5 11.4 %collective-permute-start.15 = (f16[1,328,128]{2,1,0:T(8,128)(2,1)S(1)}, f16[1,328,128]{2,1,0:T(8,128)(2,1)S(1)}, u32[]{:S(2)}, u32[]{:S(2)}) collective-permute-start(f16[1,328,128]{2,1,0:T(8,128)(2,1)S(1)} %get-tuple-element.95), channel_id=1, source_target_pairs={{0,2},{1,3},{2,0},{3,1},{4,6},{5,7},{6,4},{7,5},{8,10},{9,11},{10,... | collective-permute-start | bytes 251912 | tf_op jit(solution)/shard_map/ppermute | solution.py:490
  139.0 11.0 %collective-permute-start.16 = (f16[1,328,128]{2,1,0:T(8,128)(2,1)S(1)}, f16[1,328,128]{2,1,0:T(8,128)(2,1)S(1)}, u32[]{:S(2)}, u32[]{:S(2)}) collective-permute-start(f16[1,328,128]{2,1,0:T(8,128)(2,1)S(1)} %get-tuple-element.94), channel_id=1, source_target_pairs={{0,3},{1,2},{2,1},{3,0},{4,7},{5,6},{6,5},{7,4},{8,11},{9,10},{10,... | collective-permute-start | bytes 251912 | tf_op jit(solution)/shard_map/ppermute | solution.py:490
  139.4 10.7 %collective-permute-start.17 = (f16[1,328,128]{2,1,0:T(8,128)(2,1)S(1)}, f16[1,328,128]{2,1,0:T(8,128)(2,1)S(1)}, u32[]{:S(2)}, u32[]{:S(2)}) collective-permute-start(f16[1,328,128]{2,1,0:T(8,128)(2,1)S(1)} %get-tuple-element.93), channel_id=1, source_target_pairs={{0,4},{1,5},{2,6},{3,7},{4,0},{5,1},{6,2},{7,3},{8,12},{9,13},{10,... | collective-permute-start | bytes 251912 | tf_op jit(solution)/shard_map/ppermute | solution.py:490
  140.7 9.4 %collective-permute-start.18 = (f16[1,328,128]{2,1,0:T(8,128)(2,1)S(1)}, f16[1,328,128]{2,1,0:T(8,128)(2,1)S(1)}, u32[]{:S(2)}, u32[]{:S(2)}) collective-permute-start(f16[1,328,128]{2,1,0:T(8,128)(2,1)S(1)} %get-tuple-element.92), channel_id=1, source_target_pairs={{0,5},{1,4},{2,7},{3,6},{4,1},{5,0},{6,3},{7,2},{8,13},{9,12},{10,... | collective-permute-start | bytes 251912 | tf_op jit(solution)/shard_map/ppermute | solution.py:490
  141.1 13.8 %collective-permute-start.19 = (f16[1,328,128]{2,1,0:T(8,128)(2,1)S(1)}, f16[1,328,128]{2,1,0:T(8,128)(2,1)S(1)}, u32[]{:S(2)}, u32[]{:S(2)}) collective-permute-start(f16[1,328,128]{2,1,0:T(8,128)(2,1)S(1)} %get-tuple-element.91), channel_id=1, source_target_pairs={{0,6},{1,7},{2,4},{3,5},{4,2},{5,3},{6,0},{7,1},{8,14},{9,15},{10,... | collective-permute-start | bytes 251912 | tf_op jit(solution)/shard_map/ppermute | solution.py:490
  148.9 6.9 %collective-permute-start.20 = (f16[1,328,128]{2,1,0:T(8,128)(2,1)S(1)}, f16[1,328,128]{2,1,0:T(8,128)(2,1)S(1)}, u32[]{:S(2)}, u32[]{:S(2)}) collective-permute-start(f16[1,328,128]{2,1,0:T(8,128)(2,1)S(1)} %get-tuple-element.90), channel_id=1, source_target_pairs={{0,7},{1,6},{2,5},{3,4},{4,3},{5,2},{6,1},{7,0},{8,15},{9,14},{10,... | collective-permute-start | bytes 251912 | tf_op jit(solution)/shard_map/ppermute | solution.py:490
  (44 other events, 202.3 us)
Sparse Core Ops, SparseCore 0:
  9.6 71.8 all-gather.1

commit v5 on v4

--- a/solution.py
+++ b/solution.py
@@ -204,25 +204,24 @@
 
 
 def prepare_kernel(
-    heads_in, size, rows, x_ref, bc_ref, wx_ref, wbc_ref, bbc_ref, rim_ref, rim_bc_ref, bx_ref, dt_ref,
-    per_ref, act_ref, slope_ref, abc_ref, sbc_ref, step_ref, ld_ref, stept_ref, ldt_ref, dtw_ref, perw_ref, msg_ref,
-    xs_ref, bs_ref, st_ref,
+    heads_in, size, rows, raw_ref, rim_ref, taps_ref, dt_ref, per_ref, act_ref, slope_ref, abc_ref, sbc_ref, step_ref, ld_ref, stept_ref, ldt_ref, dtw_ref, perw_ref, msg_ref,
+    xs_ref, st_ref,
 ):
-    length = x_ref.shape[0]
-    blocks = x_ref.shape[1] // LANES
-
-    def convolved(raw, rim, padded, weight, bias, cols):
-        padded[0:8, cols] = rim[:, cols].astype(F32)[8:16]
-        padded[8 : 8 + length, cols] = raw[:, cols].astype(F32)
-        pre = bias[:, cols] + weight[0:1, cols] * padded[5 : 5 + length, cols]
+    length, channels = act_ref.shape
+    blocks = channels // LANES
+
+    def convolved(cols):
+        xs_ref[0:8, cols] = rim_ref[:, cols].astype(F32)[8:16]
+        xs_ref[8 : 8 + length, cols] = raw_ref[:, cols].astype(F32)
+        pre = taps_ref[KERNEL : KERNEL + 1, cols] + taps_ref[0:1, cols] * xs_ref[5 : 5 + length, cols]
         for k in range(1, KERNEL):
-            pre = pre + weight[k : k + 1, cols] * padded[5 + k : 5 + k + length, cols]
+            pre = pre + taps_ref[k : k + 1, cols] * xs_ref[5 + k : 5 + k + length, cols]
         gate = sigmoid(pre)
         return pre * gate, gate * (1.0 + pre * (1.0 - gate))
 
-    for j in range(bc_ref.shape[1] // LANES):
+    for j in range(abc_ref.shape[1] // LANES):
         cols = slice(j * LANES, (j + 1) * LANES)
-        value, slope = convolved(bc_ref, rim_bc_ref, bs_ref, wbc_ref, bbc_ref, cols)
+        value, slope = convolved(slice(channels + j * LANES, channels + (j + 1) * LANES))
         abc_ref[:, cols] = value
         sbc_ref[:, cols] = slope
     b_rows = split(abc_ref[:, 0:LANES])
@@ -246,7 +245,7 @@
     weight = jnp.exp(last - ld) * step
     for j in range(blocks):
         cols = slice(j * LANES, (j + 1) * LANES)
-        value, slope = convolved(x_ref, rim_ref, xs_ref, wx_ref, bx_ref, cols)
+        value, slope = convolved(cols)
         act_ref[:, cols] = value
         slope_ref[:, cols] = slope
         scaled = value * spread(weight, j, heads_in, size)
@@ -570,7 +569,14 @@
     groups = groups_of(count, size)
     gathered = lax.all_gather(grad_out, "ctx", axis_index_groups=groups, tiled=True)
 
-    rim = from_behind(jnp.concatenate([x_raw[length - 16 :], bc_raw[length - 16 :]], axis=1), "ctx")
+    raw = jnp.concatenate([x_raw, bc_raw], axis=1)
+    taps = jnp.concatenate(
+        [
+            jnp.concatenate([conv_x, conv_bc], axis=1),
+            jnp.concatenate([conv_x_bias, conv_bc_bias])[None, :],
+        ]
+    )
+    rim = from_behind(raw[length - 16 :], "ctx")
     skip = jnp.repeat(d_skip, head_size)[None, :]
     whole = (length, channels)
     square = (length, LANES)
@@ -587,22 +593,16 @@
         + [shape(square), shape((8, LANES))]
         + [shape((plane, block, LANES))],
         [
-            x_raw,
-            bc_raw,
-            conv_x,
-            conv_bc,
-            conv_bc_bias[None, :],
-            rim[:, :channels],
-            rim[:, channels:],
-            conv_x_bias[None, :],
+            raw,
+            rim,
+            taps,
             dt_raw,
             jnp.stack([dt_bias, a_log]),
         ],
         20 * unit,
         20,
         [
-            pltpu.VMEM((length + 8, channels), F32),
-            pltpu.VMEM((length + 8, bc_raw.shape[1]), F32),
+            pltpu.VMEM((length + 8, channels + bc_raw.shape[1]), F32),
             stored,
         ],
     )
@@ -636,19 +636,18 @@
         [stored],
         [SMEM] + [VMEM] * 3,
     )
+    held_carry = swapped(message)
+    total, ld_t_then = lax.optimization_barrier((group_total(me, held_state, rows, False), ld_t))
     y_within, grad_within, grad_bc_within = call(
         functools.partial(local_kernel, heads_in, head_size),
         [shape(whole), shape(whole), shape(act_bc.shape)],
-        [act_x, grad_y, act_bc, step, ld, step_t, ld_t],
+        [act_x, grad_y, act_bc, step, ld, step_t, ld_t_then],
         40 * unit,
         16,
         [pltpu.VMEM(square, F32)],
     )
-    total, y_within, message = lax.optimization_barrier(
-        (group_total(me, held_state, rows, False), y_within, message)
-    )
-    folded, message = lax.optimization_barrier((enter(me, held_state, total, rows, False), message))
-    held_carry = swapped(message)
+    folded, held_carry = lax.optimization_barrier((enter(me, held_state, total, rows, False), held_carry))
+    entered = enter(me, held_carry, group_total(me, held_carry, rows, True), rows, True)
     state_message = exchange(folded, planes).astype(F32)
     gated, y_ahead = call(
         functools.partial(forward_kernel, heads_in, head_size, rows),
@@ -658,9 +657,8 @@
         16,
         [stored],
     )
-    gated, held_carry, gathered, y_ahead = lax.optimization_barrier((gated, held_carry, gathered, y_ahead))
+    gated, gathered, y_ahead = lax.optimization_barrier((gated, gathered, y_ahead))
     held = lax.all_to_all(gated, "ctx", 0, 0, axis_index_groups=groups, tiled=True)
-    entered = enter(me, held_carry, group_total(me, held_carry, rows, True), rows, True)
     grad_z, y_sums, grad_bc_ahead = call(
         functools.partial(ahead_kernel, heads_in, head_size, rows),
         [shape(whole, BF16), shape(square), shape(act_bc.shape)],
@@ -669,7 +667,7 @@
         16,
         [stored],
     )
-    held, entered, y_sums = lax.optimization_barrier((held, entered, y_sums))
+    held, y_sums = lax.optimization_barrier((held, y_sums))
     out_rows = width // count
     part = width
     for candidate in (640, 1280):
@@ -692,7 +690,7 @@
         out_specs=pl.BlockSpec((part // out_rows, *dims), lambda i: (i, 0, 0)),
         out_shape=shape((count, *dims), BF16),
         scratch_shapes=[pltpu.VMEM((share, size * length), BF16)],
-        compiler_params=pltpu.CompilerParams(vmem_limit_bytes=54 * MIB),
+        compiler_params=pltpu.CompilerParams(vmem_limit_bytes=48 * MIB),
         cost_estimate=pl.CostEstimate(
             flops=2 * size * length * share * width, bytes_accessed=2 * size * length * width, transcendentals=0
         ),

time: 172 us -> 184 us (1.070)
  waiting for transfers between devices: 37.4 us -> 48.5 us
  local copies, waits for them, and re-layouts: 25 us -> 23.1 us
    ppermute x6, waiting for transfers between devices: 13.2 us -> 18.8 us  [enter(): others.append(lax.ppermute(total, 'ctx', pairs).astype(F32))]
    ppermute x14, waiting for transfers between devices: 23.3 us -> 28.5 us  [swapped(): lax.ppermute(half[m:m + 1], 'ctx', [(at, at ^ m) for at in range(count)])]
    ppermute x14, starting transfers between devices: 12.6 us -> 17.2 us  [swapped(): lax.ppermute(half[m:m + 1], 'ctx', [(at, at ^ m) for at in range(count)])]
    all_to_all x2, starting transfers between devices: 10.6 us -> 7.94 us  [exchange(): lax.all_to_all(half, 'ctx', 0, 0, axis_index_groups=groups, tiled=True)]
    unnamed x98 -> x117, local copies, waits for them, and re-layouts: 21.5 us -> 21.3 us
  transfers between devices with their start and end apart: 26 -> 26, of which waited for: 11 -> 10; matrix products, arithmetic and copies ran while one was open for 6% -> 7% of each run, Pallas kernels for 18% -> 17%
where the time goes in v5:
time: 184 us; the launch traced here: 182 us
  starting transfers between devices  49.6 us (27%)
  waiting for transfers between devices  48.5 us (26%)
  Pallas kernels  40.5 us (22%)
  local copies, waits for them, and re-layouts  23.1 us (13%)
  between operations  14.9 us (8%)
  other arithmetic  5.51 us (3%)
    ppermute x14, waiting for transfers between devices, swapped(): lax.ppermute(half[m:m + 1], 'ctx', [(at, at ^ m) for at in range(count)])  28.5 us
    pallas_call x11, Pallas kernels, call(): pl.pallas_call(kernel, out_shape=tuple(out_shapes), scratch_shapes=list(s...  24 us
    unnamed x117, local copies, waits for them, and re-layouts  21.3 us
    ppermute x6, waiting for transfers between devices, enter(): others.append(lax.ppermute(total, 'ctx', pairs).astype(F32))  18.8 us
    ppermute x14, starting transfers between devices, swapped(): lax.ppermute(half[m:m + 1], 'ctx', [(at, at ^ m) for at in range(count)])  17.2 us
    ppermute x6, starting transfers between devices, enter(): others.append(lax.ppermute(total, 'ctx', pairs).astype(F32))  14.1 us
    pallas_call x1, Pallas kernels, per_device(): pl.pallas_call(gate_kernel, grid=(channels // part,), in_specs=[pl.BlockS...  9.73 us
    all_to_all x2, starting transfers between devices, exchange(): lax.all_to_all(half, 'ctx', 0, 0, axis_index_groups=groups, tiled=True)  7.94 us
  transfers between devices with their start and end apart: 26, of which 10 were waited for; matrix products, arithmetic and copies ran while one was open for 7% of the time, Pallas kernels for 17%

profile of v5, /device:TPU:0, one launch (start us, length us, event | category | flops | bytes accessed | tf_op | source)
XLA Modules:
  0.0 182.1 jit_solution(10908669887481016528)
XLA Ops:
  9.2 2.4 %collective-permute-start = (bf16[16,2816]{1,0:T(8,128)(2,1)S(1)}, bf16[16,2816]{1,0:T(8,128)(2,1)S(1)}, u32[]{:S(2)}, u32[]{:S(2)}) collective-permute-start(bf16[16,2816]{1,0:T(8,128)(2,1)S(1)} %slice.68), channel_id=1, source_target_pairs={{0,1},{1,2},{2,3},{3,4},{4,5},{5,6},{6,7},{7,8},{8,9},{9,10},{10,1... | collective-permute-start | bytes 270344 | tf_op jit(solution)/shard_map/ppermute | solution.py:540
  12.4 2.8 %shard_map.164 = (f32[128,2560]{1,0:T(8,128)S(1)}, f32[128,2560]{1,0:T(8,128)S(1)}, f32[128,256]{1,0:T(8,128)S(1)}, f32[128,256]{1,0:T(8,128)S(1)}, f32[128,128]...) custom-call(bf16[128,2816]{1,0:T(8,128)(2,1)S(1)} %constant_dynamic-, ...), custom_call_target="tpu_custom_call" | custom-call | flops 1677721600 | bytes 5446976 | tf_op jit(solution)/shard_map/pallas_call | solution.py:26
  15.4 9.7 %shard_map.167 = (f32[128,2560]{1,0:T(8,128)}, f32[128,2560]{1,0:T(8,128)}) custom-call(bf16[128,2560]{1,0:T(8,128)(2,1)S(1)} %copy-done.4, bf16[2560,2560]{1,0:T(8,128)(2,1)} %refs_3_.1, bf16[2560,2560]{1,0:T(8,128)(2,1)} %refs_3_.1, bf16[2560,2560]{1,0:T(8,128)(2,1)} %refs_3_.1, bf16[2560,2560]{1,0:T(8,128)(2,1)} %refs_3_.1, bf16[128,2560]{1,0:T(8,128)(2,1)S(1)} %copy-done.3), custom_call_target="tpu_custom_call" | custom-call | flops 1677721600 | bytes 13107200 | tf_op jit(solution)/shard_map/pallas_call | solution.py:612
  29.1 3.3 %collective-permute-start.4 = (f16[1,328,128]{2,1,0:T(8,128)(2,1)}, f16[1,328,128]{2,1,0:T(8,128)(2,1)S(1)}, u32[]{:S(2)}, u32[]{:S(2)}) collective-permute-start(f16[1,328,128]{2,1,0:T(8,128)(2,1)} %get-tuple-element.98), channel_id=1, source_target_pairs={{0,1},{1,0},{2,3},{3,2},{4,5},{5,4},{6,7},{7,6},{8,9},{9,8},{10,11... | collective-permute-start | bytes 251912 | tf_op jit(solution)/shard_map/ppermute | solution.py:489
  34.7 2.7 %collective-permute-start.7 = (f16[1,328,128]{2,1,0:T(8,128)(2,1)S(1)}, f16[1,328,128]{2,1,0:T(8,128)(2,1)S(1)}, u32[]{:S(2)}, u32[]{:S(2)}) collective-permute-start(f16[1,328,128]{2,1,0:T(8,128)(2,1)S(1)} %get-tuple-element.95), channel_id=1, source_target_pairs={{0,4},{1,5},{2,6},{3,7},{4,0},{5,1},{6,2},{7,3},{8,12},{9,13},{10,... | collective-permute-start | bytes 251912 | tf_op jit(solution)/shard_map/ppermute | solution.py:489
  38.3 3.5 %all-to-all-start = ((f16[8,328,128]{2,1,0:T(8,128)(2,1)}), f16[8,328,128]{2,1,0:T(8,128)(2,1)S(1)}, u32[]{:S(2)}, u32[]{:S(2)}) async-start(f16[8,328,128]{2,1,0:T(8,128)(2,1)} %convert_element_type.51), calls=%async_computation | async-start | bytes 1343488 | tf_op jit(solution)/shard_map/all_to_all | solution.py:481
  41.9 2.8 %collective-permute-start.9 = (f16[1,328,128]{2,1,0:T(8,128)(2,1)S(1)}, f16[1,328,128]{2,1,0:T(8,128)(2,1)S(1)}, u32[]{:S(2)}, u32[]{:S(2)}) collective-permute-start(f16[1,328,128]{2,1,0:T(8,128)(2,1)S(1)} %get-tuple-element.93), channel_id=1, source_target_pairs={{0,6},{1,7},{2,4},{3,5},{4,2},{5,3},{6,0},{7,1},{8,14},{9,15},{10,... | collective-permute-start | bytes 251912 | tf_op jit(solution)/shard_map/ppermute | solution.py:489
  48.1 16.4 %collective-permute-done.9 = f16[1,328,128]{2,1,0:T(8,128)(2,1)S(1)} collective-permute-done((f16[1,328,128]{2,1,0:T(8,128)(2,1)S(1)}, f16[1,328,128]{2,1,0:T(8,128)(2,1)S(1)}, u32[]{:S(2)}, u32[]{:S(2)}) %collective-permute-start.9) | collective-permute-done | bytes 84000 | tf_op jit(solution)/shard_map/ppermute | solution.py:489
  65.9 4.4 %collective-permute-start.1 = (f16[1,328,128]{2,1,0:T(8,128)(2,1)S(1)}, f16[1,328,128]{2,1,0:T(8,128)(2,1)S(1)}, u32[]{:S(2)}, u32[]{:S(2)}) collective-permute-start(f16[1,328,128]{2,1,0:T(8,128)(2,1)S(1)} %convert_element_type.53), channel_id=1, source_target_pairs={{0,8},{1,9},{2,10},{3,11},{4,12},{5,13},{6,14},{7,15},{8,16},{9,17... | collective-permute-start | bytes 251912 | tf_op jit(solution)/shard_map/ppermute | solution.py:518
  70.3 4.5 %collective-permute-start.2 = (f16[1,328,128]{2,1,0:T(8,128)(2,1)S(1)}, f16[1,328,128]{2,1,0:T(8,128)(2,1)S(1)}, u32[]{:S(2)}, u32[]{:S(2)}) collective-permute-start(f16[1,328,128]{2,1,0:T(8,128)(2,1)S(1)} %convert_element_type.53), channel_id=1, source_target_pairs={{0,16},{1,17},{2,18},{3,19},{4,20},{5,21},{6,22},{7,23},{8,24},{9,... | collective-permute-start | bytes 251912 | tf_op jit(solution)/shard_map/ppermute | solution.py:518
  79.5 3.0 %collective-permute-done.3 = f16[1,328,128]{2,1,0:T(8,128)(2,1)S(1)} collective-permute-done((f16[1,328,128]{2,1,0:T(8,128)(2,1)S(1)}, f16[1,328,128]{2,1,0:T(8,128)(2,1)S(1)}, u32[]{:S(2)}, u32[]{:S(2)}) %collective-permute-start.3) | collective-permute-done | bytes 84000 | tf_op jit(solution)/shard_map/ppermute | solution.py:518
  84.8 4.4 %all-to-all-start.1 = ((f16[8,328,128]{2,1,0:T(8,128)(2,1)}), f16[8,328,128]{2,1,0:T(8,128)(2,1)}, u32[]{:S(2)}, u32[]{:S(2)}) async-start(f16[8,328,128]{2,1,0:T(8,128)(2,1)} %convert_element_type.59), calls=%async_computation.1 | async-start | bytes 1343488 | tf_op jit(solution)/shard_map/all_to_all | solution.py:481
  94.1 4.7 %shard_map.169 = (f32[128,2560]{1,0:T(8,128)S(1)}, f32[128,2560]{1,0:T(8,128)S(1)}, f32[128,256]{1,0:T(8,128)S(1)}) custom-call(f32[128,2560]{1,0:T(8,128)S(1)} %get-tuple-element.51.act_ref, f32[128,2560]{1,0:T(8,128)S(1)} %copy-done.10, f32[128,256]{1,0:T(8,128)S(1)} %copy-done.24, f32[128,128]{1,0:T(8,128)S(1)} %copy-done.34, ...), custom_call_target="tpu_custom_call" | custom-call | flops 3355443200 | bytes 5767168 | tf_op jit(solution)/shard_map/pallas_call | solution.py:26
  107.7 4.3 %all-to-all-start.2 = ((bf16[16,160,128]{2,1,0:T(8,128)(2,1)}), bf16[16,160,128]{2,1,0:T(8,128)(2,1)}, u32[]{:S(2)}, u32[]{:S(2)}) async-start(bf16[16,160,128]{2,1,0:T(8,128)(2,1)} %copy-done.16), calls=%async_computation.2 | async-start | bytes 1310720 | tf_op jit(solution)/shard_map/all_to_all | solution.py:661
  116.6 9.0 %collective-permute-done.11 = f16[1,328,128]{2,1,0:T(8,128)(2,1)S(1)} collective-permute-done((f16[1,328,128]{2,1,0:T(8,128)(2,1)S(1)}, f16[1,328,128]{2,1,0:T(8,128)(2,1)S(1)}, u32[]{:S(2)}, u32[]{:S(2)}) %collective-permute-start.11) | collective-permute-done | bytes 84000 | tf_op jit(solution)/shard_map/ppermute | solution.py:518
  125.7 5.3 %collective-permute-done.13 = f16[1,328,128]{2,1,0:T(8,128)(2,1)S(1)} collective-permute-done((f16[1,328,128]{2,1,0:T(8,128)(2,1)S(1)}, f16[1,328,128]{2,1,0:T(8,128)(2,1)S(1)}, u32[]{:S(2)}, u32[]{:S(2)}) %collective-permute-start.13) | collective-permute-done | bytes 84000 | tf_op jit(solution)/shard_map/ppermute | solution.py:518
  133.6 2.4 %shard_map.171 = (bf16[128,2560]{1,0:T(8,128)(2,1)}, f32[128,128]{1,0:T(8,128)S(1)}, f32[128,256]{1,0:T(8,128)S(1)}) custom-call(f32[8,328,128]{2,1,0:T(8,128)S(1)} %convert_element_type.60.msg_ref.msgf_ref, f32[128,2560]{1,0:T(8,128)S(1)} %copy-done.7, f32[128,2560]{1,0:T(8,128)S(1)} %copy-done.11, f32[128,128]{1,0:T(8,128)S(1)} %get-tuple-element.49.ld_ref, ...), custom_call_target="tpu_custom_call" | custom-call | flops 1677721600 | bytes 8300544 | tf_op jit(solution)/shard_map/pallas_call | solution.py:26
  137.2 6.8 %shard_map.172 = bf16[32,112,128]{2,1,0:T(8,128)(2,1)S(1)} custom-call(bf16[16,160,128]{2,1,0:T(8,128)(2,1)} %all-to-all-done.2.held_ref, bf16[2048,2560]{1,0:T(8,128)(2,1)} %all-gather.2.cloned.1.call-done.refs_0_.refs_1_.refs_2_.refs_3_, bf16[2048,2560]{1,0:T(8,128)(2,1)} %all-gather.2.cloned.1.call-done.refs_0_.refs_1_.refs_2_.refs_3_, ...), custom_call_target="tpu_custom_call" | custom-call | flops 1677721600 | bytes 10485760 | tf_op jit(solution)/shard_map/pallas_call | solution.py:680
  145.0 3.7 %all-to-all-start.3 = ((bf16[32,112,128]{2,1,0:T(8,128)(2,1)}), bf16[32,112,128]{2,1,0:T(8,128)(2,1)}, u32[]{:S(2)}, u32[]{:S(2)}) async-start(bf16[32,112,128]{2,1,0:T(8,128)(2,1)} %copy-done.2), calls=%async_computation.3 | async-start | bytes 1835008 | tf_op jit(solution)/shard_map/all_to_all | solution.py:699
  152.6 2.4 %collective-permute-start.19 = (f16[1,328,128]{2,1,0:T(8,128)(2,1)S(1)}, f16[1,328,128]{2,1,0:T(8,128)(2,1)S(1)}, u32[]{:S(2)}, u32[]{:S(2)}) collective-permute-start(f16[1,328,128]{2,1,0:T(8,128)(2,1)S(1)} %get-tuple-element.85), channel_id=1, source_target_pairs={{0,6},{1,7},{2,4},{3,5},{4,2},{5,3},{6,0},{7,1},{8,14},{9,15},{10,... | collective-permute-start | bytes 251912 | tf_op jit(solution)/shard_map/ppermute | solution.py:489
  155.0 5.4 %collective-permute-done.15 = f16[1,328,128]{2,1,0:T(8,128)(2,1)S(1)} collective-permute-done((f16[1,328,128]{2,1,0:T(8,128)(2,1)S(1)}, f16[1,328,128]{2,1,0:T(8,128)(2,1)S(1)}, u32[]{:S(2)}, u32[]{:S(2)}) %collective-permute-start.15) | collective-permute-done | bytes 84000 | tf_op jit(solution)/shard_map/ppermute | solution.py:489
  161.7 4.7 %collective-permute-done.19 = f16[1,328,128]{2,1,0:T(8,128)(2,1)S(1)} collective-permute-done((f16[1,328,128]{2,1,0:T(8,128)(2,1)S(1)}, f16[1,328,128]{2,1,0:T(8,128)(2,1)S(1)}, u32[]{:S(2)}, u32[]{:S(2)}) %collective-permute-start.19) | collective-permute-done | bytes 84000 | tf_op jit(solution)/shard_map/ppermute | solution.py:489
  167.5 4.2 %shard_map.175 = (bf16[128,2560]{1,0:T(8,128)(2,1)}, f32[128,256]{1,0:T(8,128)S(1)}, f32[128,40]{1,0:T(8,128)S(1)}) custom-call(s32[1]{0:T(128)} %bitcast.me_ref, f32[8,328,128]{2,1,0:T(8,128)S(1)} %convert_element_type.66.msg_ref, f32[8,328,128]{2,1,0:T(8,128)S(1)} %convert_element_type.60.msg_ref.msgf_ref, f32[128,2560]{1,0:T(8,128)S(1)} %copy-done.8, ...), custom_call_target="tpu_custom_call" | custom-call | flops 3355443200 | bytes 9275396 | tf_op jit(solution)/shard_map/pallas_call | solution.py:26
  173.0 2.3 %shard_map.176 = f32[80,2560]{1,0:T(8,128)} custom-call(bf16[32,112,128]{2,1,0:T(8,128)(2,1)} %all-to-all-done.3.parts_ref), custom_call_target="tpu_custom_call" | custom-call | flops 917504 | bytes 1736704 | tf_op jit(solution)/shard_map/pallas_call | solution.py:26
  (188 shorter events, 52.2 us)
Async XLA Ops:
  7.2 100.5 %all-gather.2.cloned.1.call-start = ((), (), s32[]{:S(2)}) async-start(), calls=%async_computation.4 | async-start | bytes 11141120 | tf_op jit(solution)/shard_map/all_gather | solution.py:570
  29.1 12.8 %collective-permute-start.4 = (f16[1,328,128]{2,1,0:T(8,128)(2,1)}, f16[1,328,128]{2,1,0:T(8,128)(2,1)S(1)}, u32[]{:S(2)}, u32[]{:S(2)}) collective-permute-start(f16[1,328,128]{2,1,0:T(8,128)(2,1)} %get-tuple-element.98), channel_id=1, source_target_pairs={{0,1},{1,0},{2,3},{3,2},{4,5},{5,4},{6,7},{7,6},{8,9},{9,8},{10,11... | collective-permute-start | bytes 251912 | tf_op jit(solution)/shard_map/ppermute | solution.py:489
  32.4 13.0 %collective-permute-start.5 = (f16[1,328,128]{2,1,0:T(8,128)(2,1)}, f16[1,328,128]{2,1,0:T(8,128)(2,1)S(1)}, u32[]{:S(2)}, u32[]{:S(2)}) collective-permute-start(f16[1,328,128]{2,1,0:T(8,128)(2,1)} %get-tuple-element.97), channel_id=1, source_target_pairs={{0,2},{1,3},{2,0},{3,1},{4,6},{5,7},{6,4},{7,5},{8,10},{9,11},{10,... | collective-permute-start | bytes 251912 | tf_op jit(solution)/shard_map/ppermute | solution.py:489
  34.6 11.5 %collective-permute-start.6 = (f16[1,328,128]{2,1,0:T(8,128)(2,1)}, f16[1,328,128]{2,1,0:T(8,128)(2,1)S(1)}, u32[]{:S(2)}, u32[]{:S(2)}) collective-permute-start(f16[1,328,128]{2,1,0:T(8,128)(2,1)} %get-tuple-element.96), channel_id=1, source_target_pairs={{0,3},{1,2},{2,1},{3,0},{4,7},{5,6},{6,5},{7,4},{8,11},{9,10},{10,... | collective-permute-start | bytes 251912 | tf_op jit(solution)/shard_map/ppermute | solution.py:489
  34.7 12.0 %collective-permute-start.7 = (f16[1,328,128]{2,1,0:T(8,128)(2,1)S(1)}, f16[1,328,128]{2,1,0:T(8,128)(2,1)S(1)}, u32[]{:S(2)}, u32[]{:S(2)}) collective-permute-start(f16[1,328,128]{2,1,0:T(8,128)(2,1)S(1)} %get-tuple-element.95), channel_id=1, source_target_pairs={{0,4},{1,5},{2,6},{3,7},{4,0},{5,1},{6,2},{7,3},{8,12},{9,13},{10,... | collective-permute-start | bytes 251912 | tf_op jit(solution)/shard_map/ppermute | solution.py:489
  37.4 10.0 %collective-permute-start.8 = (f16[1,328,128]{2,1,0:T(8,128)(2,1)S(1)}, f16[1,328,128]{2,1,0:T(8,128)(2,1)S(1)}, u32[]{:S(2)}, u32[]{:S(2)}) collective-permute-start(f16[1,328,128]{2,1,0:T(8,128)(2,1)S(1)} %get-tuple-element.94), channel_id=1, source_target_pairs={{0,5},{1,4},{2,7},{3,6},{4,1},{5,0},{6,3},{7,2},{8,13},{9,12},{10,... | collective-permute-start | bytes 251912 | tf_op jit(solution)/shard_map/ppermute | solution.py:489
  38.3 26.8 %all-to-all-start = ((f16[8,328,128]{2,1,0:T(8,128)(2,1)}), f16[8,328,128]{2,1,0:T(8,128)(2,1)S(1)}, u32[]{:S(2)}, u32[]{:S(2)}) async-start(f16[8,328,128]{2,1,0:T(8,128)(2,1)} %convert_element_type.51), calls=%async_computation | async-start | bytes 1343488 | tf_op jit(solution)/shard_map/all_to_all | solution.py:481
  41.9 22.5 %collective-permute-start.9 = (f16[1,328,128]{2,1,0:T(8,128)(2,1)S(1)}, f16[1,328,128]{2,1,0:T(8,128)(2,1)S(1)}, u32[]{:S(2)}, u32[]{:S(2)}) collective-permute-start(f16[1,328,128]{2,1,0:T(8,128)(2,1)S(1)} %get-tuple-element.93), channel_id=1, source_target_pairs={{0,6},{1,7},{2,4},{3,5},{4,2},{5,3},{6,0},{7,1},{8,14},{9,15},{10,... | collective-permute-start | bytes 251912 | tf_op jit(solution)/shard_map/ppermute | solution.py:489
  45.4 30.7 %collective-permute-start.10 = (f16[1,328,128]{2,1,0:T(8,128)(2,1)S(1)}, f16[1,328,128]{2,1,0:T(8,128)(2,1)S(1)}, u32[]{:S(2)}, u32[]{:S(2)}) collective-permute-start(f16[1,328,128]{2,1,0:T(8,128)(2,1)S(1)} %get-tuple-element.92), channel_id=1, source_target_pairs={{0,7},{1,6},{2,5},{3,4},{4,3},{5,2},{6,1},{7,0},{8,15},{9,14},{10,... | collective-permute-start | bytes 251912 | tf_op jit(solution)/shard_map/ppermute | solution.py:489
  65.9 12.1 %collective-permute-start.1 = (f16[1,328,128]{2,1,0:T(8,128)(2,1)S(1)}, f16[1,328,128]{2,1,0:T(8,128)(2,1)S(1)}, u32[]{:S(2)}, u32[]{:S(2)}) collective-permute-start(f16[1,328,128]{2,1,0:T(8,128)(2,1)S(1)} %convert_element_type.53), channel_id=1, source_target_pairs={{0,8},{1,9},{2,10},{3,11},{4,12},{5,13},{6,14},{7,15},{8,16},{9,17... | collective-permute-start | bytes 251912 | tf_op jit(solution)/shard_map/ppermute | solution.py:518
  70.3 9.1 %collective-permute-start.2 = (f16[1,328,128]{2,1,0:T(8,128)(2,1)S(1)}, f16[1,328,128]{2,1,0:T(8,128)(2,1)S(1)}, u32[]{:S(2)}, u32[]{:S(2)}) collective-permute-start(f16[1,328,128]{2,1,0:T(8,128)(2,1)S(1)} %convert_element_type.53), channel_id=1, source_target_pairs={{0,16},{1,17},{2,18},{3,19},{4,20},{5,21},{6,22},{7,23},{8,24},{9,... | collective-permute-start | bytes 251912 | tf_op jit(solution)/shard_map/ppermute | solution.py:518
  74.8 7.6 %collective-permute-start.3 = (f16[1,328,128]{2,1,0:T(8,128)(2,1)S(1)}, f16[1,328,128]{2,1,0:T(8,128)(2,1)S(1)}, u32[]{:S(2)}, u32[]{:S(2)}) collective-permute-start(f16[1,328,128]{2,1,0:T(8,128)(2,1)S(1)} %convert_element_type.53), channel_id=1, source_target_pairs={{0,24},{1,25},{2,26},{3,27},{4,28},{5,29},{6,30},{7,31}} | collective-permute-start | bytes 251912 | tf_op jit(solution)/shard_map/ppermute | solution.py:518
  84.8 16.2 %all-to-all-start.1 = ((f16[8,328,128]{2,1,0:T(8,128)(2,1)}), f16[8,328,128]{2,1,0:T(8,128)(2,1)}, u32[]{:S(2)}, u32[]{:S(2)}) async-start(f16[8,328,128]{2,1,0:T(8,128)(2,1)} %convert_element_type.59), calls=%async_computation.1 | async-start | bytes 1343488 | tf_op jit(solution)/shard_map/all_to_all | solution.py:481
  107.7 29.5 %all-to-all-start.2 = ((bf16[16,160,128]{2,1,0:T(8,128)(2,1)}), bf16[16,160,128]{2,1,0:T(8,128)(2,1)}, u32[]{:S(2)}, u32[]{:S(2)}) async-start(bf16[16,160,128]{2,1,0:T(8,128)(2,1)} %copy-done.16), calls=%async_computation.2 | async-start | bytes 1310720 | tf_op jit(solution)/shard_map/all_to_all | solution.py:661
  112.7 12.9 %collective-permute-start.11 = (f16[1,328,128]{2,1,0:T(8,128)(2,1)S(1)}, f16[1,328,128]{2,1,0:T(8,128)(2,1)S(1)}, u32[]{:S(2)}, u32[]{:S(2)}) collective-permute-start(f16[1,328,128]{2,1,0:T(8,128)(2,1)S(1)} %convert_element_type.61), channel_id=1, source_target_pairs={{8,0},{9,1},{10,2},{11,3},{12,4},{13,5},{14,6},{15,7},{16,8},{17,9... | collective-permute-start | bytes 251912 | tf_op jit(solution)/shard_map/ppermute | solution.py:518
  114.0 11.6 %collective-permute-start.12 = (f16[1,328,128]{2,1,0:T(8,128)(2,1)S(1)}, f16[1,328,128]{2,1,0:T(8,128)(2,1)S(1)}, u32[]{:S(2)}, u32[]{:S(2)}) collective-permute-start(f16[1,328,128]{2,1,0:T(8,128)(2,1)S(1)} %convert_element_type.61), channel_id=1, source_target_pairs={{16,0},{17,1},{18,2},{19,3},{20,4},{21,5},{22,6},{23,7},{24,8},{25... | collective-permute-start | bytes 251912 | tf_op jit(solution)/shard_map/ppermute | solution.py:518
  115.3 15.7 %collective-permute-start.13 = (f16[1,328,128]{2,1,0:T(8,128)(2,1)S(1)}, f16[1,328,128]{2,1,0:T(8,128)(2,1)S(1)}, u32[]{:S(2)}, u32[]{:S(2)}) collective-permute-start(f16[1,328,128]{2,1,0:T(8,128)(2,1)S(1)} %convert_element_type.61), channel_id=1, source_target_pairs={{24,0},{25,1},{26,2},{27,3},{28,4},{29,5},{30,6},{31,7}} | collective-permute-start | bytes 251912 | tf_op jit(solution)/shard_map/ppermute | solution.py:518
  145.0 28.1 %all-to-all-start.3 = ((bf16[32,112,128]{2,1,0:T(8,128)(2,1)}), bf16[32,112,128]{2,1,0:T(8,128)(2,1)}, u32[]{:S(2)}, u32[]{:S(2)}) async-start(bf16[32,112,128]{2,1,0:T(8,128)(2,1)} %copy-done.2), calls=%async_computation.3 | async-start | bytes 1835008 | tf_op jit(solution)/shard_map/all_to_all | solution.py:699
  149.0 11.4 %collective-permute-start.15 = (f16[1,328,128]{2,1,0:T(8,128)(2,1)S(1)}, f16[1,328,128]{2,1,0:T(8,128)(2,1)S(1)}, u32[]{:S(2)}, u32[]{:S(2)}) collective-permute-start(f16[1,328,128]{2,1,0:T(8,128)(2,1)S(1)} %get-tuple-element.89), channel_id=1, source_target_pairs={{0,2},{1,3},{2,0},{3,1},{4,6},{5,7},{6,4},{7,5},{8,10},{9,11},{10,... | collective-permute-start | bytes 251912 | tf_op jit(solution)/shard_map/ppermute | solution.py:489
  150.5 11.0 %collective-permute-start.16 = (f16[1,328,128]{2,1,0:T(8,128)(2,1)S(1)}, f16[1,328,128]{2,1,0:T(8,128)(2,1)S(1)}, u32[]{:S(2)}, u32[]{:S(2)}) collective-permute-start(f16[1,328,128]{2,1,0:T(8,128)(2,1)S(1)} %get-tuple-element.88), channel_id=1, source_target_pairs={{0,3},{1,2},{2,1},{3,0},{4,7},{5,6},{6,5},{7,4},{8,11},{9,10},{10,... | collective-permute-start | bytes 251912 | tf_op jit(solution)/shard_map/ppermute | solution.py:489
  150.9 10.7 %collective-permute-start.17 = (f16[1,328,128]{2,1,0:T(8,128)(2,1)S(1)}, f16[1,328,128]{2,1,0:T(8,128)(2,1)S(1)}, u32[]{:S(2)}, u32[]{:S(2)}) collective-permute-start(f16[1,328,128]{2,1,0:T(8,128)(2,1)S(1)} %get-tuple-element.87), channel_id=1, source_target_pairs={{0,4},{1,5},{2,6},{3,7},{4,0},{5,1},{6,2},{7,3},{8,12},{9,13},{10,... | collective-permute-start | bytes 251912 | tf_op jit(solution)/shard_map/ppermute | solution.py:489
  152.2 9.4 %collective-permute-start.18 = (f16[1,328,128]{2,1,0:T(8,128)(2,1)S(1)}, f16[1,328,128]{2,1,0:T(8,128)(2,1)S(1)}, u32[]{:S(2)}, u32[]{:S(2)}) collective-permute-start(f16[1,328,128]{2,1,0:T(8,128)(2,1)S(1)} %get-tuple-element.86), channel_id=1, source_target_pairs={{0,5},{1,4},{2,7},{3,6},{4,1},{5,0},{6,3},{7,2},{8,13},{9,12},{10,... | collective-permute-start | bytes 251912 | tf_op jit(solution)/shard_map/ppermute | solution.py:489
  152.6 13.8 %collective-permute-start.19 = (f16[1,328,128]{2,1,0:T(8,128)(2,1)S(1)}, f16[1,328,128]{2,1,0:T(8,128)(2,1)S(1)}, u32[]{:S(2)}, u32[]{:S(2)}) collective-permute-start(f16[1,328,128]{2,1,0:T(8,128)(2,1)S(1)} %get-tuple-element.85), channel_id=1, source_target_pairs={{0,6},{1,7},{2,4},{3,5},{4,2},{5,3},{6,0},{7,1},{8,14},{9,15},{10,... | collective-permute-start | bytes 251912 | tf_op jit(solution)/shard_map/ppermute | solution.py:489
  160.4 6.9 %collective-permute-start.20 = (f16[1,328,128]{2,1,0:T(8,128)(2,1)S(1)}, f16[1,328,128]{2,1,0:T(8,128)(2,1)S(1)}, u32[]{:S(2)}, u32[]{:S(2)}) collective-permute-start(f16[1,328,128]{2,1,0:T(8,128)(2,1)S(1)} %get-tuple-element.84), channel_id=1, source_target_pairs={{0,7},{1,6},{2,5},{3,4},{4,3},{5,2},{6,1},{7,0},{8,15},{9,14},{10,... | collective-permute-start | bytes 251912 | tf_op jit(solution)/shard_map/ppermute | solution.py:489
  (53 other events, 344.0 us)
Sparse Core Ops, SparseCore 0:
  9.7 76.4 all-gather.1

commit v6 on v5

--- a/solution.py
+++ b/solution.py
@@ -133,12 +133,12 @@
     return tables
 
 
-def pack_blocks(source, message, last_exp, size, rows, me=0):
+def pack_blocks(source, message, last_exp, size, rows):
     count = message.shape[0]
     tables = decay_tables(last_exp, source.shape[0] // size, size, rows, count)
     for d in range(count):
         block = source[rows * d : rows * (d + 1), :]
-        write_block(message, me ^ d, 0, block, tables[d], exponent_of(block))
+        write_block(message, d, 0, block, tables[d], exponent_of(block))
 
 
 def decay_lines(message, at, rows):
@@ -167,16 +167,8 @@
         target[rows * d : rows * (d + 1), :] = read_block(message, me ^ d, rows)
 
 
-def in_order(me_ref, held_ref, order_ref):
-    for s in range(held_ref.shape[0]):
-        order_ref[s] = held_ref[me_ref[0] ^ s]
-    return order_ref
-
-
-def total_kernel(rows, reverse, me_ref, held_ref, out_ref, order_ref):
+def total_kernel(rows, reverse, held_ref, out_ref):
     count = held_ref.shape[0]
-    if reverse:
-        held_ref = in_order(me_ref, held_ref, order_ref)
     columns = decay_columns(held_ref, rows)
     state = None
     for s in range(count - 1, -1, -1) if reverse else range(count):
@@ -189,10 +181,8 @@
 
 
 def fold_kernel(rows, reverse, me_ref, held_ref, *refs):
-    others, out_ref, order_ref = refs[:-2], refs[-2], refs[-1]
+    others, out_ref = refs[:-1], refs[-1]
     count = held_ref.shape[0]
-    if reverse:
-        held_ref = in_order(me_ref, held_ref, order_ref)
     columns = decay_columns(held_ref, rows)
     state = jnp.zeros((rows, LANES), F32)
     for other in reversed(others):
@@ -253,7 +243,7 @@
     pack_blocks(st_ref, msg_ref, jnp.exp(last), size, rows)
 
 
-def grad_kernel(heads_in, size, rows, me_ref, gy_ref, abc_ref, ld_ref, msg_ref, st_ref):
+def grad_kernel(heads_in, size, rows, gy_ref, abc_ref, ld_ref, msg_ref, st_ref):
     length = gy_ref.shape[0]
     c_rows = split(abc_ref[:, LANES : 2 * LANES])
     grown = jnp.exp(ld_ref[...])
@@ -261,7 +251,7 @@
         cols = slice(j * LANES, (j + 1) * LANES)
         scaled = gy_ref[:, cols] * spread(grown, j, heads_in, size)
         st_ref[cols, :] = dot3(split(scaled.T), c_rows)
-    pack_blocks(st_ref, msg_ref, grown[length - 1 : length], size, rows, me_ref[0])
+    pack_blocks(st_ref, msg_ref, grown[length - 1 : length], size, rows)
 
 
 def gate_kernel(go_ref, *refs):
@@ -494,15 +484,13 @@
     return [list(range(at, at + size)) for at in range(0, count, size)]
 
 
-def group_total(me, held, rows, reverse):
+def group_total(held, rows, reverse):
     (total,) = call(
         functools.partial(total_kernel, rows, reverse),
         [shape((1, *held.shape[1:]))],
-        [me, held],
+        [held],
         4 * held.size,
         12,
-        [pltpu.VMEM(held.shape, F32)],
-        [SMEM, VMEM],
     )
     return total.astype(jnp.float16)
 
@@ -522,8 +510,7 @@
         [me, held, *others],
         8 * held.size,
         12,
-        [pltpu.VMEM(held.shape, F32)],
-        [SMEM] + [VMEM] * (1 + len(others)),
+        specs=[SMEM] + [VMEM] * (1 + len(others)),
     )
     return folded
 
@@ -630,24 +617,26 @@
     (message,) = call(
         functools.partial(grad_kernel, heads_in, head_size, rows),
         [shape((plane, block, LANES))],
-        [me, grad_y, act_bc, ld],
+        [grad_y, act_bc, ld],
         10 * unit,
         12,
         [stored],
-        [SMEM] + [VMEM] * 3,
-    )
-    held_carry = swapped(message)
-    total, ld_t_then = lax.optimization_barrier((group_total(me, held_state, rows, False), ld_t))
+    )
     y_within, grad_within, grad_bc_within = call(
         functools.partial(local_kernel, heads_in, head_size),
         [shape(whole), shape(whole), shape(act_bc.shape)],
-        [act_x, grad_y, act_bc, step, ld, step_t, ld_t_then],
+        [act_x, grad_y, act_bc, step, ld, step_t, ld_t],
         40 * unit,
         16,
         [pltpu.VMEM(square, F32)],
     )
+    total, y_within, message = lax.optimization_barrier(
+        (group_total(held_state, rows, False), y_within, message)
+    )
+    held_carry = exchange(message, planes)
     folded, held_carry = lax.optimization_barrier((enter(me, held_state, total, rows, False), held_carry))
-    entered = enter(me, held_carry, group_total(me, held_carry, rows, True), rows, True)
+    held_carry = held_carry.astype(F32)
+    entered = enter(me, held_carry, group_total(held_carry, rows, True), rows, True)
     state_message = exchange(folded, planes).astype(F32)
     gated, y_ahead = call(
         functools.partial(forward_kernel, heads_in, head_size, rows),
@@ -657,7 +646,7 @@
         16,
         [stored],
     )
-    gated, gathered, y_ahead = lax.optimization_barrier((gated, gathered, y_ahead))
+    gated, entered, gathered, y_ahead = lax.optimization_barrier((gated, entered, gathered, y_ahead))
     held = lax.all_to_all(gated, "ctx", 0, 0, axis_index_groups=groups, tiled=True)
     grad_z, y_sums, grad_bc_ahead = call(
         functools.partial(ahead_kernel, heads_in, head_size, rows),

time: 184 us -> 168 us (0.913)
  waiting for transfers between devices: 48.5 us -> 33.4 us
  other arithmetic: 5.51 us -> 8.07 us
    ppermute x14 -> x7, waiting for transfers between devices: 28.5 us -> 12.1 us  [swapped(): lax.ppermute(half[m:m + 1], 'ctx', [(at, at ^ m) for at in range(count)])]
    ppermute x14 -> x7, starting transfers between devices: 17.2 us -> 6.23 us  [swapped(): lax.ppermute(half[m:m + 1], 'ctx', [(at, at ^ m) for at in range(count)])]
    all_to_all x2 -> x3, starting transfers between devices: 7.94 us -> 16.1 us  [exchange(): lax.all_to_all(half, 'ctx', 0, 0, axis_index_groups=groups, tiled=True)]
    all_to_all x1, waiting for transfers between devices: 0.01 us -> 3.13 us  [per_device(): lax.all_to_all(gated, 'ctx', 0, 0, axis_index_groups=groups, tiled=True)]
    ppermute x6, waiting for transfers between devices: 18.8 us -> 16.8 us  [enter(): others.append(lax.ppermute(total, 'ctx', pairs).astype(F32))]
    unnamed x117 -> x109, local copies, waits for them, and re-layouts: 21.3 us -> 22.9 us
  transfers between devices with their start and end apart: 26 -> 20, of which waited for: 10 -> 10; matrix products, arithmetic and copies ran while one was open for 7% -> 6% of each run, Pallas kernels for 17% -> 18%
where the time goes in v6:
time: 168 us; the launch traced here: 167 us
  starting transfers between devices  48 us (29%)
  Pallas kernels  39.1 us (23%)
  waiting for transfers between devices  33.4 us (20%)
  local copies, waits for them, and re-layouts  23.3 us (14%)
  between operations  14.8 us (9%)
  other arithmetic  8.07 us (5%)
    pallas_call x11, Pallas kernels, call(): pl.pallas_call(kernel, out_shape=tuple(out_shapes), scratch_shapes=list(s...  23.6 us
    unnamed x109, local copies, waits for them, and re-layouts  22.9 us
    ppermute x6, waiting for transfers between devices, enter(): others.append(lax.ppermute(total, 'ctx', pairs).astype(F32))  16.8 us
    all_to_all x3, starting transfers between devices, exchange(): lax.all_to_all(half, 'ctx', 0, 0, axis_index_groups=groups, tiled=True)  16.1 us
    ppermute x6, starting transfers between devices, enter(): others.append(lax.ppermute(total, 'ctx', pairs).astype(F32))  15.6 us
    ppermute x7, waiting for transfers between devices, swapped(): lax.ppermute(half[m:m + 1], 'ctx', [(at, at ^ m) for at in range(count)])  12.1 us
    pallas_call x1, Pallas kernels, per_device(): pl.pallas_call(gate_kernel, grid=(channels // part,), in_specs=[pl.BlockS...  8.72 us
    pallas_call x1, Pallas kernels, per_device(): pl.pallas_call(functools.partial(product_kernel, out_rows), grid=(width /...  6.78 us
  transfers between devices with their start and end apart: 20, of which 10 were waited for; matrix products, arithmetic and copies ran while one was open for 6% of the time, Pallas kernels for 18%

profile of v6, /device:TPU:0, one launch (start us, length us, event | category | flops | bytes accessed | tf_op | source)
XLA Modules:
  0.0 166.7 jit_solution(3803531475681542236)
XLA Ops:
  9.2 2.4 %collective-permute-start = (bf16[16,2816]{1,0:T(8,128)(2,1)S(1)}, bf16[16,2816]{1,0:T(8,128)(2,1)S(1)}, u32[]{:S(2)}, u32[]{:S(2)}) collective-permute-start(bf16[16,2816]{1,0:T(8,128)(2,1)S(1)} %slice.36), channel_id=1, source_target_pairs={{0,1},{1,2},{2,3},{3,4},{4,5},{5,6},{6,7},{7,8},{8,9},{9,10},{10,1... | collective-permute-start | bytes 270344 | tf_op jit(solution)/shard_map/ppermute | solution.py:527
  12.4 2.8 %shard_map.164 = (f32[128,2560]{1,0:T(8,128)S(1)}, f32[128,2560]{1,0:T(8,128)S(1)}, f32[128,256]{1,0:T(8,128)S(1)}, f32[128,256]{1,0:T(8,128)S(1)}, f32[128,128]...) custom-call(bf16[128,2816]{1,0:T(8,128)(2,1)S(1)} %constant_dynamic-, ...), custom_call_target="tpu_custom_call" | custom-call | flops 1677721600 | bytes 5446976 | tf_op jit(solution)/shard_map/pallas_call | solution.py:26
  21.5 7.7 %all-to-all-start = ((f16[8,328,128]{2,1,0:T(8,128)(2,1)}), f16[8,328,128]{2,1,0:T(8,128)(2,1)}, u32[]{:S(2)}, u32[]{:S(2)}) async-start(f16[8,328,128]{2,1,0:T(8,128)(2,1)} %convert_element_type.51), calls=%async_computation | async-start | bytes 1343488 | tf_op jit(solution)/shard_map/all_to_all | solution.py:471
  29.3 8.7 %shard_map.166 = (f32[128,2560]{1,0:T(8,128)}, f32[128,2560]{1,0:T(8,128)}) custom-call(bf16[128,2560]{1,0:T(8,128)(2,1)S(1)} %copy-done.2, bf16[2560,2560]{1,0:T(8,128)(2,1)} %refs_3_.1, bf16[2560,2560]{1,0:T(8,128)(2,1)} %refs_3_.1, bf16[2560,2560]{1,0:T(8,128)(2,1)} %refs_3_.1, bf16[2560,2560]{1,0:T(8,128)(2,1)} %refs_3_.1, bf16[128,2560]{1,0:T(8,128)(2,1)S(1)} %copy-done.1), custom_call_target="tpu_custom_call" | custom-call | flops 1677721600 | bytes 13107200 | tf_op jit(solution)/shard_map/pallas_call | solution.py:599
  42.0 4.7 %shard_map.167 = (f32[128,2560]{1,0:T(8,128)S(1)}, f32[128,2560]{1,0:T(8,128)S(1)}, f32[128,256]{1,0:T(8,128)S(1)}) custom-call(f32[128,2560]{1,0:T(8,128)S(1)} %copy-done.4, f32[128,2560]{1,0:T(8,128)S(1)} %copy-done.9, f32[128,256]{1,0:T(8,128)S(1)} %copy-done.23, f32[128,128]{1,0:T(8,128)S(1)} %copy-done.33, f32[128,128]{1,0:T(8,128)S(1)} %get-tuple-element.51.ld_ref, ...), custom_call_target="tpu_custom_call" | custom-call | flops 3355443200 | bytes 5767168 | tf_op jit(solution)/shard_map/pallas_call | solution.py:26
  52.3 4.2 %all-to-all-start.1 = ((f16[8,328,128]{2,1,0:T(8,128)(2,1)}), f16[8,328,128]{2,1,0:T(8,128)(2,1)}, u32[]{:S(2)}, u32[]{:S(2)}) async-start(f16[8,328,128]{2,1,0:T(8,128)(2,1)} %convert_element_type.57), calls=%async_computation.1 | async-start | bytes 1343488 | tf_op jit(solution)/shard_map/all_to_all | solution.py:471
  56.5 5.7 %collective-permute-start.1 = (f16[1,328,128]{2,1,0:T(8,128)(2,1)}, f16[1,328,128]{2,1,0:T(8,128)(2,1)S(1)}, u32[]{:S(2)}, u32[]{:S(2)}) collective-permute-start(f16[1,328,128]{2,1,0:T(8,128)(2,1)} %convert_element_type.53), channel_id=1, source_target_pairs={{0,8},{1,9},{2,10},{3,11},{4,12},{5,13},{6,14},{7,15},{8,16},{9,17... | collective-permute-start | bytes 251912 | tf_op jit(solution)/shard_map/ppermute | solution.py:506
  62.2 4.6 %collective-permute-start.2 = (f16[1,328,128]{2,1,0:T(8,128)(2,1)}, f16[1,328,128]{2,1,0:T(8,128)(2,1)S(1)}, u32[]{:S(2)}, u32[]{:S(2)}) collective-permute-start(f16[1,328,128]{2,1,0:T(8,128)(2,1)} %convert_element_type.53), channel_id=1, source_target_pairs={{0,16},{1,17},{2,18},{3,19},{4,20},{5,21},{6,22},{7,23},{8,24},{9,... | collective-permute-start | bytes 251912 | tf_op jit(solution)/shard_map/ppermute | solution.py:506
  68.3 2.7 %collective-permute-done.2 = f16[1,328,128]{2,1,0:T(8,128)(2,1)S(1)} collective-permute-done((f16[1,328,128]{2,1,0:T(8,128)(2,1)}, f16[1,328,128]{2,1,0:T(8,128)(2,1)S(1)}, u32[]{:S(2)}, u32[]{:S(2)}) %collective-permute-start.2) | collective-permute-done | bytes 84000 | tf_op jit(solution)/shard_map/ppermute | solution.py:506
  71.1 3.0 %collective-permute-done.3 = f16[1,328,128]{2,1,0:T(8,128)(2,1)S(1)} collective-permute-done((f16[1,328,128]{2,1,0:T(8,128)(2,1)}, f16[1,328,128]{2,1,0:T(8,128)(2,1)S(1)}, u32[]{:S(2)}, u32[]{:S(2)}) %collective-permute-start.3) | collective-permute-done | bytes 84000 | tf_op jit(solution)/shard_map/ppermute | solution.py:506
  76.4 4.2 %all-to-all-start.2 = ((f16[8,328,128]{2,1,0:T(8,128)(2,1)}), f16[8,328,128]{2,1,0:T(8,128)(2,1)}, u32[]{:S(2)}, u32[]{:S(2)}) async-start(f16[8,328,128]{2,1,0:T(8,128)(2,1)} %convert_element_type.58), calls=%async_computation.2 | async-start | bytes 1343488 | tf_op jit(solution)/shard_map/all_to_all | solution.py:471
  86.6 4.5 %collective-permute-done.4 = f16[1,328,128]{2,1,0:T(8,128)(2,1)S(1)} collective-permute-done((f16[1,328,128]{2,1,0:T(8,128)(2,1)S(1)}, f16[1,328,128]{2,1,0:T(8,128)(2,1)S(1)}, u32[]{:S(2)}, u32[]{:S(2)}) %collective-permute-start.4) | collective-permute-done | bytes 84000 | tf_op jit(solution)/shard_map/ppermute | solution.py:506
  91.2 6.6 %collective-permute-done.5 = f16[1,328,128]{2,1,0:T(8,128)(2,1)S(1)} collective-permute-done((f16[1,328,128]{2,1,0:T(8,128)(2,1)S(1)}, f16[1,328,128]{2,1,0:T(8,128)(2,1)S(1)}, u32[]{:S(2)}, u32[]{:S(2)}) %collective-permute-start.5) | collective-permute-done | bytes 84000 | tf_op jit(solution)/shard_map/ppermute | solution.py:506
  102.0 1.8 %shard_map.170 = (bf16[16,160,128]{2,1,0:T(8,128)(2,1)S(1)}, f32[128,2560]{1,0:T(8,128)S(1)}) custom-call(f32[8,328,128]{2,1,0:T(8,128)S(1)} %convert_element_type.59.msg_ref.msgf_ref, f32[128,2560]{1,0:T(8,128)S(1)} %copy-done.5, bf16[128,2560]{1,0:T(8,128)(2,1)S(1)} %copy-done.1, f32[128,256]{1,0:T(8,128)S(1)} %copy-done.24, ...), custom_call_target="tpu_custom_call" | custom-call | flops 1677721600 | bytes 6793216 | tf_op jit(solution)/shard_map/pallas_call | solution.py:26
  105.7 4.3 %all-to-all-start.3 = ((bf16[16,160,128]{2,1,0:T(8,128)(2,1)}), bf16[16,160,128]{2,1,0:T(8,128)(2,1)}, u32[]{:S(2)}, u32[]{:S(2)}) async-start(bf16[16,160,128]{2,1,0:T(8,128)(2,1)} %copy-done.15), calls=%async_computation.3 | async-start | bytes 1310720 | tf_op jit(solution)/shard_map/all_to_all | solution.py:650
  115.2 2.3 %shard_map.173 = (bf16[128,2560]{1,0:T(8,128)(2,1)}, f32[128,128]{1,0:T(8,128)S(1)}, f32[128,256]{1,0:T(8,128)S(1)}) custom-call(f32[8,328,128]{2,1,0:T(8,128)S(1)} %convert_element_type.59.msg_ref.msgf_ref, f32[128,2560]{1,0:T(8,128)S(1)} %copy-done.6, f32[128,2560]{1,0:T(8,128)S(1)} %copy-done.10, f32[128,128]{1,0:T(8,128)S(1)} %get-tuple-element.51.ld_ref, ...), custom_call_target="tpu_custom_call" | custom-call | flops 1677721600 | bytes 8300544 | tf_op jit(solution)/shard_map/pallas_call | solution.py:26
  118.8 3.1 %all-to-all-done.3.held_ref = bf16[16,160,128]{2,1,0:T(8,128)(2,1)} async-done(((bf16[16,160,128]{2,1,0:T(8,128)(2,1)}), bf16[16,160,128]{2,1,0:T(8,128)(2,1)}, u32[]{:S(2)}, u32[]{:S(2)}) %all-to-all-start.3) | async-done | bytes 655392 | tf_op jit(solution)/shard_map/all_to_all | solution.py:650
  121.9 6.8 %shard_map.174 = bf16[32,112,128]{2,1,0:T(8,128)(2,1)S(1)} custom-call(bf16[16,160,128]{2,1,0:T(8,128)(2,1)} %all-to-all-done.3.held_ref, bf16[2048,2560]{1,0:T(8,128)(2,1)} %all-gather.2.cloned.1.call-done.refs_0_.refs_1_.refs_2_.refs_3_, bf16[2048,2560]{1,0:T(8,128)(2,1)} %all-gather.2.cloned.1.call-done.refs_0_.refs_1_.refs_2_.refs_3_, ...), custom_call_target="tpu_custom_call" | custom-call | flops 1677721600 | bytes 10485760 | tf_op jit(solution)/shard_map/pallas_call | solution.py:669
  129.7 3.3 %all-to-all-start.4 = ((bf16[32,112,128]{2,1,0:T(8,128)(2,1)}), bf16[32,112,128]{2,1,0:T(8,128)(2,1)}, u32[]{:S(2)}, u32[]{:S(2)}) async-start(bf16[32,112,128]{2,1,0:T(8,128)(2,1)} %copy-done), calls=%async_computation.4 | async-start | bytes 1835008 | tf_op jit(solution)/shard_map/all_to_all | solution.py:688
  136.9 2.6 %collective-permute-start.12 = (f16[1,328,128]{2,1,0:T(8,128)(2,1)S(1)}, f16[1,328,128]{2,1,0:T(8,128)(2,1)S(1)}, u32[]{:S(2)}, u32[]{:S(2)}) collective-permute-start(f16[1,328,128]{2,1,0:T(8,128)(2,1)S(1)} %get-tuple-element.89), channel_id=1, source_target_pairs={{0,6},{1,7},{2,4},{3,5},{4,2},{5,3},{6,0},{7,1},{8,14},{9,15},{10,... | collective-permute-start | bytes 251912 | tf_op jit(solution)/shard_map/ppermute | solution.py:479
  139.6 5.4 %collective-permute-done.8 = f16[1,328,128]{2,1,0:T(8,128)(2,1)S(1)} collective-permute-done((f16[1,328,128]{2,1,0:T(8,128)(2,1)S(1)}, f16[1,328,128]{2,1,0:T(8,128)(2,1)S(1)}, u32[]{:S(2)}, u32[]{:S(2)}) %collective-permute-start.8) | collective-permute-done | bytes 84000 | tf_op jit(solution)/shard_map/ppermute | solution.py:479
  146.3 4.7 %collective-permute-done.12 = f16[1,328,128]{2,1,0:T(8,128)(2,1)S(1)} collective-permute-done((f16[1,328,128]{2,1,0:T(8,128)(2,1)S(1)}, f16[1,328,128]{2,1,0:T(8,128)(2,1)S(1)}, u32[]{:S(2)}, u32[]{:S(2)}) %collective-permute-start.12) | collective-permute-done | bytes 84000 | tf_op jit(solution)/shard_map/ppermute | solution.py:479
  152.1 4.1 %shard_map.175 = (bf16[128,2560]{1,0:T(8,128)(2,1)}, f32[128,256]{1,0:T(8,128)S(1)}, f32[128,40]{1,0:T(8,128)S(1)}) custom-call(s32[1]{0:T(128)} %bitcast.me_ref, f32[8,328,128]{2,1,0:T(8,128)S(1)} %convert_element_type.66.msg_ref, f32[8,328,128]{2,1,0:T(8,128)S(1)} %convert_element_type.59.msg_ref.msgf_ref, f32[128,2560]{1,0:T(8,128)S(1)} %copy-done.7, ...), custom_call_target="tpu_custom_call" | custom-call | flops 3355443200 | bytes 9275396 | tf_op jit(solution)/shard_map/pallas_call | solution.py:26
  157.5 2.3 %shard_map.176 = f32[80,2560]{1,0:T(8,128)} custom-call(bf16[32,112,128]{2,1,0:T(8,128)(2,1)} %all-to-all-done.4.parts_ref), custom_call_target="tpu_custom_call" | custom-call | flops 917504 | bytes 1736704 | tf_op jit(solution)/shard_map/pallas_call | solution.py:26
  (166 shorter events, 49.4 us)
Async XLA Ops:
  7.2 98.5 %all-gather.2.cloned.1.call-start = ((), (), s32[]{:S(2)}) async-start(), calls=%async_computation.5 | async-start | bytes 11141120 | tf_op jit(solution)/shard_map/all_gather | solution.py:557
  9.2 3.3 %collective-permute-start = (bf16[16,2816]{1,0:T(8,128)(2,1)S(1)}, bf16[16,2816]{1,0:T(8,128)(2,1)S(1)}, u32[]{:S(2)}, u32[]{:S(2)}) collective-permute-start(bf16[16,2816]{1,0:T(8,128)(2,1)S(1)} %slice.36), channel_id=1, source_target_pairs={{0,1},{1,2},{2,3},{3,4},{4,5},{5,6},{6,7},{7,8},{8,9},{9,10},{10,1... | collective-permute-start | bytes 270344 | tf_op jit(solution)/shard_map/ppermute | solution.py:527
  20.6 17.4 %copy-start.22 = (f32[128,256]{1,0:T(8,128)}, f32[128,256]{1,0:T(8,128)S(1)}, u32[]{:S(2)}) copy-start(f32[128,256]{1,0:T(8,128)S(1)} %get-tuple-element.49.abc_ref) | copy-start | bytes 393220
  21.5 27.3 %all-to-all-start = ((f16[8,328,128]{2,1,0:T(8,128)(2,1)}), f16[8,328,128]{2,1,0:T(8,128)(2,1)}, u32[]{:S(2)}, u32[]{:S(2)}) async-start(f16[8,328,128]{2,1,0:T(8,128)(2,1)} %convert_element_type.51), calls=%async_computation | async-start | bytes 1343488 | tf_op jit(solution)/shard_map/all_to_all | solution.py:471
  52.3 23.2 %all-to-all-start.1 = ((f16[8,328,128]{2,1,0:T(8,128)(2,1)}), f16[8,328,128]{2,1,0:T(8,128)(2,1)}, u32[]{:S(2)}, u32[]{:S(2)}) async-start(f16[8,328,128]{2,1,0:T(8,128)(2,1)} %convert_element_type.57), calls=%async_computation.1 | async-start | bytes 1343488 | tf_op jit(solution)/shard_map/all_to_all | solution.py:471
  56.5 11.8 %collective-permute-start.1 = (f16[1,328,128]{2,1,0:T(8,128)(2,1)}, f16[1,328,128]{2,1,0:T(8,128)(2,1)S(1)}, u32[]{:S(2)}, u32[]{:S(2)}) collective-permute-start(f16[1,328,128]{2,1,0:T(8,128)(2,1)} %convert_element_type.53), channel_id=1, source_target_pairs={{0,8},{1,9},{2,10},{3,11},{4,12},{5,13},{6,14},{7,15},{8,16},{9,17... | collective-permute-start | bytes 251912 | tf_op jit(solution)/shard_map/ppermute | solution.py:506
  62.2 8.8 %collective-permute-start.2 = (f16[1,328,128]{2,1,0:T(8,128)(2,1)}, f16[1,328,128]{2,1,0:T(8,128)(2,1)S(1)}, u32[]{:S(2)}, u32[]{:S(2)}) collective-permute-start(f16[1,328,128]{2,1,0:T(8,128)(2,1)} %convert_element_type.53), channel_id=1, source_target_pairs={{0,16},{1,17},{2,18},{3,19},{4,20},{5,21},{6,22},{7,23},{8,24},{9,... | collective-permute-start | bytes 251912 | tf_op jit(solution)/shard_map/ppermute | solution.py:506
  66.8 7.3 %collective-permute-start.3 = (f16[1,328,128]{2,1,0:T(8,128)(2,1)}, f16[1,328,128]{2,1,0:T(8,128)(2,1)S(1)}, u32[]{:S(2)}, u32[]{:S(2)}) collective-permute-start(f16[1,328,128]{2,1,0:T(8,128)(2,1)} %convert_element_type.53), channel_id=1, source_target_pairs={{0,24},{1,25},{2,26},{3,27},{4,28},{5,29},{6,30},{7,31}} | collective-permute-start | bytes 251912 | tf_op jit(solution)/shard_map/ppermute | solution.py:506
  76.4 22.7 %all-to-all-start.2 = ((f16[8,328,128]{2,1,0:T(8,128)(2,1)}), f16[8,328,128]{2,1,0:T(8,128)(2,1)}, u32[]{:S(2)}, u32[]{:S(2)}) async-start(f16[8,328,128]{2,1,0:T(8,128)(2,1)} %convert_element_type.58), calls=%async_computation.2 | async-start | bytes 1343488 | tf_op jit(solution)/shard_map/all_to_all | solution.py:471
  82.5 8.6 %collective-permute-start.4 = (f16[1,328,128]{2,1,0:T(8,128)(2,1)S(1)}, f16[1,328,128]{2,1,0:T(8,128)(2,1)S(1)}, u32[]{:S(2)}, u32[]{:S(2)}) collective-permute-start(f16[1,328,128]{2,1,0:T(8,128)(2,1)S(1)} %convert_element_type.61), channel_id=1, source_target_pairs={{8,0},{9,1},{10,2},{11,3},{12,4},{13,5},{14,6},{15,7},{16,8},{17,9... | collective-permute-start | bytes 251912 | tf_op jit(solution)/shard_map/ppermute | solution.py:506
  83.8 13.9 %collective-permute-start.5 = (f16[1,328,128]{2,1,0:T(8,128)(2,1)S(1)}, f16[1,328,128]{2,1,0:T(8,128)(2,1)S(1)}, u32[]{:S(2)}, u32[]{:S(2)}) collective-permute-start(f16[1,328,128]{2,1,0:T(8,128)(2,1)S(1)} %convert_element_type.61), channel_id=1, source_target_pairs={{16,0},{17,1},{18,2},{19,3},{20,4},{21,5},{22,6},{23,7},{24,8},{25... | collective-permute-start | bytes 251912 | tf_op jit(solution)/shard_map/ppermute | solution.py:506
  85.1 12.6 %collective-permute-start.6 = (f16[1,328,128]{2,1,0:T(8,128)(2,1)S(1)}, f16[1,328,128]{2,1,0:T(8,128)(2,1)S(1)}, u32[]{:S(2)}, u32[]{:S(2)}) collective-permute-start(f16[1,328,128]{2,1,0:T(8,128)(2,1)S(1)} %convert_element_type.61), channel_id=1, source_target_pairs={{24,0},{25,1},{26,2},{27,3},{28,4},{29,5},{30,6},{31,7}} | collective-permute-start | bytes 251912 | tf_op jit(solution)/shard_map/ppermute | solution.py:506
  105.7 16.2 %all-to-all-start.3 = ((bf16[16,160,128]{2,1,0:T(8,128)(2,1)}), bf16[16,160,128]{2,1,0:T(8,128)(2,1)}, u32[]{:S(2)}, u32[]{:S(2)}) async-start(bf16[16,160,128]{2,1,0:T(8,128)(2,1)} %copy-done.15), calls=%async_computation.3 | async-start | bytes 1310720 | tf_op jit(solution)/shard_map/all_to_all | solution.py:650
  129.7 27.9 %all-to-all-start.4 = ((bf16[32,112,128]{2,1,0:T(8,128)(2,1)}), bf16[32,112,128]{2,1,0:T(8,128)(2,1)}, u32[]{:S(2)}, u32[]{:S(2)}) async-start(bf16[32,112,128]{2,1,0:T(8,128)(2,1)} %copy-done), calls=%async_computation.4 | async-start | bytes 1835008 | tf_op jit(solution)/shard_map/all_to_all | solution.py:688
  133.0 19.0 %copy-start.31 = (f32[128,2560]{1,0:T(8,128)S(1)}, f32[128,2560]{1,0:T(8,128)}, u32[]{:S(2)}) copy-start(f32[128,2560]{1,0:T(8,128)} %copy-done.30) | copy-start | bytes 3932164
  133.1 18.9 %copy-start.29 = (f32[128,2560]{1,0:T(8,128)S(1)}, f32[128,2560]{1,0:T(8,128)}, u32[]{:S(2)}) copy-start(f32[128,2560]{1,0:T(8,128)} %copy-done.28) | copy-start | bytes 3932164
  133.3 3.6 %collective-permute-start.7 = (f16[1,328,128]{2,1,0:T(8,128)(2,1)S(1)}, f16[1,328,128]{2,1,0:T(8,128)(2,1)S(1)}, u32[]{:S(2)}, u32[]{:S(2)}) collective-permute-start(f16[1,328,128]{2,1,0:T(8,128)(2,1)S(1)} %get-tuple-element.94), channel_id=1, source_target_pairs={{0,1},{1,0},{2,3},{3,2},{4,5},{5,4},{6,7},{7,6},{8,9},{9,8},{10,11... | collective-permute-start | bytes 251912 | tf_op jit(solution)/shard_map/ppermute | solution.py:479
  133.4 11.6 %collective-permute-start.8 = (f16[1,328,128]{2,1,0:T(8,128)(2,1)S(1)}, f16[1,328,128]{2,1,0:T(8,128)(2,1)S(1)}, u32[]{:S(2)}, u32[]{:S(2)}) collective-permute-start(f16[1,328,128]{2,1,0:T(8,128)(2,1)S(1)} %get-tuple-element.93), channel_id=1, source_target_pairs={{0,2},{1,3},{2,0},{3,1},{4,6},{5,7},{6,4},{7,5},{8,10},{9,11},{10,... | collective-permute-start | bytes 251912 | tf_op jit(solution)/shard_map/ppermute | solution.py:479
  135.1 11.0 %collective-permute-start.9 = (f16[1,328,128]{2,1,0:T(8,128)(2,1)S(1)}, f16[1,328,128]{2,1,0:T(8,128)(2,1)S(1)}, u32[]{:S(2)}, u32[]{:S(2)}) collective-permute-start(f16[1,328,128]{2,1,0:T(8,128)(2,1)S(1)} %get-tuple-element.92), channel_id=1, source_target_pairs={{0,3},{1,2},{2,1},{3,0},{4,7},{5,6},{6,5},{7,4},{8,11},{9,10},{10,... | collective-permute-start | bytes 251912 | tf_op jit(solution)/shard_map/ppermute | solution.py:479
  135.2 11.0 %collective-permute-start.10 = (f16[1,328,128]{2,1,0:T(8,128)(2,1)S(1)}, f16[1,328,128]{2,1,0:T(8,128)(2,1)S(1)}, u32[]{:S(2)}, u32[]{:S(2)}) collective-permute-start(f16[1,328,128]{2,1,0:T(8,128)(2,1)S(1)} %get-tuple-element.91), channel_id=1, source_target_pairs={{0,4},{1,5},{2,6},{3,7},{4,0},{5,1},{6,2},{7,3},{8,12},{9,13},{10,... | collective-permute-start | bytes 251912 | tf_op jit(solution)/shard_map/ppermute | solution.py:479
  136.8 9.4 %collective-permute-start.11 = (f16[1,328,128]{2,1,0:T(8,128)(2,1)S(1)}, f16[1,328,128]{2,1,0:T(8,128)(2,1)S(1)}, u32[]{:S(2)}, u32[]{:S(2)}) collective-permute-start(f16[1,328,128]{2,1,0:T(8,128)(2,1)S(1)} %get-tuple-element.90), channel_id=1, source_target_pairs={{0,5},{1,4},{2,7},{3,6},{4,1},{5,0},{6,3},{7,2},{8,13},{9,12},{10,... | collective-permute-start | bytes 251912 | tf_op jit(solution)/shard_map/ppermute | solution.py:479
  136.9 14.0 %collective-permute-start.12 = (f16[1,328,128]{2,1,0:T(8,128)(2,1)S(1)}, f16[1,328,128]{2,1,0:T(8,128)(2,1)S(1)}, u32[]{:S(2)}, u32[]{:S(2)}) collective-permute-start(f16[1,328,128]{2,1,0:T(8,128)(2,1)S(1)} %get-tuple-element.89), channel_id=1, source_target_pairs={{0,6},{1,7},{2,4},{3,5},{4,2},{5,3},{6,0},{7,1},{8,14},{9,15},{10,... | collective-permute-start | bytes 251912 | tf_op jit(solution)/shard_map/ppermute | solution.py:479
  139.5 12.5 %copy-start.36 = (f32[128,128]{1,0:T(8,128)S(1)}, f32[128,128]{1,0:T(8,128)}, u32[]{:S(2)}) copy-start(f32[128,128]{1,0:T(8,128)} %copy-done.35) | copy-start | bytes 196612
  145.0 6.9 %collective-permute-start.13 = (f16[1,328,128]{2,1,0:T(8,128)(2,1)S(1)}, f16[1,328,128]{2,1,0:T(8,128)(2,1)S(1)}, u32[]{:S(2)}, u32[]{:S(2)}) collective-permute-start(f16[1,328,128]{2,1,0:T(8,128)(2,1)S(1)} %get-tuple-element.88), channel_id=1, source_target_pairs={{0,7},{1,6},{2,5},{3,4},{4,3},{5,2},{6,1},{7,0},{8,15},{9,14},{10,... | collective-permute-start | bytes 251912 | tf_op jit(solution)/shard_map/ppermute | solution.py:479
  (46 other events, 129.4 us)
Sparse Core Ops, SparseCore 0:
  9.7 77.2 all-gather.1

commit v7 on v6

--- a/solution.py
+++ b/solution.py
@@ -193,13 +193,7 @@
             state = columns[:, s : s + 1] * state + read_block(held_ref, s, rows)
 
 
-def prepare_kernel(
-    heads_in, size, rows, raw_ref, rim_ref, taps_ref, dt_ref, per_ref, act_ref, slope_ref, abc_ref, sbc_ref, step_ref, ld_ref, stept_ref, ldt_ref, dtw_ref, perw_ref, msg_ref,
-    xs_ref, st_ref,
-):
-    length, channels = act_ref.shape
-    blocks = channels // LANES
-
+def prepare(heads_in, size, raw_ref, rim_ref, taps_ref, dt_ref, per_ref, xs_ref, dtw_ref, perw_ref, length, channels):
     def convolved(cols):
         xs_ref[0:8, cols] = rim_ref[:, cols].astype(F32)[8:16]
         xs_ref[8 : 8 + length, cols] = raw_ref[:, cols].astype(F32)
@@ -209,12 +203,6 @@
         gate = sigmoid(pre)
         return pre * gate, gate * (1.0 + pre * (1.0 - gate))
 
-    for j in range(abc_ref.shape[1] // LANES):
-        cols = slice(j * LANES, (j + 1) * LANES)
-        value, slope = convolved(slice(channels + j * LANES, channels + (j + 1) * LANES))
-        abc_ref[:, cols] = value
-        sbc_ref[:, cols] = slope
-    b_rows = split(abc_ref[:, 0:LANES])
     heads = dt_ref.shape[1]
     dtw_ref[...] = jnp.zeros_like(dtw_ref)
     dtw_ref[:, 0:heads] = dt_ref[...]
@@ -227,20 +215,50 @@
     ld = lax.dot_general(
         lower, step * -jnp.exp(perw_ref[1:2, :]), (NN, ((), ())), precision=HIGH, preferred_element_type=F32
     )
-    step_ref[...] = step
+    return convolved, step, ld
+
+
+def prepare_kernel(
+    heads_in, size, rows, raw_ref, rim_ref, taps_ref, dt_ref, per_ref, abc_ref, ld_ref, msg_ref,
+    xs_ref, st_ref, dtw_ref, perw_ref,
+):
+    length = raw_ref.shape[0]
+    channels = st_ref.shape[0]
+    convolved, step, ld = prepare(
+        heads_in, size, raw_ref, rim_ref, taps_ref, dt_ref, per_ref, xs_ref, dtw_ref, perw_ref, length, channels
+    )
     ld_ref[...] = ld
-    stept_ref[...] = step.T
-    ldt_ref[...] = ld.T
+    for j in range(abc_ref.shape[1] // LANES):
+        value, _ = convolved(slice(channels + j * LANES, channels + (j + 1) * LANES))
+        abc_ref[:, j * LANES : (j + 1) * LANES] = value
+    b_rows = split(abc_ref[:, 0:LANES])
     last = ld[length - 1 : length]
     weight = jnp.exp(last - ld) * step
-    for j in range(blocks):
+    for j in range(channels // LANES):
         cols = slice(j * LANES, (j + 1) * LANES)
-        value, slope = convolved(cols)
-        act_ref[:, cols] = value
-        slope_ref[:, cols] = slope
+        value, _ = convolved(cols)
         scaled = value * spread(weight, j, heads_in, size)
         st_ref[cols, :] = dot3(split(scaled.T), b_rows)
     pack_blocks(st_ref, msg_ref, jnp.exp(last), size, rows)
+
+
+def keep_kernel(
+    heads_in, size, raw_ref, rim_ref, taps_ref, dt_ref, per_ref, act_ref, slope_ref, sbc_ref, step_ref,
+    stept_ref, ldt_ref, dtw_ref, perw_ref, xs_ref,
+):
+    length, channels = act_ref.shape
+    convolved, step, ld = prepare(
+        heads_in, size, raw_ref, rim_ref, taps_ref, dt_ref, per_ref, xs_ref, dtw_ref, perw_ref, length, channels
+    )
+    step_ref[...] = step
+    stept_ref[...] = step.T
+    ldt_ref[...] = ld.T
+    for j in range(sbc_ref.shape[1] // LANES):
+        _, slope = convolved(slice(channels + j * LANES, channels + (j + 1) * LANES))
+        sbc_ref[:, j * LANES : (j + 1) * LANES] = slope
+    for j in range(channels // LANES):
+        cols = slice(j * LANES, (j + 1) * LANES)
+        act_ref[:, cols], slope_ref[:, cols] = convolved(cols)
 
 
 def grad_kernel(heads_in, size, rows, gy_ref, abc_ref, ld_ref, msg_ref, st_ref):
@@ -572,28 +590,17 @@
     unit = 2 * length * channels * LANES
     me = (lax.axis_index("ctx") % plane).astype(jnp.int32).reshape(1)
 
-    act_x, slope_x, act_bc, slope_bc, step, ld, step_t, ld_t, raised, per_head, message = call(
+    padded = pltpu.VMEM((length + 8, channels + bc_raw.shape[1]), F32)
+    per_raw = jnp.stack([dt_bias, a_log])
+    act_bc, ld, message = call(
         functools.partial(prepare_kernel, heads_in, head_size, rows),
-        [shape(whole), shape(whole), shape(bc_raw.shape), shape(bc_raw.shape)]
-        + [shape(square)] * 2
-        + [shape((LANES, length))] * 2
-        + [shape(square), shape((8, LANES))]
-        + [shape((plane, block, LANES))],
-        [
-            raw,
-            rim,
-            taps,
-            dt_raw,
-            jnp.stack([dt_bias, a_log]),
-        ],
+        [shape(bc_raw.shape), shape(square), shape((plane, block, LANES))],
+        [raw, rim, taps, dt_raw, per_raw],
         20 * unit,
         20,
-        [
-            pltpu.VMEM((length + 8, channels + bc_raw.shape[1]), F32),
-            stored,
-        ],
-    )
-    message, grad_out_then = lax.optimization_barrier((message, grad_out))
+        [padded, stored, pltpu.VMEM(square, F32), pltpu.VMEM((8, LANES), F32)],
+    )
+    message, grad_out_then, raw_then = lax.optimization_barrier((message, grad_out, raw))
     held_state = exchange(message, planes).astype(F32)
     part = 640 if channels % 640 == 0 else channels
     grad_gated, grad_y = pl.pallas_call(
@@ -622,6 +629,16 @@
         12,
         [stored],
     )
+    act_x, slope_x, slope_bc, step, step_t, ld_t, raised, per_head = call(
+        functools.partial(keep_kernel, heads_in, head_size),
+        [shape(whole), shape(whole), shape(bc_raw.shape), shape(square)]
+        + [shape((LANES, length))] * 2
+        + [shape(square), shape((8, LANES))],
+        [raw_then, rim, taps, dt_raw, per_raw],
+        10 * unit,
+        20,
+        [padded],
+    )
     y_within, grad_within, grad_bc_within = call(
         functools.partial(local_kernel, heads_in, head_size),
         [shape(whole), shape(whole), shape(act_bc.shape)],
@@ -636,8 +653,9 @@
     held_carry = exchange(message, planes)
     folded, held_carry = lax.optimization_barrier((enter(me, held_state, total, rows, False), held_carry))
     held_carry = held_carry.astype(F32)
-    entered = enter(me, held_carry, group_total(held_carry, rows, True), rows, True)
     state_message = exchange(folded, planes).astype(F32)
+    total, state_message = lax.optimization_barrier((group_total(held_carry, rows, True), state_message))
+    entered = enter(me, held_carry, total, rows, True)
     gated, y_ahead = call(
         functools.partial(forward_kernel, heads_in, head_size, rows),
         [shape((size, share, length), BF16), shape(whole)],
@@ -646,7 +664,7 @@
         16,
         [stored],
     )
-    gated, entered, gathered, y_ahead = lax.optimization_barrier((gated, entered, gathered, y_ahead))
+    gated, gathered, y_ahead = lax.optimization_barrier((gated, gathered, y_ahead))
     held = lax.all_to_all(gated, "ctx", 0, 0, axis_index_groups=groups, tiled=True)
     grad_z, y_sums, grad_bc_ahead = call(
         functools.partial(ahead_kernel, heads_in, head_size, rows),

time: 168 us -> 178 us (1.060)
  waiting for transfers between devices: 33.4 us -> 43.4 us
  local copies, waits for them, and re-layouts: 23.3 us -> 20.9 us
    all_to_all x3, waiting for transfers between devices: 0.01 us -> 9.21 us  [exchange(): lax.all_to_all(half, 'ctx', 0, 0, axis_index_groups=groups, tiled=True)]
    ppermute x6, waiting for transfers between devices: 16.8 us -> 20.8 us  [enter(): others.append(lax.ppermute(total, 'ctx', pairs).astype(F32))]
    all_to_all x1, waiting for transfers between devices: 3.13 us -> 0.01 us  [per_device(): lax.all_to_all(gated, 'ctx', 0, 0, axis_index_groups=groups, tiled=True)]
    unnamed x109 -> x113, local copies, waits for them, and re-layouts: 22.9 us -> 20.5 us
    pallas_call x11 -> x12, Pallas kernels: 23.6 us -> 24.9 us  [call(): pl.pallas_call(kernel, out_shape=tuple(out_shapes), scratch_shapes=list(s...]
where the time goes in v7:
time: 178 us; the launch traced here: 177 us
  starting transfers between devices  48.5 us (27%)
  waiting for transfers between devices  43.4 us (24%)
  Pallas kernels  40.5 us (23%)
  local copies, waits for them, and re-layouts  20.9 us (12%)
  between operations  14.8 us (8%)
  other arithmetic  8.59 us (5%)
    pallas_call x12, Pallas kernels, call(): pl.pallas_call(kernel, out_shape=tuple(out_shapes), scratch_shapes=list(s...  24.9 us
    ppermute x6, waiting for transfers between devices, enter(): others.append(lax.ppermute(total, 'ctx', pairs).astype(F32))  20.8 us
    unnamed x113, local copies, waits for them, and re-layouts  20.5 us
    all_to_all x3, starting transfers between devices, exchange(): lax.all_to_all(half, 'ctx', 0, 0, axis_index_groups=groups, tiled=True)  16.5 us
    ppermute x6, starting transfers between devices, enter(): others.append(lax.ppermute(total, 'ctx', pairs).astype(F32))  15.5 us
    ppermute x7, waiting for transfers between devices, swapped(): lax.ppermute(half[m:m + 1], 'ctx', [(at, at ^ m) for at in range(count)])  12.1 us
    all_to_all x3, waiting for transfers between devices, exchange(): lax.all_to_all(half, 'ctx', 0, 0, axis_index_groups=groups, tiled=True)  9.21 us
    pallas_call x1, Pallas kernels, per_device(): pl.pallas_call(gate_kernel, grid=(channels // part,), in_specs=[pl.BlockS...  8.78 us
  transfers between devices with their start and end apart: 20, of which 10 were waited for; matrix products, arithmetic and copies ran while one was open for 6% of the time, Pallas kernels for 18%

profile of v7, /device:TPU:0, one launch (start us, length us, event | category | flops | bytes accessed | tf_op | source)
XLA Modules:
  0.0 176.7 jit_solution(16535200562652281299)
XLA Ops:
  9.2 2.4 %collective-permute-start = (bf16[16,2816]{1,0:T(8,128)(2,1)S(1)}, bf16[16,2816]{1,0:T(8,128)(2,1)S(1)}, u32[]{:S(2)}, u32[]{:S(2)}) collective-permute-start(bf16[16,2816]{1,0:T(8,128)(2,1)S(1)} %slice.36), channel_id=1, source_target_pairs={{0,1},{1,2},{2,3},{3,4},{4,5},{5,6},{6,7},{7,8},{8,9},{9,10},{10,1... | collective-permute-start | bytes 270344 | tf_op jit(solution)/shard_map/ppermute | solution.py:545
  12.5 2.3 %shard_map.164 = (f32[128,256]{1,0:T(8,128)S(1)}, f32[128,128]{1,0:T(8,128)S(1)}, f32[8,328,128]{2,1,0:T(8,128)S(1)}) custom-call(bf16[128,2816]{1,0:T(8,128)(2,1)S(1)} %constant_dynamic-update-slice_fusion.raw_ref, bf16[16,2816]{1,0:T(8,128)(2,1)S(1)} %collective-permute-done.rim_ref, f32[5,2816]{1,0:T(8,128)S(1)} %pad_maximum_fusion.taps_ref, ...), custom_call_target="tpu_custom_call" | custom-call | flops 1677721600 | bytes 2428224 | tf_op jit(solution)/shard_map/pallas_call | solution.py:26
  16.4 7.7 %all-to-all-start = ((f16[8,328,128]{2,1,0:T(8,128)(2,1)}), f16[8,328,128]{2,1,0:T(8,128)(2,1)}, u32[]{:S(2)}, u32[]{:S(2)}) async-start(f16[8,328,128]{2,1,0:T(8,128)(2,1)} %convert_element_type.51), calls=%async_computation | async-start | bytes 1343488 | tf_op jit(solution)/shard_map/all_to_all | solution.py:489
  24.2 8.8 %shard_map.167 = (f32[128,2560]{1,0:T(8,128)}, f32[128,2560]{1,0:T(8,128)}) custom-call(bf16[128,2560]{1,0:T(8,128)(2,1)S(1)} %copy-done.4, bf16[2560,2560]{1,0:T(8,128)(2,1)} %refs_3_.1, bf16[2560,2560]{1,0:T(8,128)(2,1)} %refs_3_.1, bf16[2560,2560]{1,0:T(8,128)(2,1)} %refs_3_.1, bf16[2560,2560]{1,0:T(8,128)(2,1)} %refs_3_.1, bf16[128,2560]{1,0:T(8,128)(2,1)S(1)} %copy-done.3), custom_call_target="tpu_custom_call" | custom-call | flops 1677721600 | bytes 13107200 | tf_op jit(solution)/shard_map/pallas_call | solution.py:606
  35.9 1.9 %shard_map.166 = (f32[128,2560]{1,0:T(8,128)S(1)}, f32[128,2560]{1,0:T(8,128)S(1)}, f32[128,256]{1,0:T(8,128)S(1)}, f32[128,128]{1,0:T(8,128)S(1)}, f32[128,128]...) custom-call(bf16[128,2816]{1,0:T(8,128)(2,1)S(1)} %copy-done.17, ...), custom_call_target="tpu_custom_call" | custom-call | flops 838860800 | bytes 3906880 | tf_op jit(solution)/shard_map/pallas_call | solution.py:26
  40.2 4.6 %shard_map.168 = (f32[128,2560]{1,0:T(8,128)S(1)}, f32[128,2560]{1,0:T(8,128)S(1)}, f32[128,256]{1,0:T(8,128)S(1)}) custom-call(f32[128,2560]{1,0:T(8,128)S(1)} %get-tuple-element.49.act_ref, f32[128,2560]{1,0:T(8,128)S(1)} %copy-done.6, f32[128,256]{1,0:T(8,128)S(1)} %copy-done.30, f32[128,128]{1,0:T(8,128)S(1)} %get-tuple-element.53.step_ref, ...), custom_call_target="tpu_custom_call" | custom-call | flops 3355443200 | bytes 5767168 | tf_op jit(solution)/shard_map/pallas_call | solution.py:26
  52.1 4.3 %all-to-all-start.1 = ((f16[8,328,128]{2,1,0:T(8,128)(2,1)}), f16[8,328,128]{2,1,0:T(8,128)(2,1)}, u32[]{:S(2)}, u32[]{:S(2)}) async-start(f16[8,328,128]{2,1,0:T(8,128)(2,1)} %convert_element_type.57), calls=%async_computation.1 | async-start | bytes 1343488 | tf_op jit(solution)/shard_map/all_to_all | solution.py:489
  56.4 5.9 %collective-permute-start.1 = (f16[1,328,128]{2,1,0:T(8,128)(2,1)}, f16[1,328,128]{2,1,0:T(8,128)(2,1)S(1)}, u32[]{:S(2)}, u32[]{:S(2)}) collective-permute-start(f16[1,328,128]{2,1,0:T(8,128)(2,1)} %convert_element_type.53), channel_id=1, source_target_pairs={{0,8},{1,9},{2,10},{3,11},{4,12},{5,13},{6,14},{7,15},{8,16},{9,17... | collective-permute-start | bytes 251912 | tf_op jit(solution)/shard_map/ppermute | solution.py:524
  62.3 4.5 %collective-permute-start.2 = (f16[1,328,128]{2,1,0:T(8,128)(2,1)}, f16[1,328,128]{2,1,0:T(8,128)(2,1)S(1)}, u32[]{:S(2)}, u32[]{:S(2)}) collective-permute-start(f16[1,328,128]{2,1,0:T(8,128)(2,1)} %convert_element_type.53), channel_id=1, source_target_pairs={{0,16},{1,17},{2,18},{3,19},{4,20},{5,21},{6,22},{7,23},{8,24},{9,... | collective-permute-start | bytes 251912 | tf_op jit(solution)/shard_map/ppermute | solution.py:524
  68.1 2.9 %collective-permute-done.2 = f16[1,328,128]{2,1,0:T(8,128)(2,1)S(1)} collective-permute-done((f16[1,328,128]{2,1,0:T(8,128)(2,1)}, f16[1,328,128]{2,1,0:T(8,128)(2,1)S(1)}, u32[]{:S(2)}, u32[]{:S(2)}) %collective-permute-start.2) | collective-permute-done | bytes 84000 | tf_op jit(solution)/shard_map/ppermute | solution.py:524
  71.0 3.1 %collective-permute-done.3 = f16[1,328,128]{2,1,0:T(8,128)(2,1)S(1)} collective-permute-done((f16[1,328,128]{2,1,0:T(8,128)(2,1)}, f16[1,328,128]{2,1,0:T(8,128)(2,1)S(1)}, u32[]{:S(2)}, u32[]{:S(2)}) %collective-permute-start.3) | collective-permute-done | bytes 84000 | tf_op jit(solution)/shard_map/ppermute | solution.py:524
  76.4 4.4 %all-to-all-start.2 = ((f16[8,328,128]{2,1,0:T(8,128)(2,1)}), f16[8,328,128]{2,1,0:T(8,128)(2,1)}, u32[]{:S(2)}, u32[]{:S(2)}) async-start(f16[8,328,128]{2,1,0:T(8,128)(2,1)} %convert_element_type.60), calls=%async_computation.2 | async-start | bytes 1343488 | tf_op jit(solution)/shard_map/all_to_all | solution.py:489
  83.5 9.2 %all-to-all-done.2 = f16[8,328,128]{2,1,0:T(8,128)(2,1)} async-done(((f16[8,328,128]{2,1,0:T(8,128)(2,1)}), f16[8,328,128]{2,1,0:T(8,128)(2,1)}, u32[]{:S(2)}, u32[]{:S(2)}) %all-to-all-start.2) | async-done | bytes 671776 | tf_op jit(solution)/shard_map/all_to_all | solution.py:489
  101.2 4.4 %all-to-all-start.3 = ((bf16[16,160,128]{2,1,0:T(8,128)(2,1)}), bf16[16,160,128]{2,1,0:T(8,128)(2,1)}, u32[]{:S(2)}, u32[]{:S(2)}) async-start(bf16[16,160,128]{2,1,0:T(8,128)(2,1)} %copy-done.18), calls=%async_computation.3 | async-start | bytes 1310720 | tf_op jit(solution)/shard_map/all_to_all | solution.py:668
  109.5 9.8 %collective-permute-done.4 = f16[1,328,128]{2,1,0:T(8,128)(2,1)S(1)} collective-permute-done((f16[1,328,128]{2,1,0:T(8,128)(2,1)}, f16[1,328,128]{2,1,0:T(8,128)(2,1)S(1)}, u32[]{:S(2)}, u32[]{:S(2)}) %collective-permute-start.4) | collective-permute-done | bytes 84000 | tf_op jit(solution)/shard_map/ppermute | solution.py:524
  119.3 5.0 %collective-permute-done.6 = f16[1,328,128]{2,1,0:T(8,128)(2,1)S(1)} collective-permute-done((f16[1,328,128]{2,1,0:T(8,128)(2,1)}, f16[1,328,128]{2,1,0:T(8,128)(2,1)S(1)}, u32[]{:S(2)}, u32[]{:S(2)}) %collective-permute-start.6) | collective-permute-done | bytes 84000 | tf_op jit(solution)/shard_map/ppermute | solution.py:524
  128.2 2.3 %shard_map.173 = (bf16[128,2560]{1,0:T(8,128)(2,1)}, f32[128,128]{1,0:T(8,128)S(1)}, f32[128,256]{1,0:T(8,128)S(1)}) custom-call(f32[8,328,128]{2,1,0:T(8,128)S(1)} %convert_element_type.61.msg_ref.msgf_ref, f32[128,2560]{1,0:T(8,128)S(1)} %copy-done.11, f32[128,2560]{1,0:T(8,128)S(1)} %copy-done.7, f32[128,128]{1,0:T(8,128)S(1)} %get-tuple-element.54.ld_ref, ...), custom_call_target="tpu_custom_call" | custom-call | flops 1677721600 | bytes 8300544 | tf_op jit(solution)/shard_map/pallas_call | solution.py:26
  131.8 6.8 %shard_map.174 = bf16[32,112,128]{2,1,0:T(8,128)(2,1)S(1)} custom-call(bf16[16,160,128]{2,1,0:T(8,128)(2,1)} %all-to-all-done.3.held_ref, bf16[2048,2560]{1,0:T(8,128)(2,1)} %all-gather.2.cloned.1.call-done.refs_0_.refs_1_.refs_2_.refs_3_, bf16[2048,2560]{1,0:T(8,128)(2,1)} %all-gather.2.cloned.1.call-done.refs_0_.refs_1_.refs_2_.refs_3_, ...), custom_call_target="tpu_custom_call" | custom-call | flops 1677721600 | bytes 10485760 | tf_op jit(solution)/shard_map/pallas_call | solution.py:687
  139.5 3.5 %all-to-all-start.4 = ((bf16[32,112,128]{2,1,0:T(8,128)(2,1)}), bf16[32,112,128]{2,1,0:T(8,128)(2,1)}, u32[]{:S(2)}, u32[]{:S(2)}) async-start(bf16[32,112,128]{2,1,0:T(8,128)(2,1)} %copy-done.2), calls=%async_computation.4 | async-start | bytes 1835008 | tf_op jit(solution)/shard_map/all_to_all | solution.py:706
  146.9 2.6 %collective-permute-start.12 = (f16[1,328,128]{2,1,0:T(8,128)(2,1)S(1)}, f16[1,328,128]{2,1,0:T(8,128)(2,1)S(1)}, u32[]{:S(2)}, u32[]{:S(2)}) collective-permute-start(f16[1,328,128]{2,1,0:T(8,128)(2,1)S(1)} %get-tuple-element.93), channel_id=1, source_target_pairs={{0,6},{1,7},{2,4},{3,5},{4,2},{5,3},{6,0},{7,1},{8,14},{9,15},{10,... | collective-permute-start | bytes 251912 | tf_op jit(solution)/shard_map/ppermute | solution.py:497
  149.6 5.4 %collective-permute-done.8 = f16[1,328,128]{2,1,0:T(8,128)(2,1)S(1)} collective-permute-done((f16[1,328,128]{2,1,0:T(8,128)(2,1)S(1)}, f16[1,328,128]{2,1,0:T(8,128)(2,1)S(1)}, u32[]{:S(2)}, u32[]{:S(2)}) %collective-permute-start.8) | collective-permute-done | bytes 84000 | tf_op jit(solution)/shard_map/ppermute | solution.py:497
  156.3 4.7 %collective-permute-done.12 = f16[1,328,128]{2,1,0:T(8,128)(2,1)S(1)} collective-permute-done((f16[1,328,128]{2,1,0:T(8,128)(2,1)S(1)}, f16[1,328,128]{2,1,0:T(8,128)(2,1)S(1)}, u32[]{:S(2)}, u32[]{:S(2)}) %collective-permute-start.12) | collective-permute-done | bytes 84000 | tf_op jit(solution)/shard_map/ppermute | solution.py:497
  162.1 4.1 %shard_map.176 = (bf16[128,2560]{1,0:T(8,128)(2,1)}, f32[128,256]{1,0:T(8,128)S(1)}, f32[128,40]{1,0:T(8,128)S(1)}) custom-call(s32[1]{0:T(128)} %bitcast.me_ref, f32[8,328,128]{2,1,0:T(8,128)S(1)} %convert_element_type.66.msg_ref, f32[8,328,128]{2,1,0:T(8,128)S(1)} %convert_element_type.61.msg_ref.msgf_ref, f32[128,2560]{1,0:T(8,128)S(1)} %copy-done.12, ...), custom_call_target="tpu_custom_call" | custom-call | flops 3355443200 | bytes 9275396 | tf_op jit(solution)/shard_map/pallas_call | solution.py:26
  167.5 2.3 %shard_map.177 = f32[80,2560]{1,0:T(8,128)} custom-call(bf16[32,112,128]{2,1,0:T(8,128)(2,1)} %all-to-all-done.4.parts_ref), custom_call_target="tpu_custom_call" | custom-call | flops 917504 | bytes 1736704 | tf_op jit(solution)/shard_map/pallas_call | solution.py:26
  (171 shorter events, 49.1 us)
Async XLA Ops:
  7.2 94.0 %all-gather.2.cloned.1.call-start = ((), (), s32[]{:S(2)}) async-start(), calls=%async_computation.5 | async-start | bytes 11141120 | tf_op jit(solution)/shard_map/all_gather | solution.py:575
  9.2 3.3 %collective-permute-start = (bf16[16,2816]{1,0:T(8,128)(2,1)S(1)}, bf16[16,2816]{1,0:T(8,128)(2,1)S(1)}, u32[]{:S(2)}, u32[]{:S(2)}) collective-permute-start(bf16[16,2816]{1,0:T(8,128)(2,1)S(1)} %slice.36), channel_id=1, source_target_pairs={{0,1},{1,2},{2,3},{3,4},{4,5},{5,6},{6,7},{7,8},{8,9},{9,10},{10,1... | collective-permute-start | bytes 270344 | tf_op jit(solution)/shard_map/ppermute | solution.py:545
  16.4 32.2 %all-to-all-start = ((f16[8,328,128]{2,1,0:T(8,128)(2,1)}), f16[8,328,128]{2,1,0:T(8,128)(2,1)}, u32[]{:S(2)}, u32[]{:S(2)}) async-start(f16[8,328,128]{2,1,0:T(8,128)(2,1)} %convert_element_type.51), calls=%async_computation | async-start | bytes 1343488 | tf_op jit(solution)/shard_map/all_to_all | solution.py:489
  24.2 8.8 %copy-start.30 = (f32[128,256]{1,0:T(8,128)S(1)}, f32[128,256]{1,0:T(8,128)}, u32[]{:S(2)}) copy-start(f32[128,256]{1,0:T(8,128)} %copy-done.29) | copy-start | bytes 393220
  52.1 23.4 %all-to-all-start.1 = ((f16[8,328,128]{2,1,0:T(8,128)(2,1)}), f16[8,328,128]{2,1,0:T(8,128)(2,1)}, u32[]{:S(2)}, u32[]{:S(2)}) async-start(f16[8,328,128]{2,1,0:T(8,128)(2,1)} %convert_element_type.57), calls=%async_computation.1 | async-start | bytes 1343488 | tf_op jit(solution)/shard_map/all_to_all | solution.py:489
  56.4 11.7 %collective-permute-start.1 = (f16[1,328,128]{2,1,0:T(8,128)(2,1)}, f16[1,328,128]{2,1,0:T(8,128)(2,1)S(1)}, u32[]{:S(2)}, u32[]{:S(2)}) collective-permute-start(f16[1,328,128]{2,1,0:T(8,128)(2,1)} %convert_element_type.53), channel_id=1, source_target_pairs={{0,8},{1,9},{2,10},{3,11},{4,12},{5,13},{6,14},{7,15},{8,16},{9,17... | collective-permute-start | bytes 251912 | tf_op jit(solution)/shard_map/ppermute | solution.py:524
  62.3 8.7 %collective-permute-start.2 = (f16[1,328,128]{2,1,0:T(8,128)(2,1)}, f16[1,328,128]{2,1,0:T(8,128)(2,1)S(1)}, u32[]{:S(2)}, u32[]{:S(2)}) collective-permute-start(f16[1,328,128]{2,1,0:T(8,128)(2,1)} %convert_element_type.53), channel_id=1, source_target_pairs={{0,16},{1,17},{2,18},{3,19},{4,20},{5,21},{6,22},{7,23},{8,24},{9,... | collective-permute-start | bytes 251912 | tf_op jit(solution)/shard_map/ppermute | solution.py:524
  66.8 7.3 %collective-permute-start.3 = (f16[1,328,128]{2,1,0:T(8,128)(2,1)}, f16[1,328,128]{2,1,0:T(8,128)(2,1)S(1)}, u32[]{:S(2)}, u32[]{:S(2)}) collective-permute-start(f16[1,328,128]{2,1,0:T(8,128)(2,1)} %convert_element_type.53), channel_id=1, source_target_pairs={{0,24},{1,25},{2,26},{3,27},{4,28},{5,29},{6,30},{7,31}} | collective-permute-start | bytes 251912 | tf_op jit(solution)/shard_map/ppermute | solution.py:524
  76.4 16.3 %all-to-all-start.2 = ((f16[8,328,128]{2,1,0:T(8,128)(2,1)}), f16[8,328,128]{2,1,0:T(8,128)(2,1)}, u32[]{:S(2)}, u32[]{:S(2)}) async-start(f16[8,328,128]{2,1,0:T(8,128)(2,1)} %convert_element_type.60), calls=%async_computation.2 | async-start | bytes 1343488 | tf_op jit(solution)/shard_map/all_to_all | solution.py:489
  101.2 30.6 %all-to-all-start.3 = ((bf16[16,160,128]{2,1,0:T(8,128)(2,1)}), bf16[16,160,128]{2,1,0:T(8,128)(2,1)}, u32[]{:S(2)}, u32[]{:S(2)}) async-start(bf16[16,160,128]{2,1,0:T(8,128)(2,1)} %copy-done.18), calls=%async_computation.3 | async-start | bytes 1310720 | tf_op jit(solution)/shard_map/all_to_all | solution.py:668
  105.6 13.7 %collective-permute-start.4 = (f16[1,328,128]{2,1,0:T(8,128)(2,1)}, f16[1,328,128]{2,1,0:T(8,128)(2,1)S(1)}, u32[]{:S(2)}, u32[]{:S(2)}) collective-permute-start(f16[1,328,128]{2,1,0:T(8,128)(2,1)} %convert_element_type.59), channel_id=1, source_target_pairs={{8,0},{9,1},{10,2},{11,3},{12,4},{13,5},{14,6},{15,7},{16,8},{17,9... | collective-permute-start | bytes 251912 | tf_op jit(solution)/shard_map/ppermute | solution.py:524
  106.9 12.4 %collective-permute-start.5 = (f16[1,328,128]{2,1,0:T(8,128)(2,1)}, f16[1,328,128]{2,1,0:T(8,128)(2,1)S(1)}, u32[]{:S(2)}, u32[]{:S(2)}) collective-permute-start(f16[1,328,128]{2,1,0:T(8,128)(2,1)} %convert_element_type.59), channel_id=1, source_target_pairs={{16,0},{17,1},{18,2},{19,3},{20,4},{21,5},{22,6},{23,7},{24,8},{25... | collective-permute-start | bytes 251912 | tf_op jit(solution)/shard_map/ppermute | solution.py:524
  108.2 16.2 %collective-permute-start.6 = (f16[1,328,128]{2,1,0:T(8,128)(2,1)}, f16[1,328,128]{2,1,0:T(8,128)(2,1)S(1)}, u32[]{:S(2)}, u32[]{:S(2)}) collective-permute-start(f16[1,328,128]{2,1,0:T(8,128)(2,1)} %convert_element_type.59), channel_id=1, source_target_pairs={{24,0},{25,1},{26,2},{27,3},{28,4},{29,5},{30,6},{31,7}} | collective-permute-start | bytes 251912 | tf_op jit(solution)/shard_map/ppermute | solution.py:524
  139.5 28.0 %all-to-all-start.4 = ((bf16[32,112,128]{2,1,0:T(8,128)(2,1)}), bf16[32,112,128]{2,1,0:T(8,128)(2,1)}, u32[]{:S(2)}, u32[]{:S(2)}) async-start(bf16[32,112,128]{2,1,0:T(8,128)(2,1)} %copy-done.2), calls=%async_computation.4 | async-start | bytes 1835008 | tf_op jit(solution)/shard_map/all_to_all | solution.py:706
  143.0 19.0 %copy-start.38 = (f32[128,2560]{1,0:T(8,128)S(1)}, f32[128,2560]{1,0:T(8,128)}, u32[]{:S(2)}) copy-start(f32[128,2560]{1,0:T(8,128)} %copy-done.37) | copy-start | bytes 3932164
  143.1 18.9 %copy-start.36 = (f32[128,2560]{1,0:T(8,128)S(1)}, f32[128,2560]{1,0:T(8,128)}, u32[]{:S(2)}) copy-start(f32[128,2560]{1,0:T(8,128)} %copy-done.35) | copy-start | bytes 3932164
  143.3 3.6 %collective-permute-start.7 = (f16[1,328,128]{2,1,0:T(8,128)(2,1)S(1)}, f16[1,328,128]{2,1,0:T(8,128)(2,1)S(1)}, u32[]{:S(2)}, u32[]{:S(2)}) collective-permute-start(f16[1,328,128]{2,1,0:T(8,128)(2,1)S(1)} %get-tuple-element.98), channel_id=1, source_target_pairs={{0,1},{1,0},{2,3},{3,2},{4,5},{5,4},{6,7},{7,6},{8,9},{9,8},{10,11... | collective-permute-start | bytes 251912 | tf_op jit(solution)/shard_map/ppermute | solution.py:497
  143.4 11.6 %collective-permute-start.8 = (f16[1,328,128]{2,1,0:T(8,128)(2,1)S(1)}, f16[1,328,128]{2,1,0:T(8,128)(2,1)S(1)}, u32[]{:S(2)}, u32[]{:S(2)}) collective-permute-start(f16[1,328,128]{2,1,0:T(8,128)(2,1)S(1)} %get-tuple-element.97), channel_id=1, source_target_pairs={{0,2},{1,3},{2,0},{3,1},{4,6},{5,7},{6,4},{7,5},{8,10},{9,11},{10,... | collective-permute-start | bytes 251912 | tf_op jit(solution)/shard_map/ppermute | solution.py:497
  145.1 11.0 %collective-permute-start.9 = (f16[1,328,128]{2,1,0:T(8,128)(2,1)S(1)}, f16[1,328,128]{2,1,0:T(8,128)(2,1)S(1)}, u32[]{:S(2)}, u32[]{:S(2)}) collective-permute-start(f16[1,328,128]{2,1,0:T(8,128)(2,1)S(1)} %get-tuple-element.96), channel_id=1, source_target_pairs={{0,3},{1,2},{2,1},{3,0},{4,7},{5,6},{6,5},{7,4},{8,11},{9,10},{10,... | collective-permute-start | bytes 251912 | tf_op jit(solution)/shard_map/ppermute | solution.py:497
  145.2 11.0 %collective-permute-start.10 = (f16[1,328,128]{2,1,0:T(8,128)(2,1)S(1)}, f16[1,328,128]{2,1,0:T(8,128)(2,1)S(1)}, u32[]{:S(2)}, u32[]{:S(2)}) collective-permute-start(f16[1,328,128]{2,1,0:T(8,128)(2,1)S(1)} %get-tuple-element.95), channel_id=1, source_target_pairs={{0,4},{1,5},{2,6},{3,7},{4,0},{5,1},{6,2},{7,3},{8,12},{9,13},{10,... | collective-permute-start | bytes 251912 | tf_op jit(solution)/shard_map/ppermute | solution.py:497
  146.8 9.4 %collective-permute-start.11 = (f16[1,328,128]{2,1,0:T(8,128)(2,1)S(1)}, f16[1,328,128]{2,1,0:T(8,128)(2,1)S(1)}, u32[]{:S(2)}, u32[]{:S(2)}) collective-permute-start(f16[1,328,128]{2,1,0:T(8,128)(2,1)S(1)} %get-tuple-element.94), channel_id=1, source_target_pairs={{0,5},{1,4},{2,7},{3,6},{4,1},{5,0},{6,3},{7,2},{8,13},{9,12},{10,... | collective-permute-start | bytes 251912 | tf_op jit(solution)/shard_map/ppermute | solution.py:497
  146.9 14.0 %collective-permute-start.12 = (f16[1,328,128]{2,1,0:T(8,128)(2,1)S(1)}, f16[1,328,128]{2,1,0:T(8,128)(2,1)S(1)}, u32[]{:S(2)}, u32[]{:S(2)}) collective-permute-start(f16[1,328,128]{2,1,0:T(8,128)(2,1)S(1)} %get-tuple-element.93), channel_id=1, source_target_pairs={{0,6},{1,7},{2,4},{3,5},{4,2},{5,3},{6,0},{7,1},{8,14},{9,15},{10,... | collective-permute-start | bytes 251912 | tf_op jit(solution)/shard_map/ppermute | solution.py:497
  149.5 12.5 %copy-start.42 = (f32[128,128]{1,0:T(8,128)S(1)}, f32[128,128]{1,0:T(8,128)}, u32[]{:S(2)}) copy-start(f32[128,128]{1,0:T(8,128)} %copy-done.41) | copy-start | bytes 196612
  155.0 6.9 %collective-permute-start.13 = (f16[1,328,128]{2,1,0:T(8,128)(2,1)S(1)}, f16[1,328,128]{2,1,0:T(8,128)(2,1)S(1)}, u32[]{:S(2)}, u32[]{:S(2)}) collective-permute-start(f16[1,328,128]{2,1,0:T(8,128)(2,1)S(1)} %get-tuple-element.92), channel_id=1, source_target_pairs={{0,7},{1,6},{2,5},{3,4},{4,3},{5,2},{6,1},{7,0},{8,15},{9,14},{10,... | collective-permute-start | bytes 251912 | tf_op jit(solution)/shard_map/ppermute | solution.py:497
  (48 other events, 152.9 us)
Sparse Core Ops, SparseCore 0:
  9.7 77.2 all-gather.1

commit v8 on v7

--- a/solution.py
+++ b/solution.py
@@ -639,23 +639,22 @@
         20,
         [padded],
     )
+    total, ld_t_then, message = lax.optimization_barrier((group_total(held_state, rows, False), ld_t, message))
+    held_carry = exchange(message, planes)
     y_within, grad_within, grad_bc_within = call(
         functools.partial(local_kernel, heads_in, head_size),
         [shape(whole), shape(whole), shape(act_bc.shape)],
-        [act_x, grad_y, act_bc, step, ld, step_t, ld_t],
+        [act_x, grad_y, act_bc, step, ld, step_t, ld_t_then],
         40 * unit,
         16,
         [pltpu.VMEM(square, F32)],
     )
-    total, y_within, message = lax.optimization_barrier(
-        (group_total(held_state, rows, False), y_within, message)
-    )
-    held_carry = exchange(message, planes)
-    folded, held_carry = lax.optimization_barrier((enter(me, held_state, total, rows, False), held_carry))
+    folded, held_carry, y_within = lax.optimization_barrier(
+        (enter(me, held_state, total, rows, False), held_carry, y_within)
+    )
     held_carry = held_carry.astype(F32)
+    entered = enter(me, held_carry, group_total(held_carry, rows, True), rows, True)
     state_message = exchange(folded, planes).astype(F32)
-    total, state_message = lax.optimization_barrier((group_total(held_carry, rows, True), state_message))
-    entered = enter(me, held_carry, total, rows, True)
     gated, y_ahead = call(
         functools.partial(forward_kernel, heads_in, head_size, rows),
         [shape((size, share, length), BF16), shape(whole)],
@@ -664,7 +663,7 @@
         16,
         [stored],
     )
-    gated, gathered, y_ahead = lax.optimization_barrier((gated, gathered, y_ahead))
+    gated, entered, gathered, y_ahead = lax.optimization_barrier((gated, entered, gathered, y_ahead))
     held = lax.all_to_all(gated, "ctx", 0, 0, axis_index_groups=groups, tiled=True)
     grad_z, y_sums, grad_bc_ahead = call(
         functools.partial(ahead_kernel, heads_in, head_size, rows),

time: 178 us -> 166 us (0.933)
  waiting for transfers between devices: 43.4 us -> 24.9 us
  local copies, waits for them, and re-layouts: 20.9 us -> 26.9 us
    ppermute x6, waiting for transfers between devices: 20.8 us -> 8.37 us  [enter(): others.append(lax.ppermute(total, 'ctx', pairs).astype(F32))]
    all_to_all x3, waiting for transfers between devices: 9.21 us -> 0.04 us  [exchange(): lax.all_to_all(half, 'ctx', 0, 0, axis_index_groups=groups, tiled=True)]
    unnamed x113, local copies, waits for them, and re-layouts: 20.5 us -> 26.5 us
    all_to_all x1, waiting for transfers between devices: 0.01 us -> 3.09 us  [per_device(): lax.all_to_all(gated, 'ctx', 0, 0, axis_index_groups=groups, tiled=True)]
  transfers between devices with their start and end apart: 20 -> 20, of which waited for: 10 -> 9; matrix products, arithmetic and copies ran while one was open for 6% -> 6% of each run, Pallas kernels for 18% -> 19%
where the time goes in v8:
time: 166 us; the launch traced here: 164 us
  starting transfers between devices  48.2 us (29%)
  Pallas kernels  40.9 us (25%)
  local copies, waits for them, and re-layouts  26.9 us (16%)
  waiting for transfers between devices  24.9 us (15%)
  between operations  14.8 us (9%)
  other arithmetic  8.07 us (5%)
    unnamed x113, local copies, waits for them, and re-layouts  26.5 us
    pallas_call x12, Pallas kernels, call(): pl.pallas_call(kernel, out_shape=tuple(out_shapes), scratch_shapes=list(s...  25.4 us
    all_to_all x3, starting transfers between devices, exchange(): lax.all_to_all(half, 'ctx', 0, 0, axis_index_groups=groups, tiled=True)  16.3 us
    ppermute x6, starting transfers between devices, enter(): others.append(lax.ppermute(total, 'ctx', pairs).astype(F32))  15.6 us
    ppermute x7, waiting for transfers between devices, swapped(): lax.ppermute(half[m:m + 1], 'ctx', [(at, at ^ m) for at in range(count)])  12.1 us
    pallas_call x1, Pallas kernels, per_device(): pl.pallas_call(gate_kernel, grid=(channels // part,), in_specs=[pl.BlockS...  8.79 us
    ppermute x6, waiting for transfers between devices, enter(): others.append(lax.ppermute(total, 'ctx', pairs).astype(F32))  8.37 us
    pallas_call x1, Pallas kernels, per_device(): pl.pallas_call(functools.partial(product_kernel, out_rows), grid=(width /...  6.78 us
  transfers between devices with their start and end apart: 20, of which 9 were waited for; matrix products, arithmetic and copies ran while one was open for 6% of the time, Pallas kernels for 19%

profile of v8, /device:TPU:0, one launch (start us, length us, event | category | flops | bytes accessed | tf_op | source)
XLA Modules:
  0.0 163.8 jit_solution(2843758128833805728)
XLA Ops:
  9.2 2.4 %collective-permute-start = (bf16[16,2816]{1,0:T(8,128)(2,1)S(1)}, bf16[16,2816]{1,0:T(8,128)(2,1)S(1)}, u32[]{:S(2)}, u32[]{:S(2)}) collective-permute-start(bf16[16,2816]{1,0:T(8,128)(2,1)S(1)} %slice.36), channel_id=1, source_target_pairs={{0,1},{1,2},{2,3},{3,4},{4,5},{5,6},{6,7},{7,8},{8,9},{9,10},{10,1... | collective-permute-start | bytes 270344 | tf_op jit(solution)/shard_map/ppermute | solution.py:545
  12.5 2.3 %shard_map.164 = (f32[128,256]{1,0:T(8,128)S(1)}, f32[128,128]{1,0:T(8,128)S(1)}, f32[8,328,128]{2,1,0:T(8,128)S(1)}) custom-call(bf16[128,2816]{1,0:T(8,128)(2,1)S(1)} %constant_dynamic-update-slice_fusion.raw_ref, bf16[16,2816]{1,0:T(8,128)(2,1)S(1)} %collective-permute-done.rim_ref, f32[5,2816]{1,0:T(8,128)S(1)} %pad_maximum_fusion.taps_ref, ...), custom_call_target="tpu_custom_call" | custom-call | flops 1677721600 | bytes 2428224 | tf_op jit(solution)/shard_map/pallas_call | solution.py:26
  15.8 7.7 %all-to-all-start = ((f16[8,328,128]{2,1,0:T(8,128)(2,1)}), f16[8,328,128]{2,1,0:T(8,128)(2,1)}, u32[]{:S(2)}, u32[]{:S(2)}) async-start(f16[8,328,128]{2,1,0:T(8,128)(2,1)} %convert_element_type.51), calls=%async_computation | async-start | bytes 1343488 | tf_op jit(solution)/shard_map/all_to_all | solution.py:489
  23.5 8.8 %shard_map.167 = (f32[128,2560]{1,0:T(8,128)}, f32[128,2560]{1,0:T(8,128)}) custom-call(bf16[128,2560]{1,0:T(8,128)(2,1)S(1)} %copy-done.2, bf16[2560,2560]{1,0:T(8,128)(2,1)} %refs_3_.1, bf16[2560,2560]{1,0:T(8,128)(2,1)} %refs_3_.1, bf16[2560,2560]{1,0:T(8,128)(2,1)} %refs_3_.1, bf16[2560,2560]{1,0:T(8,128)(2,1)} %refs_3_.1, bf16[128,2560]{1,0:T(8,128)(2,1)S(1)} %copy-done.1), custom_call_target="tpu_custom_call" | custom-call | flops 1677721600 | bytes 13107200 | tf_op jit(solution)/shard_map/pallas_call | solution.py:606
  35.3 1.9 %shard_map.166 = (f32[128,2560]{1,0:T(8,128)S(1)}, f32[128,2560]{1,0:T(8,128)S(1)}, f32[128,256]{1,0:T(8,128)S(1)}, f32[128,128]{1,0:T(8,128)S(1)}, f32[128,128]...) custom-call(bf16[128,2816]{1,0:T(8,128)(2,1)S(1)} %copy-done.16, ...), custom_call_target="tpu_custom_call" | custom-call | flops 838860800 | bytes 3906880 | tf_op jit(solution)/shard_map/pallas_call | solution.py:26
  45.9 4.3 %all-to-all-start.1 = ((f16[8,328,128]{2,1,0:T(8,128)(2,1)}), f16[8,328,128]{2,1,0:T(8,128)(2,1)}, u32[]{:S(2)}, u32[]{:S(2)}) async-start(f16[8,328,128]{2,1,0:T(8,128)(2,1)} %convert_element_type.57), calls=%async_computation.1 | async-start | bytes 1343488 | tf_op jit(solution)/shard_map/all_to_all | solution.py:489
  50.3 5.8 %collective-permute-start.1 = (f16[1,328,128]{2,1,0:T(8,128)(2,1)}, f16[1,328,128]{2,1,0:T(8,128)(2,1)S(1)}, u32[]{:S(2)}, u32[]{:S(2)}) collective-permute-start(f16[1,328,128]{2,1,0:T(8,128)(2,1)} %convert_element_type.53), channel_id=1, source_target_pairs={{0,8},{1,9},{2,10},{3,11},{4,12},{5,13},{6,14},{7,15},{8,16},{9,17... | collective-permute-start | bytes 251912 | tf_op jit(solution)/shard_map/ppermute | solution.py:524
  56.1 4.5 %collective-permute-start.2 = (f16[1,328,128]{2,1,0:T(8,128)(2,1)}, f16[1,328,128]{2,1,0:T(8,128)(2,1)S(1)}, u32[]{:S(2)}, u32[]{:S(2)}) collective-permute-start(f16[1,328,128]{2,1,0:T(8,128)(2,1)} %convert_element_type.53), channel_id=1, source_target_pairs={{0,16},{1,17},{2,18},{3,19},{4,20},{5,21},{6,22},{7,23},{8,24},{9,... | collective-permute-start | bytes 251912 | tf_op jit(solution)/shard_map/ppermute | solution.py:524
  66.8 4.8 %shard_map.170 = (f32[128,2560]{1,0:T(8,128)S(1)}, f32[128,2560]{1,0:T(8,128)S(1)}, f32[128,256]{1,0:T(8,128)S(1)}) custom-call(f32[128,2560]{1,0:T(8,128)S(1)} %copy-done.8, f32[128,2560]{1,0:T(8,128)S(1)} %copy-done.4, f32[128,256]{1,0:T(8,128)S(1)} %copy-done.25, f32[128,128]{1,0:T(8,128)S(1)} %copy-done.35, f32[128,128]{1,0:T(8,128)S(1)} %get-tuple-element.53.ld_ref, ...), custom_call_target="tpu_custom_call" | custom-call | flops 3355443200 | bytes 5767168 | tf_op jit(solution)/shard_map/pallas_call | solution.py:26
  76.1 4.2 %all-to-all-start.2 = ((f16[8,328,128]{2,1,0:T(8,128)(2,1)}), f16[8,328,128]{2,1,0:T(8,128)(2,1)}, u32[]{:S(2)}, u32[]{:S(2)}) async-start(f16[8,328,128]{2,1,0:T(8,128)(2,1)} %convert_element_type.58), calls=%async_computation.2 | async-start | bytes 1343488 | tf_op jit(solution)/shard_map/all_to_all | solution.py:489
  86.3 2.6 %collective-permute-done.4 = f16[1,328,128]{2,1,0:T(8,128)(2,1)S(1)} collective-permute-done((f16[1,328,128]{2,1,0:T(8,128)(2,1)S(1)}, f16[1,328,128]{2,1,0:T(8,128)(2,1)S(1)}, u32[]{:S(2)}, u32[]{:S(2)}) %collective-permute-start.4) | collective-permute-done | bytes 84000 | tf_op jit(solution)/shard_map/ppermute | solution.py:524
  88.9 2.2 %collective-permute-done.5 = f16[1,328,128]{2,1,0:T(8,128)(2,1)S(1)} collective-permute-done((f16[1,328,128]{2,1,0:T(8,128)(2,1)S(1)}, f16[1,328,128]{2,1,0:T(8,128)(2,1)S(1)}, u32[]{:S(2)}, u32[]{:S(2)}) %collective-permute-start.5) | collective-permute-done | bytes 84000 | tf_op jit(solution)/shard_map/ppermute | solution.py:524
  91.1 3.6 %collective-permute-done.6 = f16[1,328,128]{2,1,0:T(8,128)(2,1)S(1)} collective-permute-done((f16[1,328,128]{2,1,0:T(8,128)(2,1)S(1)}, f16[1,328,128]{2,1,0:T(8,128)(2,1)S(1)}, u32[]{:S(2)}, u32[]{:S(2)}) %collective-permute-start.6) | collective-permute-done | bytes 84000 | tf_op jit(solution)/shard_map/ppermute | solution.py:524
  98.9 1.9 %shard_map.171 = (bf16[16,160,128]{2,1,0:T(8,128)(2,1)S(1)}, f32[128,2560]{1,0:T(8,128)S(1)}) custom-call(f32[8,328,128]{2,1,0:T(8,128)S(1)} %convert_element_type.59.msg_ref.msgf_ref, f32[128,2560]{1,0:T(8,128)S(1)} %copy-done.9, bf16[128,2560]{1,0:T(8,128)(2,1)S(1)} %copy-done.1, f32[128,256]{1,0:T(8,128)S(1)} %copy-done.26, ...), custom_call_target="tpu_custom_call" | custom-call | flops 1677721600 | bytes 6793216 | tf_op jit(solution)/shard_map/pallas_call | solution.py:26
  102.7 4.3 %all-to-all-start.3 = ((bf16[16,160,128]{2,1,0:T(8,128)(2,1)}), bf16[16,160,128]{2,1,0:T(8,128)(2,1)}, u32[]{:S(2)}, u32[]{:S(2)}) async-start(bf16[16,160,128]{2,1,0:T(8,128)(2,1)} %copy-done.17), calls=%async_computation.3 | async-start | bytes 1310720 | tf_op jit(solution)/shard_map/all_to_all | solution.py:667
  112.3 2.4 %shard_map.174 = (bf16[128,2560]{1,0:T(8,128)(2,1)}, f32[128,128]{1,0:T(8,128)S(1)}, f32[128,256]{1,0:T(8,128)S(1)}) custom-call(f32[8,328,128]{2,1,0:T(8,128)S(1)} %convert_element_type.59.msg_ref.msgf_ref, f32[128,2560]{1,0:T(8,128)S(1)} %copy-done.10, f32[128,2560]{1,0:T(8,128)S(1)} %copy-done.5, f32[128,128]{1,0:T(8,128)S(1)} %get-tuple-element.53.ld_ref, ...), custom_call_target="tpu_custom_call" | custom-call | flops 1677721600 | bytes 8300544 | tf_op jit(solution)/shard_map/pallas_call | solution.py:26
  115.9 3.1 %all-to-all-done.3.held_ref = bf16[16,160,128]{2,1,0:T(8,128)(2,1)} async-done(((bf16[16,160,128]{2,1,0:T(8,128)(2,1)}), bf16[16,160,128]{2,1,0:T(8,128)(2,1)}, u32[]{:S(2)}, u32[]{:S(2)}) %all-to-all-start.3) | async-done | bytes 655392 | tf_op jit(solution)/shard_map/all_to_all | solution.py:667
  119.0 6.8 %shard_map.175 = bf16[32,112,128]{2,1,0:T(8,128)(2,1)S(1)} custom-call(bf16[16,160,128]{2,1,0:T(8,128)(2,1)} %all-to-all-done.3.held_ref, bf16[2048,2560]{1,0:T(8,128)(2,1)} %all-gather.2.cloned.1.call-done.refs_0_.refs_1_.refs_2_.refs_3_, bf16[2048,2560]{1,0:T(8,128)(2,1)} %all-gather.2.cloned.1.call-done.refs_0_.refs_1_.refs_2_.refs_3_, ...), custom_call_target="tpu_custom_call" | custom-call | flops 1677721600 | bytes 10485760 | tf_op jit(solution)/shard_map/pallas_call | solution.py:686
  126.7 3.6 %all-to-all-start.4 = ((bf16[32,112,128]{2,1,0:T(8,128)(2,1)}), bf16[32,112,128]{2,1,0:T(8,128)(2,1)}, u32[]{:S(2)}, u32[]{:S(2)}) async-start(bf16[32,112,128]{2,1,0:T(8,128)(2,1)} %copy-done), calls=%async_computation.4 | async-start | bytes 1835008 | tf_op jit(solution)/shard_map/all_to_all | solution.py:705
  134.2 2.4 %collective-permute-start.12 = (f16[1,328,128]{2,1,0:T(8,128)(2,1)S(1)}, f16[1,328,128]{2,1,0:T(8,128)(2,1)S(1)}, u32[]{:S(2)}, u32[]{:S(2)}) collective-permute-start(f16[1,328,128]{2,1,0:T(8,128)(2,1)S(1)} %get-tuple-element.93), channel_id=1, source_target_pairs={{0,6},{1,7},{2,4},{3,5},{4,2},{5,3},{6,0},{7,1},{8,14},{9,15},{10,... | collective-permute-start | bytes 251912 | tf_op jit(solution)/shard_map/ppermute | solution.py:497
  136.6 5.4 %collective-permute-done.8 = f16[1,328,128]{2,1,0:T(8,128)(2,1)S(1)} collective-permute-done((f16[1,328,128]{2,1,0:T(8,128)(2,1)S(1)}, f16[1,328,128]{2,1,0:T(8,128)(2,1)S(1)}, u32[]{:S(2)}, u32[]{:S(2)}) %collective-permute-start.8) | collective-permute-done | bytes 84000 | tf_op jit(solution)/shard_map/ppermute | solution.py:497
  143.3 4.7 %collective-permute-done.12 = f16[1,328,128]{2,1,0:T(8,128)(2,1)S(1)} collective-permute-done((f16[1,328,128]{2,1,0:T(8,128)(2,1)S(1)}, f16[1,328,128]{2,1,0:T(8,128)(2,1)S(1)}, u32[]{:S(2)}, u32[]{:S(2)}) %collective-permute-start.12) | collective-permute-done | bytes 84000 | tf_op jit(solution)/shard_map/ppermute | solution.py:497
  149.2 4.2 %shard_map.176 = (bf16[128,2560]{1,0:T(8,128)(2,1)}, f32[128,256]{1,0:T(8,128)S(1)}, f32[128,40]{1,0:T(8,128)S(1)}) custom-call(s32[1]{0:T(128)} %bitcast.me_ref, f32[8,328,128]{2,1,0:T(8,128)S(1)} %convert_element_type.66.msg_ref, f32[8,328,128]{2,1,0:T(8,128)S(1)} %convert_element_type.59.msg_ref.msgf_ref, f32[128,2560]{1,0:T(8,128)S(1)} %copy-done.11, ...), custom_call_target="tpu_custom_call" | custom-call | flops 3355443200 | bytes 9275396 | tf_op jit(solution)/shard_map/pallas_call | solution.py:26
  154.7 2.3 %shard_map.177 = f32[80,2560]{1,0:T(8,128)} custom-call(bf16[32,112,128]{2,1,0:T(8,128)(2,1)} %all-to-all-done.4.parts_ref), custom_call_target="tpu_custom_call" | custom-call | flops 917504 | bytes 1736704 | tf_op jit(solution)/shard_map/pallas_call | solution.py:26
  (171 shorter events, 53.0 us)
Async XLA Ops:
  7.2 95.5 %all-gather.2.cloned.1.call-start = ((), (), s32[]{:S(2)}) async-start(), calls=%async_computation.5 | async-start | bytes 11141120 | tf_op jit(solution)/shard_map/all_gather | solution.py:575
  9.2 3.3 %collective-permute-start = (bf16[16,2816]{1,0:T(8,128)(2,1)S(1)}, bf16[16,2816]{1,0:T(8,128)(2,1)S(1)}, u32[]{:S(2)}, u32[]{:S(2)}) collective-permute-start(bf16[16,2816]{1,0:T(8,128)(2,1)S(1)} %slice.36), channel_id=1, source_target_pairs={{0,1},{1,2},{2,3},{3,4},{4,5},{5,6},{6,7},{7,8},{8,9},{9,10},{10,1... | collective-permute-start | bytes 270344 | tf_op jit(solution)/shard_map/ppermute | solution.py:545
  14.8 17.5 %copy-start.24 = (f32[128,256]{1,0:T(8,128)}, f32[128,256]{1,0:T(8,128)S(1)}, u32[]{:S(2)}) copy-start(f32[128,256]{1,0:T(8,128)S(1)} %get-tuple-element.52.abc_ref) | copy-start | bytes 393220
  15.8 26.7 %all-to-all-start = ((f16[8,328,128]{2,1,0:T(8,128)(2,1)}), f16[8,328,128]{2,1,0:T(8,128)(2,1)}, u32[]{:S(2)}, u32[]{:S(2)}) async-start(f16[8,328,128]{2,1,0:T(8,128)(2,1)} %convert_element_type.51), calls=%async_computation | async-start | bytes 1343488 | tf_op jit(solution)/shard_map/all_to_all | solution.py:489
  45.9 16.1 %copy-start.4 = (f32[128,2560]{1,0:T(8,128)S(1)}, f32[128,2560]{1,0:T(8,128)}, u32[]{:S(2)}) copy-start(f32[128,2560]{1,0:T(8,128)} %get-tuple-element.51.gy_ref) | copy-start | bytes 3932164
  45.9 29.3 %all-to-all-start.1 = ((f16[8,328,128]{2,1,0:T(8,128)(2,1)}), f16[8,328,128]{2,1,0:T(8,128)(2,1)}, u32[]{:S(2)}, u32[]{:S(2)}) async-start(f16[8,328,128]{2,1,0:T(8,128)(2,1)} %convert_element_type.57), calls=%async_computation.1 | async-start | bytes 1343488 | tf_op jit(solution)/shard_map/all_to_all | solution.py:489
  50.3 23.4 %collective-permute-start.1 = (f16[1,328,128]{2,1,0:T(8,128)(2,1)}, f16[1,328,128]{2,1,0:T(8,128)(2,1)S(1)}, u32[]{:S(2)}, u32[]{:S(2)}) collective-permute-start(f16[1,328,128]{2,1,0:T(8,128)(2,1)} %convert_element_type.53), channel_id=1, source_target_pairs={{0,8},{1,9},{2,10},{3,11},{4,12},{5,13},{6,14},{7,15},{8,16},{9,17... | collective-permute-start | bytes 251912 | tf_op jit(solution)/shard_map/ppermute | solution.py:524
  56.1 17.6 %collective-permute-start.2 = (f16[1,328,128]{2,1,0:T(8,128)(2,1)}, f16[1,328,128]{2,1,0:T(8,128)(2,1)S(1)}, u32[]{:S(2)}, u32[]{:S(2)}) collective-permute-start(f16[1,328,128]{2,1,0:T(8,128)(2,1)} %convert_element_type.53), channel_id=1, source_target_pairs={{0,16},{1,17},{2,18},{3,19},{4,20},{5,21},{6,22},{7,23},{8,24},{9,... | collective-permute-start | bytes 251912 | tf_op jit(solution)/shard_map/ppermute | solution.py:524
  60.6 13.2 %collective-permute-start.3 = (f16[1,328,128]{2,1,0:T(8,128)(2,1)}, f16[1,328,128]{2,1,0:T(8,128)(2,1)S(1)}, u32[]{:S(2)}, u32[]{:S(2)}) collective-permute-start(f16[1,328,128]{2,1,0:T(8,128)(2,1)} %convert_element_type.53), channel_id=1, source_target_pairs={{0,24},{1,25},{2,26},{3,27},{4,28},{5,29},{6,30},{7,31}} | collective-permute-start | bytes 251912 | tf_op jit(solution)/shard_map/ppermute | solution.py:524
  76.1 19.9 %all-to-all-start.2 = ((f16[8,328,128]{2,1,0:T(8,128)(2,1)}), f16[8,328,128]{2,1,0:T(8,128)(2,1)}, u32[]{:S(2)}, u32[]{:S(2)}) async-start(f16[8,328,128]{2,1,0:T(8,128)(2,1)} %convert_element_type.58), calls=%async_computation.2 | async-start | bytes 1343488 | tf_op jit(solution)/shard_map/all_to_all | solution.py:489
  82.2 6.7 %collective-permute-start.4 = (f16[1,328,128]{2,1,0:T(8,128)(2,1)S(1)}, f16[1,328,128]{2,1,0:T(8,128)(2,1)S(1)}, u32[]{:S(2)}, u32[]{:S(2)}) collective-permute-start(f16[1,328,128]{2,1,0:T(8,128)(2,1)S(1)} %convert_element_type.61), channel_id=1, source_target_pairs={{8,0},{9,1},{10,2},{11,3},{12,4},{13,5},{14,6},{15,7},{16,8},{17,9... | collective-permute-start | bytes 251912 | tf_op jit(solution)/shard_map/ppermute | solution.py:524
  83.5 7.6 %collective-permute-start.5 = (f16[1,328,128]{2,1,0:T(8,128)(2,1)S(1)}, f16[1,328,128]{2,1,0:T(8,128)(2,1)S(1)}, u32[]{:S(2)}, u32[]{:S(2)}) collective-permute-start(f16[1,328,128]{2,1,0:T(8,128)(2,1)S(1)} %convert_element_type.61), channel_id=1, source_target_pairs={{16,0},{17,1},{18,2},{19,3},{20,4},{21,5},{22,6},{23,7},{24,8},{25... | collective-permute-start | bytes 251912 | tf_op jit(solution)/shard_map/ppermute | solution.py:524
  84.8 9.9 %collective-permute-start.6 = (f16[1,328,128]{2,1,0:T(8,128)(2,1)S(1)}, f16[1,328,128]{2,1,0:T(8,128)(2,1)S(1)}, u32[]{:S(2)}, u32[]{:S(2)}) collective-permute-start(f16[1,328,128]{2,1,0:T(8,128)(2,1)S(1)} %convert_element_type.61), channel_id=1, source_target_pairs={{24,0},{25,1},{26,2},{27,3},{28,4},{29,5},{30,6},{31,7}} | collective-permute-start | bytes 251912 | tf_op jit(solution)/shard_map/ppermute | solution.py:524
  102.7 16.3 %all-to-all-start.3 = ((bf16[16,160,128]{2,1,0:T(8,128)(2,1)}), bf16[16,160,128]{2,1,0:T(8,128)(2,1)}, u32[]{:S(2)}, u32[]{:S(2)}) async-start(bf16[16,160,128]{2,1,0:T(8,128)(2,1)} %copy-done.17), calls=%async_computation.3 | async-start | bytes 1310720 | tf_op jit(solution)/shard_map/all_to_all | solution.py:667
  126.7 27.9 %all-to-all-start.4 = ((bf16[32,112,128]{2,1,0:T(8,128)(2,1)}), bf16[32,112,128]{2,1,0:T(8,128)(2,1)}, u32[]{:S(2)}, u32[]{:S(2)}) async-start(bf16[32,112,128]{2,1,0:T(8,128)(2,1)} %copy-done), calls=%async_computation.4 | async-start | bytes 1835008 | tf_op jit(solution)/shard_map/all_to_all | solution.py:705
  130.3 18.7 %copy-start.33 = (f32[128,2560]{1,0:T(8,128)S(1)}, f32[128,2560]{1,0:T(8,128)}, u32[]{:S(2)}) copy-start(f32[128,2560]{1,0:T(8,128)} %copy-done.32) | copy-start | bytes 3932164
  130.4 18.7 %copy-start.31 = (f32[128,2560]{1,0:T(8,128)S(1)}, f32[128,2560]{1,0:T(8,128)}, u32[]{:S(2)}) copy-start(f32[128,2560]{1,0:T(8,128)} %copy-done.30) | copy-start | bytes 3932164
  130.6 3.6 %collective-permute-start.7 = (f16[1,328,128]{2,1,0:T(8,128)(2,1)S(1)}, f16[1,328,128]{2,1,0:T(8,128)(2,1)S(1)}, u32[]{:S(2)}, u32[]{:S(2)}) collective-permute-start(f16[1,328,128]{2,1,0:T(8,128)(2,1)S(1)} %get-tuple-element.98), channel_id=1, source_target_pairs={{0,1},{1,0},{2,3},{3,2},{4,5},{5,4},{6,7},{7,6},{8,9},{9,8},{10,11... | collective-permute-start | bytes 251912 | tf_op jit(solution)/shard_map/ppermute | solution.py:497
  130.6 11.4 %collective-permute-start.8 = (f16[1,328,128]{2,1,0:T(8,128)(2,1)S(1)}, f16[1,328,128]{2,1,0:T(8,128)(2,1)S(1)}, u32[]{:S(2)}, u32[]{:S(2)}) collective-permute-start(f16[1,328,128]{2,1,0:T(8,128)(2,1)S(1)} %get-tuple-element.97), channel_id=1, source_target_pairs={{0,2},{1,3},{2,0},{3,1},{4,6},{5,7},{6,4},{7,5},{8,10},{9,11},{10,... | collective-permute-start | bytes 251912 | tf_op jit(solution)/shard_map/ppermute | solution.py:497
  132.2 11.0 %collective-permute-start.9 = (f16[1,328,128]{2,1,0:T(8,128)(2,1)S(1)}, f16[1,328,128]{2,1,0:T(8,128)(2,1)S(1)}, u32[]{:S(2)}, u32[]{:S(2)}) collective-permute-start(f16[1,328,128]{2,1,0:T(8,128)(2,1)S(1)} %get-tuple-element.96), channel_id=1, source_target_pairs={{0,3},{1,2},{2,1},{3,0},{4,7},{5,6},{6,5},{7,4},{8,11},{9,10},{10,... | collective-permute-start | bytes 251912 | tf_op jit(solution)/shard_map/ppermute | solution.py:497
  132.5 10.7 %collective-permute-start.10 = (f16[1,328,128]{2,1,0:T(8,128)(2,1)S(1)}, f16[1,328,128]{2,1,0:T(8,128)(2,1)S(1)}, u32[]{:S(2)}, u32[]{:S(2)}) collective-permute-start(f16[1,328,128]{2,1,0:T(8,128)(2,1)S(1)} %get-tuple-element.95), channel_id=1, source_target_pairs={{0,4},{1,5},{2,6},{3,7},{4,0},{5,1},{6,2},{7,3},{8,12},{9,13},{10,... | collective-permute-start | bytes 251912 | tf_op jit(solution)/shard_map/ppermute | solution.py:497
  133.9 9.4 %collective-permute-start.11 = (f16[1,328,128]{2,1,0:T(8,128)(2,1)S(1)}, f16[1,328,128]{2,1,0:T(8,128)(2,1)S(1)}, u32[]{:S(2)}, u32[]{:S(2)}) collective-permute-start(f16[1,328,128]{2,1,0:T(8,128)(2,1)S(1)} %get-tuple-element.94), channel_id=1, source_target_pairs={{0,5},{1,4},{2,7},{3,6},{4,1},{5,0},{6,3},{7,2},{8,13},{9,12},{10,... | collective-permute-start | bytes 251912 | tf_op jit(solution)/shard_map/ppermute | solution.py:497
  134.2 13.8 %collective-permute-start.12 = (f16[1,328,128]{2,1,0:T(8,128)(2,1)S(1)}, f16[1,328,128]{2,1,0:T(8,128)(2,1)S(1)}, u32[]{:S(2)}, u32[]{:S(2)}) collective-permute-start(f16[1,328,128]{2,1,0:T(8,128)(2,1)S(1)} %get-tuple-element.93), channel_id=1, source_target_pairs={{0,6},{1,7},{2,4},{3,5},{4,2},{5,3},{6,0},{7,1},{8,14},{9,15},{10,... | collective-permute-start | bytes 251912 | tf_op jit(solution)/shard_map/ppermute | solution.py:497
  142.0 6.9 %collective-permute-start.13 = (f16[1,328,128]{2,1,0:T(8,128)(2,1)S(1)}, f16[1,328,128]{2,1,0:T(8,128)(2,1)S(1)}, u32[]{:S(2)}, u32[]{:S(2)}) collective-permute-start(f16[1,328,128]{2,1,0:T(8,128)(2,1)S(1)} %get-tuple-element.92), channel_id=1, source_target_pairs={{0,7},{1,6},{2,5},{3,4},{4,3},{5,2},{6,1},{7,0},{8,15},{9,14},{10,... | collective-permute-start | bytes 251912 | tf_op jit(solution)/shard_map/ppermute | solution.py:497
  (48 other events, 144.6 us)
Sparse Core Ops, SparseCore 0:
  9.7 77.5 all-gather.1

commit v9 on v8

--- a/solution.py
+++ b/solution.py
@@ -636,7 +636,7 @@
         + [shape(square), shape((8, LANES))],
         [raw_then, rim, taps, dt_raw, per_raw],
         10 * unit,
-        20,
+        60,
         [padded],
     )
     total, ld_t_then, message = lax.optimization_barrier((group_total(held_state, rows, False), ld_t, message))
@@ -646,7 +646,7 @@
         [shape(whole), shape(whole), shape(act_bc.shape)],
         [act_x, grad_y, act_bc, step, ld, step_t, ld_t_then],
         40 * unit,
-        16,
+        60,
         [pltpu.VMEM(square, F32)],
     )
     folded, held_carry, y_within = lax.optimization_barrier(

time: 166 us -> 162 us (0.976)
  local copies, waits for them, and re-layouts: 26.9 us -> 15.6 us
  Pallas kernels: 40.9 us -> 45.7 us
  waiting for transfers between devices: 24.9 us -> 29 us
    unnamed x113 -> x99, local copies, waits for them, and re-layouts: 26.5 us -> 15.2 us
    pallas_call x12, Pallas kernels: 25.4 us -> 30.1 us  [call(): pl.pallas_call(kernel, out_shape=tuple(out_shapes), scratch_shapes=list(s...]
    all_to_all x3, waiting for transfers between devices: 0.04 us -> 2.98 us  [exchange(): lax.all_to_all(half, 'ctx', 0, 0, axis_index_groups=groups, tiled=True)]
  transfers between devices with their start and end apart: 20 -> 20, of which waited for: 9 -> 9; matrix products, arithmetic and copies ran while one was open for 6% -> 6% of each run, Pallas kernels for 19% -> 23%
where the time goes in v9:
time: 162 us; the launch traced here: 161 us
  starting transfers between devices  48 us (30%)
  Pallas kernels  45.7 us (28%)
  waiting for transfers between devices  29 us (18%)
  local copies, waits for them, and re-layouts  15.6 us (10%)
  between operations  14.9 us (9%)
  other arithmetic  7.46 us (5%)
    pallas_call x12, Pallas kernels, call(): pl.pallas_call(kernel, out_shape=tuple(out_shapes), scratch_shapes=list(s...  30.1 us
    all_to_all x3, starting transfers between devices, exchange(): lax.all_to_all(half, 'ctx', 0, 0, axis_index_groups=groups, tiled=True)  16.1 us
    ppermute x6, starting transfers between devices, enter(): others.append(lax.ppermute(total, 'ctx', pairs).astype(F32))  15.5 us
    unnamed x99, local copies, waits for them, and re-layouts  15.2 us
    ppermute x7, waiting for transfers between devices, swapped(): lax.ppermute(half[m:m + 1], 'ctx', [(at, at ^ m) for at in range(count)])  12.1 us
    ppermute x6, waiting for transfers between devices, enter(): others.append(lax.ppermute(total, 'ctx', pairs).astype(F32))  9.48 us
    pallas_call x1, Pallas kernels, per_device(): pl.pallas_call(gate_kernel, grid=(channels // part,), in_specs=[pl.BlockS...  8.75 us
    pallas_call x1, Pallas kernels, per_device(): pl.pallas_call(functools.partial(product_kernel, out_rows), grid=(width /...  6.78 us
  transfers between devices with their start and end apart: 20, of which 9 were waited for; matrix products, arithmetic and copies ran while one was open for 6% of the time, Pallas kernels for 23%

profile of v9, /device:TPU:0, one launch (start us, length us, event | category | flops | bytes accessed | tf_op | source)
XLA Modules:
  0.0 160.6 jit_solution(2914494355402360450)
XLA Ops:
  9.2 2.4 %collective-permute-start = (bf16[16,2816]{1,0:T(8,128)(2,1)S(1)}, bf16[16,2816]{1,0:T(8,128)(2,1)S(1)}, u32[]{:S(2)}, u32[]{:S(2)}) collective-permute-start(bf16[16,2816]{1,0:T(8,128)(2,1)S(1)} %slice.36), channel_id=1, source_target_pairs={{0,1},{1,2},{2,3},{3,4},{4,5},{5,6},{6,7},{7,8},{8,9},{9,10},{10,1... | collective-permute-start | bytes 270344 | tf_op jit(solution)/shard_map/ppermute | solution.py:545
  12.5 2.3 %shard_map.164 = (f32[128,256]{1,0:T(8,128)S(1)}, f32[128,128]{1,0:T(8,128)S(1)}, f32[8,328,128]{2,1,0:T(8,128)S(1)}) custom-call(bf16[128,2816]{1,0:T(8,128)(2,1)S(1)} %constant_dynamic-update-slice_fusion.raw_ref, bf16[16,2816]{1,0:T(8,128)(2,1)S(1)} %collective-permute-done.rim_ref, f32[5,2816]{1,0:T(8,128)S(1)} %pad_maximum_fusion.taps_ref, ...), custom_call_target="tpu_custom_call" | custom-call | flops 1677721600 | bytes 2428224 | tf_op jit(solution)/shard_map/pallas_call | solution.py:26
  16.4 7.7 %all-to-all-start = ((f16[8,328,128]{2,1,0:T(8,128)(2,1)}), f16[8,328,128]{2,1,0:T(8,128)(2,1)}, u32[]{:S(2)}, u32[]{:S(2)}) async-start(f16[8,328,128]{2,1,0:T(8,128)(2,1)} %convert_element_type.51), calls=%async_computation | async-start | bytes 1343488 | tf_op jit(solution)/shard_map/all_to_all | solution.py:489
  24.2 8.8 %shard_map.167 = (f32[128,2560]{1,0:T(8,128)}, f32[128,2560]{1,0:T(8,128)}) custom-call(bf16[128,2560]{1,0:T(8,128)(2,1)S(1)} %copy-done.2, bf16[2560,2560]{1,0:T(8,128)(2,1)} %refs_3_.1, bf16[2560,2560]{1,0:T(8,128)(2,1)} %refs_3_.1, bf16[2560,2560]{1,0:T(8,128)(2,1)} %refs_3_.1, bf16[2560,2560]{1,0:T(8,128)(2,1)} %refs_3_.1, bf16[128,2560]{1,0:T(8,128)(2,1)S(1)} %copy-done.1), custom_call_target="tpu_custom_call" | custom-call | flops 1677721600 | bytes 13107200 | tf_op jit(solution)/shard_map/pallas_call | solution.py:606
  35.9 4.3 %shard_map.166 = (f32[128,2560]{1,0:T(8,128)}, f32[128,2560]{1,0:T(8,128)}, f32[128,256]{1,0:T(8,128)}, f32[128,128]{1,0:T(8,128)}, f32[128,128]{1,0:T(8,128)}, ...) custom-call(bf16[128,2816]{1,0:T(8,128)(2,1)} %copy-done.12, bf16[16,2816]{1,0:T(8,128)(2,1)} %copy-done.22, ...), custom_call_target="tpu_custom_call" | custom-call | flops 838860800 | bytes 3906880 | tf_op jit(solution)/shard_map/pallas_call | solution.py:26
  40.1 3.0 %all-to-all-done = f16[8,328,128]{2,1,0:T(8,128)(2,1)} async-done(((f16[8,328,128]{2,1,0:T(8,128)(2,1)}), f16[8,328,128]{2,1,0:T(8,128)(2,1)}, u32[]{:S(2)}, u32[]{:S(2)}) %all-to-all-start) | async-done | bytes 671776 | tf_op jit(solution)/shard_map/all_to_all | solution.py:489
  45.9 4.2 %all-to-all-start.1 = ((f16[8,328,128]{2,1,0:T(8,128)(2,1)}), f16[8,328,128]{2,1,0:T(8,128)(2,1)}, u32[]{:S(2)}, u32[]{:S(2)}) async-start(f16[8,328,128]{2,1,0:T(8,128)(2,1)} %convert_element_type.57), calls=%async_computation.1 | async-start | bytes 1343488 | tf_op jit(solution)/shard_map/all_to_all | solution.py:489
  50.1 5.7 %collective-permute-start.1 = (f16[1,328,128]{2,1,0:T(8,128)(2,1)S(1)}, f16[1,328,128]{2,1,0:T(8,128)(2,1)S(1)}, u32[]{:S(2)}, u32[]{:S(2)}) collective-permute-start(f16[1,328,128]{2,1,0:T(8,128)(2,1)S(1)} %convert_element_type.53), channel_id=1, source_target_pairs={{0,8},{1,9},{2,10},{3,11},{4,12},{5,13},{6,14},{7,15},{8,16},{9,17... | collective-permute-start | bytes 251912 | tf_op jit(solution)/shard_map/ppermute | solution.py:524
  55.8 4.5 %collective-permute-start.2 = (f16[1,328,128]{2,1,0:T(8,128)(2,1)S(1)}, f16[1,328,128]{2,1,0:T(8,128)(2,1)S(1)}, u32[]{:S(2)}, u32[]{:S(2)}) collective-permute-start(f16[1,328,128]{2,1,0:T(8,128)(2,1)S(1)} %convert_element_type.53), channel_id=1, source_target_pairs={{0,16},{1,17},{2,18},{3,19},{4,20},{5,21},{6,22},{7,23},{8,24},{9,... | collective-permute-start | bytes 251912 | tf_op jit(solution)/shard_map/ppermute | solution.py:524
  61.8 7.4 %shard_map.170 = (f32[128,2560]{1,0:T(8,128)}, f32[128,2560]{1,0:T(8,128)}, f32[128,256]{1,0:T(8,128)}) custom-call(f32[128,2560]{1,0:T(8,128)} %get-tuple-element.56.act_ref, f32[128,2560]{1,0:T(8,128)} %get-tuple-element.51.gy_ref, f32[128,256]{1,0:T(8,128)} %copy-done.25, f32[128,128]{1,0:T(8,128)} %get-tuple-element.57.step_ref, f32[128,128]{1,0:T(8,128)} %copy-done.16, ...), custom_call_target="tpu_custom_call" | custom-call | flops 3355443200 | bytes 5767168 | tf_op jit(solution)/shard_map/pallas_call | solution.py:26
  71.6 4.2 %all-to-all-start.2 = ((f16[8,328,128]{2,1,0:T(8,128)(2,1)}), f16[8,328,128]{2,1,0:T(8,128)(2,1)}, u32[]{:S(2)}, u32[]{:S(2)}) async-start(f16[8,328,128]{2,1,0:T(8,128)(2,1)} %convert_element_type.58), calls=%async_computation.2 | async-start | bytes 1343488 | tf_op jit(solution)/shard_map/all_to_all | solution.py:489
  81.8 2.9 %collective-permute-done.4 = f16[1,328,128]{2,1,0:T(8,128)(2,1)S(1)} collective-permute-done((f16[1,328,128]{2,1,0:T(8,128)(2,1)S(1)}, f16[1,328,128]{2,1,0:T(8,128)(2,1)S(1)}, u32[]{:S(2)}, u32[]{:S(2)}) %collective-permute-start.4) | collective-permute-done | bytes 84000 | tf_op jit(solution)/shard_map/ppermute | solution.py:524
  84.8 6.6 %collective-permute-done.5 = f16[1,328,128]{2,1,0:T(8,128)(2,1)S(1)} collective-permute-done((f16[1,328,128]{2,1,0:T(8,128)(2,1)S(1)}, f16[1,328,128]{2,1,0:T(8,128)(2,1)S(1)}, u32[]{:S(2)}, u32[]{:S(2)}) %collective-permute-start.5) | collective-permute-done | bytes 84000 | tf_op jit(solution)/shard_map/ppermute | solution.py:524
  95.7 1.8 %shard_map.171 = (bf16[16,160,128]{2,1,0:T(8,128)(2,1)S(1)}, f32[128,2560]{1,0:T(8,128)S(1)}) custom-call(f32[8,328,128]{2,1,0:T(8,128)S(1)} %convert_element_type.59.msg_ref.msgf_ref, f32[128,2560]{1,0:T(8,128)S(1)} %copy-done.6, bf16[128,2560]{1,0:T(8,128)(2,1)S(1)} %copy-done.1, f32[128,256]{1,0:T(8,128)S(1)} %copy-done.27, f32[128,128]{1,0:T(8,128)S(1)} %copy-done.17, ...), custom_call_target="tpu_custom_call" | custom-call | flops 1677721600 | bytes 6793216 | tf_op jit(solution)/shard_map/pallas_call | solution.py:26
  99.4 4.4 %all-to-all-start.3 = ((bf16[16,160,128]{2,1,0:T(8,128)(2,1)}), bf16[16,160,128]{2,1,0:T(8,128)(2,1)}, u32[]{:S(2)}, u32[]{:S(2)}) async-start(bf16[16,160,128]{2,1,0:T(8,128)(2,1)} %copy-done.13), calls=%async_computation.3 | async-start | bytes 1310720 | tf_op jit(solution)/shard_map/all_to_all | solution.py:667
  109.1 2.3 %shard_map.174 = (bf16[128,2560]{1,0:T(8,128)(2,1)}, f32[128,128]{1,0:T(8,128)S(1)}, f32[128,256]{1,0:T(8,128)S(1)}) custom-call(f32[8,328,128]{2,1,0:T(8,128)S(1)} %convert_element_type.59.msg_ref.msgf_ref, f32[128,2560]{1,0:T(8,128)S(1)} %copy-done.7, f32[128,2560]{1,0:T(8,128)S(1)} %copy-done.4, f32[128,128]{1,0:T(8,128)S(1)} %copy-done.17, ...), custom_call_target="tpu_custom_call" | custom-call | flops 1677721600 | bytes 8300544 | tf_op jit(solution)/shard_map/pallas_call | solution.py:26
  112.7 3.1 %all-to-all-done.3.held_ref = bf16[16,160,128]{2,1,0:T(8,128)(2,1)} async-done(((bf16[16,160,128]{2,1,0:T(8,128)(2,1)}), bf16[16,160,128]{2,1,0:T(8,128)(2,1)}, u32[]{:S(2)}, u32[]{:S(2)}) %all-to-all-start.3) | async-done | bytes 655392 | tf_op jit(solution)/shard_map/all_to_all | solution.py:667
  115.8 6.8 %shard_map.175 = bf16[32,112,128]{2,1,0:T(8,128)(2,1)S(1)} custom-call(bf16[16,160,128]{2,1,0:T(8,128)(2,1)} %all-to-all-done.3.held_ref, bf16[2048,2560]{1,0:T(8,128)(2,1)} %all-gather.2.cloned.1.call-done.refs_0_.refs_1_.refs_2_.refs_3_, bf16[2048,2560]{1,0:T(8,128)(2,1)} %all-gather.2.cloned.1.call-done.refs_0_.refs_1_.refs_2_.refs_3_, ...), custom_call_target="tpu_custom_call" | custom-call | flops 1677721600 | bytes 10485760 | tf_op jit(solution)/shard_map/pallas_call | solution.py:686
  123.5 3.6 %all-to-all-start.4 = ((bf16[32,112,128]{2,1,0:T(8,128)(2,1)}), bf16[32,112,128]{2,1,0:T(8,128)(2,1)}, u32[]{:S(2)}, u32[]{:S(2)}) async-start(bf16[32,112,128]{2,1,0:T(8,128)(2,1)} %copy-done), calls=%async_computation.4 | async-start | bytes 1835008 | tf_op jit(solution)/shard_map/all_to_all | solution.py:705
  131.0 2.4 %collective-permute-start.12 = (f16[1,328,128]{2,1,0:T(8,128)(2,1)S(1)}, f16[1,328,128]{2,1,0:T(8,128)(2,1)S(1)}, u32[]{:S(2)}, u32[]{:S(2)}) collective-permute-start(f16[1,328,128]{2,1,0:T(8,128)(2,1)S(1)} %get-tuple-element.93), channel_id=1, source_target_pairs={{0,6},{1,7},{2,4},{3,5},{4,2},{5,3},{6,0},{7,1},{8,14},{9,15},{10,... | collective-permute-start | bytes 251912 | tf_op jit(solution)/shard_map/ppermute | solution.py:497
  133.4 5.4 %collective-permute-done.8 = f16[1,328,128]{2,1,0:T(8,128)(2,1)S(1)} collective-permute-done((f16[1,328,128]{2,1,0:T(8,128)(2,1)S(1)}, f16[1,328,128]{2,1,0:T(8,128)(2,1)S(1)}, u32[]{:S(2)}, u32[]{:S(2)}) %collective-permute-start.8) | collective-permute-done | bytes 84000 | tf_op jit(solution)/shard_map/ppermute | solution.py:497
  140.2 4.7 %collective-permute-done.12 = f16[1,328,128]{2,1,0:T(8,128)(2,1)S(1)} collective-permute-done((f16[1,328,128]{2,1,0:T(8,128)(2,1)S(1)}, f16[1,328,128]{2,1,0:T(8,128)(2,1)S(1)}, u32[]{:S(2)}, u32[]{:S(2)}) %collective-permute-start.12) | collective-permute-done | bytes 84000 | tf_op jit(solution)/shard_map/ppermute | solution.py:497
  146.0 4.1 %shard_map.176 = (bf16[128,2560]{1,0:T(8,128)(2,1)}, f32[128,256]{1,0:T(8,128)S(1)}, f32[128,40]{1,0:T(8,128)S(1)}) custom-call(s32[1]{0:T(128)} %bitcast.me_ref, f32[8,328,128]{2,1,0:T(8,128)S(1)} %convert_element_type.66.msg_ref, f32[8,328,128]{2,1,0:T(8,128)S(1)} %convert_element_type.59.msg_ref.msgf_ref, f32[128,2560]{1,0:T(8,128)S(1)} %copy-done.8, ...), custom_call_target="tpu_custom_call" | custom-call | flops 3355443200 | bytes 9275396 | tf_op jit(solution)/shard_map/pallas_call | solution.py:26
  151.4 2.3 %shard_map.177 = f32[80,2560]{1,0:T(8,128)} custom-call(bf16[32,112,128]{2,1,0:T(8,128)(2,1)} %all-to-all-done.4.parts_ref), custom_call_target="tpu_custom_call" | custom-call | flops 917504 | bytes 1736704 | tf_op jit(solution)/shard_map/pallas_call | solution.py:26
  (157 shorter events, 41.0 us)
Async XLA Ops:
  7.2 92.2 %all-gather.2.cloned.1.call-start = ((), (), s32[]{:S(2)}) async-start(), calls=%async_computation.5 | async-start | bytes 11141120 | tf_op jit(solution)/shard_map/all_gather | solution.py:575
  9.2 3.3 %collective-permute-start = (bf16[16,2816]{1,0:T(8,128)(2,1)S(1)}, bf16[16,2816]{1,0:T(8,128)(2,1)S(1)}, u32[]{:S(2)}, u32[]{:S(2)}) collective-permute-start(bf16[16,2816]{1,0:T(8,128)(2,1)S(1)} %slice.36), channel_id=1, source_target_pairs={{0,1},{1,2},{2,3},{3,4},{4,5},{5,6},{6,7},{7,8},{8,9},{9,10},{10,1... | collective-permute-start | bytes 270344 | tf_op jit(solution)/shard_map/ppermute | solution.py:545
  15.5 17.5 %copy-start.16 = (f32[128,128]{1,0:T(8,128)}, f32[128,128]{1,0:T(8,128)S(1)}, u32[]{:S(2)}) copy-start(f32[128,128]{1,0:T(8,128)S(1)} %get-tuple-element.53.ld_ref) | copy-start | bytes 196612
  16.4 26.7 %all-to-all-start = ((f16[8,328,128]{2,1,0:T(8,128)(2,1)}), f16[8,328,128]{2,1,0:T(8,128)(2,1)}, u32[]{:S(2)}, u32[]{:S(2)}) async-start(f16[8,328,128]{2,1,0:T(8,128)(2,1)} %convert_element_type.51), calls=%async_computation | async-start | bytes 1343488 | tf_op jit(solution)/shard_map/all_to_all | solution.py:489
  45.9 24.8 %all-to-all-start.1 = ((f16[8,328,128]{2,1,0:T(8,128)(2,1)}), f16[8,328,128]{2,1,0:T(8,128)(2,1)}, u32[]{:S(2)}, u32[]{:S(2)}) async-start(f16[8,328,128]{2,1,0:T(8,128)(2,1)} %convert_element_type.57), calls=%async_computation.1 | async-start | bytes 1343488 | tf_op jit(solution)/shard_map/all_to_all | solution.py:489
  50.1 19.1 %collective-permute-start.1 = (f16[1,328,128]{2,1,0:T(8,128)(2,1)S(1)}, f16[1,328,128]{2,1,0:T(8,128)(2,1)S(1)}, u32[]{:S(2)}, u32[]{:S(2)}) collective-permute-start(f16[1,328,128]{2,1,0:T(8,128)(2,1)S(1)} %convert_element_type.53), channel_id=1, source_target_pairs={{0,8},{1,9},{2,10},{3,11},{4,12},{5,13},{6,14},{7,15},{8,16},{9,17... | collective-permute-start | bytes 251912 | tf_op jit(solution)/shard_map/ppermute | solution.py:524
  55.8 13.4 %collective-permute-start.2 = (f16[1,328,128]{2,1,0:T(8,128)(2,1)S(1)}, f16[1,328,128]{2,1,0:T(8,128)(2,1)S(1)}, u32[]{:S(2)}, u32[]{:S(2)}) collective-permute-start(f16[1,328,128]{2,1,0:T(8,128)(2,1)S(1)} %convert_element_type.53), channel_id=1, source_target_pairs={{0,16},{1,17},{2,18},{3,19},{4,20},{5,21},{6,22},{7,23},{8,24},{9,... | collective-permute-start | bytes 251912 | tf_op jit(solution)/shard_map/ppermute | solution.py:524
  60.3 9.0 %collective-permute-start.3 = (f16[1,328,128]{2,1,0:T(8,128)(2,1)S(1)}, f16[1,328,128]{2,1,0:T(8,128)(2,1)S(1)}, u32[]{:S(2)}, u32[]{:S(2)}) collective-permute-start(f16[1,328,128]{2,1,0:T(8,128)(2,1)S(1)} %convert_element_type.53), channel_id=1, source_target_pairs={{0,24},{1,25},{2,26},{3,27},{4,28},{5,29},{6,30},{7,31}} | collective-permute-start | bytes 251912 | tf_op jit(solution)/shard_map/ppermute | solution.py:524
  71.6 21.1 %all-to-all-start.2 = ((f16[8,328,128]{2,1,0:T(8,128)(2,1)}), f16[8,328,128]{2,1,0:T(8,128)(2,1)}, u32[]{:S(2)}, u32[]{:S(2)}) async-start(f16[8,328,128]{2,1,0:T(8,128)(2,1)} %convert_element_type.58), calls=%async_computation.2 | async-start | bytes 1343488 | tf_op jit(solution)/shard_map/all_to_all | solution.py:489
  77.8 7.0 %collective-permute-start.4 = (f16[1,328,128]{2,1,0:T(8,128)(2,1)S(1)}, f16[1,328,128]{2,1,0:T(8,128)(2,1)S(1)}, u32[]{:S(2)}, u32[]{:S(2)}) collective-permute-start(f16[1,328,128]{2,1,0:T(8,128)(2,1)S(1)} %convert_element_type.61), channel_id=1, source_target_pairs={{8,0},{9,1},{10,2},{11,3},{12,4},{13,5},{14,6},{15,7},{16,8},{17,9... | collective-permute-start | bytes 251912 | tf_op jit(solution)/shard_map/ppermute | solution.py:524
  79.1 12.3 %collective-permute-start.5 = (f16[1,328,128]{2,1,0:T(8,128)(2,1)S(1)}, f16[1,328,128]{2,1,0:T(8,128)(2,1)S(1)}, u32[]{:S(2)}, u32[]{:S(2)}) collective-permute-start(f16[1,328,128]{2,1,0:T(8,128)(2,1)S(1)} %convert_element_type.61), channel_id=1, source_target_pairs={{16,0},{17,1},{18,2},{19,3},{20,4},{21,5},{22,6},{23,7},{24,8},{25... | collective-permute-start | bytes 251912 | tf_op jit(solution)/shard_map/ppermute | solution.py:524
  80.4 11.0 %collective-permute-start.6 = (f16[1,328,128]{2,1,0:T(8,128)(2,1)S(1)}, f16[1,328,128]{2,1,0:T(8,128)(2,1)S(1)}, u32[]{:S(2)}, u32[]{:S(2)}) collective-permute-start(f16[1,328,128]{2,1,0:T(8,128)(2,1)S(1)} %convert_element_type.61), channel_id=1, source_target_pairs={{24,0},{25,1},{26,2},{27,3},{28,4},{29,5},{30,6},{31,7}} | collective-permute-start | bytes 251912 | tf_op jit(solution)/shard_map/ppermute | solution.py:524
  99.4 16.4 %all-to-all-start.3 = ((bf16[16,160,128]{2,1,0:T(8,128)(2,1)}), bf16[16,160,128]{2,1,0:T(8,128)(2,1)}, u32[]{:S(2)}, u32[]{:S(2)}) async-start(bf16[16,160,128]{2,1,0:T(8,128)(2,1)} %copy-done.13), calls=%async_computation.3 | async-start | bytes 1310720 | tf_op jit(solution)/shard_map/all_to_all | solution.py:667
  123.5 27.9 %all-to-all-start.4 = ((bf16[32,112,128]{2,1,0:T(8,128)(2,1)}), bf16[32,112,128]{2,1,0:T(8,128)(2,1)}, u32[]{:S(2)}, u32[]{:S(2)}) async-start(bf16[32,112,128]{2,1,0:T(8,128)(2,1)} %copy-done), calls=%async_computation.4 | async-start | bytes 1835008 | tf_op jit(solution)/shard_map/all_to_all | solution.py:705
  127.1 18.7 %copy-start.31 = (f32[128,2560]{1,0:T(8,128)S(1)}, f32[128,2560]{1,0:T(8,128)}, u32[]{:S(2)}) copy-start(f32[128,2560]{1,0:T(8,128)} %get-tuple-element.76.gw_ref) | copy-start | bytes 3932164
  127.2 18.7 %copy-start.30 = (f32[128,2560]{1,0:T(8,128)S(1)}, f32[128,2560]{1,0:T(8,128)}, u32[]{:S(2)}) copy-start(f32[128,2560]{1,0:T(8,128)} %get-tuple-element.75.slope_ref) | copy-start | bytes 3932164
  127.4 3.6 %collective-permute-start.7 = (f16[1,328,128]{2,1,0:T(8,128)(2,1)S(1)}, f16[1,328,128]{2,1,0:T(8,128)(2,1)S(1)}, u32[]{:S(2)}, u32[]{:S(2)}) collective-permute-start(f16[1,328,128]{2,1,0:T(8,128)(2,1)S(1)} %get-tuple-element.98), channel_id=1, source_target_pairs={{0,1},{1,0},{2,3},{3,2},{4,5},{5,4},{6,7},{7,6},{8,9},{9,8},{10,11... | collective-permute-start | bytes 251912 | tf_op jit(solution)/shard_map/ppermute | solution.py:497
  127.5 11.4 %collective-permute-start.8 = (f16[1,328,128]{2,1,0:T(8,128)(2,1)S(1)}, f16[1,328,128]{2,1,0:T(8,128)(2,1)S(1)}, u32[]{:S(2)}, u32[]{:S(2)}) collective-permute-start(f16[1,328,128]{2,1,0:T(8,128)(2,1)S(1)} %get-tuple-element.97), channel_id=1, source_target_pairs={{0,2},{1,3},{2,0},{3,1},{4,6},{5,7},{6,4},{7,5},{8,10},{9,11},{10,... | collective-permute-start | bytes 251912 | tf_op jit(solution)/shard_map/ppermute | solution.py:497
  129.0 11.0 %collective-permute-start.9 = (f16[1,328,128]{2,1,0:T(8,128)(2,1)S(1)}, f16[1,328,128]{2,1,0:T(8,128)(2,1)S(1)}, u32[]{:S(2)}, u32[]{:S(2)}) collective-permute-start(f16[1,328,128]{2,1,0:T(8,128)(2,1)S(1)} %get-tuple-element.96), channel_id=1, source_target_pairs={{0,3},{1,2},{2,1},{3,0},{4,7},{5,6},{6,5},{7,4},{8,11},{9,10},{10,... | collective-permute-start | bytes 251912 | tf_op jit(solution)/shard_map/ppermute | solution.py:497
  129.3 10.8 %collective-permute-start.10 = (f16[1,328,128]{2,1,0:T(8,128)(2,1)S(1)}, f16[1,328,128]{2,1,0:T(8,128)(2,1)S(1)}, u32[]{:S(2)}, u32[]{:S(2)}) collective-permute-start(f16[1,328,128]{2,1,0:T(8,128)(2,1)S(1)} %get-tuple-element.95), channel_id=1, source_target_pairs={{0,4},{1,5},{2,6},{3,7},{4,0},{5,1},{6,2},{7,3},{8,12},{9,13},{10,... | collective-permute-start | bytes 251912 | tf_op jit(solution)/shard_map/ppermute | solution.py:497
  130.7 9.4 %collective-permute-start.11 = (f16[1,328,128]{2,1,0:T(8,128)(2,1)S(1)}, f16[1,328,128]{2,1,0:T(8,128)(2,1)S(1)}, u32[]{:S(2)}, u32[]{:S(2)}) collective-permute-start(f16[1,328,128]{2,1,0:T(8,128)(2,1)S(1)} %get-tuple-element.94), channel_id=1, source_target_pairs={{0,5},{1,4},{2,7},{3,6},{4,1},{5,0},{6,3},{7,2},{8,13},{9,12},{10,... | collective-permute-start | bytes 251912 | tf_op jit(solution)/shard_map/ppermute | solution.py:497
  131.0 13.8 %collective-permute-start.12 = (f16[1,328,128]{2,1,0:T(8,128)(2,1)S(1)}, f16[1,328,128]{2,1,0:T(8,128)(2,1)S(1)}, u32[]{:S(2)}, u32[]{:S(2)}) collective-permute-start(f16[1,328,128]{2,1,0:T(8,128)(2,1)S(1)} %get-tuple-element.93), channel_id=1, source_target_pairs={{0,6},{1,7},{2,4},{3,5},{4,2},{5,3},{6,0},{7,1},{8,14},{9,15},{10,... | collective-permute-start | bytes 251912 | tf_op jit(solution)/shard_map/ppermute | solution.py:497
  133.4 12.5 %copy-start.33 = (f32[128,128]{1,0:T(8,128)S(1)}, f32[128,128]{1,0:T(8,128)}, u32[]{:S(2)}) copy-start(f32[128,128]{1,0:T(8,128)} %get-tuple-element.79.dtw_ref) | copy-start | bytes 196612
  138.9 6.9 %collective-permute-start.13 = (f16[1,328,128]{2,1,0:T(8,128)(2,1)S(1)}, f16[1,328,128]{2,1,0:T(8,128)(2,1)S(1)}, u32[]{:S(2)}, u32[]{:S(2)}) collective-permute-start(f16[1,328,128]{2,1,0:T(8,128)(2,1)S(1)} %get-tuple-element.92), channel_id=1, source_target_pairs={{0,7},{1,6},{2,5},{3,4},{4,3},{5,2},{6,1},{7,0},{8,15},{9,14},{10,... | collective-permute-start | bytes 251912 | tf_op jit(solution)/shard_map/ppermute | solution.py:497
  (41 other events, 150.8 us)
Sparse Core Ops, SparseCore 0:
  9.7 81.9 all-gather.1

commit v10 on v9

--- a/solution.py
+++ b/solution.py
@@ -517,11 +517,11 @@
     size = held.shape[0]
     count = lax.axis_size("ctx")
     others = []
-    for hops in range(size, count, size):
+    for hops in reversed(range(size, count, size)):
         pairs = [(at, at + hops) for at in range(count - hops)]
         if reverse:
             pairs = [(b, a) for a, b in pairs]
-        others.append(lax.ppermute(total, "ctx", pairs).astype(F32))
+        others.insert(0, lax.ppermute(total, "ctx", pairs).astype(F32))
     (folded,) = call(
         functools.partial(fold_kernel, rows, reverse),
         [shape(held.shape)],

time: 162 us -> 162 us (level)
  no operation moved by 1% of the time
where the time goes in v10:
time: 162 us; the launch traced here: 161 us
  starting transfers between devices  48 us (30%)
  Pallas kernels  45.7 us (28%)
  waiting for transfers between devices  29 us (18%)
  local copies, waits for them, and re-layouts  15.6 us (10%)
  between operations  14.9 us (9%)
  other arithmetic  7.46 us (5%)
    pallas_call x12, Pallas kernels, call(): pl.pallas_call(kernel, out_shape=tuple(out_shapes), scratch_shapes=list(s...  30.1 us
    all_to_all x3, starting transfers between devices, exchange(): lax.all_to_all(half, 'ctx', 0, 0, axis_index_groups=groups, tiled=True)  16.1 us
    ppermute x6, starting transfers between devices, enter(): others.insert(0, lax.ppermute(total, 'ctx', pairs).astype(F32))  15.5 us
    unnamed x99, local copies, waits for them, and re-layouts  15.2 us
    ppermute x7, waiting for transfers between devices, swapped(): lax.ppermute(half[m:m + 1], 'ctx', [(at, at ^ m) for at in range(count)])  12.1 us
    ppermute x6, waiting for transfers between devices, enter(): others.insert(0, lax.ppermute(total, 'ctx', pairs).astype(F32))  9.48 us
    pallas_call x1, Pallas kernels, per_device(): pl.pallas_call(gate_kernel, grid=(channels // part,), in_specs=[pl.BlockS...  8.75 us
    pallas_call x1, Pallas kernels, per_device(): pl.pallas_call(functools.partial(product_kernel, out_rows), grid=(width /...  6.78 us
  transfers between devices with their start and end apart: 20, of which 9 were waited for; matrix products, arithmetic and copies ran while one was open for 6% of the time, Pallas kernels for 23%

profile of v10, /device:TPU:0, one launch (start us, length us, event | category | flops | bytes accessed | tf_op | source)
XLA Modules:
  0.0 160.6 jit_solution(2914494355402360450)
XLA Ops:
  9.2 2.4 %collective-permute-start = (bf16[16,2816]{1,0:T(8,128)(2,1)S(1)}, bf16[16,2816]{1,0:T(8,128)(2,1)S(1)}, u32[]{:S(2)}, u32[]{:S(2)}) collective-permute-start(bf16[16,2816]{1,0:T(8,128)(2,1)S(1)} %slice.36), channel_id=1, source_target_pairs={{0,1},{1,2},{2,3},{3,4},{4,5},{5,6},{6,7},{7,8},{8,9},{9,10},{10,1... | collective-permute-start | bytes 270344 | tf_op jit(solution)/shard_map/ppermute | solution.py:545
  12.5 2.3 %shard_map.164 = (f32[128,256]{1,0:T(8,128)S(1)}, f32[128,128]{1,0:T(8,128)S(1)}, f32[8,328,128]{2,1,0:T(8,128)S(1)}) custom-call(bf16[128,2816]{1,0:T(8,128)(2,1)S(1)} %constant_dynamic-update-slice_fusion.raw_ref, bf16[16,2816]{1,0:T(8,128)(2,1)S(1)} %collective-permute-done.rim_ref, f32[5,2816]{1,0:T(8,128)S(1)} %pad_maximum_fusion.taps_ref, ...), custom_call_target="tpu_custom_call" | custom-call | flops 1677721600 | bytes 2428224 | tf_op jit(solution)/shard_map/pallas_call | solution.py:26
  16.4 7.7 %all-to-all-start = ((f16[8,328,128]{2,1,0:T(8,128)(2,1)}), f16[8,328,128]{2,1,0:T(8,128)(2,1)}, u32[]{:S(2)}, u32[]{:S(2)}) async-start(f16[8,328,128]{2,1,0:T(8,128)(2,1)} %convert_element_type.51), calls=%async_computation | async-start | bytes 1343488 | tf_op jit(solution)/shard_map/all_to_all | solution.py:489
  24.2 8.8 %shard_map.167 = (f32[128,2560]{1,0:T(8,128)}, f32[128,2560]{1,0:T(8,128)}) custom-call(bf16[128,2560]{1,0:T(8,128)(2,1)S(1)} %copy-done.2, bf16[2560,2560]{1,0:T(8,128)(2,1)} %refs_3_.1, bf16[2560,2560]{1,0:T(8,128)(2,1)} %refs_3_.1, bf16[2560,2560]{1,0:T(8,128)(2,1)} %refs_3_.1, bf16[2560,2560]{1,0:T(8,128)(2,1)} %refs_3_.1, bf16[128,2560]{1,0:T(8,128)(2,1)S(1)} %copy-done.1), custom_call_target="tpu_custom_call" | custom-call | flops 1677721600 | bytes 13107200 | tf_op jit(solution)/shard_map/pallas_call | solution.py:606
  35.9 4.3 %shard_map.166 = (f32[128,2560]{1,0:T(8,128)}, f32[128,2560]{1,0:T(8,128)}, f32[128,256]{1,0:T(8,128)}, f32[128,128]{1,0:T(8,128)}, f32[128,128]{1,0:T(8,128)}, ...) custom-call(bf16[128,2816]{1,0:T(8,128)(2,1)} %copy-done.12, bf16[16,2816]{1,0:T(8,128)(2,1)} %copy-done.22, ...), custom_call_target="tpu_custom_call" | custom-call | flops 838860800 | bytes 3906880 | tf_op jit(solution)/shard_map/pallas_call | solution.py:26
  40.1 3.0 %all-to-all-done = f16[8,328,128]{2,1,0:T(8,128)(2,1)} async-done(((f16[8,328,128]{2,1,0:T(8,128)(2,1)}), f16[8,328,128]{2,1,0:T(8,128)(2,1)}, u32[]{:S(2)}, u32[]{:S(2)}) %all-to-all-start) | async-done | bytes 671776 | tf_op jit(solution)/shard_map/all_to_all | solution.py:489
  45.9 4.2 %all-to-all-start.1 = ((f16[8,328,128]{2,1,0:T(8,128)(2,1)}), f16[8,328,128]{2,1,0:T(8,128)(2,1)}, u32[]{:S(2)}, u32[]{:S(2)}) async-start(f16[8,328,128]{2,1,0:T(8,128)(2,1)} %convert_element_type.57), calls=%async_computation.1 | async-start | bytes 1343488 | tf_op jit(solution)/shard_map/all_to_all | solution.py:489
  50.1 5.7 %collective-permute-start.1 = (f16[1,328,128]{2,1,0:T(8,128)(2,1)S(1)}, f16[1,328,128]{2,1,0:T(8,128)(2,1)S(1)}, u32[]{:S(2)}, u32[]{:S(2)}) collective-permute-start(f16[1,328,128]{2,1,0:T(8,128)(2,1)S(1)} %convert_element_type.53), channel_id=1, source_target_pairs={{0,8},{1,9},{2,10},{3,11},{4,12},{5,13},{6,14},{7,15},{8,16},{9,17... | collective-permute-start | bytes 251912 | tf_op jit(solution)/shard_map/ppermute | solution.py:524
  55.8 4.5 %collective-permute-start.2 = (f16[1,328,128]{2,1,0:T(8,128)(2,1)S(1)}, f16[1,328,128]{2,1,0:T(8,128)(2,1)S(1)}, u32[]{:S(2)}, u32[]{:S(2)}) collective-permute-start(f16[1,328,128]{2,1,0:T(8,128)(2,1)S(1)} %convert_element_type.53), channel_id=1, source_target_pairs={{0,16},{1,17},{2,18},{3,19},{4,20},{5,21},{6,22},{7,23},{8,24},{9,... | collective-permute-start | bytes 251912 | tf_op jit(solution)/shard_map/ppermute | solution.py:524
  61.8 7.4 %shard_map.170 = (f32[128,2560]{1,0:T(8,128)}, f32[128,2560]{1,0:T(8,128)}, f32[128,256]{1,0:T(8,128)}) custom-call(f32[128,2560]{1,0:T(8,128)} %get-tuple-element.56.act_ref, f32[128,2560]{1,0:T(8,128)} %get-tuple-element.51.gy_ref, f32[128,256]{1,0:T(8,128)} %copy-done.25, f32[128,128]{1,0:T(8,128)} %get-tuple-element.57.step_ref, f32[128,128]{1,0:T(8,128)} %copy-done.16, ...), custom_call_target="tpu_custom_call" | custom-call | flops 3355443200 | bytes 5767168 | tf_op jit(solution)/shard_map/pallas_call | solution.py:26
  71.6 4.2 %all-to-all-start.2 = ((f16[8,328,128]{2,1,0:T(8,128)(2,1)}), f16[8,328,128]{2,1,0:T(8,128)(2,1)}, u32[]{:S(2)}, u32[]{:S(2)}) async-start(f16[8,328,128]{2,1,0:T(8,128)(2,1)} %convert_element_type.58), calls=%async_computation.2 | async-start | bytes 1343488 | tf_op jit(solution)/shard_map/all_to_all | solution.py:489
  81.8 2.9 %collective-permute-done.4 = f16[1,328,128]{2,1,0:T(8,128)(2,1)S(1)} collective-permute-done((f16[1,328,128]{2,1,0:T(8,128)(2,1)S(1)}, f16[1,328,128]{2,1,0:T(8,128)(2,1)S(1)}, u32[]{:S(2)}, u32[]{:S(2)}) %collective-permute-start.4) | collective-permute-done | bytes 84000 | tf_op jit(solution)/shard_map/ppermute | solution.py:524
  84.8 6.6 %collective-permute-done.5 = f16[1,328,128]{2,1,0:T(8,128)(2,1)S(1)} collective-permute-done((f16[1,328,128]{2,1,0:T(8,128)(2,1)S(1)}, f16[1,328,128]{2,1,0:T(8,128)(2,1)S(1)}, u32[]{:S(2)}, u32[]{:S(2)}) %collective-permute-start.5) | collective-permute-done | bytes 84000 | tf_op jit(solution)/shard_map/ppermute | solution.py:524
  95.7 1.8 %shard_map.171 = (bf16[16,160,128]{2,1,0:T(8,128)(2,1)S(1)}, f32[128,2560]{1,0:T(8,128)S(1)}) custom-call(f32[8,328,128]{2,1,0:T(8,128)S(1)} %convert_element_type.59.msg_ref.msgf_ref, f32[128,2560]{1,0:T(8,128)S(1)} %copy-done.6, bf16[128,2560]{1,0:T(8,128)(2,1)S(1)} %copy-done.1, f32[128,256]{1,0:T(8,128)S(1)} %copy-done.27, f32[128,128]{1,0:T(8,128)S(1)} %copy-done.17, ...), custom_call_target="tpu_custom_call" | custom-call | flops 1677721600 | bytes 6793216 | tf_op jit(solution)/shard_map/pallas_call | solution.py:26
  99.4 4.4 %all-to-all-start.3 = ((bf16[16,160,128]{2,1,0:T(8,128)(2,1)}), bf16[16,160,128]{2,1,0:T(8,128)(2,1)}, u32[]{:S(2)}, u32[]{:S(2)}) async-start(bf16[16,160,128]{2,1,0:T(8,128)(2,1)} %copy-done.13), calls=%async_computation.3 | async-start | bytes 1310720 | tf_op jit(solution)/shard_map/all_to_all | solution.py:667
  109.1 2.3 %shard_map.174 = (bf16[128,2560]{1,0:T(8,128)(2,1)}, f32[128,128]{1,0:T(8,128)S(1)}, f32[128,256]{1,0:T(8,128)S(1)}) custom-call(f32[8,328,128]{2,1,0:T(8,128)S(1)} %convert_element_type.59.msg_ref.msgf_ref, f32[128,2560]{1,0:T(8,128)S(1)} %copy-done.7, f32[128,2560]{1,0:T(8,128)S(1)} %copy-done.4, f32[128,128]{1,0:T(8,128)S(1)} %copy-done.17, ...), custom_call_target="tpu_custom_call" | custom-call | flops 1677721600 | bytes 8300544 | tf_op jit(solution)/shard_map/pallas_call | solution.py:26
  112.7 3.1 %all-to-all-done.3.held_ref = bf16[16,160,128]{2,1,0:T(8,128)(2,1)} async-done(((bf16[16,160,128]{2,1,0:T(8,128)(2,1)}), bf16[16,160,128]{2,1,0:T(8,128)(2,1)}, u32[]{:S(2)}, u32[]{:S(2)}) %all-to-all-start.3) | async-done | bytes 655392 | tf_op jit(solution)/shard_map/all_to_all | solution.py:667
  115.8 6.8 %shard_map.175 = bf16[32,112,128]{2,1,0:T(8,128)(2,1)S(1)} custom-call(bf16[16,160,128]{2,1,0:T(8,128)(2,1)} %all-to-all-done.3.held_ref, bf16[2048,2560]{1,0:T(8,128)(2,1)} %all-gather.2.cloned.1.call-done.refs_0_.refs_1_.refs_2_.refs_3_, bf16[2048,2560]{1,0:T(8,128)(2,1)} %all-gather.2.cloned.1.call-done.refs_0_.refs_1_.refs_2_.refs_3_, ...), custom_call_target="tpu_custom_call" | custom-call | flops 1677721600 | bytes 10485760 | tf_op jit(solution)/shard_map/pallas_call | solution.py:686
  123.5 3.6 %all-to-all-start.4 = ((bf16[32,112,128]{2,1,0:T(8,128)(2,1)}), bf16[32,112,128]{2,1,0:T(8,128)(2,1)}, u32[]{:S(2)}, u32[]{:S(2)}) async-start(bf16[32,112,128]{2,1,0:T(8,128)(2,1)} %copy-done), calls=%async_computation.4 | async-start | bytes 1835008 | tf_op jit(solution)/shard_map/all_to_all | solution.py:705
  131.0 2.4 %collective-permute-start.12 = (f16[1,328,128]{2,1,0:T(8,128)(2,1)S(1)}, f16[1,328,128]{2,1,0:T(8,128)(2,1)S(1)}, u32[]{:S(2)}, u32[]{:S(2)}) collective-permute-start(f16[1,328,128]{2,1,0:T(8,128)(2,1)S(1)} %get-tuple-element.93), channel_id=1, source_target_pairs={{0,6},{1,7},{2,4},{3,5},{4,2},{5,3},{6,0},{7,1},{8,14},{9,15},{10,... | collective-permute-start | bytes 251912 | tf_op jit(solution)/shard_map/ppermute | solution.py:497
  133.4 5.4 %collective-permute-done.8 = f16[1,328,128]{2,1,0:T(8,128)(2,1)S(1)} collective-permute-done((f16[1,328,128]{2,1,0:T(8,128)(2,1)S(1)}, f16[1,328,128]{2,1,0:T(8,128)(2,1)S(1)}, u32[]{:S(2)}, u32[]{:S(2)}) %collective-permute-start.8) | collective-permute-done | bytes 84000 | tf_op jit(solution)/shard_map/ppermute | solution.py:497
  140.2 4.7 %collective-permute-done.12 = f16[1,328,128]{2,1,0:T(8,128)(2,1)S(1)} collective-permute-done((f16[1,328,128]{2,1,0:T(8,128)(2,1)S(1)}, f16[1,328,128]{2,1,0:T(8,128)(2,1)S(1)}, u32[]{:S(2)}, u32[]{:S(2)}) %collective-permute-start.12) | collective-permute-done | bytes 84000 | tf_op jit(solution)/shard_map/ppermute | solution.py:497
  146.0 4.1 %shard_map.176 = (bf16[128,2560]{1,0:T(8,128)(2,1)}, f32[128,256]{1,0:T(8,128)S(1)}, f32[128,40]{1,0:T(8,128)S(1)}) custom-call(s32[1]{0:T(128)} %bitcast.me_ref, f32[8,328,128]{2,1,0:T(8,128)S(1)} %convert_element_type.66.msg_ref, f32[8,328,128]{2,1,0:T(8,128)S(1)} %convert_element_type.59.msg_ref.msgf_ref, f32[128,2560]{1,0:T(8,128)S(1)} %copy-done.8, ...), custom_call_target="tpu_custom_call" | custom-call | flops 3355443200 | bytes 9275396 | tf_op jit(solution)/shard_map/pallas_call | solution.py:26
  151.4 2.3 %shard_map.177 = f32[80,2560]{1,0:T(8,128)} custom-call(bf16[32,112,128]{2,1,0:T(8,128)(2,1)} %all-to-all-done.4.parts_ref), custom_call_target="tpu_custom_call" | custom-call | flops 917504 | bytes 1736704 | tf_op jit(solution)/shard_map/pallas_call | solution.py:26
  (157 shorter events, 41.0 us)
Async XLA Ops:
  7.2 92.2 %all-gather.2.cloned.1.call-start = ((), (), s32[]{:S(2)}) async-start(), calls=%async_computation.5 | async-start | bytes 11141120 | tf_op jit(solution)/shard_map/all_gather | solution.py:575
  9.2 3.3 %collective-permute-start = (bf16[16,2816]{1,0:T(8,128)(2,1)S(1)}, bf16[16,2816]{1,0:T(8,128)(2,1)S(1)}, u32[]{:S(2)}, u32[]{:S(2)}) collective-permute-start(bf16[16,2816]{1,0:T(8,128)(2,1)S(1)} %slice.36), channel_id=1, source_target_pairs={{0,1},{1,2},{2,3},{3,4},{4,5},{5,6},{6,7},{7,8},{8,9},{9,10},{10,1... | collective-permute-start | bytes 270344 | tf_op jit(solution)/shard_map/ppermute | solution.py:545
  15.5 17.5 %copy-start.16 = (f32[128,128]{1,0:T(8,128)}, f32[128,128]{1,0:T(8,128)S(1)}, u32[]{:S(2)}) copy-start(f32[128,128]{1,0:T(8,128)S(1)} %get-tuple-element.53.ld_ref) | copy-start | bytes 196612
  16.4 26.7 %all-to-all-start = ((f16[8,328,128]{2,1,0:T(8,128)(2,1)}), f16[8,328,128]{2,1,0:T(8,128)(2,1)}, u32[]{:S(2)}, u32[]{:S(2)}) async-start(f16[8,328,128]{2,1,0:T(8,128)(2,1)} %convert_element_type.51), calls=%async_computation | async-start | bytes 1343488 | tf_op jit(solution)/shard_map/all_to_all | solution.py:489
  45.9 24.8 %all-to-all-start.1 = ((f16[8,328,128]{2,1,0:T(8,128)(2,1)}), f16[8,328,128]{2,1,0:T(8,128)(2,1)}, u32[]{:S(2)}, u32[]{:S(2)}) async-start(f16[8,328,128]{2,1,0:T(8,128)(2,1)} %convert_element_type.57), calls=%async_computation.1 | async-start | bytes 1343488 | tf_op jit(solution)/shard_map/all_to_all | solution.py:489
  50.1 19.1 %collective-permute-start.1 = (f16[1,328,128]{2,1,0:T(8,128)(2,1)S(1)}, f16[1,328,128]{2,1,0:T(8,128)(2,1)S(1)}, u32[]{:S(2)}, u32[]{:S(2)}) collective-permute-start(f16[1,328,128]{2,1,0:T(8,128)(2,1)S(1)} %convert_element_type.53), channel_id=1, source_target_pairs={{0,8},{1,9},{2,10},{3,11},{4,12},{5,13},{6,14},{7,15},{8,16},{9,17... | collective-permute-start | bytes 251912 | tf_op jit(solution)/shard_map/ppermute | solution.py:524
  55.8 13.4 %collective-permute-start.2 = (f16[1,328,128]{2,1,0:T(8,128)(2,1)S(1)}, f16[1,328,128]{2,1,0:T(8,128)(2,1)S(1)}, u32[]{:S(2)}, u32[]{:S(2)}) collective-permute-start(f16[1,328,128]{2,1,0:T(8,128)(2,1)S(1)} %convert_element_type.53), channel_id=1, source_target_pairs={{0,16},{1,17},{2,18},{3,19},{4,20},{5,21},{6,22},{7,23},{8,24},{9,... | collective-permute-start | bytes 251912 | tf_op jit(solution)/shard_map/ppermute | solution.py:524
  60.3 9.0 %collective-permute-start.3 = (f16[1,328,128]{2,1,0:T(8,128)(2,1)S(1)}, f16[1,328,128]{2,1,0:T(8,128)(2,1)S(1)}, u32[]{:S(2)}, u32[]{:S(2)}) collective-permute-start(f16[1,328,128]{2,1,0:T(8,128)(2,1)S(1)} %convert_element_type.53), channel_id=1, source_target_pairs={{0,24},{1,25},{2,26},{3,27},{4,28},{5,29},{6,30},{7,31}} | collective-permute-start | bytes 251912 | tf_op jit(solution)/shard_map/ppermute | solution.py:524
  71.6 21.1 %all-to-all-start.2 = ((f16[8,328,128]{2,1,0:T(8,128)(2,1)}), f16[8,328,128]{2,1,0:T(8,128)(2,1)}, u32[]{:S(2)}, u32[]{:S(2)}) async-start(f16[8,328,128]{2,1,0:T(8,128)(2,1)} %convert_element_type.58), calls=%async_computation.2 | async-start | bytes 1343488 | tf_op jit(solution)/shard_map/all_to_all | solution.py:489
  77.8 7.0 %collective-permute-start.4 = (f16[1,328,128]{2,1,0:T(8,128)(2,1)S(1)}, f16[1,328,128]{2,1,0:T(8,128)(2,1)S(1)}, u32[]{:S(2)}, u32[]{:S(2)}) collective-permute-start(f16[1,328,128]{2,1,0:T(8,128)(2,1)S(1)} %convert_element_type.61), channel_id=1, source_target_pairs={{8,0},{9,1},{10,2},{11,3},{12,4},{13,5},{14,6},{15,7},{16,8},{17,9... | collective-permute-start | bytes 251912 | tf_op jit(solution)/shard_map/ppermute | solution.py:524
  79.1 12.3 %collective-permute-start.5 = (f16[1,328,128]{2,1,0:T(8,128)(2,1)S(1)}, f16[1,328,128]{2,1,0:T(8,128)(2,1)S(1)}, u32[]{:S(2)}, u32[]{:S(2)}) collective-permute-start(f16[1,328,128]{2,1,0:T(8,128)(2,1)S(1)} %convert_element_type.61), channel_id=1, source_target_pairs={{16,0},{17,1},{18,2},{19,3},{20,4},{21,5},{22,6},{23,7},{24,8},{25... | collective-permute-start | bytes 251912 | tf_op jit(solution)/shard_map/ppermute | solution.py:524
  80.4 11.0 %collective-permute-start.6 = (f16[1,328,128]{2,1,0:T(8,128)(2,1)S(1)}, f16[1,328,128]{2,1,0:T(8,128)(2,1)S(1)}, u32[]{:S(2)}, u32[]{:S(2)}) collective-permute-start(f16[1,328,128]{2,1,0:T(8,128)(2,1)S(1)} %convert_element_type.61), channel_id=1, source_target_pairs={{24,0},{25,1},{26,2},{27,3},{28,4},{29,5},{30,6},{31,7}} | collective-permute-start | bytes 251912 | tf_op jit(solution)/shard_map/ppermute | solution.py:524
  99.4 16.4 %all-to-all-start.3 = ((bf16[16,160,128]{2,1,0:T(8,128)(2,1)}), bf16[16,160,128]{2,1,0:T(8,128)(2,1)}, u32[]{:S(2)}, u32[]{:S(2)}) async-start(bf16[16,160,128]{2,1,0:T(8,128)(2,1)} %copy-done.13), calls=%async_computation.3 | async-start | bytes 1310720 | tf_op jit(solution)/shard_map/all_to_all | solution.py:667
  123.5 27.9 %all-to-all-start.4 = ((bf16[32,112,128]{2,1,0:T(8,128)(2,1)}), bf16[32,112,128]{2,1,0:T(8,128)(2,1)}, u32[]{:S(2)}, u32[]{:S(2)}) async-start(bf16[32,112,128]{2,1,0:T(8,128)(2,1)} %copy-done), calls=%async_computation.4 | async-start | bytes 1835008 | tf_op jit(solution)/shard_map/all_to_all | solution.py:705
  127.1 18.7 %copy-start.31 = (f32[128,2560]{1,0:T(8,128)S(1)}, f32[128,2560]{1,0:T(8,128)}, u32[]{:S(2)}) copy-start(f32[128,2560]{1,0:T(8,128)} %get-tuple-element.76.gw_ref) | copy-start | bytes 3932164
  127.2 18.7 %copy-start.30 = (f32[128,2560]{1,0:T(8,128)S(1)}, f32[128,2560]{1,0:T(8,128)}, u32[]{:S(2)}) copy-start(f32[128,2560]{1,0:T(8,128)} %get-tuple-element.75.slope_ref) | copy-start | bytes 3932164
  127.4 3.6 %collective-permute-start.7 = (f16[1,328,128]{2,1,0:T(8,128)(2,1)S(1)}, f16[1,328,128]{2,1,0:T(8,128)(2,1)S(1)}, u32[]{:S(2)}, u32[]{:S(2)}) collective-permute-start(f16[1,328,128]{2,1,0:T(8,128)(2,1)S(1)} %get-tuple-element.98), channel_id=1, source_target_pairs={{0,1},{1,0},{2,3},{3,2},{4,5},{5,4},{6,7},{7,6},{8,9},{9,8},{10,11... | collective-permute-start | bytes 251912 | tf_op jit(solution)/shard_map/ppermute | solution.py:497
  127.5 11.4 %collective-permute-start.8 = (f16[1,328,128]{2,1,0:T(8,128)(2,1)S(1)}, f16[1,328,128]{2,1,0:T(8,128)(2,1)S(1)}, u32[]{:S(2)}, u32[]{:S(2)}) collective-permute-start(f16[1,328,128]{2,1,0:T(8,128)(2,1)S(1)} %get-tuple-element.97), channel_id=1, source_target_pairs={{0,2},{1,3},{2,0},{3,1},{4,6},{5,7},{6,4},{7,5},{8,10},{9,11},{10,... | collective-permute-start | bytes 251912 | tf_op jit(solution)/shard_map/ppermute | solution.py:497
  129.0 11.0 %collective-permute-start.9 = (f16[1,328,128]{2,1,0:T(8,128)(2,1)S(1)}, f16[1,328,128]{2,1,0:T(8,128)(2,1)S(1)}, u32[]{:S(2)}, u32[]{:S(2)}) collective-permute-start(f16[1,328,128]{2,1,0:T(8,128)(2,1)S(1)} %get-tuple-element.96), channel_id=1, source_target_pairs={{0,3},{1,2},{2,1},{3,0},{4,7},{5,6},{6,5},{7,4},{8,11},{9,10},{10,... | collective-permute-start | bytes 251912 | tf_op jit(solution)/shard_map/ppermute | solution.py:497
  129.3 10.8 %collective-permute-start.10 = (f16[1,328,128]{2,1,0:T(8,128)(2,1)S(1)}, f16[1,328,128]{2,1,0:T(8,128)(2,1)S(1)}, u32[]{:S(2)}, u32[]{:S(2)}) collective-permute-start(f16[1,328,128]{2,1,0:T(8,128)(2,1)S(1)} %get-tuple-element.95), channel_id=1, source_target_pairs={{0,4},{1,5},{2,6},{3,7},{4,0},{5,1},{6,2},{7,3},{8,12},{9,13},{10,... | collective-permute-start | bytes 251912 | tf_op jit(solution)/shard_map/ppermute | solution.py:497
  130.7 9.4 %collective-permute-start.11 = (f16[1,328,128]{2,1,0:T(8,128)(2,1)S(1)}, f16[1,328,128]{2,1,0:T(8,128)(2,1)S(1)}, u32[]{:S(2)}, u32[]{:S(2)}) collective-permute-start(f16[1,328,128]{2,1,0:T(8,128)(2,1)S(1)} %get-tuple-element.94), channel_id=1, source_target_pairs={{0,5},{1,4},{2,7},{3,6},{4,1},{5,0},{6,3},{7,2},{8,13},{9,12},{10,... | collective-permute-start | bytes 251912 | tf_op jit(solution)/shard_map/ppermute | solution.py:497
  131.0 13.8 %collective-permute-start.12 = (f16[1,328,128]{2,1,0:T(8,128)(2,1)S(1)}, f16[1,328,128]{2,1,0:T(8,128)(2,1)S(1)}, u32[]{:S(2)}, u32[]{:S(2)}) collective-permute-start(f16[1,328,128]{2,1,0:T(8,128)(2,1)S(1)} %get-tuple-element.93), channel_id=1, source_target_pairs={{0,6},{1,7},{2,4},{3,5},{4,2},{5,3},{6,0},{7,1},{8,14},{9,15},{10,... | collective-permute-start | bytes 251912 | tf_op jit(solution)/shard_map/ppermute | solution.py:497
  133.4 12.5 %copy-start.33 = (f32[128,128]{1,0:T(8,128)S(1)}, f32[128,128]{1,0:T(8,128)}, u32[]{:S(2)}) copy-start(f32[128,128]{1,0:T(8,128)} %get-tuple-element.79.dtw_ref) | copy-start | bytes 196612
  138.9 6.9 %collective-permute-start.13 = (f16[1,328,128]{2,1,0:T(8,128)(2,1)S(1)}, f16[1,328,128]{2,1,0:T(8,128)(2,1)S(1)}, u32[]{:S(2)}, u32[]{:S(2)}) collective-permute-start(f16[1,328,128]{2,1,0:T(8,128)(2,1)S(1)} %get-tuple-element.92), channel_id=1, source_target_pairs={{0,7},{1,6},{2,5},{3,4},{4,3},{5,2},{6,1},{7,0},{8,15},{9,14},{10,... | collective-permute-start | bytes 251912 | tf_op jit(solution)/shard_map/ppermute | solution.py:497
  (41 other events, 150.8 us)
Sparse Core Ops, SparseCore 0:
  9.7 81.9 all-gather.1
